TPU v7x, 128 devices: a whole 4x4x4 slice. The times are simulated.
128 devices in a mesh: prow: 16 (over y, z), pcol: 8 (over x, core).
Axes of the slice: x: 4, y: 4, z: 4, core: 2. Of those that a mesh axis runs over, the one named last changes fastest.
Arguments:
- front: float32 [4, 4096, 8, 2048], P(None, 'prow', None, 'pcol')
- child_update: bfloat16 [8192, 4096], P('prow', 'pcol'), may hold values from -6 to 6
- child_map: int32 [2, 16], replicated, may hold values from 0 to 63, as said below
- pivots: int32 [4, 256], replicated, may hold values from 0 to 255, as said below
Outputs:
- factored: float32 [4, 4096, 8, 2048], P(None, 'prow', None, 'pcol')
Inputs may be any that keep to these rules, and one draw needn't show every extreme that they name: `child_map`: each row rises strictly, consecutive entries differing by 1 or 2; row 0 begins at 0 and row 1 ends at 63. `pivots`: each row is a permutation.
All inputs are finite; a program needn't handle non-finite values.
Results may differ from a plain program's by a relative error of at most 0.0003.
Values may be sent and summed in bfloat16 or wider, within the bound.
No kernel may reach another device: no remote copies, remote signals or barrier semaphores. Data moves between devices by JAX's collectives and lax.ppermute only.
A program may use at most 128 MiB of HBM per device.

v0:
```python
import jax
import jax.numpy as jnp
from jax import lax
from jax.sharding import PartitionSpec as P

NPIV = 4
NS = 2


def from_root(value, axis, source):
    kept = jnp.where(lax.axis_index(axis) == source, value, 0).astype(value.dtype)
    return lax.psum(kept, axis)


def newton(pivot_block):
    diagonal = jnp.diagonal(pivot_block)
    approx = jnp.diag(diagonal / (diagonal * diagonal + 1.0))
    for sweep_index in range(NS):
        product = jnp.dot(
            jnp.dot(approx, pivot_block, precision=lax.Precision.HIGHEST),
            approx,
            precision=lax.Precision.HIGHEST,
        )
        approx = 2.0 * approx - product
    return approx


def shards(front, child_update, child_map, pivots):
    prow_count = lax.axis_size("prow")
    pcol_count = lax.axis_size("pcol")
    my_row = lax.axis_index("prow")
    my_col = lax.axis_index("pcol")
    row_tiles, block, col_tiles = (front.shape[0], front.shape[1], front.shape[2])
    child_blocks = child_map.shape[1]
    every_block = 2 * child_blocks
    slot_count = (every_block - 2) // prow_count + 1
    lands_here = child_map % prow_count == my_row
    hit_rank = jnp.cumsum(lands_here.astype(jnp.int32), axis=1) - 1
    slot_ids = jnp.arange(slot_count, dtype=jnp.int32)
    chosen = lands_here[:, :, None] & (hit_rank[:, :, None] == slot_ids[None, None, :])
    slot_tile = jnp.sum(jnp.where(chosen, (child_map // prow_count)[:, :, None], 0), axis=1)
    slot_used = jnp.any(chosen, axis=1)
    child_ids = jnp.arange(2, dtype=jnp.int32)
    owner_child = jnp.arange(every_block, dtype=jnp.int32) // child_blocks
    chosen_flat = jnp.transpose(chosen.reshape(every_block, slot_count))
    target = (
        (child_ids[:, None, None] == owner_child[None, None, :]) & chosen_flat[None, :, :]
    ).astype(jnp.bfloat16)
    all_blocks = jnp.arange(every_block, dtype=jnp.int32)
    shard_part = lax.all_gather(child_update, "prow", axis=0, tiled=True)
    block_count = shard_part.shape[0] // block
    block_ids = jnp.arange(block_count, dtype=jnp.int32)
    picker = (block_ids[:, None] == all_blocks[None, :]).astype(jnp.bfloat16)
    weights = jnp.einsum("chg,ug->chu", target, picker, preferred_element_type=jnp.float32).astype(
        jnp.bfloat16
    )
    tiles = shard_part.reshape(block_count, block, shard_part.shape[1])
    gathered = jnp.einsum("chu,uij->chij", weights, tiles, preferred_element_type=jnp.float32)
    packed = gathered.astype(jnp.bfloat16)
    col_hits = (
        (child_map % pcol_count == my_col)[:, :, None]
        & (
            (child_map // pcol_count)[:, :, None]
            == jnp.arange(col_tiles, dtype=jnp.int32)[None, None, :]
        )
    ).astype(jnp.bfloat16)
    row_place = (
        slot_used[:, :, None]
        & (slot_tile[:, :, None] == jnp.arange(row_tiles, dtype=jnp.int32)[None, None, :])
    ).astype(jnp.float32)
    child_range = jnp.arange(child_blocks, dtype=jnp.int32)
    shard_part = lax.all_gather(packed, "pcol", axis=3, tiled=True)
    block_count = shard_part.shape[3] // block
    block_ids = jnp.arange(block_count, dtype=jnp.int32)
    picker = (block_ids[:, None] == child_range[None, :]).astype(jnp.bfloat16)
    col_select = jnp.einsum(
        "vb,cbs->cvs", picker, col_hits, preferred_element_type=jnp.float32
    ).astype(jnp.bfloat16)
    tiles = shard_part.reshape(2, slot_count, block, block_count, block)
    col_parts = jnp.einsum(
        "cvs,chivj->chisj", col_select, tiles, preferred_element_type=jnp.float32
    )
    assembled = jnp.einsum("cht,chisj->tisj", row_place, col_parts, precision=lax.Precision.HIGHEST)
    matrix = (front + assembled).reshape(row_tiles * block, col_tiles * block)
    row_global = jnp.arange(row_tiles, dtype=jnp.int32) * prow_count + my_row
    col_global = jnp.arange(col_tiles, dtype=jnp.int32) * pcol_count + my_col
    for column_step in range(NPIV):
        root_row = column_step % prow_count
        tile_row = column_step // prow_count
        root_col = column_step % pcol_count
        tile_col = column_step // pcol_count
        row_edge = tile_row * block
        col_edge = tile_col * block
        block_row = matrix[row_edge : row_edge + block]
        block_row = jnp.where(my_row == root_row, block_row[pivots[column_step]], block_row)
        matrix = matrix.at[row_edge : row_edge + block].set(block_row)
        upper_rows = from_root(block_row, "prow", root_row)
        pivot_block = from_root(block_row[:, col_edge : col_edge + block], "prow", root_row)
        inverse = newton(pivot_block)
        column = matrix[:, col_edge : col_edge + block]
        lower_part = jnp.dot(column, inverse, precision=lax.Precision.HIGHEST)
        rows_below = jnp.repeat(row_global > column_step, block)
        lower_kept = jnp.where(rows_below[:, None], lower_part, 0.0)
        new_column = jnp.where(rows_below[:, None] & (my_col == root_col), lower_part, column)
        matrix = matrix.at[:, col_edge : col_edge + block].set(new_column)
        lower_sent = from_root(lower_kept, "pcol", root_col)
        cols_right = jnp.repeat(col_global > column_step, block)
        upper_kept = jnp.where(cols_right[None, :], upper_rows, 0.0)
        matrix = matrix - jnp.dot(lower_sent, upper_kept, precision=lax.Precision.HIGHEST)
    return matrix.reshape(row_tiles, block, col_tiles, block)


def solution(mesh):
    return jax.shard_map(
        shards,
        mesh=mesh,
        in_specs=(P(None, "prow", None, "pcol"), P("prow", "pcol"), P(), P()),
        out_specs=P(None, "prow", None, "pcol"),
        check_vma=False,
    )
```

profile of v0, /device:TPU:1, one launch (start us, length us, event | category | flops | bytes accessed | tf_op | source)
XLA Modules:
  0.0 962.5 jit_solution(6389124931580866079)
XLA Ops:
  8.4 75.2 %all-gather.3.cloned.1.call-done = bf16[8192,512]{1,0:T(8,128)(2,1)} async-done(((bf16[512,512]{1,0:T(8,128)(2,1)}), bf16[8192,512]{1,0:T(8,128)(2,1)}) %all-gather.3.cloned.1.call-update) | async-done | bytes 8388624 | tf_op jit(solution)/shard_map/all_gather | solution.py:50
  83.6 9.5 fusion.16
  93.8 53.3 %all-gather.5.cloned.1.call-done = bf16[2,2,256,4096]{3,1,2,0:T(2,128)(2,1)} async-done(((bf16[2,2,256,512]{3,1,2,0:T(2,128)(2,1)}), bf16[2,2,256,4096]{3,1,2,0:T(2,128)(2,1)}) %all-gather.5.cloned.1.call-update) | async-done | bytes 8388624 | tf_op jit(solution)/shard_map/all_gather | solution.py:72
  147.2 14.0 %reshape.426 = bf16[2,2,256,16,256]{4,3,1,2,0:T(8,128)(2,1)} reshape(bf16[2,2,256,4096]{3,1,2,0:T(2,128)(2,1)} %all-gather.5.cloned.1.call-done) | data formatting | bytes 16777216 | tf_op jit(solution)/shard_map/reshape | solution.py:79
  161.2 8.0 fusion.9
  169.2 34.2 %bitcast_add_fusion = f32[4,256,8,256]{3,0,2,1:T(4,128)} fusion(f32[4,256,8,256]{3,2,1,0:T(8,128)} %param.20, f32[2,2,256,8,256]{4,3,2,1,0:T(8,128)} %fusion.9, pred[2,2,4,1,1]{2,1,0,4,3:T(4,128)(4,1)S(1)} %fusion.149), kind=kOutput, calls=%fused_computation.8 | convolution fusion | flops 102760448 | bytes 25165840 | tf_op jit(solution)/shard_map/cht,chisj->tisj/dot_general | solution.py:83
  203.5 10.3 %slice_reduce_fusion = f32[256,8,256]{2,1,0:T(8,128)} fusion(f32[4,256,8,256]{3,0,2,1:T(4,128)} %bitcast_add_fusion), kind=kLoop, calls=%fused_computation.21 | loop fusion | bytes 4194304 | tf_op jit(solution)/shard_map/slice | solution.py:94
  219.0 3.6 broadcast_select_fusion.3
  225.9 5.0 copy.16
  230.9 7.5 copy.21
  239.9 75.0 %all-reduce.27.cloned.1.call-done = (f32[256,256]{1,0:T(8,128)}, f32[256,2048]{1,0:T(8,128)}) async-done(((f32[256,256]{1,0:T(8,128)}, f32[256,2048]{1,0:T(8,128)}), (f32[256,256]{1,0:T(8,128)}, f32[256,2048]{1,0:T(8,128)})) %all-reduce.27.cloned.1.call-update) | async-done | bytes 2359312 | tf_op jit(solution)/shard_map/psum | solution.py:12
  326.2 60.0 %all-reduce.13.cloned.1.call-done = f32[1024,256]{1,0:T(8,128)} async-done(((f32[1024,256]{1,0:T(8,128)}), f32[1024,256]{1,0:T(8,128)}) %all-reduce.13.cloned.1.call-update) | async-done | bytes 1048592 | tf_op jit(solution)/shard_map/psum | solution.py:12
  386.1 9.6 %convolution_subtract_fusion.3 = f32[1024,2048]{1,0:T(8,128)S(1)} fusion(f32[1024,2048]{1,0:T(8,128)} %get-tuple-element.126, f32[1024,256]{1,0:T(8,128)} %all-reduce.13.cloned.1.call-done, f32[256,2048]{1,0:T(8,128)S(1)} %copy-done.9, pred[2048]{0:T(1024)(128)(4,1)S(1)} %broadcast_in_dim.221), kind=kOutput, calls=%fused_computation.19 | convolution fusion | flops 6445072384 | bytes 19924992 | tf_op jit(solution)/shard_map/dot_general | solution.py:109
  407.7 91.1 %all-reduce.25.cloned.1.call-done = (f32[256,256]{1,0:T(8,128)}, f32[256,2048]{1,0:T(8,128)}) async-done(((f32[256,256]{1,0:T(8,128)}, f32[256,2048]{1,0:T(8,128)}), (f32[256,256]{1,0:T(8,128)}, f32[256,2048]{1,0:T(8,128)})) %all-reduce.25.cloned.1.call-update) | async-done | bytes 2359312 | tf_op jit(solution)/shard_map/psum | solution.py:12
  510.1 60.0 %all-reduce.15.cloned.1.call-done = f32[1024,256]{1,0:T(8,128)} async-done(((f32[1024,256]{1,0:T(8,128)}), f32[1024,256]{1,0:T(8,128)}) %all-reduce.15.cloned.1.call-update) | async-done | bytes 1048592 | tf_op jit(solution)/shard_map/psum | solution.py:12
  570.0 9.7 %convolution_subtract_fusion.2 = f32[1024,2048]{1,0:T(8,128)S(1)} fusion(f32[1024,2048]{1,0:T(8,128)} %get-tuple-element.124, f32[1024,256]{1,0:T(8,128)} %all-reduce.15.cloned.1.call-done, f32[256,2048]{1,0:T(8,128)S(1)} %copy-done.11, pred[2048]{0:T(1024)(128)(4,1)S(1)} %broadcast_in_dim.229), kind=kOutput, calls=%fused_computation.18 | convolution fusion | flops 6445072384 | bytes 19924992 | tf_op jit(solution)/shard_map/dot_general | solution.py:109
  591.7 91.1 %all-reduce.23.cloned.1.call-done = (f32[256,256]{1,0:T(8,128)}, f32[256,2048]{1,0:T(8,128)}) async-done(((f32[256,256]{1,0:T(8,128)}, f32[256,2048]{1,0:T(8,128)}), (f32[256,256]{1,0:T(8,128)}, f32[256,2048]{1,0:T(8,128)})) %all-reduce.23.cloned.1.call-update) | async-done | bytes 2359312 | tf_op jit(solution)/shard_map/psum | solution.py:12
  694.0 60.0 %all-reduce.17.cloned.1.call-done = f32[1024,256]{1,0:T(8,128)} async-done(((f32[1024,256]{1,0:T(8,128)}), f32[1024,256]{1,0:T(8,128)}) %all-reduce.17.cloned.1.call-update) | async-done | bytes 1048592 | tf_op jit(solution)/shard_map/psum | solution.py:12
  753.9 9.7 %convolution_subtract_fusion.1 = f32[1024,2048]{1,0:T(8,128)S(1)} fusion(f32[1024,2048]{1,0:T(8,128)} %get-tuple-element.122, f32[1024,256]{1,0:T(8,128)} %all-reduce.17.cloned.1.call-done, f32[256,2048]{1,0:T(8,128)S(1)} %copy-done.10, pred[2048]{0:T(1024)(128)(4,1)S(1)} %broadcast_in_dim.236), kind=kOutput, calls=%fused_computation.17 | convolution fusion | flops 6445072384 | bytes 19924992 | tf_op jit(solution)/shard_map/dot_general | solution.py:109
  775.6 91.1 %all-reduce.21.cloned.1.call-done = (f32[256,256]{1,0:T(8,128)}, f32[256,2048]{1,0:T(8,128)}) async-done(((f32[256,256]{1,0:T(8,128)}, f32[256,2048]{1,0:T(8,128)}), (f32[256,256]{1,0:T(8,128)}, f32[256,2048]{1,0:T(8,128)})) %all-reduce.21.cloned.1.call-update) | async-done | bytes 2359312 | tf_op jit(solution)/shard_map/psum | solution.py:12
  874.2 3.8 select_select_fusion.4
  878.1 60.1 %all-reduce.19.cloned.1.call-done = f32[1024,256]{1,0:T(8,128)} async-done(((f32[1024,256]{1,0:T(8,128)}), f32[1024,256]{1,0:T(8,128)}) %all-reduce.19.cloned.1.call-update) | async-done | bytes 1048592 | tf_op jit(solution)/shard_map/psum | solution.py:12
  938.2 9.5 convolution_subtract_fusion
  947.7 7.5 copy.23
  (145 shorter events, 89.1 us)
Async XLA Ops:
  6.5 77.1 %all-gather.3.cloned.1.call-start = ((), (), s32[]{:S(2)}) async-start(), calls=%async_computation | async-start | bytes 8912896 | tf_op jit(solution)/shard_map/all_gather | solution.py:50
  7.3 139.9 %all-gather.5.cloned.1.call-start = ((), (), s32[]{:S(2)}) async-start(), calls=%async_computation.1 | async-start | bytes 9437184 | tf_op jit(solution)/shard_map/all_gather | solution.py:72
  83.6 9.8 %copy-start.13 = (s32[4,256]{1,0:T(4,128)S(1)}, s32[4,256]{1,0:T(4,128)}, u32[]{:S(2)}) copy-start(s32[4,256]{1,0:T(4,128)} %param.23) | copy-start | bytes 12292
  83.6 10.0 %copy-start.14 = (s32[2,16]{1,0:T(2,128)S(1)}, s32[2,16]{1,0:T(2,128)}, u32[]{:S(2)}) copy-start(s32[2,16]{1,0:T(2,128)} %param.22) | copy-start | bytes 388
  93.1 221.8 %all-reduce.27.cloned.1.call-start = ((), (), s32[]{:S(2)}) async-start(), calls=%async_computation.9 | async-start | bytes 4718592 | tf_op jit(solution)/shard_map/psum | solution.py:12
  224.6 161.5 %all-reduce.13.cloned.1.call-start = ((), (), s32[]{:S(2)}) async-start(), calls=%async_computation.2 | async-start | bytes 2097152 | tf_op jit(solution)/shard_map/psum | solution.py:12
  230.9 7.6 copy-start.4
  314.9 4.5 copy-start.5
  322.4 63.7 %copy-start.9 = (f32[256,2048]{1,0:T(8,128)S(1)}, f32[256,2048]{1,0:T(8,128)}, u32[]{:S(2)}) copy-start(f32[256,2048]{1,0:T(8,128)} %get-tuple-element.108) | copy-start | bytes 6291460
  326.0 172.9 %all-reduce.25.cloned.1.call-start = ((), (), s32[]{:S(2)}) async-start(), calls=%async_computation.8 | async-start | bytes 4718592 | tf_op jit(solution)/shard_map/psum | solution.py:12
  395.8 3.4 copy-start.1
  406.1 163.9 %all-reduce.15.cloned.1.call-start = ((), (), s32[]{:S(2)}) async-start(), calls=%async_computation.3 | async-start | bytes 2097152 | tf_op jit(solution)/shard_map/psum | solution.py:12
  498.9 4.5 copy-start.7
  506.4 63.7 %copy-start.11 = (f32[256,2048]{1,0:T(8,128)S(1)}, f32[256,2048]{1,0:T(8,128)}, u32[]{:S(2)}) copy-start(f32[256,2048]{1,0:T(8,128)} %get-tuple-element.106) | copy-start | bytes 6291460
  509.9 172.8 %all-reduce.23.cloned.1.call-start = ((), (), s32[]{:S(2)}) async-start(), calls=%async_computation.7 | async-start | bytes 4718592 | tf_op jit(solution)/shard_map/psum | solution.py:12
  579.7 3.4 copy-start.2
  590.0 163.9 %all-reduce.17.cloned.1.call-start = ((), (), s32[]{:S(2)}) async-start(), calls=%async_computation.4 | async-start | bytes 2097152 | tf_op jit(solution)/shard_map/psum | solution.py:12
  682.7 4.5 copy-start.8
  690.2 63.7 %copy-start.10 = (f32[256,2048]{1,0:T(8,128)S(1)}, f32[256,2048]{1,0:T(8,128)}, u32[]{:S(2)}) copy-start(f32[256,2048]{1,0:T(8,128)} %get-tuple-element.104) | copy-start | bytes 6291460
  693.8 172.9 %all-reduce.21.cloned.1.call-start = ((), (), s32[]{:S(2)}) async-start(), calls=%async_computation.6 | async-start | bytes 4718592 | tf_op jit(solution)/shard_map/psum | solution.py:12
  763.6 3.4 copy-start
  774.0 164.2 %all-reduce.19.cloned.1.call-start = ((), (), s32[]{:S(2)}) async-start(), calls=%async_computation.5 | async-start | bytes 2097152 | tf_op jit(solution)/shard_map/psum | solution.py:12
  866.7 4.5 copy-start.6
  874.2 64.0 %copy-start.12 = (f32[256,2048]{1,0:T(8,128)S(1)}, f32[256,2048]{1,0:T(8,128)}, u32[]{:S(2)}) copy-start(f32[256,2048]{1,0:T(8,128)} %get-tuple-element.102) | copy-start | bytes 6291460
  (1 other events, 1.3 us)
Sparse Core Ops, SparseCore 0:
  9.5 74.0 all-gather.2
  93.3 53.8 all-gather.4
  224.7 90.1 all-reduce.26
  326.1 59.9 all-reduce.12
  406.2 92.5 all-reduce.24
  510.0 59.9 all-reduce.14
  590.2 92.5 all-reduce.22
  693.9 59.9 all-reduce.16
  774.1 92.5 all-reduce.20
  878.1 59.9 all-reduce.18
where the time goes:
time: 969 us; the launch traced here: 962 us
  waiting for transfers between devices  718 us (74%)
  matrix products  109 us (11%)
  local copies, waits for them, and re-layouts  86.8 us (9%)
  other arithmetic  33.4 us (3%)
  between operations  14.5 us (1%)
    psum x8, waiting for transfers between devices, from_root(): return lax.psum(kept, axis)  588 us
    all_gather x1, waiting for transfers between devices, shards(): shard_part = lax.all_gather(child_update, 'prow', axis=0, tiled=True)  75.2 us
    all_gather x1, waiting for transfers between devices, shards(): shard_part = lax.all_gather(packed, 'pcol', axis=3, tiled=True)  53.3 us
    dot_general x4, matrix products, shards(): jnp.dot(lower_sent, upper_kept, precision=lax.Precision.HIGHEST)  38.5 us
    dot_general x1, matrix products, shards(): jnp.einsum('cht,chisj->tisj', row_place, col_parts, precision=lax.Precisi...  34.2 us
    select_n x12, other arithmetic, from_root(): jnp.where(lax.axis_index(axis) == source, value, 0).astype(value.dtype)  30.9 us
    unnamed x33, local copies, waits for them, and re-layouts  29 us
  transfers between devices with their start and end apart: 10, of which 10 were waited for; matrix products, arithmetic and copies ran while one was open for 2% of the time, Pallas kernels for 0%

commit v1 on v0

v1 whole, which is shorter than its diff:
```python
import functools

import jax
import jax.numpy as jnp
from jax import lax
from jax.experimental import pallas as pl
from jax.experimental.pallas import tpu as pltpu
from jax.sharding import PartitionSpec as P

NPIV = 4
NS = 2
BS = 256
HALF = 128
REACH = 6.0
TOP = 30000.0
HIGHEST = lax.Precision.HIGHEST
F32 = jnp.float32
BF16 = jnp.bfloat16
F16 = jnp.float16
SMEM = pl.BlockSpec(memory_space=pltpu.SMEM)
VMEM = pl.BlockSpec(memory_space=pltpu.VMEM)
LIMIT = 60 * 1024 * 1024


def call(body, outs, ins, flops=0):
    smem = [a.dtype == jnp.int32 for a in ins]
    moved = sum(a.size * a.dtype.itemsize for a in ins)
    moved += sum(o.size * o.dtype.itemsize for o in outs)
    return pl.pallas_call(
        body,
        out_shape=outs,
        in_specs=[SMEM if flag else VMEM for flag in smem],
        out_specs=[VMEM] * len(outs),
        compiler_params=pltpu.CompilerParams(vmem_limit_bytes=LIMIT),
        cost_estimate=pl.CostEstimate(flops=flops, bytes_accessed=moved, transcendentals=0),
    )(*ins)


def shape(dims, kind):
    return jax.ShapeDtypeStruct(dims, kind)


def spot(map_ref, child, low, count, test):
    found = jnp.int32(-1)
    value = jnp.int32(-1)
    for step in range(count):
        entry = map_ref[child, low + step]
        hit = test(entry)
        found = jnp.where(hit, low + step, found)
        value = jnp.where(hit, entry, value)
    return found, value


def split(value):
    high = value.astype(BF16)
    low = (value - high.astype(F32)).astype(BF16)
    return high, low


def dot(left, right):
    return jnp.dot(left, right, preferred_element_type=F32)


def dot3(left, right):
    (a, b), (c, d) = left, right
    return dot(a, c) + (dot(a, d) + dot(b, c))


def pick_z(map_ref, rc_ref, child_ref, *out_refs):
    row = rc_ref[0]
    z = row % 4
    child = row // 8
    first = 2 * (row % 8)
    second_at = map_ref[child, first + 1] % 4
    for hop in range(4):
        which = jnp.where(second_at == (z + hop) % 4, 1, 0)
        out_refs[hop][...] = child_ref[which]
    out_refs[4][...] = child_ref[jnp.where(row == 0, 1, 0)]
    out_refs[5][...] = child_ref[jnp.where((row == 1) & (map_ref[0, 2] == 3), 0, 1)]


def held_after_z(map_ref, y, z, hop):
    source = (z - hop + 4) % 4
    child = y // 2
    first = 2 * ((4 * y + source) % 8)
    return spot(map_ref, child, first, 2, lambda entry: entry % 4 == z)


def pick_y(map_ref, rc_ref, *refs):
    held, outs = refs[:4], refs[4:]
    row = rc_ref[0]
    y, z = row // 4, row % 4
    stops = [held_after_z(map_ref, y, z, hop) for hop in range(4)]
    for shift in range(4):
        goal = (y + shift) % 4
        for hop in range(4):
            index, value = stops[hop]

            @pl.when((index >= 0) & ((value // 4) % 4 == goal))
            def _(hop=hop, shift=shift):
                outs[shift][...] = held[hop][...]


def row_of(map_ref, row, slot):
    child = slot // 2
    found, value = spot(map_ref, child, 8 * (slot % 2), 8, lambda entry: entry % 16 == row)
    return value


def col_of(map_ref, child, source, col):
    found, value = spot(map_ref, child, 4 * source, 4, lambda entry: entry % 8 == col)
    return found, value


def pick_x(map_ref, rc_ref, *refs):
    mine, other, outs = refs[:4], refs[4:8], refs[8:]
    row, col = rc_ref[0], rc_ref[1]
    y, x, core = row // 4, col // 2, col % 2
    for shift in range(4):
        child = ((y - shift + 4) % 4) // 2
        for hop in range(4):
            goal = 2 * ((x + hop) % 4) + core
            found, value = col_of(map_ref, child, x, goal)
            part = found % 4
            for half in range(2):
                cut = slice(half * BS, half * BS + BS)

                @pl.when((found >= 0) & (part == 2 * core + half))
                def _(shift=shift, hop=hop, cut=cut):
                    outs[hop][shift] = mine[shift][:, cut]

                @pl.when((found >= 0) & (part == 2 * (1 - core) + half))
                def _(shift=shift, hop=hop, cut=cut):
                    outs[hop][shift] = other[shift][:, cut]


def pick_top(map_ref, rc_ref, child_ref, a1, a2, b0, b1, b2, *outs):
    row, col = rc_ref[0], rc_ref[1]
    x, core = col // 2, col % 2
    second_first = map_ref[0, 2] == 2
    for hop in range(4):
        goal = 2 * ((x + hop) % 4) + core
        found, value = col_of(map_ref, 0, x, goal)
        part = found % 4
        for half in range(2):
            cut = slice(half * BS, half * BS + BS)
            near = (found >= 0) & (part == 2 * core + half)
            far = (found >= 0) & (part == 2 * (1 - core) + half)
            use_one = (row == 1) | ((row == 2) & second_first)
            use_two = (row == 3) | ((row == 2) & jnp.logical_not(second_first))
            for cond, here, one, two in ((near, None, a1, a2), (far, b0, b1, b2)):

                @pl.when(cond & (row == 0))
                def _(here=here, hop=hop, cut=cut):
                    source = child_ref[0] if here is None else here[...]
                    outs[hop][...] = source[:, cut]

                @pl.when(cond & use_one)
                def _(one=one, hop=hop, cut=cut):
                    outs[hop][...] = one[:, cut]

                @pl.when(cond & use_two)
                def _(two=two, hop=hop, cut=cut):
                    outs[hop][...] = two[:, cut]


def prepare_top(map_ref, rc_ref, front_ref, pivot_ref, *refs):
    parts, out_ref, work = refs[:4], refs[4], refs[5]
    row, col = rc_ref[0], rc_ref[1]
    x = col // 2

    def load(tile, carry):
        for half in range(2):
            rows = pl.ds(half * 8 + tile, BS, stride=16)
            work[tile, :, half * HALF : half * HALF + HALF] = front_ref[rows, :]
        return carry

    lax.fori_loop(0, 8, load, 0)
    has_row, value = spot(map_ref, 0, 0, 4, lambda entry: entry == row)
    for hop in range(4):
        source = (x - hop + 4) % 4
        found, value = col_of(map_ref, 0, source, col)

        @pl.when((has_row >= 0) & (found >= 0))
        def _(hop=hop, value=value):
            work[value // 8] = work[value // 8] + parts[hop][...].astype(F32)

    order = pivot_ref[...]
    spread = lax.broadcasted_iota(jnp.int32, (BS, BS), 1).astype(F32)
    select = jnp.where(order[:, :1] == spread, 1.0, 0.0).astype(BF16)

    def store(tile, carry):
        value = work[tile]
        high = value.astype(BF16)
        rest = value - high.astype(F32)
        middle = rest.astype(BF16)
        last = (rest - middle.astype(F32)).astype(BF16)
        turned = (dot(select, high) + dot(select, middle)) + dot(select, last)
        for piece in range(4):
            out_ref[piece, tile] = turned[piece * 64 : piece * 64 + 64]
        return carry

    lax.fori_loop(0, 8, store, 0)


def pick_left(map_ref, rc_ref, *refs):
    held, one, two = refs[:4], refs[4], refs[5]
    row, col = rc_ref[0], rc_ref[1]
    y = row // 4
    at_one = jnp.where(col == 0, 1, 0)
    at_two = jnp.where((col == 1) & (map_ref[0, 2] == 3), 0, 1)
    for shift in range(4):
        slot = (y - shift + 4) % 4
        for out, at in ((one, at_one), (two, at_two)):
            for half in range(2):

                @pl.when((slot < 2) & (at == half))
                def _(shift=shift, out=out, half=half, slot=slot):
                    out[slot] = held[shift][:, half * BS : half * BS + BS]


def prepare_left(map_ref, rc_ref, left_ref, top_ref, *refs):
    held, one, two, out_ref = refs[:4], refs[4], refs[5], refs[6]
    row, col = rc_ref[0], rc_ref[1]
    y = row // 4
    out_ref[...] = left_ref[...]
    found, value = spot(map_ref, 0, 0, 4, lambda entry: entry == col)
    second_first = map_ref[0, 2] == 2
    use_one = (found >= 0) & ((col == 1) | ((col == 2) & second_first))
    use_two = (found >= 0) & ((col == 3) | ((col == 2) & jnp.logical_not(second_first)))
    for shift in range(4):
        slot = (y - shift + 4) % 4
        parent = row_of(map_ref, row, slot)
        tile = parent // 16
        good = (slot < 2) & (parent >= 0)

        @pl.when(good & (col == 0))
        def _(shift=shift, tile=tile):
            out_ref[tile] = out_ref[tile] + held[shift][:, :BS].astype(F32)

        for use, part in ((use_one, one), (use_two, two)):

            @pl.when(good & use)
            def _(part=part, slot=slot, tile=tile):
                out_ref[tile] = out_ref[tile] + part[slot].astype(F32)

    @pl.when(row < NPIV)
    def _():
        for piece in range(4):
            out_ref[0, piece * 64 : piece * 64 + 64] = top_ref[piece, 0]


def high_dot(left, right):
    return jnp.dot(left, right, precision=HIGHEST, preferred_element_type=F32)


def block(step):
    return slice(step * BS, step * BS + BS)


def factor_corner(gathered_ref, out_ref, inverse_ref):
    for y in range(4):
        for z in range(4):
            for h in range(2):
                for k in range(4):
                    low = z * BS + h * HALF + y * 32
                    index = ((y * 4 + z) * 2 + h) * 4 + k
                    out_ref[low : low + 32, block(k)] = gathered_ref[index]
    diagonal = lax.broadcasted_iota(jnp.int32, (BS, BS), 0) == lax.broadcasted_iota(
        jnp.int32, (BS, BS), 1
    )
    for k in range(NPIV):
        pivot = out_ref[block(k), block(k)]
        on_line = jnp.where(diagonal, pivot, 0.0)
        approx = on_line / (on_line * on_line + 1.0)
        for sweep_index in range(NS):
            approx = 2.0 * approx - high_dot(high_dot(approx, pivot), approx)
        inverse_ref[k] = approx
        for i in range(k + 1, NPIV):
            lower = high_dot(out_ref[block(i), block(k)], approx)
            out_ref[block(i), block(k)] = lower
            for j in range(k + 1, NPIV):
                out_ref[block(i), block(j)] = out_ref[block(i), block(j)] - high_dot(
                    lower, out_ref[block(k), block(j)]
                )


def finish(
    map_ref, rc_ref, front_ref, top_ref, own_ref, left_ref, corner_ref, inverse_ref,
    p0, p1, p2, p3, out_ref, upper_hi, upper_lo, row_out, lower_hi, lower_lo, col_out,
):
    parts = (p0, p1, p2, p3)
    tile = pl.program_id(0)
    row, col = rc_ref[0], rc_ref[1]
    y, x = row // 4, col // 2

    @pl.when(tile == 0)
    def _():
        def one(s, carry):
            uppers = []
            mine = jnp.zeros((BS, BS), F32)
            for k in range(NPIV):
                raw = jnp.concatenate([top_ref[4 * piece + k, s] for piece in range(4)], axis=0)
                taken = jnp.zeros((BS, BS), F32)
                for m in range(k):
                    taken = taken + dot3(split(corner_ref[block(k), block(m)]), uppers[m])
                mine = jnp.where(row == k, taken, mine)
                high, low = split(raw - taken)
                uppers.append((high, low))
                dead = (s == 0) & (col < NPIV)
                upper_hi[s, block(k)] = jnp.where(dead, jnp.zeros_like(high), high)
                upper_lo[s, block(k)] = jnp.where(dead, jnp.zeros_like(low), low)
            own = jnp.concatenate([own_ref[piece, s] for piece in range(4)], axis=0)
            row_out[s] = own - mine
            return carry

        lax.fori_loop(0, 8, one, 0)

    def lower_step():
        lowers = []
        kept = jnp.zeros((BS, BS), F32)
        for k in range(NPIV):
            value = left_ref[k, 0]
            for m in range(k):
                value = value - dot3(lowers[m], split(corner_ref[block(m), block(k)]))
            lower = dot3(split(value), split(inverse_ref[k]))
            kept = jnp.where(col == k, lower, kept)
            lowers.append(split(lower))
            lower_hi[:, block(k)] = lowers[k][0]
            lower_lo[:, block(k)] = lowers[k][1]
        col_out[...] = kept

    lower_step()

    def at(s, half):
        return pl.ds(half * 8 + s, BS, stride=16)

    def put(s, value):
        for half in range(2):
            out_ref[0, at(s, half), :] = value[:, half * HALF : half * HALF + HALF]

    top_tile = (tile == 0) & (row < NPIV)

    @pl.when(top_tile)
    def _():
        def one(s, carry):
            put(s, row_out[s])
            return carry

        lax.fori_loop(0, 8, one, 0)

        for r in range(NPIV):
            for c in range(NPIV):

                @pl.when((row == r) & (col == c))
                def _(r=r, c=c):
                    put(0, corner_ref[block(r), block(c)])

    @pl.when(jnp.logical_not(top_tile))
    def _():
        def one(s, carry):
            total = dot(lower_hi[...], upper_hi[s])
            total = total + dot(lower_hi[...], upper_lo[s])
            total = total + dot(lower_lo[...], upper_hi[s])
            for half in range(2):
                out_ref[0, at(s, half), :] = (
                    front_ref[0, at(s, half), :] - total[:, half * HALF : half * HALF + HALF]
                )
            return carry

        lax.fori_loop(0, 8, one, 0)

        for shift in range(4):
            slot = (y - shift + 4) % 4
            parent = row_of(map_ref, row, slot)
            for hop in range(4):
                source = (x - hop + 4) % 4
                found, value = col_of(map_ref, slot // 2, source, col)

                @pl.when((parent >= 0) & (parent // 16 == tile) & (found >= 0))
                def _(shift=shift, hop=hop, s=value // 8):
                    for half in range(2):
                        out_ref[0, at(s, half), :] = out_ref[0, at(s, half), :] + parts[hop][
                            shift, :, half * HALF : half * HALF + HALF
                        ].astype(F32)

        @pl.when(col < NPIV)
        def _():
            put(0, col_out[...])


def run_finish(child_map, rc, view, top, own, left, corner, inverse, parts):
    once = pl.Buffered(1)
    whole = lambda a: pl.BlockSpec(
        a.shape, functools.partial(lambda n, t: (0,) * n, a.ndim), pipeline_mode=once
    )
    rows = pl.BlockSpec((1,) + view.shape[1:], lambda t: (t, 0, 0))
    return pl.pallas_call(
        finish,
        grid=(view.shape[0],),
        out_shape=shape(view.shape, F32),
        in_specs=[
            SMEM, SMEM, rows, whole(top), whole(own),
            pl.BlockSpec((NPIV, 1, BS, BS), lambda t: (0, t, 0, 0)),
            whole(corner), whole(inverse), *[whole(p) for p in parts],
        ],
        out_specs=rows,
        scratch_shapes=[
            pltpu.VMEM((8, 4 * BS, BS), BF16),
            pltpu.VMEM((8, 4 * BS, BS), BF16),
            pltpu.VMEM((8, BS, BS), F32),
            pltpu.VMEM((BS, 4 * BS), BF16),
            pltpu.VMEM((BS, 4 * BS), BF16),
            pltpu.VMEM((BS, BS), F32),
        ],
        compiler_params=pltpu.CompilerParams(vmem_limit_bytes=LIMIT),
        cost_estimate=pl.CostEstimate(
            flops=20 * 2**30, bytes_accessed=32 * 2**20, transcendentals=0
        ),
    )(child_map, rc, view, top, own, left, corner, inverse, *parts)


def shards(front, child_update, child_map, pivots):
    row = lax.axis_index("prow")
    col = lax.axis_index("pcol")
    y = row // 4
    rc = jnp.stack([row, col]).astype(jnp.int32)
    tiles = front.shape[0]

    def along_z(a, hop):
        return lax.ppermute(a, "prow", [(4 * i + j, 4 * i + (j + hop) % 4) for i in range(4) for j in range(4)])

    def along_y(a, hop):
        return lax.ppermute(a, "prow", [(4 * i + j, 4 * ((i + hop) % 4) + j) for i in range(4) for j in range(4)])

    def along_x(a, hop):
        return lax.ppermute(a, "pcol", [(2 * i + j, 2 * ((i + hop) % 4) + j) for i in range(4) for j in range(2)])

    def swap(a):
        return lax.ppermute(a, "pcol", [(i, i ^ 1) for i in range(8)])

    def rows_to(a, pairs, turn):
        full = [(8 * s + c, 8 * d + (c ^ turn)) for s, d in pairs for c in range(8)]
        return lax.ppermute(a, ("prow", "pcol"), full)

    edge = jnp.maximum(
        jnp.where(row < NPIV, jnp.max(jnp.abs(front[0])), 0.0),
        jnp.where(col < NPIV, jnp.max(jnp.abs(front[:, :, 0, :])), 0.0),
    )
    reach = lax.pmax(edge, ("prow", "pcol")) + REACH
    up = TOP / reach
    down = reach / TOP

    child = child_update.reshape(2, BS, 2 * BS)
    strip = shape((BS, 2 * BS), BF16)
    square = shape((BS, BS), BF16)
    z0, z1, z2, z3, t1, t2 = call(pick_z, [strip] * 6, [child_map, rc, child])

    a1 = rows_to(t1, [(0, 1), (1, 2)], 0)
    a2 = rows_to(t2, [(0, 2), (1, 3)], 0)
    b0 = rows_to(child[0], [(0, 0)], 1)
    b1 = rows_to(t1, [(0, 1), (1, 2)], 1)
    b2 = rows_to(t2, [(0, 2), (1, 3)], 1)
    tops = call(pick_top, [square] * 4, [child_map, rc, child, a1, a2, b0, b1, b2])

    def top_x(a, hop):
        full = [
            (8 * r + 2 * i + j, 8 * r + 2 * ((i + hop) % 4) + j)
            for r in range(4) for i in range(4) for j in range(2)
        ]
        return lax.ppermute(a, ("prow", "pcol"), full)

    tops = [tops[0]] + [top_x(tops[hop], hop) for hop in (1, 2, 3)]
    view = (
        front.reshape(tiles, BS, 8, 2, HALF).transpose(0, 1, 3, 2, 4).reshape(tiles, BS * 16, HALF)
    )
    order = jnp.where(
        row < NPIV,
        pivots[jnp.minimum(row, NPIV - 1)],
        jnp.arange(BS, dtype=jnp.int32),
    )
    order = jnp.broadcast_to(order.astype(F32)[:, None], (BS, HALF))
    own = pl.pallas_call(
        prepare_top,
        grid=(1,),
        out_shape=shape((4, 8, 64, BS), F32),
        in_specs=[
            SMEM, SMEM,
            pl.BlockSpec((None, BS * 16, HALF), lambda t: (0, 0, 0)),
            pl.BlockSpec((BS, HALF), lambda t: (0, 0)),
            *[pl.BlockSpec((BS, BS), lambda t: (0, 0))] * 4,
        ],
        out_specs=pl.BlockSpec((4, 8, 64, BS), lambda t: (0, 0, 0, 0)),
        scratch_shapes=[pltpu.VMEM((8, BS, BS), F32)],
        compiler_params=pltpu.CompilerParams(vmem_limit_bytes=LIMIT),
        cost_estimate=pl.CostEstimate(flops=2**30, bytes_accessed=4 * 2**20, transcendentals=0),
    )(child_map, rc, view, order, *tops)

    corner = own[:, 0].reshape(BS, BS)
    far = lax.ppermute(
        corner[HALF:], ("prow", "pcol"), [(8 * r + c, 8 * r + c + 4) for r in range(4) for c in range(4)]
    )
    part = jnp.where(col < NPIV, corner[:HALF], far)

    def from_plane(pieces):
        result = pieces[0]
        for hop in (1, 2, 3):
            moved = lax.ppermute(pieces[hop], "prow", [(j, 4 * hop + j) for j in range(4)])
            result = jnp.where(y == hop, moved, result)
        return result

    part = from_plane([part[32 * i : 32 * i + 32] for i in range(4)])
    gathered = lax.all_gather(part, ("prow", "pcol"), axis=0, tiled=False)
    corner, inverse = call(
        factor_corner,
        [shape((4 * BS, 4 * BS), F32), shape((NPIV, BS, BS), F32)],
        [gathered.reshape(128, 32, BS)],
        flops=2**32,
    )

    coded = (own * up).astype(F16)
    piece = from_plane([coded[i] for i in range(4)])
    top = lax.all_gather(piece, "prow", axis=0, tiled=False).astype(F32) * down

    zs = [z0] + [along_z(a, hop) for a, hop in ((z1, 1), (z2, 2), (z3, 3))]
    ys = call(pick_y, [strip] * 4, [child_map, rc, *zs])
    ys = [ys[0]] + [along_y(ys[hop], hop) for hop in (1, 2, 3)]

    pair = shape((2, BS, BS), BF16)
    l1, l2 = call(pick_left, [pair] * 2, [child_map, rc, *ys])

    def cols_to(a, pairs):
        return lax.ppermute(a, "pcol", pairs)

    l1 = cols_to(l1, [(0, 1), (1, 2)])
    l2 = cols_to(l2, [(0, 2), (1, 3)])
    (left,) = call(
        prepare_left,
        [shape((tiles, BS, BS), F32)],
        [child_map, rc, front[:, :, 0, :], own, *ys, l1, l2],
    )
    coded = (left * up).astype(F16)
    half = cols_to(coded[2:], [(c, c + 4) for c in range(4)])
    half = jnp.where(col < NPIV, coded[:2], half)
    left = lax.all_gather(half, "pcol", axis=0, tiled=False).astype(F32) * down
    left = left.reshape(2, 4, 2, BS, BS).transpose(1, 0, 2, 3, 4).reshape(4, 4, BS, BS)

    others = [swap(a) for a in ys]
    xs = call(pick_x, [shape((4, BS, BS), BF16)] * 4, [child_map, rc, *ys, *others])
    xs = [xs[0]] + [along_x(xs[hop], hop) for hop in (1, 2, 3)]

    done = run_finish(child_map, rc, view, top, own, left, corner, inverse, xs)
    done = done.reshape(tiles, BS, 2, 8, HALF).transpose(0, 1, 3, 2, 4)
    return done.reshape(front.shape)


def solution(mesh):
    return jax.shard_map(
        shards,
        mesh=mesh,
        in_specs=(P(None, "prow", None, "pcol"), P("prow", "pcol"), P(), P()),
        out_specs=P(None, "prow", None, "pcol"),
        check_vma=False,
    )
```

time: 969 us -> 364 us (0.38)
  waiting for transfers between devices: 718 us -> 25.2 us
  blocking collectives: 0 us -> 135 us
  matrix products: 109 us -> 0 us
  Pallas kernels: 0 us -> 85.8 us
  local copies, waits for them, and re-layouts: 86.8 us -> 16.2 us
  starting transfers between devices: 0.59 us -> 66.1 us
  other arithmetic: 33.4 us -> 14.2 us
    psum x8 -> x0, waiting for transfers between devices: 588 us -> none  [from_root(): return lax.psum(kept, axis)]
    all_gather x2 -> x1, waiting for transfers between devices: 129 us -> 0.01 us  [shards(): gathered = lax.all_gather(part, ('prow', 'pcol'), axis=0, tiled=False)]
    dot_general x27 -> x0, matrix products: 109 us -> none  [the longest x4 38.5 us: shards(): jnp.dot(lower_sent, upper_kept, precision=lax.Precision.HIGHEST)]
    pallas_call x0 -> x9, Pallas kernels: none -> 85.8 us  [the longest x1 45.9 us: run_finish(): pl.pallas_call(finish, grid=(view.shape[0],), out_shape=shape(view.shape,...]
    pmax x0 -> x1, blocking collectives: none -> 70.1 us  [shards(): reach = lax.pmax(edge, ('prow', 'pcol')) + REACH]
    ppermute x0 -> x31, starting transfers between devices: none -> 66.1 us  [the longest x5 11.8 us: rows_to(): return lax.ppermute(a, ('prow', 'pcol'), full)]
    all_gather x0 -> x2, blocking collectives: none -> 65.1 us  [the longest x1 35.6 us: shards(): left = lax.all_gather(half, 'pcol', axis=0, tiled=False).astype(F32) * down]
    select_n x15 -> x4, other arithmetic: 30.9 us -> 1.88 us  [the longest x2 1.78 us: from_plane(): result = jnp.where(y == hop, moved, result)]
  transfers between devices with their start and end apart: 10 -> 32, of which waited for: 10 -> 9; matrix products, arithmetic and copies ran while one was open for 2% -> 6% of each run, Pallas kernels for 0% -> 9%
where the time goes in v1:
time: 364 us; the launch traced here: 358 us
  blocking collectives  135 us (37%)
  Pallas kernels  85.8 us (24%)
  starting transfers between devices  66.1 us (18%)
  waiting for transfers between devices  25.2 us (7%)
  local copies, waits for them, and re-layouts  16.2 us (4%)
  between operations  15.8 us (4%)
  other arithmetic  14.2 us (4%)
    pmax x1, blocking collectives, shards(): reach = lax.pmax(edge, ('prow', 'pcol')) + REACH  70.1 us
    pallas_call x1, Pallas kernels, run_finish(): pl.pallas_call(finish, grid=(view.shape[0],), out_shape=shape(view.shape,...  45.9 us
    all_gather x1, blocking collectives, shards(): left = lax.all_gather(half, 'pcol', axis=0, tiled=False).astype(F32) * down  35.6 us
    pallas_call x7, Pallas kernels, call(): pl.pallas_call(body, out_shape=outs, in_specs=[SMEM if flag else VMEM for...  33.3 us
    all_gather x1, blocking collectives, shards(): top = lax.all_gather(piece, 'prow', axis=0, tiled=False).astype(F32) * down  29.5 us
    ppermute x5, waiting for transfers between devices, rows_to(): return lax.ppermute(a, ('prow', 'pcol'), full)  17.1 us
    ppermute x5, starting transfers between devices, rows_to(): return lax.ppermute(a, ('prow', 'pcol'), full)  11.8 us
    ppermute x3, starting transfers between devices, top_x(): return lax.ppermute(a, ('prow', 'pcol'), full)  10.5 us
  transfers between devices with their start and end apart: 32, of which 9 were waited for; matrix products, arithmetic and copies ran while one was open for 6% of the time, Pallas kernels for 9%

profile of v1, /device:TPU:1, one launch (start us, length us, event | category | flops | bytes accessed | tf_op | source)
XLA Modules:
  0.0 358.5 jit_solution(5978494993017831345)
XLA Ops:
  7.5 3.3 collective-permute-start.2
  16.1 3.5 collective-permute-start
  22.5 5.6 %collective-permute-done.a1 = bf16[256,512]{1,0:T(8,128)(2,1)S(1)} collective-permute-done((bf16[256,512]{1,0:T(8,128)(2,1)}, bf16[256,512]{1,0:T(8,128)(2,1)S(1)}, u32[]{:S(2)}, u32[]{:S(2)}) %collective-permute-start) | collective-permute-done | bytes 262176 | tf_op jit(solution)/shard_map/ppermute | solution.py:444
  28.1 5.7 %collective-permute-done.4.b2 = bf16[256,512]{1,0:T(8,128)(2,1)S(1)} collective-permute-done((bf16[256,512]{1,0:T(8,128)(2,1)}, bf16[256,512]{1,0:T(8,128)(2,1)S(1)}, u32[]{:S(2)}, u32[]{:S(2)}) %collective-permute-start.4) | collective-permute-done | bytes 262176 | tf_op jit(solution)/shard_map/ppermute | solution.py:444
  33.8 5.6 %collective-permute-done.1.a2 = bf16[256,512]{1,0:T(8,128)(2,1)S(1)} collective-permute-done((bf16[256,512]{1,0:T(8,128)(2,1)}, bf16[256,512]{1,0:T(8,128)(2,1)S(1)}, u32[]{:S(2)}, u32[]{:S(2)}) %collective-permute-start.1) | collective-permute-done | bytes 262176 | tf_op jit(solution)/shard_map/ppermute | solution.py:444
  40.1 2.6 shard_map.47
  42.7 3.1 collective-permute-start.5
  45.9 4.3 %collective-permute-start.6 = (bf16[256,256]{1,0:T(8,128)(2,1)}, bf16[256,256]{1,0:T(8,128)(2,1)S(1)}, u32[]{:S(2)}, u32[]{:S(2)}) collective-permute-start(bf16[256,256]{1,0:T(8,128)(2,1)} %get-tuple-element.31), channel_id=1, source_target_pairs={{0,4},{1,5},{2,6},{3,7},{4,0},{5,1},{6,2},{7,3},{8,12},{9,13},{10,... | collective-permute-start | bytes 393224 | tf_op jit(solution)/shard_map/ppermute | solution.py:471
  50.2 3.1 collective-permute-start.7
  56.9 6.6 %shard_map.48.top_ref.own_ref = f32[4,8,64,256]{3,2,1,0:T(8,128)} custom-call(s32[2,16]{1,0:T(2,128)} %map_ref.15, s32[2]{0:T(128)} %pad_add_fusion.rc_ref, f32[4,4096,128]{2,1,0:T(8,128)} %bitcast.43, f32[256,128]{1,0:T(8,128)} %broadcast_in_dim.2.pivot_ref, bf16[256,256]{1,0:T(8,128)(2,1)} %get-tuple-element.29.refs_0_, bf16[256,256]{1,0:T(8,128)(2,1)} %copy-done.17, ...), custom_call_target="tpu_custom_call" | custom-call | flops 1073741824 | bytes 4194304 | tf_op jit(solution)/shard_map/pallas_call | solution.py:483
  64.6 4.4 %collective-permute-start.20 = (f32[128,256]{1,0:T(8,128)S(1)}, f32[128,256]{1,0:T(8,128)S(1)}, u32[]{:S(2)}, u32[]{:S(2)}) collective-permute-start(f32[128,256]{1,0:T(8,128)S(1)} %bitcast.50), channel_id=1, source_target_pairs={{0,4},{1,5},{2,6},{3,7},{8,12},{9,13},{10,14},{11,15},{16,20},{17,... | collective-permute-start | bytes 393224 | tf_op jit(solution)/shard_map/ppermute | solution.py:500
  76.7 4.8 %collective-permute-start.12 = (bf16[256,512]{1,0:T(8,128)(2,1)}, bf16[256,512]{1,0:T(8,128)(2,1)}, u32[]{:S(2)}, u32[]{:S(2)}) collective-permute-start(bf16[256,512]{1,0:T(8,128)(2,1)} %get-tuple-element.35), channel_id=1, source_target_pairs={{0,16},{8,24},{16,0},{24,8},{32,48},{40,56},{48,32},{56,40},{64,80... | collective-permute-start | bytes 786440 | tf_op jit(solution)/shard_map/ppermute | solution.py:431
  83.5 3.9 %slice.58 = f32[4,256,1,256]{3,2,1,0:T(1,128)S(1)} slice(f32[4,256,8,256]{3,2,1,0:T(8,128)} %param.4), slice={[0:4], [0:256], [0:1], [0:256]} | slice | bytes 2097152 | tf_op jit(solution)/shard_map/slice | solution.py:448
  91.7 70.1 %pmax.7 = f32[]{:T(128)} all-reduce(f32[]{:T(128)S(6)} %max.5), channel_id=1, replica_groups=mesh['prow'=16,'pcol'=8] {'prow','pcol'}, use_global_device_ids=true, to_apply=%region_2.3 | all-reduce | flops 1 | bytes 8 | tf_op jit(solution)/shard_map/pmax | solution.py:450
  179.7 4.4 %collective-permute-start.24 = (bf16[256,512]{1,0:T(8,128)(2,1)S(1)}, bf16[256,512]{1,0:T(8,128)(2,1)S(1)}, u32[]{:S(2)}, u32[]{:S(2)}) collective-permute-start(bf16[256,512]{1,0:T(8,128)(2,1)S(1)} %copy-done.4), channel_id=1, source_target_pairs={{0,1},{1,0},{2,3},{3,2},{4,5},{5,4},{6,7},{7,6},{8,9},{9,8},{10,11... | collective-permute-start | bytes 786440 | tf_op jit(solution)/shard_map/ppermute | solution.py:440
  191.3 29.5 %all-gather.9 = f16[128,64,256]{2,1,0:T(8,128)(2,1)} all-gather(f16[8,64,256]{2,1,0:T(8,128)(2,1)S(1)} %fusion.2), channel_id=2, replica_groups=mesh['prow'=16,'pcol'=8] {'prow'}, dimensions={0}, use_global_device_ids=true | all-gather | bytes 4456448 | tf_op jit(solution)/shard_map/all_gather | solution.py:523
  220.8 4.6 %collective-permute-start.27 = (bf16[256,512]{1,0:T(8,128)(2,1)}, bf16[256,512]{1,0:T(8,128)(2,1)S(1)}, u32[]{:S(2)}, u32[]{:S(2)}) collective-permute-start(bf16[256,512]{1,0:T(8,128)(2,1)} %collective-permute-done.16.refs_3_), channel_id=1, source_target_pairs={{0,1},{1,0},{2,3},{3,2},{4,5},{5,4},{6,7},{7,6},{8,9},{9,8},{10,11... | collective-permute-start | bytes 786440 | tf_op jit(solution)/shard_map/ppermute | solution.py:440
  226.1 3.6 %shard_map.51 = f32[4,256,256]{2,1,0:T(8,128)} custom-call(s32[2,16]{1,0:T(2,128)} %map_ref.15, s32[2]{0:T(128)} %pad_add_fusion.rc_ref, f32[4,256,256]{2,1,0:T(8,128)} %bitcast.46, f32[4,8,64,256]{3,2,1,0:T(8,128)} %shard_map.48.top_ref.own_ref, bf16[256,512]{1,0:T(8,128)(2,1)} %get-tuple-element.37.refs_0_, ...), custom_call_target="tpu_custom_call" | custom-call | bytes 5767304 | tf_op jit(solution)/shard_map/pallas_call | solution.py:29
  231.2 3.5 collective-permute-start.19
  234.7 6.6 %convert_multiply_fusion = f32[128,64,256]{2,1,0:T(8,128)} fusion(f16[128,64,256]{2,1,0:T(8,128)(2,1)} %all-gather.9, f32[]{:T(128)S(6)} %div.18), kind=kLoop, calls=%fused_computation | loop fusion | flops 4194304 | bytes 12582916 | tf_op jit(solution)/shard_map/mul | solution.py:523
  242.9 3.7 %shard_map.53 = (bf16[4,256,256]{2,1,0:T(8,128)(2,1)}, bf16[4,256,256]{2,1,0:T(8,128)(2,1)}, bf16[4,256,256]{2,1,0:T(8,128)(2,1)}, bf16[4,256,256]{2,1,0:T(8,128)(2,1)}) custom-call(s32[2,16]{1,0:T(2,128)} %map_ref.15, s32[2]{0:T(128)} %pad_add_fusion.rc_ref, bf16[256,512]{1,0:T(8,128)(2,1)} %get-tuple-element.37.refs_0_, ...), custom_call_target="tpu_custom_call" | custom-call | bytes 4194440 | tf_op jit(solution)/shard_map/pallas_call | solution.py:29
  249.7 35.6 %all-gather.8 = f16[16,256,256]{2,1,0:T(8,128)(2,1)S(1)} all-gather(f16[2,256,256]{2,1,0:T(8,128)(2,1)S(1)} %slice_select_fusion), channel_id=3, replica_groups=mesh['prow'=16,'pcol'=8] {'pcol'}, dimensions={0}, use_global_device_ids=true | all-gather | bytes 2359296 | tf_op jit(solution)/shard_map/all_gather | solution.py:545
  288.1 16.5 %shard_map.52 = (f32[1024,1024]{1,0:T(8,128)}, f32[4,256,256]{2,1,0:T(8,128)}) custom-call(f32[128,32,256]{2,1,0:T(8,128)} %bitcast.52), custom_call_target="tpu_custom_call" | custom-call | flops 4294967296 | bytes 9437184 | tf_op jit(solution)/shard_map/pallas_call | solution.py:29
  305.8 45.9 %shard_map.54 = f32[4,4096,128]{2,1,0:T(8,128)} custom-call(s32[2,16]{1,0:T(2,128)} %map_ref.15, s32[2]{0:T(128)} %pad_add_fusion.rc_ref, f32[4,4096,128]{2,1,0:T(8,128)} %bitcast.44, f32[16,8,64,256]{3,2,1,0:T(8,128)} %bitcast.45, f32[4,8,64,256]{3,2,1,0:T(8,128)} %shard_map.48.top_ref.own_ref, f32[4,4,256,256]{3,2,1,0:T(8,128)} %bitcast.47, ...), custom_call_target="tpu_custom_call" | custom-call | flops 21474836480 | bytes 33554432 | tf_op jit(solution)/shard_map/pallas_call | solution.py:398
  (121 shorter events, 61.9 us)
Async XLA Ops:
  6.5 281.5 %all-gather.7.cloned.1.call-start = ((), (), s32[]{:S(2)}) async-start(), calls=%async_computation | async-start | bytes 4227072 | tf_op jit(solution)/shard_map/all_gather | solution.py:513
  7.5 14.8 %collective-permute-start.2 = (bf16[256,512]{1,0:T(8,128)(2,1)S(1)}, bf16[256,512]{1,0:T(8,128)(2,1)S(1)}, u32[]{:S(2)}, u32[]{:S(2)}) collective-permute-start(bf16[256,512]{1,0:T(8,128)(2,1)S(1)} %slice.56), channel_id=1, source_target_pairs={{0,1},{1,0},{2,3},{3,2},{4,5},{5,4},{6,7},{7,6}} | collective-permute-start | bytes 786440 | tf_op jit(solution)/shard_map/ppermute | solution.py:444
  16.1 12.0 %collective-permute-start = (bf16[256,512]{1,0:T(8,128)(2,1)}, bf16[256,512]{1,0:T(8,128)(2,1)S(1)}, u32[]{:S(2)}, u32[]{:S(2)}) collective-permute-start(bf16[256,512]{1,0:T(8,128)(2,1)} %get-tuple-element.27), channel_id=1, source_target_pairs={{0,8},{1,9},{2,10},{3,11},{4,12},{5,13},{6,14},{7,15},{8,16},{9,17... | collective-permute-start | bytes 786440 | tf_op jit(solution)/shard_map/ppermute | solution.py:444
  19.7 14.1 %collective-permute-start.4 = (bf16[256,512]{1,0:T(8,128)(2,1)}, bf16[256,512]{1,0:T(8,128)(2,1)S(1)}, u32[]{:S(2)}, u32[]{:S(2)}) collective-permute-start(bf16[256,512]{1,0:T(8,128)(2,1)} %get-tuple-element.28), channel_id=1, source_target_pairs={{0,17},{1,16},{2,19},{3,18},{4,21},{5,20},{6,23},{7,22},{8,25},{9,... | collective-permute-start | bytes 786440 | tf_op jit(solution)/shard_map/ppermute | solution.py:444
  21.0 18.4 %collective-permute-start.1 = (bf16[256,512]{1,0:T(8,128)(2,1)}, bf16[256,512]{1,0:T(8,128)(2,1)S(1)}, u32[]{:S(2)}, u32[]{:S(2)}) collective-permute-start(bf16[256,512]{1,0:T(8,128)(2,1)} %get-tuple-element.28), channel_id=1, source_target_pairs={{0,16},{1,17},{2,18},{3,19},{4,20},{5,21},{6,22},{7,23},{8,24},{9,... | collective-permute-start | bytes 786440 | tf_op jit(solution)/shard_map/ppermute | solution.py:444
  42.7 10.6 %collective-permute-start.5 = (bf16[256,256]{1,0:T(8,128)(2,1)}, bf16[256,256]{1,0:T(8,128)(2,1)S(1)}, u32[]{:S(2)}, u32[]{:S(2)}) collective-permute-start(bf16[256,256]{1,0:T(8,128)(2,1)} %get-tuple-element.30), channel_id=1, source_target_pairs={{0,2},{1,3},{2,4},{3,5},{4,6},{5,7},{6,0},{7,1},{8,10},{9,11},{10,... | collective-permute-start | bytes 393224 | tf_op jit(solution)/shard_map/ppermute | solution.py:471
  76.6 85.9 %collective-permute-start.11 = (bf16[256,512]{1,0:T(8,128)(2,1)}, bf16[256,512]{1,0:T(8,128)(2,1)S(1)}, u32[]{:S(2)}, u32[]{:S(2)}) collective-permute-start(bf16[256,512]{1,0:T(8,128)(2,1)} %get-tuple-element.34), channel_id=1, source_target_pairs={{0,8},{8,16},{16,24},{24,0},{32,40},{40,48},{48,56},{56,32},{64,72... | collective-permute-start | bytes 786440 | tf_op jit(solution)/shard_map/ppermute | solution.py:431
  76.7 85.8 %collective-permute-start.12 = (bf16[256,512]{1,0:T(8,128)(2,1)}, bf16[256,512]{1,0:T(8,128)(2,1)}, u32[]{:S(2)}, u32[]{:S(2)}) collective-permute-start(bf16[256,512]{1,0:T(8,128)(2,1)} %get-tuple-element.35), channel_id=1, source_target_pairs={{0,16},{8,24},{16,0},{24,8},{32,48},{40,56},{48,32},{56,40},{64,80... | collective-permute-start | bytes 786440 | tf_op jit(solution)/shard_map/ppermute | solution.py:431
  81.5 81.0 %collective-permute-start.13 = (bf16[256,512]{1,0:T(8,128)(2,1)}, bf16[256,512]{1,0:T(8,128)(2,1)}, u32[]{:S(2)}, u32[]{:S(2)}) collective-permute-start(bf16[256,512]{1,0:T(8,128)(2,1)} %get-tuple-element.36), channel_id=1, source_target_pairs={{0,24},{8,0},{16,8},{24,16},{32,56},{40,32},{48,40},{56,48},{64,88... | collective-permute-start | bytes 786440 | tf_op jit(solution)/shard_map/ppermute | solution.py:431
  165.6 14.1 %collective-permute-start.15 = (bf16[256,512]{1,0:T(8,128)(2,1)}, bf16[256,512]{1,0:T(8,128)(2,1)}, u32[]{:S(2)}, u32[]{:S(2)}) collective-permute-start(bf16[256,512]{1,0:T(8,128)(2,1)} %get-tuple-element.39), channel_id=1, source_target_pairs={{0,64},{8,72},{16,80},{24,88},{32,96},{40,104},{48,112},{56,120},{... | collective-permute-start | bytes 786440 | tf_op jit(solution)/shard_map/ppermute | solution.py:434
  167.4 16.6 %collective-permute-start.16 = (bf16[256,512]{1,0:T(8,128)(2,1)}, bf16[256,512]{1,0:T(8,128)(2,1)}, u32[]{:S(2)}, u32[]{:S(2)}) collective-permute-start(bf16[256,512]{1,0:T(8,128)(2,1)} %get-tuple-element.40), channel_id=1, source_target_pairs={{0,96},{8,104},{16,112},{24,120},{32,0},{40,8},{48,16},{56,24},{64... | collective-permute-start | bytes 786440 | tf_op jit(solution)/shard_map/ppermute | solution.py:434
  170.5 17.6 %collective-permute-start.10 = (f16[8,64,256]{2,1,0:T(8,128)(2,1)S(1)}, f16[8,64,256]{2,1,0:T(8,128)(2,1)S(1)}, u32[]{:S(2)}, u32[]{:S(2)}) collective-permute-start(f16[8,64,256]{2,1,0:T(8,128)(2,1)S(1)} %get-tuple-element.51), channel_id=1, source_target_pairs={{0,32},{8,40},{16,48},{24,56},{1,33},{9,41},{17,49},{25,57},{2,34}... | collective-permute-start | bytes 786440 | tf_op jit(solution)/shard_map/ppermute | solution.py:508
  172.3 17.1 %collective-permute-start.9 = (f16[8,64,256]{2,1,0:T(8,128)(2,1)S(1)}, f16[8,64,256]{2,1,0:T(8,128)(2,1)S(1)}, u32[]{:S(2)}, u32[]{:S(2)}) collective-permute-start(f16[8,64,256]{2,1,0:T(8,128)(2,1)S(1)} %get-tuple-element.52), channel_id=1, source_target_pairs={{0,64},{8,72},{16,80},{24,88},{1,65},{9,73},{17,81},{25,89},{2,66}... | collective-permute-start | bytes 786440 | tf_op jit(solution)/shard_map/ppermute | solution.py:508
  174.7 15.3 %collective-permute-start.8 = (f16[8,64,256]{2,1,0:T(8,128)(2,1)S(1)}, f16[8,64,256]{2,1,0:T(8,128)(2,1)S(1)}, u32[]{:S(2)}, u32[]{:S(2)}) collective-permute-start(f16[8,64,256]{2,1,0:T(8,128)(2,1)S(1)} %get-tuple-element.53), channel_id=1, source_target_pairs={{0,96},{8,104},{16,112},{24,120},{1,97},{9,105},{17,113},{25,121},... | collective-permute-start | bytes 786440 | tf_op jit(solution)/shard_map/ppermute | solution.py:508
  179.7 61.6 %collective-permute-start.24 = (bf16[256,512]{1,0:T(8,128)(2,1)S(1)}, bf16[256,512]{1,0:T(8,128)(2,1)S(1)}, u32[]{:S(2)}, u32[]{:S(2)}) collective-permute-start(bf16[256,512]{1,0:T(8,128)(2,1)S(1)} %copy-done.4), channel_id=1, source_target_pairs={{0,1},{1,0},{2,3},{3,2},{4,5},{5,4},{6,7},{7,6},{8,9},{9,8},{10,11... | collective-permute-start | bytes 786440 | tf_op jit(solution)/shard_map/ppermute | solution.py:440
  186.2 34.6 %collective-permute-start.17 = (bf16[2,256,256]{2,1,0:T(8,128)(2,1)}, bf16[2,256,256]{2,1,0:T(8,128)(2,1)S(1)}, u32[]{:S(2)}, u32[]{:S(2)}) collective-permute-start(bf16[2,256,256]{2,1,0:T(8,128)(2,1)} %get-tuple-element.41), channel_id=1, source_target_pairs={{0,1},{1,2},{8,9},{9,10},{16,17},{17,18},{24,25},{25,26},{32,33},{... | collective-permute-start | bytes 786440 | tf_op jit(solution)/shard_map/ppermute | solution.py:533
  188.1 37.3 %collective-permute-start.18 = (bf16[2,256,256]{2,1,0:T(8,128)(2,1)}, bf16[2,256,256]{2,1,0:T(8,128)(2,1)S(1)}, u32[]{:S(2)}, u32[]{:S(2)}) collective-permute-start(bf16[2,256,256]{2,1,0:T(8,128)(2,1)} %get-tuple-element.42), channel_id=1, source_target_pairs={{0,2},{1,3},{8,10},{9,11},{16,18},{17,19},{24,26},{25,27},{32,34},... | collective-permute-start | bytes 786440 | tf_op jit(solution)/shard_map/ppermute | solution.py:533
  189.4 51.9 %collective-permute-start.25 = (bf16[256,512]{1,0:T(8,128)(2,1)}, bf16[256,512]{1,0:T(8,128)(2,1)S(1)}, u32[]{:S(2)}, u32[]{:S(2)}) collective-permute-start(bf16[256,512]{1,0:T(8,128)(2,1)} %collective-permute-done.14.refs_1_), channel_id=1, source_target_pairs={{0,1},{1,0},{2,3},{3,2},{4,5},{5,4},{6,7},{7,6},{8,9},{9,8},{10,11... | collective-permute-start | bytes 786440 | tf_op jit(solution)/shard_map/ppermute | solution.py:440
  190.0 51.3 %collective-permute-start.26 = (bf16[256,512]{1,0:T(8,128)(2,1)}, bf16[256,512]{1,0:T(8,128)(2,1)S(1)}, u32[]{:S(2)}, u32[]{:S(2)}) collective-permute-start(bf16[256,512]{1,0:T(8,128)(2,1)} %collective-permute-done.15.refs_2_), channel_id=1, source_target_pairs={{0,1},{1,0},{2,3},{3,2},{4,5},{5,4},{6,7},{7,6},{8,9},{9,8},{10,11... | collective-permute-start | bytes 786440 | tf_op jit(solution)/shard_map/ppermute | solution.py:440
  220.8 20.5 %collective-permute-start.27 = (bf16[256,512]{1,0:T(8,128)(2,1)}, bf16[256,512]{1,0:T(8,128)(2,1)S(1)}, u32[]{:S(2)}, u32[]{:S(2)}) collective-permute-start(bf16[256,512]{1,0:T(8,128)(2,1)} %collective-permute-done.16.refs_3_), channel_id=1, source_target_pairs={{0,1},{1,0},{2,3},{3,2},{4,5},{5,4},{6,7},{7,6},{8,9},{9,8},{10,11... | collective-permute-start | bytes 786440 | tf_op jit(solution)/shard_map/ppermute | solution.py:440
  231.2 18.5 %collective-permute-start.19 = (f16[2,256,256]{2,1,0:T(8,128)(2,1)S(1)}, f16[2,256,256]{2,1,0:T(8,128)(2,1)S(1)}, u32[]{:S(2)}, u32[]{:S(2)}) collective-permute-start(f16[2,256,256]{2,1,0:T(8,128)(2,1)S(1)} %slice.78), channel_id=1, source_target_pairs={{0,4},{1,5},{2,6},{3,7},{8,12},{9,13},{10,14},{11,15},{16,20},{17,... | collective-permute-start | bytes 786440 | tf_op jit(solution)/shard_map/ppermute | solution.py:533
  246.6 58.0 %collective-permute-start.28 = (bf16[4,256,256]{2,1,0:T(8,128)(2,1)}, bf16[4,256,256]{2,1,0:T(8,128)(2,1)S(1)}, u32[]{:S(2)}, u32[]{:S(2)}) collective-permute-start(bf16[4,256,256]{2,1,0:T(8,128)(2,1)} %get-tuple-element.46), channel_id=1, source_target_pairs={{0,2},{1,3},{2,4},{3,5},{4,6},{5,7},{6,0},{7,1},{8,10},{9,11},{10,... | collective-permute-start | bytes 1572872 | tf_op jit(solution)/shard_map/ppermute | solution.py:437
  247.2 57.4 %collective-permute-start.29 = (bf16[4,256,256]{2,1,0:T(8,128)(2,1)}, bf16[4,256,256]{2,1,0:T(8,128)(2,1)S(1)}, u32[]{:S(2)}, u32[]{:S(2)}) collective-permute-start(bf16[4,256,256]{2,1,0:T(8,128)(2,1)} %get-tuple-element.47), channel_id=1, source_target_pairs={{0,4},{1,5},{2,6},{3,7},{4,0},{5,1},{6,2},{7,3},{8,12},{9,13},{10,... | collective-permute-start | bytes 1572872 | tf_op jit(solution)/shard_map/ppermute | solution.py:437
  247.2 57.4 %collective-permute-start.30 = (bf16[4,256,256]{2,1,0:T(8,128)(2,1)}, bf16[4,256,256]{2,1,0:T(8,128)(2,1)S(1)}, u32[]{:S(2)}, u32[]{:S(2)}) collective-permute-start(bf16[4,256,256]{2,1,0:T(8,128)(2,1)} %get-tuple-element.48), channel_id=1, source_target_pairs={{0,6},{1,7},{2,0},{3,1},{4,2},{5,3},{6,4},{7,5},{8,14},{9,15},{10,... | collective-permute-start | bytes 1572872 | tf_op jit(solution)/shard_map/ppermute | solution.py:437
  (31 other events, 300.1 us)
Sparse Core Ops, SparseCore 0:
  76.7 74.6 all-gather.6

commit v2 on v0

v2 whole, which is shorter than its diff:
```python
import functools

import jax
import jax.numpy as jnp
from jax import lax
from jax.experimental import pallas as pl
from jax.experimental.pallas import tpu as pltpu
from jax.sharding import PartitionSpec as P

NPIV = 4
NS = 2
BS = 256
HALF = 128
PIECE = 64
FULL = 32767.0
HIGHEST = lax.Precision.HIGHEST
F32 = jnp.float32
BF16 = jnp.bfloat16
I16 = jnp.int16
I32 = jnp.int32
SMEM = pl.BlockSpec(memory_space=pltpu.SMEM)
VMEM = pl.BlockSpec(memory_space=pltpu.VMEM)
LIMIT = 56 * 1024 * 1024


def shape(dims, kind):
    return jax.ShapeDtypeStruct(dims, kind)


def call(body, outs, ins, smem=2, flops=0, scratch=()):
    moved = sum(a.size * a.dtype.itemsize for a in ins)
    moved += sum(o.size * o.dtype.itemsize for o in outs)
    return pl.pallas_call(
        body,
        out_shape=outs,
        in_specs=[SMEM] * smem + [VMEM] * (len(ins) - smem),
        out_specs=[VMEM] * len(outs),
        scratch_shapes=list(scratch),
        compiler_params=pltpu.CompilerParams(vmem_limit_bytes=LIMIT),
        cost_estimate=pl.CostEstimate(flops=flops, bytes_accessed=moved, transcendentals=0),
    )(*ins)


def spot(map_ref, child, low, count, test):
    found = jnp.int32(-1)
    value = jnp.int32(-1)
    for step in range(count):
        entry = map_ref[child, low + step]
        hit = test(entry)
        found = jnp.where(hit, low + step, found)
        value = jnp.where(hit, entry, value)
    return found, value


def row_of(map_ref, row, slot):
    return spot(map_ref, slot // 2, 8 * (slot % 2), 8, lambda entry: entry % 16 == row)[1]


def col_of(map_ref, child, source, col):
    return spot(map_ref, child, 4 * source, 4, lambda entry: entry % 8 == col)


def split(value):
    high = value.astype(BF16)
    low = (value - high.astype(F32)).astype(BF16)
    return high, low


def dot(left, right):
    return jnp.dot(left, right, preferred_element_type=F32)


def dot3(left, right):
    (a, b), (c, d) = left, right
    return dot(a, c) + (dot(a, d) + dot(b, c))


def high_dot(left, right):
    return jnp.dot(left, right, precision=HIGHEST, preferred_element_type=F32)


def block(step):
    return slice(step * BS, step * BS + BS)


def one_hot(order):
    spread = lax.broadcasted_iota(I32, (BS, BS), 1).astype(F32)
    return jnp.where(order[:, :1] == spread, 1.0, 0.0).astype(BF16)


def reorder(select, value):
    high = value.astype(BF16)
    rest = value - high.astype(F32)
    middle = rest.astype(BF16)
    last = (rest - middle.astype(F32)).astype(BF16)
    return (dot(select, high) + dot(select, middle)) + dot(select, last)


def level(peak):
    return jnp.ceil(jnp.log2(jnp.full((8, HALF), jnp.maximum(peak, 1e-30))) * 4.0)


def encode(value, n):
    scaled = jnp.abs(value) * jnp.exp2(n * -0.25)[:1, :1]
    code = jnp.minimum(jnp.floor(jnp.sqrt(scaled) * FULL + 0.5), FULL)
    return jnp.where(value < 0.0, -code, code).astype(I32)


def decode(code, n):
    code = code.astype(F32)
    return code * jnp.abs(code) * (jnp.exp2(n.astype(F32)[:1, :1] * 0.25) * (1.0 / (FULL * FULL)))


def cut_front(front_ref, order_ref, *outs):
    select = one_hot(order_ref[...])

    def one(tile, carry):
        halves = [front_ref[pl.ds(half * 8 + tile, BS, stride=16), :] for half in range(2)]
        turned = reorder(select, jnp.concatenate(halves, axis=1))
        for piece in range(4):
            outs[piece][tile] = turned[piece * PIECE : piece * PIECE + PIECE]
        return carry

    lax.fori_loop(0, 8, one, 0)


def pick_rows(map_ref, rc_ref, order_ref, held, *outs):
    pieces, hops = outs[:4], outs[4:]
    row = rc_ref[0]
    y, z = row // 4, row % 4
    found, value = spot(map_ref, 0, 0, 4, lambda entry: entry == row)
    live = (found >= 0) & (row < NPIV)
    at = jnp.maximum(found, 0)

    @pl.when(live)
    def _():
        turned = dot(one_hot(order_ref[...]), held[at // 2, at % 2]).astype(BF16)
        for piece in range(4):
            pieces[piece][...] = turned[piece * PIECE : piece * PIECE + PIECE]

    @pl.when(jnp.logical_not(live))
    def _():
        for piece in range(4):
            pieces[piece][...] = jnp.zeros((PIECE, 2 * BS), BF16)

    low = 8 * (y % 2)
    for shift in range(4):
        goal = 4 * ((y + shift) % 4) + z
        index, value = spot(map_ref, y // 2, low, 8, lambda entry: entry % 16 == goal)
        index = jnp.maximum(index - low, 0)
        hops[shift][...] = held[index // 2, index % 2]


def assemble(map_ref, rc_ref, f0, f1, f2, f3, strip, code_ref, corner_ref, work):
    row, col = rc_ref[0], rc_ref[1]
    y = row // 4
    for piece, source in enumerate((f0, f1, f2, f3)):

        @pl.when(y == piece)
        def _(source=source):
            work[...] = source[...]

    for index in range(16):
        parent = map_ref[0, index]
        cut = slice((index % 2) * BS, (index % 2) * BS + BS)

        @pl.when(parent % 8 == col)
        def _(index=index, cut=cut, tile=parent // 8):
            work[tile] = work[tile] + strip[index // 2, :, cut].astype(F32)

    corner_ref[...] = work[0]

    @pl.when(col < NPIV)
    def _():
        work[0] = jnp.zeros((PIECE, BS), F32)

    n = level(jnp.max(jnp.abs(work[...])))
    for tile in range(8):
        code_ref[tile * PIECE : tile * PIECE + PIECE] = encode(work[tile], n).astype(I16)
    code_ref[8 * PIECE :] = jnp.broadcast_to(n[:1, :1].astype(I32), (16, BS)).astype(I16)


def pick_left(map_ref, rc_ref, *refs):
    held, one, two = refs[:4], refs[4], refs[5]
    row, col = rc_ref[0], rc_ref[1]
    y = row // 4
    at_one = jnp.where(col == 0, 1, 0)
    at_two = jnp.where((col == 1) & (map_ref[0, 2] == 3), 0, 1)
    for shift in range(4):
        slot = (y - shift + 4) % 4
        for out, at in ((one, at_one), (two, at_two)):
            for half in range(2):

                @pl.when((slot < 2) & (at == half))
                def _(shift=shift, out=out, half=half, slot=slot):
                    out[slot] = held[shift][:, half * BS : half * BS + BS]


def prepare_left(map_ref, rc_ref, left_ref, *refs):
    held, one, two, near, far, work = refs[:4], refs[4], refs[5], refs[6], refs[7], refs[8]
    row, col = rc_ref[0], rc_ref[1]
    y = row // 4
    work[...] = left_ref[...]
    found, value = spot(map_ref, 0, 0, 4, lambda entry: entry == col)
    second_first = map_ref[0, 2] == 2
    use_one = (found >= 0) & ((col == 1) | ((col == 2) & second_first))
    use_two = (found >= 0) & ((col == 3) | ((col == 2) & jnp.logical_not(second_first)))
    for shift in range(4):
        slot = (y - shift + 4) % 4
        parent = row_of(map_ref, row, slot)
        tile = parent // 16
        good = (slot < 2) & (parent >= 0)

        @pl.when(good & (col == 0))
        def _(shift=shift, tile=tile):
            work[tile] = work[tile] + held[shift][:, :BS].astype(F32)

        for use, part in ((use_one, one), (use_two, two)):

            @pl.when(good & use)
            def _(part=part, slot=slot, tile=tile):
                work[tile] = work[tile] + part[slot].astype(F32)

    @pl.when(row < NPIV)
    def _():
        work[0] = jnp.zeros((BS, BS), F32)

    n = level(jnp.max(jnp.abs(work[...])))
    for out, first in ((near, 0), (far, 1)):
        out[:BS] = encode(work[first], n) * 65536 + (encode(work[first + 2], n) & 65535)
        out[BS:] = jnp.broadcast_to(n[:1, :1].astype(I32), (8, BS))


def pick_x(map_ref, rc_ref, *refs):
    mine, other, outs = refs[:4], refs[4:8], refs[8:]
    row, col = rc_ref[0], rc_ref[1]
    y, x, core = row // 4, col // 2, col % 2
    for shift in range(4):
        child = ((y - shift + 4) % 4) // 2
        for hop in range(4):
            goal = 2 * ((x + hop) % 4) + core
            found, value = col_of(map_ref, child, x, goal)
            part = found % 4
            for half in range(2):
                cut = slice(half * BS, half * BS + BS)

                @pl.when((found >= 0) & (part == 2 * core + half))
                def _(shift=shift, hop=hop, cut=cut):
                    outs[hop][shift] = mine[shift][:, cut]

                @pl.when((found >= 0) & (part == 2 * (1 - core) + half))
                def _(shift=shift, hop=hop, cut=cut):
                    outs[hop][shift] = other[shift][:, cut]


def factor_corner(gathered, out_ref, inverse_ref):
    for h in range(2):
        for k in range(4):
            for y in range(4):
                for z in range(4):
                    low = z * BS + y * PIECE + h * 32
                    out_ref[low : low + 32, block(k)] = gathered[4 * h + k, 4 * y + z]
    diagonal = lax.broadcasted_iota(I32, (BS, BS), 0) == lax.broadcasted_iota(I32, (BS, BS), 1)
    for k in range(NPIV):
        pivot = out_ref[block(k), block(k)]
        on_line = jnp.where(diagonal, pivot, 0.0)
        across = jnp.sum(on_line, axis=0, keepdims=True)
        down = jnp.sum(on_line, axis=1, keepdims=True)
        across = across / (across * across + 1.0)
        down = down / (down * down + 1.0)
        approx = 2.0 * jnp.where(diagonal, across, 0.0) - (down * pivot) * across
        for sweep_index in range(NS - 1):
            approx = 2.0 * approx - high_dot(high_dot(approx, pivot), approx)
        inverse_ref[k] = approx
        if k + 1 < NPIV:
            below = slice((k + 1) * BS, NPIV * BS)
            lower = dot3(split(out_ref[below, block(k)]), split(approx))
            out_ref[below, block(k)] = lower
            out_ref[below, below] = out_ref[below, below] - dot3(
                split(lower), split(out_ref[block(k), below])
            )


def upper_rows(rc_ref, corner_ref, code_ref, high_ref, low_ref, taken_ref):
    row, col = rc_ref[0], rc_ref[1]
    high_parts = {}

    def one(tile, carry):
        uppers = []
        mine = jnp.zeros((BS, BS), F32)
        low = pl.multiple_of(tile * PIECE, PIECE)
        for k in range(NPIV):
            raw = jnp.concatenate(
                [
                    decode(
                        code_ref[4 * piece + k, pl.ds(low, PIECE), :].astype(I32),
                        code_ref[4 * piece + k, 8 * PIECE :, :].astype(I32),
                    )
                    for piece in range(4)
                ],
                axis=0,
            )
            taken = jnp.zeros((BS, BS), F32)
            for m in range(k):
                taken = taken + dot3(split(corner_ref[block(k), block(m)]), uppers[m])
            mine = jnp.where(row == k, taken, mine)
            uppers.append(split(raw - taken))
            high_ref[tile, block(k)] = uppers[k][0]
            low_ref[tile, block(k)] = uppers[k][1]
        taken_ref[tile] = mine
        return carry

    lax.fori_loop(0, 8, one, 0)


def lower_cols(rc_ref, corner_ref, inverse_ref, code_ref, high_ref, low_ref, own_ref):
    row, col = rc_ref[0], rc_ref[1]
    lowers = []
    kept = jnp.zeros((4 * BS, BS), F32)
    for k in range(NPIV):
        tiles = []
        for tile in range(4):
            word = code_ref[4 * (tile % 2) + k, :BS]
            if tile >= 2:
                word = lax.shift_left(word, 16)
            tiles.append(
                decode(lax.shift_right_arithmetic(word, 16), code_ref[4 * (tile % 2) + k, BS:])
            )
        value = jnp.concatenate(tiles, axis=0)
        for m in range(k):
            value = value - dot3(lowers[m], split(corner_ref[block(m), block(k)]))
        lower = dot3(split(value), split(inverse_ref[k]))
        kept = jnp.where(col == k, lower, kept)
        lowers.append(split(lower))
        high_ref[:, block(k)] = lowers[k][0]
        low_ref[:, block(k)] = lowers[k][1]
    own_ref[...] = kept


SPAN = 2


def finish(
    map_ref, rc_ref, front_ref, high_ref, low_ref, left_high, left_low, own_ref, taken_ref,
    corner_ref, order_ref, p0, p1, p2, p3, out_ref,
):
    parts = (p0, p1, p2, p3)
    step = pl.program_id(0)
    row, col = rc_ref[0], rc_ref[1]
    y, x = row // 4, col // 2

    def at(s, half, tile=0, count=1):
        return pl.ds(tile * BS * 16 + half * 8 + s, count * BS, stride=16)

    def put(s, tile, value):
        for half in range(2):
            out_ref[at(s, half, tile), :] = value[:, half * HALF : half * HALF + HALF]

    def one(s, carry):
        total = dot(left_high[...], high_ref[s])
        total = total + dot(left_high[...], low_ref[s])
        total = total + dot(left_low[...], high_ref[s])
        for half in range(2):
            rows = at(s, half, 0, SPAN)
            out_ref[rows, :] = front_ref[rows, :] - total[:, half * HALF : half * HALF + HALF]
        return carry

    lax.fori_loop(0, 8, one, 0)

    for shift in range(4):
        slot = (y - shift + 4) % 4
        parent = row_of(map_ref, row, slot)
        for hop in range(4):
            source = (x - hop + 4) % 4
            found, value = col_of(map_ref, slot // 2, source, col)
            for tile in range(SPAN):

                @pl.when((parent >= 0) & (parent // 16 == SPAN * step + tile) & (found >= 0))
                def _(shift=shift, hop=hop, tile=tile, s=value // 8):
                    for half in range(2):
                        rows = at(s, half, tile)
                        lanes = slice(half * HALF, half * HALF + HALF)
                        out_ref[rows, :] = out_ref[rows, :] + parts[hop][shift, :, lanes].astype(F32)

    @pl.when(col < NPIV)
    def _():
        for tile in range(SPAN):
            put(0, tile, own_ref[tile * BS : tile * BS + BS])

    @pl.when((step == 0) & (row < NPIV))
    def _():
        select = one_hot(order_ref[...])

        def turn(s, carry):
            value = jnp.concatenate([out_ref[at(s, half), :] for half in range(2)], axis=1)
            put(s, 0, reorder(select, value) - taken_ref[s])
            return carry

        lax.fori_loop(0, 8, turn, 0)

        for r in range(NPIV):
            for c in range(NPIV):

                @pl.when((row == r) & (col == c))
                def _(r=r, c=c):
                    put(0, 0, corner_ref[block(r), block(c)])


def run_finish(child_map, rc, view, upper, lower, own, taken, corner, order, parts):
    once = pl.Buffered(1)
    whole = lambda a: pl.BlockSpec(
        a.shape, functools.partial(lambda n, t: (0,) * n, a.ndim), pipeline_mode=once
    )
    rows = pl.BlockSpec((SPAN * BS * 16, HALF), lambda t: (t, 0))
    lefts = pl.BlockSpec((SPAN * BS, 4 * BS), lambda t: (t, 0))
    return pl.pallas_call(
        finish,
        grid=(4 // SPAN,),
        out_shape=shape(view.shape, F32),
        in_specs=[
            SMEM, SMEM, rows, whole(upper[0]), whole(upper[1]), lefts, lefts,
            pl.BlockSpec((SPAN * BS, BS), lambda t: (t, 0)),
            whole(taken), whole(corner), whole(order), *[whole(p) for p in parts],
        ],
        out_specs=rows,
        compiler_params=pltpu.CompilerParams(vmem_limit_bytes=LIMIT),
        cost_estimate=pl.CostEstimate(
            flops=13 * 2**30, bytes_accessed=32 * 2**20, transcendentals=0
        ),
    )(child_map, rc, view, *upper, *lower, own, taken, corner, order, *parts)


def shards(front, child_update, child_map, pivots):
    row = lax.axis_index("prow")
    col = lax.axis_index("pcol")
    y = row // 4
    rc = jnp.stack([row, col]).astype(I32)
    tiles = front.shape[0]
    planes = [[4 * i + j for j in range(4)] for i in range(4)]

    def along_y(a, hop):
        return lax.ppermute(
            a, "prow", [(4 * i + j, 4 * ((i + hop) % 4) + j) for i in range(4) for j in range(4)]
        )

    def along_x(a, hop):
        return lax.ppermute(
            a, "pcol", [(2 * i + j, 2 * ((i + hop) % 4) + j) for i in range(4) for j in range(2)]
        )

    def from_plane(a, hop):
        return lax.ppermute(a, "prow", [(j, 4 * hop + j) for j in range(4)])

    def cols_to(a, pairs):
        return lax.ppermute(a, "pcol", pairs)

    held = lax.all_gather(child_update, "prow", axis=0, tiled=False, axis_index_groups=planes)
    held = held.reshape(4, 2, BS, 2 * BS)

    order = jnp.where(
        row < NPIV, pivots[jnp.minimum(row, NPIV - 1)], jnp.arange(BS, dtype=I32)
    )
    order = jnp.broadcast_to(order.astype(F32)[:, None], (BS, HALF))
    view = front.reshape(tiles, BS, 8, 2, HALF).transpose(0, 1, 3, 2, 4)
    view = view.reshape(tiles * BS * 16, HALF)

    cuts = pl.pallas_call(
        cut_front,
        grid=(1,),
        out_shape=[shape((8, PIECE, BS), F32)] * 4,
        in_specs=[
            pl.BlockSpec((BS * 16, HALF), lambda t: (0, 0)),
            pl.BlockSpec((BS, HALF), lambda t: (0, 0)),
        ],
        out_specs=[pl.BlockSpec((8, PIECE, BS), lambda t: (0, 0, 0))] * 4,
        compiler_params=pltpu.CompilerParams(vmem_limit_bytes=LIMIT),
        cost_estimate=pl.CostEstimate(flops=2**30, bytes_accessed=4 * 2**20, transcendentals=0),
    )(view, order)
    cuts = [cuts[0]] + [from_plane(cuts[hop], hop) for hop in (1, 2, 3)]

    strip = shape((BS, 2 * BS), BF16)
    thin = shape((PIECE, 2 * BS), BF16)
    picked = call(pick_rows, [thin] * 4 + [strip] * 4, [child_map, rc, order, held])
    thin = picked[0]
    for hop in (1, 2, 3):
        thin = jnp.where(y == hop, from_plane(picked[hop], hop), thin)
    thin = lax.all_gather(thin, "pcol", axis=0, tiled=False)
    ys = [picked[4]] + [along_y(picked[4 + hop], hop) for hop in (1, 2, 3)]

    code, piece = call(
        assemble,
        [shape((8 * PIECE + 16, BS), I16), shape((PIECE, BS), F32)],
        [child_map, rc, *cuts, thin],
        scratch=[pltpu.VMEM((8, PIECE, BS), F32)],
    )

    far = lax.ppermute(
        piece[32:], "pcol", [(c, c + 4) for c in range(4)]
    )
    piece = jnp.where(col < NPIV, piece[:32], far)
    corner = lax.all_gather(piece, "prow", axis=0, tiled=False)
    corner = lax.all_gather(corner, "pcol", axis=0, tiled=False)

    pair = shape((2, BS, BS), BF16)
    l1, l2 = call(pick_left, [pair] * 2, [child_map, rc, *ys])
    l1 = cols_to(l1, [(0, 1), (1, 2)])
    l2 = cols_to(l2, [(0, 2), (1, 3)])
    near, far = call(
        prepare_left,
        [shape((BS + 8, BS), I32)] * 2,
        [child_map, rc, front[:, :, 0, :], *ys, l1, l2],
        scratch=[pltpu.VMEM((tiles, BS, BS), F32)],
    )
    far = cols_to(far, [(c, c + 4) for c in range(4)])
    left = lax.all_gather(jnp.where(col < NPIV, near, far), "pcol", axis=0, tiled=False)

    others = cols_to(jnp.stack(ys), [(i, i ^ 1) for i in range(8)])
    xs = call(
        pick_x, [shape((4, BS, BS), BF16)] * 4, [child_map, rc, *ys, *[others[i] for i in range(4)]]
    )
    xs = [xs[0]] + [along_x(xs[hop], hop) for hop in (1, 2, 3)]

    top = lax.all_gather(code, "prow", axis=0, tiled=False)

    corner, inverse = call(
        factor_corner,
        [shape((4 * BS, 4 * BS), F32), shape((NPIV, BS, BS), F32)],
        [corner],
        smem=0,
        flops=2**32,
    )
    *upper, taken = call(
        upper_rows,
        [shape((8, 4 * BS, BS), BF16)] * 2 + [shape((8, BS, BS), F32)],
        [rc, corner, top],
        smem=1,
        flops=5 * 2**30,
    )
    *lower, own = call(
        lower_cols,
        [shape((4 * BS, 4 * BS), BF16)] * 2 + [shape((4 * BS, BS), F32)],
        [rc, corner, inverse, left],
        smem=1,
        flops=4 * 2**30,
    )
    done = run_finish(child_map, rc, view, upper, lower, own, taken, corner, order, xs)
    done = done.reshape(tiles, BS, 2, 8, HALF).transpose(0, 1, 3, 2, 4)
    return done.reshape(front.shape)


def solution(mesh):
    return jax.shard_map(
        shards,
        mesh=mesh,
        in_specs=(P(None, "prow", None, "pcol"), P("prow", "pcol"), P(), P()),
        out_specs=P(None, "prow", None, "pcol"),
        check_vma=False,
    )
```

time: 969 us -> 299 us (0.31)
  waiting for transfers between devices: 718 us -> 64.1 us
  matrix products: 109 us -> 0 us
  Pallas kernels: 0 us -> 95.4 us
  local copies, waits for them, and re-layouts: 86.8 us -> 11.2 us
  blocking collectives: 0 us -> 66.4 us
  starting transfers between devices: 0.59 us -> 40.2 us
  other arithmetic: 33.4 us -> 3.2 us
    psum x8 -> x0, waiting for transfers between devices: 588 us -> none  [from_root(): return lax.psum(kept, axis)]
    dot_general x27 -> x0, matrix products: 109 us -> none  [the longest x4 38.5 us: shards(): jnp.dot(lower_sent, upper_kept, precision=lax.Precision.HIGHEST)]
    pallas_call x0 -> x10, Pallas kernels: none -> 95.4 us  [the longest x8 55.8 us: call(): pl.pallas_call(body, out_shape=outs, in_specs=[SMEM] * smem + [VMEM] * (l...]
    all_gather x2 -> x3, waiting for transfers between devices: 129 us -> 35.4 us  [the longest x1 35.4 us: shards(): lax.all_gather(child_update, 'prow', axis=0, tiled=False, axis_index_grou...]
    all_gather x0 -> x3, blocking collectives: none -> 66.4 us  [the longest x1 31.4 us: shards(): top = lax.all_gather(code, 'prow', axis=0, tiled=False)]
    ppermute x0 -> x17, starting transfers between devices: none -> 40.2 us  [the longest x4 14.7 us: cols_to(): return lax.ppermute(a, 'pcol', pairs)]
    select_n x15 -> x3, other arithmetic: 30.9 us -> 2.47 us  [the longest x1 1.69 us: shards(): jnp.where(col < NPIV, near, far)]
    ppermute x0 -> x17, waiting for transfers between devices: none -> 27.9 us  [the longest x4 17.2 us: cols_to(): return lax.ppermute(a, 'pcol', pairs)]
  transfers between devices with their start and end apart: 10 -> 20, of which waited for: 10 -> 8; matrix products, arithmetic and copies ran while one was open for 2% -> 3% of each run, Pallas kernels for 0% -> 19%
where the time goes in v2:
time: 299 us; the launch traced here: 294 us
  Pallas kernels  95.4 us (32%)
  blocking collectives  66.4 us (22%)
  waiting for transfers between devices  64.1 us (21%)
  starting transfers between devices  40.2 us (13%)
  between operations  13.4 us (4%)
  local copies, waits for them, and re-layouts  11.2 us (4%)
  other arithmetic  3.2 us (1%)
    pallas_call x8, Pallas kernels, call(): pl.pallas_call(body, out_shape=outs, in_specs=[SMEM] * smem + [VMEM] * (l...  55.8 us
    all_gather x1, waiting for transfers between devices, shards(): lax.all_gather(child_update, 'prow', axis=0, tiled=False, axis_index_grou...  35.4 us
    pallas_call x1, Pallas kernels, run_finish(): pl.pallas_call(finish, grid=(4 // SPAN,), out_shape=shape(view.shape, F32...  34.1 us
    all_gather x1, blocking collectives, shards(): top = lax.all_gather(code, 'prow', axis=0, tiled=False)  31.4 us
    all_gather x1, blocking collectives, shards(): corner = lax.all_gather(piece, 'prow', axis=0, tiled=False)  19.7 us
    ppermute x4, waiting for transfers between devices, cols_to(): return lax.ppermute(a, 'pcol', pairs)  17.2 us
    all_gather x1, blocking collectives, shards(): thin = lax.all_gather(thin, 'pcol', axis=0, tiled=False)  15.3 us
    ppermute x4, starting transfers between devices, cols_to(): return lax.ppermute(a, 'pcol', pairs)  14.7 us
  transfers between devices with their start and end apart: 20, of which 8 were waited for; matrix products, arithmetic and copies ran while one was open for 3% of the time, Pallas kernels for 19%

profile of v2, /device:TPU:1, one launch (start us, length us, event | category | flops | bytes accessed | tf_op | source)
XLA Modules:
  0.0 294.0 jit_solution(10264906013854203714)
XLA Ops:
  7.9 35.4 %all-gather.11.cloned.1.call-done = bf16[2048,512]{1,0:T(8,128)(2,1)} async-done(((bf16[512,512]{1,0:T(8,128)(2,1)}), bf16[2048,512]{1,0:T(8,128)(2,1)}) %all-gather.11.cloned.1.call-update) | async-done | bytes 2097168 | tf_op jit(solution)/shard_map/all_gather | solution.py:457
  44.1 3.2 %shard_map.47 = (bf16[64,512]{1,0:T(8,128)(2,1)}, bf16[64,512]{1,0:T(8,128)(2,1)}, bf16[64,512]{1,0:T(8,128)(2,1)}, bf16[64,512]{1,0:T(8,128)(2,1)}, bf16[256,51...) custom-call(s32[2,16]{1,0:T(2,128)} %map_ref.11, ...), custom_call_target="tpu_custom_call" | custom-call | bytes 3539080 | tf_op jit(solution)/shard_map/pallas_call | solution.py:33
  47.3 4.1 %collective-permute-start.3 = (bf16[64,512]{1,0:T(8,128)(2,1)}, bf16[64,512]{1,0:T(8,128)(2,1)S(1)}, u32[]{:S(2)}, u32[]{:S(2)}) collective-permute-start(bf16[64,512]{1,0:T(8,128)(2,1)} %get-tuple-element.39), channel_id=1, source_target_pairs={{0,96},{8,104},{16,112},{24,120},{1,97},{9,105},{17,113},{25,121},... | collective-permute-start | bytes 196616 | tf_op jit(solution)/shard_map/ppermute | solution.py:452
  54.0 5.6 %shard_map.46 = (f32[8,64,256]{2,1,0:T(8,128)}, f32[8,64,256]{2,1,0:T(8,128)}, f32[8,64,256]{2,1,0:T(8,128)}, f32[8,64,256]{2,1,0:T(8,128)}) custom-call(f32[16384,128]{1,0:T(8,128)} %bitcast.34, f32[256,128]{1,0:T(8,128)} %broadcast_in_dim.2.order_ref), custom_call_target="tpu_custom_call" | custom-call | flops 1073741824 | bytes 4194304 | tf_op jit(solution)/shard_map/pallas_call | solution.py:467
  63.8 15.3 %all-gather.1 = bf16[512,512]{1,0:T(8,128)(2,1)} all-gather(bf16[64,512]{1,0:T(8,128)(2,1)S(1)} %select_select_fusion), channel_id=3, replica_groups=mesh['prow'=16,'pcol'=8] {'pcol'}, dimensions={0}, use_global_device_ids=true | all-gather | bytes 589824 | tf_op jit(solution)/shard_map/all_gather | solution.py:487
  79.1 4.0 %collective-permute-done.1.f2 = f32[8,64,256]{2,1,0:T(8,128)S(1)} collective-permute-done((f32[8,64,256]{2,1,0:T(8,128)}, f32[8,64,256]{2,1,0:T(8,128)S(1)}, u32[]{:S(2)}, u32[]{:S(2)}) %collective-permute-start.1) | collective-permute-done | bytes 524320 | tf_op jit(solution)/shard_map/ppermute | solution.py:452
  84.1 3.1 %shard_map.48 = (s16[528,256]{1,0:T(8,128)(2,1)}, f32[64,256]{1,0:T(8,128)}) custom-call(s32[2,16]{1,0:T(2,128)} %map_ref.11, s32[2]{0:T(128)} %pad_add_fusion.rc_ref, f32[8,64,256]{2,1,0:T(8,128)} %get-tuple-element.35.f0, f32[8,64,256]{2,1,0:T(8,128)} %copy-done.9, f32[8,64,256]{2,1,0:T(8,128)} %copy-done.10, f32[8,64,256]{2,1,0:T(8,128)} %copy-done.11, ...), custom_call_target="tpu_custom_call" | custom-call | bytes 2957448 | tf_op jit(solution)/shard_map/pallas_call | solution.py:33
  88.0 4.6 %collective-permute-start.6 = (f32[32,256]{1,0:T(8,128)S(1)}, f32[32,256]{1,0:T(8,128)S(1)}, u32[]{:S(2)}, u32[]{:S(2)}) collective-permute-start(f32[32,256]{1,0:T(8,128)S(1)} %slice.22), channel_id=1, source_target_pairs={{0,4},{1,5},{2,6},{3,7},{8,12},{9,13},{10,14},{11,15},{16,20},{17,... | collective-permute-start | bytes 98312 | tf_op jit(solution)/shard_map/ppermute | solution.py:497
  94.4 19.7 %all-gather.2 = f32[512,256]{1,0:T(8,128)} all-gather(f32[32,256]{1,0:T(8,128)S(1)} %slice_select_fusion), channel_id=4, replica_groups=mesh['prow'=16,'pcol'=8] {'prow'}, dimensions={0}, use_global_device_ids=true | all-gather | bytes 557056 | tf_op jit(solution)/shard_map/all_gather | solution.py:501
  119.0 2.6 collective-permute-done.7.refs_1_
  121.6 3.1 %collective-permute-done.8.refs_2_ = bf16[256,512]{1,0:T(8,128)(2,1)S(1)} collective-permute-done((bf16[256,512]{1,0:T(8,128)(2,1)S(1)}, bf16[256,512]{1,0:T(8,128)(2,1)S(1)}, u32[]{:S(2)}, u32[]{:S(2)}) %collective-permute-start.8) | collective-permute-done | bytes 262176 | tf_op jit(solution)/shard_map/ppermute | solution.py:442
  127.7 12.0 %collective-permute-start.10 = (bf16[2,256,256]{2,1,0:T(8,128)(2,1)}, bf16[2,256,256]{2,1,0:T(8,128)(2,1)S(1)}, u32[]{:S(2)}, u32[]{:S(2)}) collective-permute-start(bf16[2,256,256]{2,1,0:T(8,128)(2,1)} %get-tuple-element.53), channel_id=1, source_target_pairs={{0,1},{1,2},{8,9},{9,10},{16,17},{17,18},{24,25},{25,26},{32,33},{... | collective-permute-start | bytes 786440 | tf_op jit(solution)/shard_map/ppermute | solution.py:455
  141.0 4.0 %slice.23 = f32[4,256,1,256]{3,2,1,0:T(1,128)S(1)} slice(f32[4,256,8,256]{3,2,1,0:T(8,128)} %param.4), slice={[0:4], [0:256], [0:1], [0:256]} | slice | bytes 2097152 | tf_op jit(solution)/shard_map/slice | solution.py:511
  146.1 4.7 %collective-permute-done.10.refs_4_ = bf16[2,256,256]{2,1,0:T(8,128)(2,1)S(1)} collective-permute-done((bf16[2,256,256]{2,1,0:T(8,128)(2,1)}, bf16[2,256,256]{2,1,0:T(8,128)(2,1)S(1)}, u32[]{:S(2)}, u32[]{:S(2)}) %collective-permute-start.10) | collective-permute-done | bytes 262176 | tf_op jit(solution)/shard_map/ppermute | solution.py:455
  150.7 8.8 %collective-permute-done.11.refs_5_ = bf16[2,256,256]{2,1,0:T(8,128)(2,1)S(1)} collective-permute-done((bf16[2,256,256]{2,1,0:T(8,128)(2,1)}, bf16[2,256,256]{2,1,0:T(8,128)(2,1)S(1)}, u32[]{:S(2)}, u32[]{:S(2)}) %collective-permute-start.11) | collective-permute-done | bytes 262176 | tf_op jit(solution)/shard_map/ppermute | solution.py:455
  160.3 3.7 %shard_map.52 = (s32[264,256]{1,0:T(8,128)}, s32[264,256]{1,0:T(8,128)}) custom-call(s32[2,16]{1,0:T(2,128)} %map_ref.11, s32[2]{0:T(128)} %pad_add_fusion.rc_ref, f32[4,256,256]{2,1,0:T(8,128)} %bitcast.37, bf16[256,512]{1,0:T(8,128)(2,1)} %get-tuple-element.49.refs_0_, bf16[256,512]{1,0:T(8,128)(2,1)} %copy-done.3, bf16[256,512]{1,0:T(8,128)(2,1)} %copy-done.5, ...), custom_call_target="tpu_custom_call" | custom-call | bytes 3162248 | tf_op jit(solution)/shard_map/pallas_call | solution.py:33
  165.3 3.7 %collective-permute-done.12 = s32[264,256]{1,0:T(8,128)S(1)} collective-permute-done((s32[264,256]{1,0:T(8,128)}, s32[264,256]{1,0:T(8,128)S(1)}, u32[]{:S(2)}, u32[]{:S(2)}) %collective-permute-start.12) | collective-permute-done | bytes 270368 | tf_op jit(solution)/shard_map/ppermute | solution.py:455
  170.9 31.4 %all-gather.16 = s16[8448,256]{1,0:T(8,128)(2,1)} all-gather(s16[528,256]{1,0:T(8,128)(2,1)S(1)} %copy-done.12), channel_id=6, replica_groups=mesh['prow'=16,'pcol'=8] {'prow'}, dimensions={0}, use_global_device_ids=true | all-gather | bytes 4595712 | tf_op jit(solution)/shard_map/all_gather | solution.py:523
  203.3 3.7 %shard_map.54 = (bf16[4,256,256]{2,1,0:T(8,128)(2,1)}, bf16[4,256,256]{2,1,0:T(8,128)(2,1)}, bf16[4,256,256]{2,1,0:T(8,128)(2,1)}, bf16[4,256,256]{2,1,0:T(8,128)(2,1)}) custom-call(s32[2,16]{1,0:T(2,128)} %map_ref.11, s32[2]{0:T(128)} %pad_add_fusion.rc_ref, bf16[256,512]{1,0:T(8,128)(2,1)} %get-tuple-element.49.refs_0_, bf16[256,512]{1,0:T(8,128)(2,1)} %copy-done.3, ...), custom_call_target="tpu_custom_call" | custom-call | bytes 4194440 | tf_op jit(solution)/shard_map/pallas_call | solution.py:33
  209.1 3.2 %collective-permute-start.15 = (bf16[4,256,256]{2,1,0:T(8,128)(2,1)}, bf16[4,256,256]{2,1,0:T(8,128)(2,1)S(1)}, u32[]{:S(2)}, u32[]{:S(2)}) collective-permute-start(bf16[4,256,256]{2,1,0:T(8,128)(2,1)} %get-tuple-element.63), channel_id=1, source_target_pairs={{0,4},{1,5},{2,6},{3,7},{4,0},{5,1},{6,2},{7,3},{8,12},{9,13},{10,... | collective-permute-start | bytes 1572872 | tf_op jit(solution)/shard_map/ppermute | solution.py:447
  212.3 11.3 %shard_map.49 = (f32[1024,1024]{1,0:T(8,128)}, f32[4,256,256]{2,1,0:T(8,128)}) custom-call(f32[8,16,32,256]{3,2,1,0:T(8,128)} %bitcast.46), custom_call_target="tpu_custom_call" | custom-call | flops 4294967296 | bytes 9437184 | tf_op jit(solution)/shard_map/pallas_call | solution.py:33
  223.6 11.2 %shard_map.53 = (bf16[1024,1024]{1,0:T(8,128)(2,1)}, bf16[1024,1024]{1,0:T(8,128)(2,1)}, f32[1024,256]{1,0:T(8,128)}) custom-call(s32[2]{0:T(128)} %pad_add_fusion.rc_ref, f32[1024,1024]{1,0:T(8,128)} %get-tuple-element.44.corner_ref, f32[4,256,256]{2,1,0:T(8,128)} %get-tuple-element.48.inverse_ref, s32[8,264,256]{2,1,0:T(8,128)} %bitcast.47), custom_call_target="tpu_custom_call" | custom-call | flops 4294967296 | bytes 12648456 | tf_op jit(solution)/shard_map/pallas_call | solution.py:33
  234.8 17.4 %shard_map.50 = (bf16[8,1024,256]{2,1,0:T(8,128)(2,1)}, bf16[8,1024,256]{2,1,0:T(8,128)(2,1)}, f32[8,256,256]{2,1,0:T(8,128)}) custom-call(s32[2]{0:T(128)} %pad_add_fusion.rc_ref, f32[1024,1024]{1,0:T(8,128)} %get-tuple-element.44.corner_ref, s16[16,528,256]{2,1,0:T(8,128)(2,1)} %bitcast.36), custom_call_target="tpu_custom_call" | custom-call | flops 5368709120 | bytes 19005448 | tf_op jit(solution)/shard_map/pallas_call | solution.py:33
  253.4 34.1 %shard_map.55 = f32[16384,128]{1,0:T(8,128)} custom-call(s32[2,16]{1,0:T(2,128)} %map_ref.11, s32[2]{0:T(128)} %pad_add_fusion.rc_ref, f32[16384,128]{1,0:T(8,128)} %bitcast.35, bf16[8,1024,256]{2,1,0:T(8,128)(2,1)} %get-tuple-element.46.high_ref, bf16[8,1024,256]{2,1,0:T(8,128)(2,1)} %get-tuple-element.47.low_ref, ...), custom_call_target="tpu_custom_call" | custom-call | flops 13958643712 | bytes 33554432 | tf_op jit(solution)/shard_map/pallas_call | solution.py:416
  (88 shorter events, 30.6 us)
Async XLA Ops:
  6.5 36.8 %all-gather.11.cloned.1.call-start = ((), (), s32[]{:S(2)}) async-start(), calls=%async_computation | async-start | bytes 2621440 | tf_op jit(solution)/shard_map/all_gather | solution.py:457
  7.3 205.1 %all-gather.13.cloned.1.call-start = ((), (), s32[]{:S(2)}) async-start(), calls=%async_computation.1 | async-start | bytes 4718592 | tf_op jit(solution)/shard_map/all_gather | solution.py:502
  47.3 15.1 %collective-permute-start.3 = (bf16[64,512]{1,0:T(8,128)(2,1)}, bf16[64,512]{1,0:T(8,128)(2,1)S(1)}, u32[]{:S(2)}, u32[]{:S(2)}) collective-permute-start(bf16[64,512]{1,0:T(8,128)(2,1)} %get-tuple-element.39), channel_id=1, source_target_pairs={{0,96},{8,104},{16,112},{24,120},{1,97},{9,105},{17,113},{25,121},... | collective-permute-start | bytes 196616 | tf_op jit(solution)/shard_map/ppermute | solution.py:452
  51.4 12.3 %collective-permute-start.4 = (bf16[64,512]{1,0:T(8,128)(2,1)}, bf16[64,512]{1,0:T(8,128)(2,1)S(1)}, u32[]{:S(2)}, u32[]{:S(2)}) collective-permute-start(bf16[64,512]{1,0:T(8,128)(2,1)} %get-tuple-element.40), channel_id=1, source_target_pairs={{0,64},{8,72},{16,80},{24,88},{1,65},{9,73},{17,81},{25,89},{2,66}... | collective-permute-start | bytes 196616 | tf_op jit(solution)/shard_map/ppermute | solution.py:452
  52.7 11.0 %collective-permute-start.5 = (bf16[64,512]{1,0:T(8,128)(2,1)}, bf16[64,512]{1,0:T(8,128)(2,1)S(1)}, u32[]{:S(2)}, u32[]{:S(2)}) collective-permute-start(bf16[64,512]{1,0:T(8,128)(2,1)} %get-tuple-element.41), channel_id=1, source_target_pairs={{0,32},{8,40},{16,48},{24,56},{1,33},{9,41},{17,49},{25,57},{2,34}... | collective-permute-start | bytes 196616 | tf_op jit(solution)/shard_map/ppermute | solution.py:452
  59.6 54.6 %copy-start.21 = (bf16[256,512]{1,0:T(8,128)(2,1)S(1)}, bf16[256,512]{1,0:T(8,128)(2,1)}, u32[]{:S(2)}) copy-start(bf16[256,512]{1,0:T(8,128)(2,1)} %get-tuple-element.50) | copy-start | bytes 786436
  59.6 56.4 %copy-start.20 = (bf16[256,512]{1,0:T(8,128)(2,1)S(1)}, bf16[256,512]{1,0:T(8,128)(2,1)}, u32[]{:S(2)}) copy-start(bf16[256,512]{1,0:T(8,128)(2,1)} %get-tuple-element.51) | copy-start | bytes 786436
  59.6 58.2 %copy-start.19 = (bf16[256,512]{1,0:T(8,128)(2,1)S(1)}, bf16[256,512]{1,0:T(8,128)(2,1)}, u32[]{:S(2)}) copy-start(bf16[256,512]{1,0:T(8,128)(2,1)} %get-tuple-element.52) | copy-start | bytes 786436
  59.6 19.5 %collective-permute-start = (f32[8,64,256]{2,1,0:T(8,128)}, f32[8,64,256]{2,1,0:T(8,128)S(1)}, u32[]{:S(2)}, u32[]{:S(2)}) collective-permute-start(f32[8,64,256]{2,1,0:T(8,128)} %get-tuple-element.36), channel_id=1, source_target_pairs={{0,32},{8,40},{16,48},{24,56},{1,33},{9,41},{17,49},{25,57},{2,34}... | collective-permute-start | bytes 1572872 | tf_op jit(solution)/shard_map/ppermute | solution.py:452
  61.1 22.1 %collective-permute-start.1 = (f32[8,64,256]{2,1,0:T(8,128)}, f32[8,64,256]{2,1,0:T(8,128)S(1)}, u32[]{:S(2)}, u32[]{:S(2)}) collective-permute-start(f32[8,64,256]{2,1,0:T(8,128)} %get-tuple-element.37), channel_id=1, source_target_pairs={{0,64},{8,72},{16,80},{24,88},{1,65},{9,73},{17,81},{25,89},{2,66}... | collective-permute-start | bytes 1572872 | tf_op jit(solution)/shard_map/ppermute | solution.py:452
  62.4 20.8 %collective-permute-start.2 = (f32[8,64,256]{2,1,0:T(8,128)}, f32[8,64,256]{2,1,0:T(8,128)S(1)}, u32[]{:S(2)}, u32[]{:S(2)}) collective-permute-start(f32[8,64,256]{2,1,0:T(8,128)} %get-tuple-element.38), channel_id=1, source_target_pairs={{0,96},{8,104},{16,112},{24,120},{1,97},{9,105},{17,113},{25,121},... | collective-permute-start | bytes 1572872 | tf_op jit(solution)/shard_map/ppermute | solution.py:452
  88.0 5.6 %collective-permute-start.6 = (f32[32,256]{1,0:T(8,128)S(1)}, f32[32,256]{1,0:T(8,128)S(1)}, u32[]{:S(2)}, u32[]{:S(2)}) collective-permute-start(f32[32,256]{1,0:T(8,128)S(1)} %slice.22), channel_id=1, source_target_pairs={{0,4},{1,5},{2,6},{3,7},{8,12},{9,13},{10,14},{11,15},{16,20},{17,... | collective-permute-start | bytes 98312 | tf_op jit(solution)/shard_map/ppermute | solution.py:497
  114.1 109.5 %all-gather.15.cloned.1.call-start = ((), (), s32[]{:S(2)}) async-start(), calls=%async_computation.2 | async-start | bytes 2433024 | tf_op jit(solution)/shard_map/all_gather | solution.py:515
  114.2 7.4 %collective-permute-start.7 = (bf16[256,512]{1,0:T(8,128)(2,1)S(1)}, bf16[256,512]{1,0:T(8,128)(2,1)S(1)}, u32[]{:S(2)}, u32[]{:S(2)}) collective-permute-start(bf16[256,512]{1,0:T(8,128)(2,1)S(1)} %copy-done.21), channel_id=1, source_target_pairs={{0,32},{8,40},{16,48},{24,56},{32,64},{40,72},{48,80},{56,88},{64,... | collective-permute-start | bytes 786440 | tf_op jit(solution)/shard_map/ppermute | solution.py:442
  116.0 8.7 %collective-permute-start.8 = (bf16[256,512]{1,0:T(8,128)(2,1)S(1)}, bf16[256,512]{1,0:T(8,128)(2,1)S(1)}, u32[]{:S(2)}, u32[]{:S(2)}) collective-permute-start(bf16[256,512]{1,0:T(8,128)(2,1)S(1)} %copy-done.20), channel_id=1, source_target_pairs={{0,64},{8,72},{16,80},{24,88},{32,96},{40,104},{48,112},{56,120},{... | collective-permute-start | bytes 786440 | tf_op jit(solution)/shard_map/ppermute | solution.py:442
  117.8 6.9 %collective-permute-start.9 = (bf16[256,512]{1,0:T(8,128)(2,1)S(1)}, bf16[256,512]{1,0:T(8,128)(2,1)S(1)}, u32[]{:S(2)}, u32[]{:S(2)}) collective-permute-start(bf16[256,512]{1,0:T(8,128)(2,1)S(1)} %copy-done.19), channel_id=1, source_target_pairs={{0,96},{8,104},{16,112},{24,120},{32,0},{40,8},{48,16},{56,24},{64... | collective-permute-start | bytes 786440 | tf_op jit(solution)/shard_map/ppermute | solution.py:442
  127.6 43.0 %copy-start.8 = (bf16[256,512]{1,0:T(8,128)(2,1)S(1)}, bf16[256,512]{1,0:T(8,128)(2,1)}, u32[]{:S(2)}) copy-start(bf16[256,512]{1,0:T(8,128)(2,1)} %copy-done.7) | copy-start | bytes 786436
  127.7 23.1 %collective-permute-start.10 = (bf16[2,256,256]{2,1,0:T(8,128)(2,1)}, bf16[2,256,256]{2,1,0:T(8,128)(2,1)S(1)}, u32[]{:S(2)}, u32[]{:S(2)}) collective-permute-start(bf16[2,256,256]{2,1,0:T(8,128)(2,1)} %get-tuple-element.53), channel_id=1, source_target_pairs={{0,1},{1,2},{8,9},{9,10},{16,17},{17,18},{24,25},{25,26},{32,33},{... | collective-permute-start | bytes 786440 | tf_op jit(solution)/shard_map/ppermute | solution.py:455
  139.7 19.9 %collective-permute-start.11 = (bf16[2,256,256]{2,1,0:T(8,128)(2,1)}, bf16[2,256,256]{2,1,0:T(8,128)(2,1)S(1)}, u32[]{:S(2)}, u32[]{:S(2)}) collective-permute-start(bf16[2,256,256]{2,1,0:T(8,128)(2,1)} %get-tuple-element.54), channel_id=1, source_target_pairs={{0,2},{1,3},{8,10},{9,11},{16,18},{17,19},{24,26},{25,27},{32,34},... | collective-permute-start | bytes 786440 | tf_op jit(solution)/shard_map/ppermute | solution.py:455
  164.0 5.0 %collective-permute-start.12 = (s32[264,256]{1,0:T(8,128)}, s32[264,256]{1,0:T(8,128)S(1)}, u32[]{:S(2)}, u32[]{:S(2)}) collective-permute-start(s32[264,256]{1,0:T(8,128)} %get-tuple-element.56), channel_id=1, source_target_pairs={{0,4},{1,5},{2,6},{3,7},{8,12},{9,13},{10,14},{11,15},{16,20},{17,... | collective-permute-start | bytes 811016 | tf_op jit(solution)/shard_map/ppermute | solution.py:455
  170.8 31.5 %collective-permute-start.13 = (bf16[4,256,512]{2,1,0:T(8,128)(2,1)S(1)}, bf16[4,256,512]{2,1,0:T(8,128)(2,1)S(1)}, u32[]{:S(2)}, u32[]{:S(2)}) collective-permute-start(bf16[4,256,512]{2,1,0:T(8,128)(2,1)S(1)} %pad_maximum_fusion), channel_id=1, source_target_pairs={{0,1},{1,0},{2,3},{3,2},{4,5},{5,4},{6,7},{7,6},{8,9},{9,8},{10,11... | collective-permute-start | bytes 3145736 | tf_op jit(solution)/shard_map/ppermute | solution.py:455
  207.0 45.2 %collective-permute-start.14 = (bf16[4,256,256]{2,1,0:T(8,128)(2,1)}, bf16[4,256,256]{2,1,0:T(8,128)(2,1)S(1)}, u32[]{:S(2)}, u32[]{:S(2)}) collective-permute-start(bf16[4,256,256]{2,1,0:T(8,128)(2,1)} %get-tuple-element.62), channel_id=1, source_target_pairs={{0,2},{1,3},{2,4},{3,5},{4,6},{5,7},{6,0},{7,1},{8,10},{9,11},{10,... | collective-permute-start | bytes 1572872 | tf_op jit(solution)/shard_map/ppermute | solution.py:447
  209.1 43.1 %collective-permute-start.15 = (bf16[4,256,256]{2,1,0:T(8,128)(2,1)}, bf16[4,256,256]{2,1,0:T(8,128)(2,1)S(1)}, u32[]{:S(2)}, u32[]{:S(2)}) collective-permute-start(bf16[4,256,256]{2,1,0:T(8,128)(2,1)} %get-tuple-element.63), channel_id=1, source_target_pairs={{0,4},{1,5},{2,6},{3,7},{4,0},{5,1},{6,2},{7,3},{8,12},{9,13},{10,... | collective-permute-start | bytes 1572872 | tf_op jit(solution)/shard_map/ppermute | solution.py:447
  212.3 39.9 %collective-permute-start.16 = (bf16[4,256,256]{2,1,0:T(8,128)(2,1)}, bf16[4,256,256]{2,1,0:T(8,128)(2,1)S(1)}, u32[]{:S(2)}, u32[]{:S(2)}) collective-permute-start(bf16[4,256,256]{2,1,0:T(8,128)(2,1)} %get-tuple-element.64), channel_id=1, source_target_pairs={{0,6},{1,7},{2,0},{3,1},{4,2},{5,3},{6,4},{7,5},{8,14},{9,15},{10,... | collective-permute-start | bytes 1572872 | tf_op jit(solution)/shard_map/ppermute | solution.py:447
  (18 other events, 223.2 us)
Sparse Core Ops, SparseCore 0:
  9.0 34.2 all-gather.10
  114.3 44.6 all-gather.12
  170.8 27.5 all-gather.14

commit v3 on v2

v3 whole, which is shorter than its diff:
```python
import functools

import jax
import jax.numpy as jnp
from jax import lax
from jax.experimental import pallas as pl
from jax.experimental.pallas import tpu as pltpu
from jax.sharding import PartitionSpec as P

NPIV = 4
NS = 2
BS = 256
HALF = 128
PIECE = 64
FULL = 32767.0
HIGHEST = lax.Precision.HIGHEST
F32 = jnp.float32
BF16 = jnp.bfloat16
I16 = jnp.int16
I32 = jnp.int32
SMEM = pl.BlockSpec(memory_space=pltpu.SMEM)
VMEM = pl.BlockSpec(memory_space=pltpu.VMEM)
LIMIT = 56 * 1024 * 1024


def shape(dims, kind):
    return jax.ShapeDtypeStruct(dims, kind)


def call(body, outs, ins, smem=2, flops=0, scratch=()):
    moved = sum(a.size * a.dtype.itemsize for a in ins)
    moved += sum(o.size * o.dtype.itemsize for o in outs)
    return pl.pallas_call(
        body,
        out_shape=outs,
        in_specs=[SMEM] * smem + [VMEM] * (len(ins) - smem),
        out_specs=[VMEM] * len(outs),
        scratch_shapes=list(scratch),
        compiler_params=pltpu.CompilerParams(vmem_limit_bytes=LIMIT),
        cost_estimate=pl.CostEstimate(flops=flops, bytes_accessed=moved, transcendentals=0),
    )(*ins)


def spot(map_ref, child, low, count, test):
    found = jnp.int32(-1)
    value = jnp.int32(-1)
    for step in range(count):
        entry = map_ref[child, low + step]
        hit = test(entry)
        found = jnp.where(hit, low + step, found)
        value = jnp.where(hit, entry, value)
    return found, value


def row_of(map_ref, row, slot):
    return spot(map_ref, slot // 2, 8 * (slot % 2), 8, lambda entry: entry % 16 == row)[1]


def col_of(map_ref, child, source, col):
    return spot(map_ref, child, 4 * source, 4, lambda entry: entry % 8 == col)


def split(value):
    high = value.astype(BF16)
    low = (value - high.astype(F32)).astype(BF16)
    return high, low


def dot(left, right):
    return jnp.dot(left, right, preferred_element_type=F32)


def dot3(left, right):
    (a, b), (c, d) = left, right
    return dot(a, c) + (dot(a, d) + dot(b, c))


def high_dot(left, right):
    return jnp.dot(left, right, precision=HIGHEST, preferred_element_type=F32)


def block(step):
    return slice(step * BS, step * BS + BS)


def one_hot(order):
    spread = lax.broadcasted_iota(I32, (BS, BS), 1).astype(F32)
    return jnp.where(order[:, :1] == spread, 1.0, 0.0).astype(BF16)


def reorder(select, value):
    high = value.astype(BF16)
    rest = value - high.astype(F32)
    middle = rest.astype(BF16)
    last = (rest - middle.astype(F32)).astype(BF16)
    return (dot(select, high) + dot(select, middle)) + dot(select, last)


def level(peak):
    return jnp.ceil(jnp.log2(jnp.full((8, HALF), jnp.maximum(peak, 1e-30))) * 4.0)


def encode(value, n):
    scaled = jnp.abs(value) * jnp.exp2(n * -0.25)[:1, :1]
    code = jnp.minimum(jnp.floor(jnp.sqrt(scaled) * FULL + 0.5), FULL)
    return jnp.where(value < 0.0, -code, code).astype(I32)


def decode(code, n):
    code = code.astype(F32)
    return code * jnp.abs(code) * (jnp.exp2(n.astype(F32)[:1, :1] * 0.25) * (1.0 / (FULL * FULL)))


def cut_front(front_ref, order_ref, *outs):
    select = one_hot(order_ref[...])

    def one(tile, carry):
        halves = [front_ref[pl.ds(half * 8 + tile, BS, stride=16), :] for half in range(2)]
        turned = reorder(select, jnp.concatenate(halves, axis=1))
        for piece in range(4):
            outs[piece][tile] = turned[piece * PIECE : piece * PIECE + PIECE]
        return carry

    lax.fori_loop(0, 8, one, 0)


def pick_z(map_ref, rc_ref, child_ref, *outs):
    row = rc_ref[0]
    z = row % 4
    second_at = map_ref[row // 8, 2 * (row % 8) + 1] % 4
    for hop in range(4):
        outs[hop][...] = child_ref[jnp.where(second_at == (z + hop) % 4, 1, 0)]


def pick_rows(map_ref, rc_ref, order_ref, *refs):
    held, pieces, hops = refs[:4], refs[4:8], refs[8:]
    row = rc_ref[0]
    y, z = row // 4, row % 4
    found, value = spot(map_ref, 0, 0, 4, lambda entry: entry == row)
    live = (found >= 0) & (row < NPIV)
    for hop in range(4):

        @pl.when(live & (found // 2 == (z - hop + 4) % 4))
        def _(hop=hop):
            turned = dot(one_hot(order_ref[...]), held[hop][...]).astype(BF16)
            for piece in range(4):
                pieces[piece][...] = turned[piece * PIECE : piece * PIECE + PIECE]

    @pl.when(jnp.logical_not(live))
    def _():
        for piece in range(4):
            pieces[piece][...] = jnp.zeros((PIECE, 2 * BS), BF16)

    for hop in range(4):
        first = 2 * ((4 * y + (z - hop + 4) % 4) % 8)
        index, value = spot(map_ref, y // 2, first, 2, lambda entry: entry % 4 == z)
        for shift in range(4):

            @pl.when((index >= 0) & ((value // 4) % 4 == (y + shift) % 4))
            def _(hop=hop, shift=shift):
                hops[shift][...] = held[hop][...]


def assemble(map_ref, rc_ref, f0, f1, f2, f3, far_ref, strip, code_ref, corner_ref, work):
    row, col = rc_ref[0], rc_ref[1]
    y = row // 4
    for piece, source in enumerate((f0, f1, f2, f3)):

        @pl.when(y == piece)
        def _(source=source):
            work[...] = source[...]

    for index in range(16):
        parent = map_ref[0, index]
        cut = slice((index % 2) * BS, (index % 2) * BS + BS)

        @pl.when(parent % 8 == col)
        def _(index=index, cut=cut, tile=parent // 8):
            work[tile] = work[tile] + strip[index // 2, :, cut].astype(F32)

    @pl.when(col < NPIV)
    def _():
        corner_ref[...] = work[0, :32]
        work[0] = jnp.zeros((PIECE, BS), F32)

    @pl.when(col >= NPIV)
    def _():
        corner_ref[...] = far_ref[...]

    for index in range(4):
        cut = slice((index % 2) * BS, (index % 2) * BS + BS)

        @pl.when((col >= NPIV) & (map_ref[0, index] == col - NPIV))
        def _(index=index, cut=cut):
            corner_ref[...] = corner_ref[...] + strip[index // 2, 32:, cut].astype(F32)

    n = level(jnp.max(jnp.abs(work[...])))
    for tile in range(8):
        code_ref[tile * PIECE : tile * PIECE + PIECE] = encode(work[tile], n).astype(I16)
    code_ref[8 * PIECE :] = jnp.broadcast_to(n[:1, :1].astype(I32), (16, BS)).astype(I16)


def pick_left(map_ref, rc_ref, h0, h1, h2, h3, out_ref):
    y = rc_ref[0] // 4
    for shift, source in enumerate((h0, h1, h2, h3)):
        slot = (y - shift + 4) % 4

        @pl.when(slot < 2)
        def _(source=source, slot=slot):
            out_ref[slot] = source[...]


def pick_x(map_ref, rc_ref, *refs):
    mine, other, outs = refs[:4], refs[4:8], refs[8:]
    row, col = rc_ref[0], rc_ref[1]
    y, x, core = row // 4, col // 2, col % 2
    for shift in range(4):
        child = ((y - shift + 4) % 4) // 2
        for hop in range(4):
            goal = 2 * ((x + hop) % 4) + core
            found, value = col_of(map_ref, child, x, goal)
            part = found % 4
            for half in range(2):
                cut = slice(half * BS, half * BS + BS)

                @pl.when((found >= 0) & (part == 2 * core + half))
                def _(shift=shift, hop=hop, cut=cut):
                    outs[hop][shift] = mine[shift][:, cut]

                @pl.when((found >= 0) & (part == 2 * (1 - core) + half))
                def _(shift=shift, hop=hop, cut=cut):
                    outs[hop][shift] = other[shift][:, cut]


def factor_corner(gathered, work, inverse_ref):
    for h in range(2):
        for k in range(4):
            for y in range(4):
                for z in range(4):
                    low = z * BS + y * PIECE + h * 32
                    work[low : low + 32, block(k)] = gathered[4 * h + k, y, z]
    diagonal = lax.broadcasted_iota(I32, (BS, BS), 0) == lax.broadcasted_iota(I32, (BS, BS), 1)
    for k in range(NPIV):
        pivot = work[block(k), block(k)]
        on_line = jnp.where(diagonal, pivot, 0.0)
        across = jnp.sum(on_line, axis=0, keepdims=True)
        down = jnp.sum(on_line, axis=1, keepdims=True)
        across = across / (across * across + 1.0)
        down = down / (down * down + 1.0)
        approx = 2.0 * jnp.where(diagonal, across, 0.0) - (down * pivot) * across
        for sweep_index in range(NS - 1):
            approx = 2.0 * approx - high_dot(high_dot(approx, pivot), approx)
        inverse_ref[k] = approx
        if k + 1 < NPIV:
            below = slice((k + 1) * BS, NPIV * BS)
            lower = dot3(split(work[below, block(k)]), split(approx))
            work[below, block(k)] = lower
            work[below, below] = work[below, below] - dot3(
                split(lower), split(work[block(k), below])
            )


def panels(
    map_ref, rc_ref, gathered, code_ref, level_ref, front_ref, near_ref, far_ref,
    high_ref, low_ref, taken_ref, left_high, left_low, own_ref, block_ref,
    work, inverse, chi, clo, xhi, xlo, left,
):
    step = pl.program_id(0)
    row, col = rc_ref[0], rc_ref[1]
    core = col % 2

    @pl.when(step == 0)
    def _():
        factor_corner(gathered, work, inverse)
        for k in range(NPIV):
            chi[block(k)], clo[block(k)] = split(work[block(k)])
            xhi[k], xlo[k] = split(inverse[k])
        for r in range(NPIV):
            for c in range(NPIV):

                @pl.when((row == r) & (col == c))
                def _(r=r, c=c):
                    block_ref[...] = work[block(r), block(c)]

    mine = jnp.zeros((BS, BS), F32)
    for k in range(NPIV):
        raw = jnp.concatenate(
            [
                decode(code_ref[4 * piece + k].astype(I32), level_ref[4 * piece + k].astype(I32))
                for piece in range(4)
            ],
            axis=0,
        )
        if k:
            done = slice(0, k * BS)
            taken = dot3(
                (chi[block(k), done], clo[block(k), done]), (high_ref[0, done], low_ref[0, done])
            )
            mine = jnp.where(row == k, taken, mine)
            raw = raw - taken
        high_ref[0, block(k)], low_ref[0, block(k)] = split(raw)
    taken_ref[0] = mine

    @pl.when(step % 2 == 1)
    def _():
        tile = step // 2
        left[...] = front_ref[...]
        for slot in range(2):
            parent = row_of(map_ref, row, slot)
            for index in range(4):
                target = map_ref[0, index]
                good = (parent >= 0) & (parent // 16 == tile) & (target < NPIV)
                cut = slice((index % 2) * BS, (index % 2) * BS + BS)

                @pl.when(good & (core == index // 2))
                def _(slot=slot, cut=cut, target=target):
                    left[target] = left[target] + near_ref[slot, :, cut].astype(F32)

                @pl.when(good & (core != index // 2))
                def _(slot=slot, cut=cut, target=target):
                    left[target] = left[target] + far_ref[slot, :, cut].astype(F32)

        @pl.when((tile == 0) & (row < NPIV))
        def _():
            left[...] = jnp.zeros((NPIV, BS, BS), F32)

        kept = jnp.zeros((BS, BS), F32)
        for k in range(NPIV):
            value = left[k]
            if k:
                done = slice(0, k * BS)
                value = value - dot3(
                    (left_high[:, done], left_low[:, done]), (chi[done, block(k)], clo[done, block(k)])
                )
            lower = dot3(split(value), (xhi[k], xlo[k]))
            kept = jnp.where(col == k, lower, kept)
            left_high[:, block(k)], left_low[:, block(k)] = split(lower)
        own_ref[...] = kept


def run_panels(child_map, rc, gathered, top, front_left, near, far):
    once = pl.Buffered(1)
    whole = lambda a: pl.BlockSpec(
        a.shape, functools.partial(lambda n, s: (0,) * n, a.ndim), pipeline_mode=once
    )
    upper = pl.BlockSpec((1, 4 * BS, BS), lambda s: (s, 0, 0))
    lower = pl.BlockSpec((BS, 4 * BS), lambda s: (s // 2, 0))
    return pl.pallas_call(
        panels,
        grid=(8,),
        out_shape=[
            shape((8, 4 * BS, BS), BF16), shape((8, 4 * BS, BS), BF16), shape((8, BS, BS), F32),
            shape((4 * BS, 4 * BS), BF16), shape((4 * BS, 4 * BS), BF16), shape((4 * BS, BS), F32),
            shape((BS, BS), F32),
        ],
        in_specs=[
            SMEM, SMEM, whole(gathered),
            pl.BlockSpec((16, PIECE, BS), lambda s: (0, s, 0)),
            pl.BlockSpec((16, 16, BS), lambda s: (0, 32, 0), pipeline_mode=once),
            pl.BlockSpec((4, BS, BS), lambda s: (0, s // 2, 0)),
            whole(near), whole(far),
        ],
        out_specs=[
            upper, upper, pl.BlockSpec((1, BS, BS), lambda s: (s, 0, 0)), lower, lower,
            pl.BlockSpec((BS, BS), lambda s: (s // 2, 0)),
            pl.BlockSpec((BS, BS), lambda s: (0, 0)),
        ],
        scratch_shapes=[
            pltpu.VMEM((4 * BS, 4 * BS), F32), pltpu.VMEM((NPIV, BS, BS), F32),
            pltpu.VMEM((4 * BS, 4 * BS), BF16), pltpu.VMEM((4 * BS, 4 * BS), BF16),
            pltpu.VMEM((NPIV, BS, BS), BF16), pltpu.VMEM((NPIV, BS, BS), BF16),
            pltpu.VMEM((NPIV, BS, BS), F32),
        ],
        compiler_params=pltpu.CompilerParams(vmem_limit_bytes=LIMIT),
        cost_estimate=pl.CostEstimate(
            flops=10 * 2**30, bytes_accessed=32 * 2**20, transcendentals=0
        ),
    )(child_map, rc, gathered, top, top, front_left, near, far)


SPAN = 2


def finish(
    map_ref, rc_ref, front_ref, high_ref, low_ref, left_high, left_low, own_ref, taken_ref,
    block_ref, order_ref, p0, p1, p2, p3, out_ref,
):
    parts = (p0, p1, p2, p3)
    step, s = pl.program_id(0), pl.program_id(1)
    row, col = rc_ref[0], rc_ref[1]
    y, x = row // 4, col // 2

    def at(s, half, tile=0, count=1):
        return pl.ds(tile * BS * 16 + half * 8 + s, count * BS, stride=16)

    def put(s, tile, value):
        for half in range(2):
            out_ref[at(s, half, tile), :] = value[:, half * HALF : half * HALF + HALF]

    total = dot(left_high[...], high_ref[0])
    total = total + dot(left_high[...], low_ref[0])
    total = total + dot(left_low[...], high_ref[0])
    for half in range(2):
        rows = at(s, half, 0, SPAN)
        out_ref[rows, :] = front_ref[rows, :] - total[:, half * HALF : half * HALF + HALF]

    @pl.when(s == 7)
    def _():
        for shift in range(4):
            slot = (y - shift + 4) % 4
            parent = row_of(map_ref, row, slot)
            for hop in range(4):
                source = (x - hop + 4) % 4
                found, value = col_of(map_ref, slot // 2, source, col)
                for tile in range(SPAN):

                    @pl.when((parent >= 0) & (parent // 16 == SPAN * step + tile) & (found >= 0))
                    def _(shift=shift, hop=hop, tile=tile, s=value // 8):
                        for half in range(2):
                            rows = at(s, half, tile)
                            lanes = slice(half * HALF, half * HALF + HALF)
                            out_ref[rows, :] = out_ref[rows, :] + parts[hop][
                                shift, :, lanes
                            ].astype(F32)

        @pl.when(col < NPIV)
        def _():
            for tile in range(SPAN):
                put(0, tile, own_ref[tile * BS : tile * BS + BS])

        @pl.when((step == 0) & (row < NPIV))
        def _():
            select = one_hot(order_ref[...])

            def turn(s, carry):
                value = jnp.concatenate([out_ref[at(s, half), :] for half in range(2)], axis=1)
                put(s, 0, reorder(select, value) - taken_ref[s])
                return carry

            lax.fori_loop(0, 8, turn, 0)

            @pl.when(col < NPIV)
            def _():
                put(0, 0, block_ref[...])


def run_finish(child_map, rc, view, upper, lower, own, taken, corner, order, parts):
    once = pl.Buffered(1)
    whole = lambda a: pl.BlockSpec(
        a.shape, functools.partial(lambda n, t, s: (0,) * n, a.ndim), pipeline_mode=once
    )
    rows = pl.BlockSpec((SPAN * BS * 16, HALF), lambda t, s: (t, 0))
    lefts = pl.BlockSpec((SPAN * BS, 4 * BS), lambda t, s: (t, 0))
    uppers = pl.BlockSpec((1, 4 * BS, BS), lambda t, s: (s, 0, 0))
    return pl.pallas_call(
        finish,
        grid=(4 // SPAN, 8),
        out_shape=shape(view.shape, F32),
        in_specs=[
            SMEM, SMEM, rows, uppers, uppers, lefts, lefts,
            pl.BlockSpec((SPAN * BS, BS), lambda t, s: (t, 0)),
            whole(taken), whole(corner), whole(order), *[whole(p) for p in parts],
        ],
        out_specs=rows,
        compiler_params=pltpu.CompilerParams(vmem_limit_bytes=LIMIT),
        cost_estimate=pl.CostEstimate(
            flops=13 * 2**30, bytes_accessed=32 * 2**20, transcendentals=0
        ),
    )(child_map, rc, view, *upper, *lower, own, taken, corner, order, *parts)


def shards(front, child_update, child_map, pivots):
    row = lax.axis_index("prow")
    col = lax.axis_index("pcol")
    y = row // 4
    x = col // 2
    rc = jnp.stack([row, col]).astype(I32)
    tiles = front.shape[0]
    planes = [[4 * i + j for j in range(4)] for i in range(4)]
    lines = [[4 * j + i for j in range(4)] for i in range(4)]

    def along_z(a, hop):
        return lax.ppermute(
            a, "prow", [(4 * i + j, 4 * i + (j + hop) % 4) for i in range(4) for j in range(4)]
        )

    def along_y(a, hop):
        return lax.ppermute(
            a, "prow", [(4 * i + j, 4 * ((i + hop) % 4) + j) for i in range(4) for j in range(4)]
        )

    def along_x(a, hop):
        return lax.ppermute(
            a, "pcol", [(2 * i + j, 2 * ((i + hop) % 4) + j) for i in range(4) for j in range(2)]
        )

    def from_plane(a, hop):
        return lax.ppermute(a, "prow", [(j, 4 * hop + j) for j in range(4)])

    def cols_to(a, pairs):
        return lax.ppermute(a, "pcol", pairs)

    def chosen(index, options):
        result = options[0]
        for at, option in enumerate(options[1:], 1):
            result = jnp.where(index == at, option, result)
        return result

    cores = [(i, i ^ 1) for i in range(8)]
    second = [(c, c + 4) for c in range(4)]

    strip = shape((BS, 2 * BS), BF16)
    thin = shape((PIECE, 2 * BS), BF16)
    zs = call(pick_z, [strip] * 4, [child_map, rc, child_update.reshape(2, BS, 2 * BS)])
    zs = [zs[0]] + [along_z(zs[hop], hop) for hop in (1, 2, 3)]

    order = jnp.where(
        row < NPIV, pivots[jnp.minimum(row, NPIV - 1)], jnp.arange(BS, dtype=I32)
    )
    order = jnp.broadcast_to(order.astype(F32)[:, None], (BS, HALF))
    view = front.reshape(tiles, BS, 8, 2, HALF).transpose(0, 1, 3, 2, 4)
    view = view.reshape(tiles * BS * 16, HALF)

    cuts = pl.pallas_call(
        cut_front,
        grid=(1,),
        out_shape=[shape((8, PIECE, BS), F32)] * 4,
        in_specs=[
            pl.BlockSpec((BS * 16, HALF), lambda t: (0, 0)),
            pl.BlockSpec((BS, HALF), lambda t: (0, 0)),
        ],
        out_specs=[pl.BlockSpec((8, PIECE, BS), lambda t: (0, 0, 0))] * 4,
        compiler_params=pltpu.CompilerParams(vmem_limit_bytes=LIMIT),
        cost_estimate=pl.CostEstimate(flops=2**30, bytes_accessed=4 * 2**20, transcendentals=0),
    )(view, order)
    cuts = [cuts[0]] + [from_plane(cuts[hop], hop) for hop in (1, 2, 3)]
    far_front = cols_to(chosen(y, [cut[0, 32:] for cut in cuts]), second)

    first = front[:, :, 0, :].reshape(tiles * BS, BS)
    front_left = lax.all_gather(first, "pcol", axis=0, tiled=False)

    zs, cuts = lax.optimization_barrier((zs, cuts))
    picked = call(pick_rows, [thin] * 4 + [strip] * 4, [child_map, rc, order, *zs])
    thin = [picked[0]] + [from_plane(picked[hop], hop) for hop in (1, 2, 3)]
    thin = lax.all_gather(chosen(y, thin), "pcol", axis=0, tiled=False)
    ys = [picked[4]] + [along_y(picked[4 + hop], hop) for hop in (1, 2, 3)]

    thin, ys, front_left = lax.optimization_barrier((thin, ys, front_left))
    code, piece = call(
        assemble,
        [shape((8 * PIECE + 16, BS), I16), shape((32, BS), F32)],
        [child_map, rc, *cuts, far_front, thin],
        scratch=[pltpu.VMEM((8, PIECE, BS), F32)],
    )

    corner = lax.all_gather(piece, "prow", axis=0, tiled=False, axis_index_groups=planes)
    corner = lax.all_gather(corner, "prow", axis=0, tiled=False, axis_index_groups=lines)
    corner = lax.all_gather(corner, "pcol", axis=0, tiled=False)

    (near,) = call(pick_left, [shape((2, BS, 2 * BS), BF16)], [child_map, rc, *ys])
    near = chosen(
        x, [near] + [cols_to(near, [(j, 2 * hop + j) for j in range(2)]) for hop in (1, 2, 3)]
    )
    far = cols_to(near, cores)

    others = cols_to(jnp.stack(ys), cores)
    xs = call(
        pick_x, [shape((4, BS, BS), BF16)] * 4, [child_map, rc, *ys, *[others[i] for i in range(4)]]
    )
    code, *xs = lax.optimization_barrier((code, *xs))
    xs = [xs[0]] + [along_x(xs[hop], hop) for hop in (1, 2, 3)]

    top = lax.all_gather(code, "prow", axis=0, tiled=False)

    *upper, taken, low_a, low_b, own, block_own = run_panels(
        child_map, rc, corner, top, front_left, near, far
    )
    done = run_finish(
        child_map, rc, view, upper, (low_a, low_b), own, taken, block_own, order, xs
    )
    done = done.reshape(tiles, BS, 2, 8, HALF).transpose(0, 1, 3, 2, 4)
    return done.reshape(front.shape)


def solution(mesh):
    return jax.shard_map(
        shards,
        mesh=mesh,
        in_specs=(P(None, "prow", None, "pcol"), P("prow", "pcol"), P(), P()),
        out_specs=P(None, "prow", None, "pcol"),
        check_vma=False,
    )
```

time: 299 us -> 284 us (0.950)
  waiting for transfers between devices: 64.1 us -> 48.6 us
  Pallas kernels: 95.4 us -> 88.8 us
  starting transfers between devices: 40.2 us -> 46.3 us
  blocking collectives: 66.4 us -> 69.7 us
    pallas_call x8 -> x5, Pallas kernels: 55.8 us -> 14.3 us  [call(): pl.pallas_call(body, out_shape=outs, in_specs=[SMEM] * smem + [VMEM] * (l...]
    all_gather x2 -> x1, waiting for transfers between devices: 35.4 us -> 0.02 us  [shards(): front_left = lax.all_gather(first, 'pcol', axis=0, tiled=False)]
    pallas_call x1 -> x2, Pallas kernels: 34.1 us -> 68.9 us  [the longest x1 35.9 us: run_panels(): pl.pallas_call(panels, grid=(8,), out_shape=[shape((8, 4 * BS, BS), BF16)...]
    ppermute x4 -> x6, waiting for transfers between devices: 17.2 us -> 34.5 us  [cols_to(): return lax.ppermute(a, 'pcol', pairs)]
    ppermute x1 -> x3, waiting for transfers between devices: 1 us -> 9.97 us  [along_z(): lax.ppermute(a, 'prow', [(4 * i + j, 4 * i + (j + hop) % 4) for i in rang...]
    ppermute x3, waiting for transfers between devices: 5.7 us -> 0.01 us  [along_y(): lax.ppermute(a, 'prow', [(4 * i + j, 4 * ((i + hop) % 4) + j) for i in ra...]
    all_gather x2 -> x3, blocking collectives: 35 us -> 39.4 us  [the longest x1 17 us: shards(): thin = lax.all_gather(chosen(y, thin), 'pcol', axis=0, tiled=False)]
    ppermute x6, starting transfers between devices: 10.8 us -> 14.3 us  [from_plane(): return lax.ppermute(a, 'prow', [(j, 4 * hop + j) for j in range(4)])]
  transfers between devices with their start and end apart: 20 -> 23, of which waited for: 8 -> 5; matrix products, arithmetic and copies ran while one was open for 3% -> 2% of each run, Pallas kernels for 19% -> 19%
where the time goes in v3:
time: 284 us; the launch traced here: 280 us
  Pallas kernels  88.8 us (31%)
  blocking collectives  69.7 us (25%)
  waiting for transfers between devices  48.6 us (17%)
  starting transfers between devices  46.3 us (16%)
  between operations  13.8 us (5%)
  local copies, waits for them, and re-layouts  9.43 us (3%)
  other arithmetic  3.54 us (1%)
    pallas_call x1, Pallas kernels, run_panels(): pl.pallas_call(panels, grid=(8,), out_shape=[shape((8, 4 * BS, BS), BF16)...  35.9 us
    ppermute x6, waiting for transfers between devices, cols_to(): return lax.ppermute(a, 'pcol', pairs)  34.5 us
    pallas_call x1, Pallas kernels, run_finish(): pl.pallas_call(finish, grid=(4 // SPAN, 8), out_shape=shape(view.shape, F...  33 us
    all_gather x1, blocking collectives, shards(): top = lax.all_gather(code, 'prow', axis=0, tiled=False)  30.3 us
    all_gather x1, blocking collectives, shards(): thin = lax.all_gather(chosen(y, thin), 'pcol', axis=0, tiled=False)  17 us
    ppermute x6, starting transfers between devices, cols_to(): return lax.ppermute(a, 'pcol', pairs)  16.5 us
    ppermute x6, starting transfers between devices, from_plane(): return lax.ppermute(a, 'prow', [(j, 4 * hop + j) for j in range(4)])  14.3 us
    pallas_call x5, Pallas kernels, call(): pl.pallas_call(body, out_shape=outs, in_specs=[SMEM] * smem + [VMEM] * (l...  14.3 us
  transfers between devices with their start and end apart: 23, of which 5 were waited for; matrix products, arithmetic and copies ran while one was open for 2% of the time, Pallas kernels for 19%

profile of v3, /device:TPU:1, one launch (start us, length us, event | category | flops | bytes accessed | tf_op | source)
XLA Modules:
  0.0 280.0 jit_solution(4954948763341765533)
XLA Ops:
  6.5 3.9 %slice.31 = f32[4,256,1,256]{3,2,1,0:T(1,128)S(1)} slice(f32[4,256,8,256]{3,2,1,0:T(8,128)} %param.4), slice={[0:4], [0:256], [0:1], [0:256]} | slice | bytes 2097152 | tf_op jit(solution)/shard_map/slice | solution.py:539
  17.6 5.6 %shard_map.47 = (f32[8,64,256]{2,1,0:T(8,128)}, f32[8,64,256]{2,1,0:T(8,128)}, f32[8,64,256]{2,1,0:T(8,128)}, f32[8,64,256]{2,1,0:T(8,128)}) custom-call(f32[16384,128]{1,0:T(8,128)} %bitcast.34, f32[256,128]{1,0:T(8,128)} %broadcast_in_dim.2.order_ref), custom_call_target="tpu_custom_call" | custom-call | flops 1073741824 | bytes 4194304 | tf_op jit(solution)/shard_map/pallas_call | solution.py:524
  23.1 3.2 %collective-permute-start.3 = (f32[8,64,256]{2,1,0:T(8,128)}, f32[8,64,256]{2,1,0:T(8,128)S(1)}, u32[]{:S(2)}, u32[]{:S(2)}) collective-permute-start(f32[8,64,256]{2,1,0:T(8,128)} %get-tuple-element.58), channel_id=1, source_target_pairs={{0,32},{8,40},{16,48},{24,56},{1,33},{9,41},{17,49},{25,57},{2,34}... | collective-permute-start | bytes 1572872 | tf_op jit(solution)/shard_map/ppermute | solution.py:498
  30.0 3.4 %collective-permute-start.1 = (bf16[256,512]{1,0:T(8,128)(2,1)S(1)}, bf16[256,512]{1,0:T(8,128)(2,1)S(1)}, u32[]{:S(2)}, u32[]{:S(2)}) collective-permute-start(bf16[256,512]{1,0:T(8,128)(2,1)S(1)} %copy-done.20), channel_id=1, source_target_pairs={{0,16},{8,24},{16,0},{24,8},{32,48},{40,56},{48,32},{56,40},{64,80... | collective-permute-start | bytes 786440 | tf_op jit(solution)/shard_map/ppermute | solution.py:483
  34.2 4.6 %collective-permute-done.1.refs_2_ = bf16[256,512]{1,0:T(8,128)(2,1)S(1)} collective-permute-done((bf16[256,512]{1,0:T(8,128)(2,1)S(1)}, bf16[256,512]{1,0:T(8,128)(2,1)S(1)}, u32[]{:S(2)}, u32[]{:S(2)}) %collective-permute-start.1) | collective-permute-done | bytes 262176 | tf_op jit(solution)/shard_map/ppermute | solution.py:483
  38.8 5.4 %collective-permute-done.2.refs_3_ = bf16[256,512]{1,0:T(8,128)(2,1)S(1)} collective-permute-done((bf16[256,512]{1,0:T(8,128)(2,1)S(1)}, bf16[256,512]{1,0:T(8,128)(2,1)S(1)}, u32[]{:S(2)}, u32[]{:S(2)}) %collective-permute-start.2) | collective-permute-done | bytes 262176 | tf_op jit(solution)/shard_map/ppermute | solution.py:483
  44.2 4.0 %collective-permute-done.4.f2 = f32[8,64,256]{2,1,0:T(8,128)S(1)} collective-permute-done((f32[8,64,256]{2,1,0:T(8,128)}, f32[8,64,256]{2,1,0:T(8,128)S(1)}, u32[]{:S(2)}, u32[]{:S(2)}) %collective-permute-start.4) | collective-permute-done | bytes 524320 | tf_op jit(solution)/shard_map/ppermute | solution.py:498
  48.2 3.3 %shard_map.48 = (bf16[64,512]{1,0:T(8,128)(2,1)}, bf16[64,512]{1,0:T(8,128)(2,1)}, bf16[64,512]{1,0:T(8,128)(2,1)}, bf16[64,512]{1,0:T(8,128)(2,1)}, bf16[256,51...) custom-call(s32[2,16]{1,0:T(2,128)} %map_ref.13, ...), custom_call_target="tpu_custom_call" | custom-call | bytes 2490504 | tf_op jit(solution)/shard_map/pallas_call | solution.py:33
  52.9 4.8 %collective-permute-start.8 = (bf16[64,512]{1,0:T(8,128)(2,1)}, bf16[64,512]{1,0:T(8,128)(2,1)S(1)}, u32[]{:S(2)}, u32[]{:S(2)}) collective-permute-start(bf16[64,512]{1,0:T(8,128)(2,1)} %get-tuple-element.70), channel_id=1, source_target_pairs={{0,64},{8,72},{16,80},{24,88},{1,65},{9,73},{17,81},{25,89},{2,66}... | collective-permute-start | bytes 196616 | tf_op jit(solution)/shard_map/ppermute | solution.py:498
  59.7 4.5 %collective-permute-start.6 = (f32[32,256]{1,0:T(8,128)S(1)}, f32[32,256]{1,0:T(8,128)S(1)}, u32[]{:S(2)}, u32[]{:S(2)}) collective-permute-start(f32[32,256]{1,0:T(8,128)S(1)} %fusion.2), channel_id=1, source_target_pairs={{0,4},{1,5},{2,6},{3,7},{8,12},{9,13},{10,14},{11,15},{16,20},{17,... | collective-permute-start | bytes 98312 | tf_op jit(solution)/shard_map/ppermute | solution.py:501
  64.4 2.6 collective-permute-start.12
  67.9 17.0 %all-gather = bf16[512,512]{1,0:T(8,128)(2,1)} all-gather(bf16[64,512]{1,0:T(8,128)(2,1)S(1)} %select_select_fusion.1), channel_id=2, replica_groups=mesh['prow'=16,'pcol'=8] {'pcol'}, dimensions={0}, use_global_device_ids=true | all-gather | bytes 589824 | tf_op jit(solution)/shard_map/all_gather | solution.py:545
  85.8 3.2 %shard_map.49 = (s16[528,256]{1,0:T(8,128)(2,1)}, f32[32,256]{1,0:T(8,128)}) custom-call(s32[2,16]{1,0:T(2,128)} %map_ref.13, s32[2]{0:T(128)} %pad_add_fusion.rc_ref, f32[8,64,256]{2,1,0:T(8,128)} %get-tuple-element.61.f0, f32[8,64,256]{2,1,0:T(8,128)} %copy-done.6, f32[8,64,256]{2,1,0:T(8,128)} %copy-done.7, f32[8,64,256]{2,1,0:T(8,128)} %copy-done.8, ...), custom_call_target="tpu_custom_call" | custom-call | bytes 2957448 | tf_op jit(solution)/shard_map/pallas_call | solution.py:33
  89.0 10.3 %all-gather.1 = f32[128,256]{1,0:T(8,128)S(1)} all-gather(f32[32,256]{1,0:T(8,128)} %get-tuple-element.78), channel_id=3, replica_groups={{0,8,16,24},{32,40,48,56},{64,72,80,88},{96,104,112,120},{1,9,17,25},{3..., dimensions={0}, use_global_device_ids=true | all-gather | bytes 163840 | tf_op jit(solution)/shard_map/all_gather | solution.py:556
  99.3 12.1 %all-gather.2 = f32[16,32,256]{2,1,0:T(8,128)} all-gather(f32[4,32,256]{2,1,0:T(8,128)S(1)} %bitcast.45), channel_id=4, replica_groups={{0,32,64,96},{8,40,72,104},{16,48,80,112},{24,56,88,120},{1,33,65,97},{..., dimensions={0}, use_global_device_ids=true | all-gather | bytes 655360 | tf_op jit(solution)/shard_map/all_gather | solution.py:557
  111.6 4.7 %collective-permute-start.13 = (bf16[4,256,512]{2,1,0:T(8,128)(2,1)S(1)}, bf16[4,256,512]{2,1,0:T(8,128)(2,1)S(1)}, u32[]{:S(2)}, u32[]{:S(2)}) collective-permute-start(bf16[4,256,512]{2,1,0:T(8,128)(2,1)S(1)} %pad_maximum_fusion), channel_id=1, source_target_pairs={{0,1},{1,0},{2,3},{3,2},{4,5},{5,4},{6,7},{7,6},{8,9},{9,8},{10,11... | collective-permute-start | bytes 3145736 | tf_op jit(solution)/shard_map/ppermute | solution.py:501
  119.7 3.3 %collective-permute-start.15 = (bf16[2,256,512]{2,1,0:T(8,128)(2,1)}, bf16[2,256,512]{2,1,0:T(8,128)(2,1)}, u32[]{:S(2)}, u32[]{:S(2)}) collective-permute-start(bf16[2,256,512]{2,1,0:T(8,128)(2,1)} %shard_map.51), channel_id=1, source_target_pairs={{0,4},{1,5},{8,12},{9,13},{16,20},{17,21},{24,28},{25,29},{32,36},... | collective-permute-start | bytes 1572872 | tf_op jit(solution)/shard_map/ppermute | solution.py:501
  125.0 15.2 %collective-permute-done.16 = bf16[2,256,512]{2,1,0:T(8,128)(2,1)S(1)} collective-permute-done((bf16[2,256,512]{2,1,0:T(8,128)(2,1)}, bf16[2,256,512]{2,1,0:T(8,128)(2,1)S(1)}, u32[]{:S(2)}, u32[]{:S(2)}) %collective-permute-start.16) | collective-permute-done | bytes 524320 | tf_op jit(solution)/shard_map/ppermute | solution.py:501
  140.2 19.4 %collective-permute-done.15 = bf16[2,256,512]{2,1,0:T(8,128)(2,1)} collective-permute-done((bf16[2,256,512]{2,1,0:T(8,128)(2,1)}, bf16[2,256,512]{2,1,0:T(8,128)(2,1)}, u32[]{:S(2)}, u32[]{:S(2)}) %collective-permute-start.15) | collective-permute-done | bytes 524320 | tf_op jit(solution)/shard_map/ppermute | solution.py:501
  162.4 3.6 %shard_map.50 = (bf16[4,256,256]{2,1,0:T(8,128)(2,1)}, bf16[4,256,256]{2,1,0:T(8,128)(2,1)}, bf16[4,256,256]{2,1,0:T(8,128)(2,1)}, bf16[4,256,256]{2,1,0:T(8,128)(2,1)}) custom-call(s32[2,16]{1,0:T(2,128)} %map_ref.13, s32[2]{0:T(128)} %pad_add_fusion.rc_ref, bf16[256,512]{1,0:T(8,128)(2,1)} %get-tuple-element.80.refs_0_.h0, bf16[256,512]{1,0:T(8,128)(2,1)} %copy-done.3, ...), custom_call_target="tpu_custom_call" | custom-call | bytes 4194440 | tf_op jit(solution)/shard_map/pallas_call | solution.py:33
  166.0 4.0 %collective-permute-start.19 = (bf16[4,256,256]{2,1,0:T(8,128)(2,1)}, bf16[4,256,256]{2,1,0:T(8,128)(2,1)S(1)}, u32[]{:S(2)}, u32[]{:S(2)}) collective-permute-start(bf16[4,256,256]{2,1,0:T(8,128)(2,1)} %get-tuple-element.99), channel_id=1, source_target_pairs={{0,4},{1,5},{2,6},{3,7},{4,0},{5,1},{6,2},{7,3},{8,12},{9,13},{10,... | collective-permute-start | bytes 1572872 | tf_op jit(solution)/shard_map/ppermute | solution.py:493
  172.0 30.3 %all-gather.12 = s16[8448,256]{1,0:T(8,128)(2,1)} all-gather(s16[528,256]{1,0:T(8,128)(2,1)S(1)} %copy-done.10), channel_id=6, replica_groups=mesh['prow'=16,'pcol'=8] {'prow'}, dimensions={0}, use_global_device_ids=true | all-gather | bytes 4595712 | tf_op jit(solution)/shard_map/all_gather | solution.py:573
  203.1 35.9 %shard_map.52 = (bf16[8,1024,256]{2,1,0:T(8,128)(2,1)}, bf16[8,1024,256]{2,1,0:T(8,128)(2,1)}, f32[8,256,256]{2,1,0:T(8,128)}, bf16[1024,1024]{1,0:T(8,128)(2,1)...) custom-call(s32[2,16]{1,0:T(2,128)} %map_ref.13, s32[2]{0:T(128)} %pad_add_fusion.rc_ref, ...), custom_call_target="tpu_custom_call" | custom-call | flops 10737418240 | bytes 33554432 | tf_op jit(solution)/shard_map/pallas_call | solution.py:348
  240.2 33.0 %shard_map.53 = f32[16384,128]{1,0:T(8,128)} custom-call(s32[2,16]{1,0:T(2,128)} %map_ref.13, s32[2]{0:T(128)} %pad_add_fusion.rc_ref, f32[16384,128]{1,0:T(8,128)} %bitcast.35, bf16[8,1024,256]{2,1,0:T(8,128)(2,1)} %get-tuple-element.90.high_ref, bf16[8,1024,256]{2,1,0:T(8,128)(2,1)} %get-tuple-element.91.low_ref, ...), custom_call_target="tpu_custom_call" | custom-call | flops 13958643712 | bytes 33554432 | tf_op jit(solution)/shard_map/pallas_call | solution.py:455
  (89 shorter events, 29.2 us)
Async XLA Ops:
  6.5 78.5 %all-gather.9.cloned.1.call-start = ((), (), s32[]{:S(2)}) async-start(), calls=%async_computation | async-start | bytes 9437184 | tf_op jit(solution)/shard_map/all_gather | solution.py:540
  11.5 190.8 %all-gather.11.cloned.1.call-start = ((), (), s32[]{:S(2)}) async-start(), calls=%async_computation.1 | async-start | bytes 4718592 | tf_op jit(solution)/shard_map/all_gather | solution.py:558
  14.3 19.1 %collective-permute-start = (bf16[256,512]{1,0:T(8,128)(2,1)}, bf16[256,512]{1,0:T(8,128)(2,1)S(1)}, u32[]{:S(2)}, u32[]{:S(2)}) collective-permute-start(bf16[256,512]{1,0:T(8,128)(2,1)} %get-tuple-element.54), channel_id=1, source_target_pairs={{0,8},{8,16},{16,24},{24,0},{32,40},{40,48},{48,56},{56,32},{64,72... | collective-permute-start | bytes 786440 | tf_op jit(solution)/shard_map/ppermute | solution.py:483
  23.1 21.1 %collective-permute-start.3 = (f32[8,64,256]{2,1,0:T(8,128)}, f32[8,64,256]{2,1,0:T(8,128)S(1)}, u32[]{:S(2)}, u32[]{:S(2)}) collective-permute-start(f32[8,64,256]{2,1,0:T(8,128)} %get-tuple-element.58), channel_id=1, source_target_pairs={{0,32},{8,40},{16,48},{24,56},{1,33},{9,41},{17,49},{25,57},{2,34}... | collective-permute-start | bytes 1572872 | tf_op jit(solution)/shard_map/ppermute | solution.py:498
  26.4 21.8 %collective-permute-start.4 = (f32[8,64,256]{2,1,0:T(8,128)}, f32[8,64,256]{2,1,0:T(8,128)S(1)}, u32[]{:S(2)}, u32[]{:S(2)}) collective-permute-start(f32[8,64,256]{2,1,0:T(8,128)} %get-tuple-element.59), channel_id=1, source_target_pairs={{0,64},{8,72},{16,80},{24,88},{1,65},{9,73},{17,81},{25,89},{2,66}... | collective-permute-start | bytes 1572872 | tf_op jit(solution)/shard_map/ppermute | solution.py:498
  28.7 19.5 %collective-permute-start.5 = (f32[8,64,256]{2,1,0:T(8,128)}, f32[8,64,256]{2,1,0:T(8,128)S(1)}, u32[]{:S(2)}, u32[]{:S(2)}) collective-permute-start(f32[8,64,256]{2,1,0:T(8,128)} %get-tuple-element.60), channel_id=1, source_target_pairs={{0,96},{8,104},{16,112},{24,120},{1,97},{9,105},{17,113},{25,121},... | collective-permute-start | bytes 1572872 | tf_op jit(solution)/shard_map/ppermute | solution.py:498
  30.0 8.8 %collective-permute-start.1 = (bf16[256,512]{1,0:T(8,128)(2,1)S(1)}, bf16[256,512]{1,0:T(8,128)(2,1)S(1)}, u32[]{:S(2)}, u32[]{:S(2)}) collective-permute-start(bf16[256,512]{1,0:T(8,128)(2,1)S(1)} %copy-done.20), channel_id=1, source_target_pairs={{0,16},{8,24},{16,0},{24,8},{32,48},{40,56},{48,32},{56,40},{64,80... | collective-permute-start | bytes 786440 | tf_op jit(solution)/shard_map/ppermute | solution.py:483
  33.4 10.8 %collective-permute-start.2 = (bf16[256,512]{1,0:T(8,128)(2,1)S(1)}, bf16[256,512]{1,0:T(8,128)(2,1)S(1)}, u32[]{:S(2)}, u32[]{:S(2)}) collective-permute-start(bf16[256,512]{1,0:T(8,128)(2,1)S(1)} %copy-done.19), channel_id=1, source_target_pairs={{0,24},{8,0},{16,8},{24,16},{32,56},{40,32},{48,40},{56,48},{64,88... | collective-permute-start | bytes 786440 | tf_op jit(solution)/shard_map/ppermute | solution.py:483
  51.4 12.9 %collective-permute-start.7 = (bf16[64,512]{1,0:T(8,128)(2,1)}, bf16[64,512]{1,0:T(8,128)(2,1)S(1)}, u32[]{:S(2)}, u32[]{:S(2)}) collective-permute-start(bf16[64,512]{1,0:T(8,128)(2,1)} %get-tuple-element.69), channel_id=1, source_target_pairs={{0,96},{8,104},{16,112},{24,120},{1,97},{9,105},{17,113},{25,121},... | collective-permute-start | bytes 196616 | tf_op jit(solution)/shard_map/ppermute | solution.py:498
  52.9 11.6 %collective-permute-start.8 = (bf16[64,512]{1,0:T(8,128)(2,1)}, bf16[64,512]{1,0:T(8,128)(2,1)S(1)}, u32[]{:S(2)}, u32[]{:S(2)}) collective-permute-start(bf16[64,512]{1,0:T(8,128)(2,1)} %get-tuple-element.70), channel_id=1, source_target_pairs={{0,64},{8,72},{16,80},{24,88},{1,65},{9,73},{17,81},{25,89},{2,66}... | collective-permute-start | bytes 196616 | tf_op jit(solution)/shard_map/ppermute | solution.py:498
  57.6 9.4 %collective-permute-start.9 = (bf16[64,512]{1,0:T(8,128)(2,1)}, bf16[64,512]{1,0:T(8,128)(2,1)S(1)}, u32[]{:S(2)}, u32[]{:S(2)}) collective-permute-start(bf16[64,512]{1,0:T(8,128)(2,1)} %get-tuple-element.71), channel_id=1, source_target_pairs={{0,32},{8,40},{16,48},{24,56},{1,33},{9,41},{17,49},{25,57},{2,34}... | collective-permute-start | bytes 196616 | tf_op jit(solution)/shard_map/ppermute | solution.py:498
  59.7 25.3 %collective-permute-start.6 = (f32[32,256]{1,0:T(8,128)S(1)}, f32[32,256]{1,0:T(8,128)S(1)}, u32[]{:S(2)}, u32[]{:S(2)}) collective-permute-start(f32[32,256]{1,0:T(8,128)S(1)} %fusion.2), channel_id=1, source_target_pairs={{0,4},{1,5},{2,6},{3,7},{8,12},{9,13},{10,14},{11,15},{16,20},{17,... | collective-permute-start | bytes 98312 | tf_op jit(solution)/shard_map/ppermute | solution.py:501
  64.2 20.7 %collective-permute-start.10 = (bf16[256,512]{1,0:T(8,128)(2,1)}, bf16[256,512]{1,0:T(8,128)(2,1)S(1)}, u32[]{:S(2)}, u32[]{:S(2)}) collective-permute-start(bf16[256,512]{1,0:T(8,128)(2,1)} %get-tuple-element.74), channel_id=1, source_target_pairs={{0,32},{8,40},{16,48},{24,56},{32,64},{40,72},{48,80},{56,88},{64,... | collective-permute-start | bytes 786440 | tf_op jit(solution)/shard_map/ppermute | solution.py:488
  64.3 20.6 %collective-permute-start.11 = (bf16[256,512]{1,0:T(8,128)(2,1)}, bf16[256,512]{1,0:T(8,128)(2,1)S(1)}, u32[]{:S(2)}, u32[]{:S(2)}) collective-permute-start(bf16[256,512]{1,0:T(8,128)(2,1)} %get-tuple-element.75), channel_id=1, source_target_pairs={{0,64},{8,72},{16,80},{24,88},{32,96},{40,104},{48,112},{56,120},{... | collective-permute-start | bytes 786440 | tf_op jit(solution)/shard_map/ppermute | solution.py:488
  64.4 20.5 %collective-permute-start.12 = (bf16[256,512]{1,0:T(8,128)(2,1)}, bf16[256,512]{1,0:T(8,128)(2,1)S(1)}, u32[]{:S(2)}, u32[]{:S(2)}) collective-permute-start(bf16[256,512]{1,0:T(8,128)(2,1)} %get-tuple-element.76), channel_id=1, source_target_pairs={{0,96},{8,104},{16,112},{24,120},{32,0},{40,8},{48,16},{56,24},{64... | collective-permute-start | bytes 786440 | tf_op jit(solution)/shard_map/ppermute | solution.py:488
  111.6 60.4 %copy-start.10 = (s16[528,256]{1,0:T(8,128)(2,1)S(1)}, s16[528,256]{1,0:T(8,128)(2,1)}, u32[]{:S(2)}) copy-start(s16[528,256]{1,0:T(8,128)(2,1)} %get-tuple-element.88) | copy-start | bytes 811012
  111.6 49.8 %collective-permute-start.13 = (bf16[4,256,512]{2,1,0:T(8,128)(2,1)S(1)}, bf16[4,256,512]{2,1,0:T(8,128)(2,1)S(1)}, u32[]{:S(2)}, u32[]{:S(2)}) collective-permute-start(bf16[4,256,512]{2,1,0:T(8,128)(2,1)S(1)} %pad_maximum_fusion), channel_id=1, source_target_pairs={{0,1},{1,0},{2,3},{3,2},{4,5},{5,4},{6,7},{7,6},{8,9},{9,8},{10,11... | collective-permute-start | bytes 3145736 | tf_op jit(solution)/shard_map/ppermute | solution.py:501
  118.3 21.8 %collective-permute-start.16 = (bf16[2,256,512]{2,1,0:T(8,128)(2,1)}, bf16[2,256,512]{2,1,0:T(8,128)(2,1)S(1)}, u32[]{:S(2)}, u32[]{:S(2)}) collective-permute-start(bf16[2,256,512]{2,1,0:T(8,128)(2,1)} %shard_map.51), channel_id=1, source_target_pairs={{0,2},{1,3},{8,10},{9,11},{16,18},{17,19},{24,26},{25,27},{32,34},... | collective-permute-start | bytes 1572872 | tf_op jit(solution)/shard_map/ppermute | solution.py:501
  119.7 39.9 %collective-permute-start.15 = (bf16[2,256,512]{2,1,0:T(8,128)(2,1)}, bf16[2,256,512]{2,1,0:T(8,128)(2,1)}, u32[]{:S(2)}, u32[]{:S(2)}) collective-permute-start(bf16[2,256,512]{2,1,0:T(8,128)(2,1)} %shard_map.51), channel_id=1, source_target_pairs={{0,4},{1,5},{8,12},{9,13},{16,20},{17,21},{24,28},{25,29},{32,36},... | collective-permute-start | bytes 1572872 | tf_op jit(solution)/shard_map/ppermute | solution.py:501
  122.9 36.6 %collective-permute-start.14 = (bf16[2,256,512]{2,1,0:T(8,128)(2,1)}, bf16[2,256,512]{2,1,0:T(8,128)(2,1)}, u32[]{:S(2)}, u32[]{:S(2)}) collective-permute-start(bf16[2,256,512]{2,1,0:T(8,128)(2,1)} %shard_map.51), channel_id=1, source_target_pairs={{0,6},{1,7},{8,14},{9,15},{16,22},{17,23},{24,30},{25,31},{32,38},... | collective-permute-start | bytes 1572872 | tf_op jit(solution)/shard_map/ppermute | solution.py:501
  160.7 41.5 %collective-permute-start.17 = (bf16[2,256,512]{2,1,0:T(8,128)(2,1)S(1)}, bf16[2,256,512]{2,1,0:T(8,128)(2,1)S(1)}, u32[]{:S(2)}, u32[]{:S(2)}) collective-permute-start(bf16[2,256,512]{2,1,0:T(8,128)(2,1)S(1)} %select_select_fusion.near_ref), channel_id=1, source_target_pairs={{0,1},{1,0},{2,3},{3,2},{4,5},{5,4},{6,7},{7,6},{8,9},{9,8},{10,11... | collective-permute-start | bytes 1572872 | tf_op jit(solution)/shard_map/ppermute | solution.py:501
  166.0 73.0 %collective-permute-start.18 = (bf16[4,256,256]{2,1,0:T(8,128)(2,1)}, bf16[4,256,256]{2,1,0:T(8,128)(2,1)S(1)}, u32[]{:S(2)}, u32[]{:S(2)}) collective-permute-start(bf16[4,256,256]{2,1,0:T(8,128)(2,1)} %get-tuple-element.98), channel_id=1, source_target_pairs={{0,2},{1,3},{2,4},{3,5},{4,6},{5,7},{6,0},{7,1},{8,10},{9,11},{10,... | collective-permute-start | bytes 1572872 | tf_op jit(solution)/shard_map/ppermute | solution.py:493
  166.0 73.0 %collective-permute-start.19 = (bf16[4,256,256]{2,1,0:T(8,128)(2,1)}, bf16[4,256,256]{2,1,0:T(8,128)(2,1)S(1)}, u32[]{:S(2)}, u32[]{:S(2)}) collective-permute-start(bf16[4,256,256]{2,1,0:T(8,128)(2,1)} %get-tuple-element.99), channel_id=1, source_target_pairs={{0,4},{1,5},{2,6},{3,7},{4,0},{5,1},{6,2},{7,3},{8,12},{9,13},{10,... | collective-permute-start | bytes 1572872 | tf_op jit(solution)/shard_map/ppermute | solution.py:493
  170.0 69.0 %collective-permute-start.20 = (bf16[4,256,256]{2,1,0:T(8,128)(2,1)}, bf16[4,256,256]{2,1,0:T(8,128)(2,1)S(1)}, u32[]{:S(2)}, u32[]{:S(2)}) collective-permute-start(bf16[4,256,256]{2,1,0:T(8,128)(2,1)} %get-tuple-element.100), channel_id=1, source_target_pairs={{0,6},{1,7},{2,0},{3,1},{4,2},{5,3},{6,4},{7,5},{8,14},{9,15},{10,... | collective-permute-start | bytes 1572872 | tf_op jit(solution)/shard_map/ppermute | solution.py:493
  (20 other events, 414.3 us)
Sparse Core Ops, SparseCore 0:
  11.7 53.3 all-gather.8
  111.6 44.8 all-gather.10

commit v4 on v3

v4 whole, which is shorter than its diff:
```python
import functools

import jax
import jax.numpy as jnp
from jax import lax
from jax.experimental import pallas as pl
from jax.experimental.pallas import tpu as pltpu
from jax.sharding import PartitionSpec as P

NPIV = 4
NS = 2
BS = 256
HALF = 128
PIECE = 64
FULL = 32767.0
F32 = jnp.float32
BF16 = jnp.bfloat16
I16 = jnp.int16
I32 = jnp.int32
SMEM = pl.BlockSpec(memory_space=pltpu.SMEM)
VMEM = pl.BlockSpec(memory_space=pltpu.VMEM)
LIMIT = 56 * 1024 * 1024


def shape(dims, kind):
    return jax.ShapeDtypeStruct(dims, kind)


def call(body, outs, ins, smem=2, flops=0, scratch=()):
    moved = sum(a.size * a.dtype.itemsize for a in ins)
    moved += sum(o.size * o.dtype.itemsize for o in outs)
    return pl.pallas_call(
        body,
        out_shape=outs,
        in_specs=[SMEM] * smem + [VMEM] * (len(ins) - smem),
        out_specs=[VMEM] * len(outs),
        scratch_shapes=list(scratch),
        compiler_params=pltpu.CompilerParams(vmem_limit_bytes=LIMIT),
        cost_estimate=pl.CostEstimate(flops=flops, bytes_accessed=moved, transcendentals=0),
    )(*ins)


def spot(map_ref, child, low, count, test):
    found = jnp.int32(-1)
    value = jnp.int32(-1)
    for step in range(count):
        entry = map_ref[child, low + step]
        hit = test(entry)
        found = jnp.where(hit, low + step, found)
        value = jnp.where(hit, entry, value)
    return found, value


def row_of(map_ref, row, slot):
    return spot(map_ref, slot // 2, 8 * (slot % 2), 8, lambda entry: entry % 16 == row)[1]


def col_of(map_ref, child, source, col):
    return spot(map_ref, child, 4 * source, 4, lambda entry: entry % 8 == col)


def split(value):
    high = value.astype(BF16)
    low = (value - high.astype(F32)).astype(BF16)
    return high, low


def dot(left, right):
    return jnp.dot(left, right, preferred_element_type=F32)


def dot3(left, right):
    (a, b), (c, d) = left, right
    return dot(a, c) + (dot(a, d) + dot(b, c))


def block(step):
    return slice(step * BS, step * BS + BS)


def one_hot(order):
    spread = lax.broadcasted_iota(I32, (BS, BS), 1).astype(F32)
    return jnp.where(order[:, :1] == spread, 1.0, 0.0).astype(BF16)


def reorder(select, value):
    high = value.astype(BF16)
    rest = value - high.astype(F32)
    middle = rest.astype(BF16)
    last = (rest - middle.astype(F32)).astype(BF16)
    return (dot(select, high) + dot(select, middle)) + dot(select, last)


def level(peak):
    return jnp.ceil(jnp.log2(jnp.full((8, HALF), jnp.maximum(peak, 1e-30))) * 4.0)


def encode(value, n):
    scaled = jnp.abs(value) * jnp.exp2(n * -0.25)[:1, :1]
    code = jnp.minimum(jnp.floor(jnp.sqrt(scaled) * FULL + 0.5), FULL)
    return jnp.where(value < 0.0, -code, code).astype(I32)


def decode(code, n):
    code = code.astype(F32)
    return code * jnp.abs(code) * (jnp.exp2(n.astype(F32)[:1, :1] * 0.25) * (1.0 / (FULL * FULL)))


def cut_front(front_ref, order_ref, *outs):
    firsts, wholes = outs[:4], outs[4:]
    select = one_hot(order_ref[...])

    def one(tile, carry):
        halves = [front_ref[pl.ds(half * 8 + tile, BS, stride=16), :] for half in range(2)]
        turned = reorder(select, jnp.concatenate(halves, axis=1))
        for piece in range(4):
            wholes[piece][tile] = turned[piece * PIECE : piece * PIECE + PIECE]
        return carry

    lax.fori_loop(0, 8, one, 0)
    for piece in range(4):
        firsts[piece][...] = wholes[piece][0]


def pick_z(map_ref, rc_ref, child_ref, *outs):
    row = rc_ref[0]
    z = row % 4
    second_at = map_ref[row // 8, 2 * (row % 8) + 1] % 4
    for hop in range(4):
        outs[hop][...] = child_ref[jnp.where(second_at == (z + hop) % 4, 1, 0)]


def pick_rows(map_ref, rc_ref, order_ref, *refs):
    held, pieces, hops = refs[:4], refs[4:8], refs[8:]
    row = rc_ref[0]
    y, z = row // 4, row % 4
    found, value = spot(map_ref, 0, 0, 4, lambda entry: entry == row)
    live = (found >= 0) & (row < NPIV)
    for hop in range(4):

        @pl.when(live & (found // 2 == (z - hop + 4) % 4))
        def _(hop=hop):
            turned = dot(one_hot(order_ref[...]), held[hop][...]).astype(BF16)
            for piece in range(4):
                pieces[piece][...] = turned[piece * PIECE : piece * PIECE + PIECE]

    @pl.when(jnp.logical_not(live))
    def _():
        for piece in range(4):
            pieces[piece][...] = jnp.zeros((PIECE, 2 * BS), BF16)

    for hop in range(4):
        first = 2 * ((4 * y + (z - hop + 4) % 4) % 8)
        index, value = spot(map_ref, y // 2, first, 2, lambda entry: entry % 4 == z)
        for shift in range(4):

            @pl.when((index >= 0) & ((value // 4) % 4 == (y + shift) % 4))
            def _(hop=hop, shift=shift):
                hops[shift][...] = held[hop][...]


def assemble(map_ref, rc_ref, f0, f1, f2, f3, first_ref, strip, code_ref, work, corner):
    row, col = rc_ref[0], rc_ref[1]
    y = row // 4
    for piece, source in enumerate((f0, f1, f2, f3)):

        @pl.when(y == piece)
        def _(source=source):
            work[...] = source[...]

    corner[...] = first_ref[:NPIV]
    for index in range(16):
        parent = map_ref[0, index]
        cut = slice((index % 2) * BS, (index % 2) * BS + BS)

        @pl.when(parent % 8 == col)
        def _(index=index, cut=cut, tile=parent // 8):
            work[tile] = work[tile] + strip[index // 2, :, cut].astype(F32)

        if index < NPIV:

            @pl.when(parent < NPIV)
            def _(index=index, cut=cut, parent=parent):
                corner[parent] = corner[parent] + strip[index // 2, :, cut].astype(F32)

    @pl.when(col < NPIV)
    def _():
        work[0] = jnp.zeros((PIECE, BS), F32)

    n = level(jnp.max(jnp.abs(work[...])))
    for tile in range(8):
        code_ref[tile * PIECE : tile * PIECE + PIECE] = encode(work[tile], n).astype(I16)
    first = level(jnp.max(jnp.abs(corner[...])))
    low = 8 * PIECE
    for k in range(NPIV):
        code = encode(corner[k], first)
        code_ref[low + k * PIECE : low + k * PIECE + PIECE] = code.astype(I16)
        corner[k] = corner[k] - decode(code, first)
    second = level(jnp.max(jnp.abs(corner[...])))
    low = 12 * PIECE
    for k in range(NPIV):
        code_ref[low + k * PIECE : low + k * PIECE + PIECE] = encode(corner[k], second).astype(I16)
    line = lax.broadcasted_iota(I32, (16, BS), 0)
    scales = jnp.where(line == 0, n[:1, :1], jnp.where(line == 1, first[:1, :1], second[:1, :1]))
    code_ref[16 * PIECE :] = scales.astype(I32).astype(I16)


def pack(rc_ref, h0, h1, h2, h3, out_ref):
    y = rc_ref[0] // 4
    for shift, source in enumerate((h0, h1, h2, h3)):
        out_ref[(y - shift + 4) % 4] = source[...]


def factor_corner(code_ref, level_ref, work, xhi, xlo):
    for y in range(4):
        for z in range(4):
            low = z * BS + y * PIECE
            scale = level_ref[4 * y + z].astype(I32)
            for k in range(4):
                rows = slice(k * PIECE, k * PIECE + PIECE)
                rest = slice((4 + k) * PIECE, (4 + k) * PIECE + PIECE)
                work[low : low + PIECE, block(k)] = decode(
                    code_ref[4 * y + z, rows].astype(I32), scale[1:2]
                ) + decode(code_ref[4 * y + z, rest].astype(I32), scale[2:3])
    diagonal = lax.broadcasted_iota(I32, (BS, BS), 0) == lax.broadcasted_iota(I32, (BS, BS), 1)
    for k in range(NPIV):
        pivot = work[block(k), block(k)]
        parts = split(pivot)
        on_line = jnp.where(diagonal, pivot, 0.0)
        across = jnp.sum(on_line, axis=0, keepdims=True)
        down = jnp.sum(on_line, axis=1, keepdims=True)
        across = across / (across * across + 1.0)
        down = down / (down * down + 1.0)
        approx = 2.0 * jnp.where(diagonal, across, 0.0) - (down * pivot) * across
        for sweep_index in range(NS - 1):
            pair = split(approx)
            approx = 2.0 * approx - dot3(split(dot3(pair, parts)), pair)
        xhi[k], xlo[k] = split(approx)
        if k + 1 < NPIV:
            below = slice((k + 1) * BS, NPIV * BS)
            lower = dot3(split(work[below, block(k)]), (xhi[k], xlo[k]))
            work[below, block(k)] = lower
            work[below, below] = work[below, below] - dot3(
                split(lower), split(work[block(k), below])
            )


SPAN = 2
WIDE = 4


def panels(
    map_ref, rc_ref, corner_ref, code_ref, level_ref, front_ref, child_ref,
    high_ref, low_ref, taken_ref, left_high, left_low, own_ref, block_ref,
    work, chi, clo, xhi, xlo, raw, left,
):
    step = pl.program_id(0)
    row, col = rc_ref[0], rc_ref[1]

    @pl.when(step == 0)
    def _():
        factor_corner(corner_ref, level_ref, work, xhi, xlo)
        for k in range(NPIV):
            chi[block(k)], clo[block(k)] = split(work[block(k)])
        for r in range(NPIV):
            for c in range(NPIV):

                @pl.when((row == r) & (col == c))
                def _(r=r, c=c):
                    block_ref[...] = work[block(r), block(c)]

    taken_ref[0] = jnp.zeros((BS, WIDE * BS), F32)
    for k in range(NPIV):
        for piece in range(4):
            scale = level_ref[4 * piece + k].astype(I32)
            for q in range(WIDE):
                raw[piece * PIECE : piece * PIECE + PIECE, block(q)] = decode(
                    code_ref[4 * piece + k, q * PIECE : q * PIECE + PIECE].astype(I32), scale
                )
        if k:
            done = slice(0, k * BS)
            taken = dot3(
                (chi[block(k), done], clo[block(k), done]), (high_ref[0, done], low_ref[0, done])
            )
            raw[...] = raw[...] - taken

            @pl.when(row == k)
            def _(taken=taken):
                taken_ref[0] = taken

        high_ref[0, block(k)], low_ref[0, block(k)] = split(raw[...])

    for k in range(NPIV):
        left[:, block(k)] = front_ref[k]
    for slot in range(2):
        parent = row_of(map_ref, row, slot)
        for index in range(4):
            target = map_ref[0, index]
            cut = slice((index % 2) * BS, (index % 2) * BS + BS)
            for tile in range(SPAN):
                for k in range(index, NPIV):

                    @pl.when((parent >= 0) & (parent // 16 == SPAN * step + tile) & (target == k))
                    def _(slot=slot, index=index, cut=cut, tile=tile, k=k):
                        left[block(tile), block(k)] = left[block(tile), block(k)] + child_ref[
                            index // 2, slot, :, cut
                        ].astype(F32)

    @pl.when((step == 0) & (row < NPIV))
    def _():
        left[:BS] = jnp.zeros((BS, NPIV * BS), F32)

    for k in range(NPIV):
        lower = dot3(split(left[:, block(k)]), (xhi[k], xlo[k]))
        pair = split(lower)
        left_high[:, block(k)], left_low[:, block(k)] = pair

        @pl.when(col == k)
        def _(lower=lower):
            own_ref[...] = lower

        if k + 1 < NPIV:
            rest = slice((k + 1) * BS, NPIV * BS)
            left[:, rest] = left[:, rest] - dot3(pair, (chi[block(k), rest], clo[block(k), rest]))


def run_panels(child_map, rc, top, front_left, child):
    once = pl.Buffered(1)
    upper = pl.BlockSpec((1, 4 * BS, WIDE * BS), lambda s: (s, 0, 0))
    lower = pl.BlockSpec((SPAN * BS, 4 * BS), lambda s: (s, 0))
    return pl.pallas_call(
        panels,
        grid=(2,),
        out_shape=[
            shape((2, 4 * BS, WIDE * BS), BF16), shape((2, 4 * BS, WIDE * BS), BF16),
            shape((2, BS, WIDE * BS), F32),
            shape((4 * BS, 4 * BS), BF16), shape((4 * BS, 4 * BS), BF16), shape((4 * BS, BS), F32),
            shape((BS, BS), F32),
        ],
        in_specs=[
            SMEM, SMEM,
            pl.BlockSpec((16, 8 * PIECE, BS), lambda s: (0, 1, 0), pipeline_mode=once),
            pl.BlockSpec((16, WIDE * PIECE, BS), lambda s: (0, s, 0)),
            pl.BlockSpec((16, 16, BS), lambda s: (0, PIECE, 0), pipeline_mode=once),
            pl.BlockSpec((4, SPAN * BS, BS), lambda s: (0, s, 0)),
            pl.BlockSpec((2, 2, BS, 2 * BS), lambda s: (0, 0, 0, 0), pipeline_mode=once),
        ],
        out_specs=[
            upper, upper, pl.BlockSpec((1, BS, WIDE * BS), lambda s: (s, 0, 0)), lower, lower,
            pl.BlockSpec((SPAN * BS, BS), lambda s: (s, 0)),
            pl.BlockSpec((BS, BS), lambda s: (0, 0)),
        ],
        scratch_shapes=[
            pltpu.VMEM((4 * BS, 4 * BS), F32),
            pltpu.VMEM((4 * BS, 4 * BS), BF16), pltpu.VMEM((4 * BS, 4 * BS), BF16),
            pltpu.VMEM((NPIV, BS, BS), BF16), pltpu.VMEM((NPIV, BS, BS), BF16),
            pltpu.VMEM((BS, WIDE * BS), F32), pltpu.VMEM((SPAN * BS, 4 * BS), F32),
        ],
        compiler_params=pltpu.CompilerParams(vmem_limit_bytes=LIMIT),
        cost_estimate=pl.CostEstimate(
            flops=10 * 2**30, bytes_accessed=32 * 2**20, transcendentals=0
        ),
    )(child_map, rc, top, top, top, front_left, child)


def finish(
    map_ref, rc_ref, front_ref, high_ref, low_ref, left_high, left_low, own_ref, taken_ref,
    block_ref, order_ref, child_ref, out_ref, total, parts, arrived,
):
    step, group = pl.program_id(0), pl.program_id(1)
    row, col = rc_ref[0], rc_ref[1]

    def at(s, half, tile=0, count=1):
        return pl.ds(tile * BS * 16 + half * 8 + s, count * BS, stride=16)

    def put(s, tile, value):
        for half in range(2):
            out_ref[at(s, half, tile), :] = value[:, half * HALF : half * HALF + HALF]

    def each_child(act):
        for slot in range(4):
            parent = row_of(map_ref, row, slot)
            here = (parent >= 0) & (parent // 16 // SPAN == step)
            for source in range(4):
                found, value = col_of(map_ref, slot // 2, source, col)
                where = jnp.maximum(found, 0)
                start = pl.multiple_of((where % 2) * BS, BS)
                index = 4 * slot + source
                copy = pltpu.make_async_copy(
                    child_ref.at[where // 2, slot, :, pl.ds(start, BS)],
                    parts.at[index],
                    arrived.at[index],
                )

                @pl.when(here & (found >= 0))
                def _(copy=copy, index=index, tile=(parent // 16) % SPAN, s=value // 8):
                    act(copy, index, tile, s)

    @pl.when(group == 0)
    def _():
        each_child(lambda copy, index, tile, s: copy.start())

    total[...] = dot(left_high[...], high_ref[0])
    total[...] += dot(left_high[...], low_ref[0])
    total[...] += dot(left_low[...], high_ref[0])
    for q in range(WIDE):
        for half in range(2):
            rows = at(WIDE * group + q, half, 0, SPAN)
            low = q * BS + half * HALF
            out_ref[rows, :] = front_ref[rows, :] - total[:, low : low + HALF]

    @pl.when(group == 1)
    def _():
        def add(copy, index, tile, s):
            copy.wait()
            for half in range(2):
                rows = at(s, half, tile)
                lanes = slice(half * HALF, half * HALF + HALF)
                out_ref[rows, :] = out_ref[rows, :] + parts[index, :, lanes].astype(F32)

        each_child(add)

        @pl.when(col < NPIV)
        def _():
            for tile in range(SPAN):
                put(0, tile, own_ref[tile * BS : tile * BS + BS])

        @pl.when((step == 0) & (row < NPIV))
        def _():
            select = one_hot(order_ref[...])
            for s in range(2 * WIDE):
                value = jnp.concatenate([out_ref[at(s, half), :] for half in range(2)], axis=1)
                put(s, 0, reorder(select, value) - taken_ref[s // WIDE, :, block(s % WIDE)])

            @pl.when(col < NPIV)
            def _():
                put(0, 0, block_ref[...])


def run_finish(child_map, rc, view, upper, lower, own, taken, corner, order, child):
    once = pl.Buffered(1)
    whole = lambda a: pl.BlockSpec(
        a.shape, functools.partial(lambda n, t, s: (0,) * n, a.ndim), pipeline_mode=once
    )
    rows = pl.BlockSpec((SPAN * BS * 16, HALF), lambda t, s: (t, 0))
    lefts = pl.BlockSpec((SPAN * BS, 4 * BS), lambda t, s: (t, 0))
    uppers = pl.BlockSpec((1, 4 * BS, WIDE * BS), lambda t, s: (s, 0, 0))
    return pl.pallas_call(
        finish,
        grid=(4 // SPAN, 2),
        out_shape=shape(view.shape, F32),
        in_specs=[
            SMEM, SMEM, rows, uppers, uppers, lefts, lefts,
            pl.BlockSpec((SPAN * BS, BS), lambda t, s: (t, 0)),
            whole(taken), whole(corner), whole(order), pl.BlockSpec(memory_space=pl.ANY),
        ],
        out_specs=rows,
        scratch_shapes=[
            pltpu.VMEM((SPAN * BS, WIDE * BS), F32),
            pltpu.VMEM((16, BS, BS), BF16),
            pltpu.SemaphoreType.DMA((16,)),
        ],
        compiler_params=pltpu.CompilerParams(vmem_limit_bytes=LIMIT),
        cost_estimate=pl.CostEstimate(
            flops=13 * 2**30, bytes_accessed=32 * 2**20, transcendentals=0
        ),
    )(child_map, rc, view, *upper, *lower, own, taken, corner, order, child)


def shards(front, child_update, child_map, pivots):
    row = lax.axis_index("prow")
    col = lax.axis_index("pcol")
    y = row // 4
    rc = jnp.stack([row, col]).astype(I32)
    tiles = front.shape[0]

    def along_z(a, hop):
        return lax.ppermute(
            a, "prow", [(4 * i + j, 4 * i + (j + hop) % 4) for i in range(4) for j in range(4)]
        )

    def along_y(a, hop):
        return lax.ppermute(
            a, "prow", [(4 * i + j, 4 * ((i + hop) % 4) + j) for i in range(4) for j in range(4)]
        )

    def from_plane(a, hop):
        return lax.ppermute(a, "prow", [(j, 4 * hop + j) for j in range(4)])

    def spread(pieces):
        return [pieces[0]] + [from_plane(pieces[hop], hop) for hop in (1, 2, 3)]

    def chosen(index, options):
        result = options[0]
        for at, option in enumerate(options[1:], 1):
            result = jnp.where(index == at, option, result)
        return result

    strip = shape((BS, 2 * BS), BF16)
    zs = call(pick_z, [strip] * 4, [child_map, rc, child_update.reshape(2, BS, 2 * BS)])
    zs = [zs[0]] + [along_z(zs[hop], hop) for hop in (1, 2, 3)]

    order = jnp.where(
        row < NPIV, pivots[jnp.minimum(row, NPIV - 1)], jnp.arange(BS, dtype=I32)
    )
    order = jnp.broadcast_to(order.astype(F32)[:, None], (BS, HALF))
    view = front.reshape(tiles, BS, 8, 2, HALF).transpose(0, 1, 3, 2, 4)
    view = view.reshape(tiles * BS * 16, HALF)

    cuts = pl.pallas_call(
        cut_front,
        grid=(1,),
        out_shape=[shape((PIECE, BS), F32)] * 4 + [shape((8, PIECE, BS), F32)] * 4,
        in_specs=[
            pl.BlockSpec((BS * 16, HALF), lambda t: (0, 0)),
            pl.BlockSpec((BS, HALF), lambda t: (0, 0)),
        ],
        out_specs=[pl.BlockSpec((PIECE, BS), lambda t: (0, 0))] * 4
        + [pl.BlockSpec((8, PIECE, BS), lambda t: (0, 0, 0))] * 4,
        compiler_params=pltpu.CompilerParams(vmem_limit_bytes=LIMIT),
        cost_estimate=pl.CostEstimate(flops=2**30, bytes_accessed=4 * 2**20, transcendentals=0),
    )(view, order)
    firsts = lax.all_gather(chosen(y, spread(cuts[:4])), "pcol", axis=0, tiled=False)
    cuts = spread(cuts[4:])

    front_left = front[:, :, 0, :].reshape(tiles * BS, BS)
    zs, firsts, front_left = lax.optimization_barrier((zs, firsts, front_left))
    front_left = lax.all_gather(front_left, "pcol", axis=0, tiled=False)

    thin = shape((PIECE, 2 * BS), BF16)
    picked = call(pick_rows, [thin] * 4 + [strip] * 4, [child_map, rc, order, *zs])
    thin = lax.all_gather(chosen(y, spread(picked[:4])), "pcol", axis=0, tiled=False)
    ys = [picked[4]] + [along_y(picked[4 + hop], hop) for hop in (1, 2, 3)]

    thin, ys, front_left = lax.optimization_barrier((thin, ys, front_left))
    (code,) = call(
        assemble,
        [shape((16 * PIECE + 16, BS), I16)],
        [child_map, rc, *cuts, firsts, thin],
        scratch=[pltpu.VMEM((8, PIECE, BS), F32), pltpu.VMEM((NPIV, PIECE, BS), F32)],
    )

    (child,) = call(pack, [shape((4, BS, 2 * BS), BF16)], [rc, *ys], smem=1)
    code, child = lax.optimization_barrier((code, child))
    child = lax.all_gather(child, "pcol", axis=0, tiled=False)
    top = lax.all_gather(code, "prow", axis=0, tiled=False)

    *upper, taken, low_a, low_b, own, block_own = run_panels(
        child_map, rc, top, front_left, child
    )
    done = run_finish(
        child_map, rc, view, upper, (low_a, low_b), own, taken, block_own, order, child
    )
    done = done.reshape(tiles, BS, 2, 8, HALF).transpose(0, 1, 3, 2, 4)
    return done.reshape(front.shape)


def solution(mesh):
    return jax.shard_map(
        shards,
        mesh=mesh,
        in_specs=(P(None, "prow", None, "pcol"), P("prow", "pcol"), P(), P()),
        out_specs=P(None, "prow", None, "pcol"),
        check_vma=False,
    )
```

time: 284 us -> 232 us (0.82)
  waiting for transfers between devices: 48.6 us -> 13 us
  starting transfers between devices: 46.3 us -> 27.4 us
  blocking collectives: 69.7 us -> 86.7 us
  Pallas kernels: 88.8 us -> 77.5 us
    ppermute x9 -> x0, waiting for transfers between devices: 34.5 us -> none  [the longest x6 34.5 us: cols_to(): return lax.ppermute(a, 'pcol', pairs)]
    all_gather x1, blocking collectives: 30.3 us -> 53.7 us  [shards(): top = lax.all_gather(code, 'prow', axis=0, tiled=False)]
    ppermute x9 -> x0, starting transfers between devices: 22.5 us -> none  [the longest x6 16.5 us: cols_to(): return lax.ppermute(a, 'pcol', pairs)]
    ppermute x3, waiting for transfers between devices: 9.97 us -> 0.01 us  [along_z(): lax.ppermute(a, 'prow', [(4 * i + j, 4 * i + (j + hop) % 4) for i in rang...]
    pallas_call x3, Pallas kernels: 74.5 us -> 66.4 us  [the longest x1 30.4 us: run_panels(): pl.pallas_call(panels, grid=(2,), out_shape=[shape((2, 4 * BS, WIDE * BS)...]
    all_gather x2, waiting for transfers between devices: 0.04 us -> 7.02 us  [the longest x1 7.01 us: shards(): front_left = lax.all_gather(front_left, 'pcol', axis=0, tiled=False)]
    all_gather x3 -> x2, blocking collectives: 39.4 us -> 33 us  [the longest x1 16.8 us: shards(): lax.all_gather(chosen(y, spread(picked[:4])), 'pcol', axis=0, tiled=False)]
    ppermute x3, waiting for transfers between devices: 0.01 us -> 5.89 us  [along_y(): lax.ppermute(a, 'prow', [(4 * i + j, 4 * ((i + hop) % 4) + j) for i in ra...]
  transfers between devices with their start and end apart: 23 -> 17, of which waited for: 5 -> 2; matrix products, arithmetic and copies ran while one was open for 2% -> 3% of each run, Pallas kernels for 19% -> 3%
where the time goes in v4:
time: 232 us; the launch traced here: 229 us
  blocking collectives  86.7 us (37%)
  Pallas kernels  77.5 us (33%)
  starting transfers between devices  27.4 us (12%)
  between operations  13.6 us (6%)
  waiting for transfers between devices  13 us (6%)
  local copies, waits for them, and re-layouts  8.31 us (4%)
  other arithmetic  2.38 us (1%)
    all_gather x1, blocking collectives, shards(): top = lax.all_gather(code, 'prow', axis=0, tiled=False)  53.7 us
    pallas_call x1, Pallas kernels, run_panels(): pl.pallas_call(panels, grid=(2,), out_shape=[shape((2, 4 * BS, WIDE * BS)...  30.4 us
    pallas_call x1, Pallas kernels, run_finish(): pl.pallas_call(finish, grid=(4 // SPAN, 2), out_shape=shape(view.shape, F...  30.3 us
    ppermute x9, starting transfers between devices, from_plane(): return lax.ppermute(a, 'prow', [(j, 4 * hop + j) for j in range(4)])  19.7 us
    all_gather x1, blocking collectives, shards(): lax.all_gather(chosen(y, spread(picked[:4])), 'pcol', axis=0, tiled=False)  16.8 us
    all_gather x1, blocking collectives, shards(): lax.all_gather(chosen(y, spread(cuts[:4])), 'pcol', axis=0, tiled=False)  16.2 us
    pallas_call x4, Pallas kernels, call(): pl.pallas_call(body, out_shape=outs, in_specs=[SMEM] * smem + [VMEM] * (l...  11.1 us
    all_gather x1, waiting for transfers between devices, shards(): front_left = lax.all_gather(front_left, 'pcol', axis=0, tiled=False)  7.01 us
  transfers between devices with their start and end apart: 17, of which 2 were waited for; matrix products, arithmetic and copies ran while one was open for 3% of the time, Pallas kernels for 3%

profile of v4, /device:TPU:1, one launch (start us, length us, event | category | flops | bytes accessed | tf_op | source)
XLA Modules:
  0.0 228.8 jit_solution(11958488694813879318)
XLA Ops:
  8.0 5.7 %shard_map.46 = (f32[64,256]{1,0:T(8,128)}, f32[64,256]{1,0:T(8,128)}, f32[64,256]{1,0:T(8,128)}, f32[64,256]{1,0:T(8,128)}, f32[8,64,256]{2,1,0:T(8,128)}, /*in...) custom-call(f32[16384,128]{1,0:T(8,128)} %bitcast.23, f32[256,128]{1,0:T(8,128)} %broadcast_in_dim.2.order_ref), custom_call_target="tpu_custom_call" | custom-call | flops 1073741824 | bytes 4194304 | tf_op jit(solution)/shard_map/pallas_call | solution.py:510
  13.7 5.5 %collective-permute-start.6 = (f32[64,256]{1,0:T(8,128)}, f32[64,256]{1,0:T(8,128)S(1)}, u32[]{:S(2)}, u32[]{:S(2)}) collective-permute-start(f32[64,256]{1,0:T(8,128)} %get-tuple-element.54), channel_id=1, source_target_pairs={{0,96},{8,104},{16,112},{24,120},{1,97},{9,105},{17,113},{25,121},... | collective-permute-start | bytes 196616 | tf_op jit(solution)/shard_map/ppermute | solution.py:488
  20.5 1.3 collective-permute-start.8
  22.4 2.1 shard_map.47
  24.5 1.6 collective-permute-start.3
  26.2 3.3 %collective-permute-start.4 = (bf16[256,512]{1,0:T(8,128)(2,1)}, bf16[256,512]{1,0:T(8,128)(2,1)S(1)}, u32[]{:S(2)}, u32[]{:S(2)}) collective-permute-start(bf16[256,512]{1,0:T(8,128)(2,1)} %get-tuple-element.52), channel_id=1, source_target_pairs={{0,16},{8,24},{16,0},{24,8},{32,48},{40,56},{48,32},{56,40},{64,80... | collective-permute-start | bytes 786440 | tf_op jit(solution)/shard_map/ppermute | solution.py:478
  29.5 3.9 %slice.3 = f32[4,256,1,256]{3,2,1,0:T(1,128)S(1)} slice(f32[4,256,8,256]{3,2,1,0:T(8,128)} %param.4), slice={[0:4], [0:256], [0:1], [0:256]} | slice | bytes 2097152 | tf_op jit(solution)/shard_map/slice | solution.py:526
  36.0 16.2 %all-gather = f32[512,256]{1,0:T(8,128)} all-gather(f32[64,256]{1,0:T(8,128)S(1)} %select_select_fusion.1), channel_id=2, replica_groups=mesh['prow'=16,'pcol'=8] {'pcol'}, dimensions={0}, use_global_device_ids=true | all-gather | bytes 589824 | tf_op jit(solution)/shard_map/all_gather | solution.py:523
  53.1 2.9 %shard_map.48 = (bf16[64,512]{1,0:T(8,128)(2,1)}, bf16[64,512]{1,0:T(8,128)(2,1)}, bf16[64,512]{1,0:T(8,128)(2,1)}, bf16[64,512]{1,0:T(8,128)(2,1)}, bf16[256,51...) custom-call(s32[2,16]{1,0:T(2,128)} %map_ref.9, ...), custom_call_target="tpu_custom_call" | custom-call | bytes 2490504 | tf_op jit(solution)/shard_map/pallas_call | solution.py:32
  56.0 4.6 %collective-permute-start.9 = (bf16[64,512]{1,0:T(8,128)(2,1)}, bf16[64,512]{1,0:T(8,128)(2,1)S(1)}, u32[]{:S(2)}, u32[]{:S(2)}) collective-permute-start(bf16[64,512]{1,0:T(8,128)(2,1)} %get-tuple-element.63), channel_id=1, source_target_pairs={{0,96},{8,104},{16,112},{24,120},{1,97},{9,105},{17,113},{25,121},... | collective-permute-start | bytes 196616 | tf_op jit(solution)/shard_map/ppermute | solution.py:488
  60.5 1.3 collective-permute-start.10
  61.8 1.3 collective-permute-start.11
  63.1 1.3 collective-permute-start
  64.5 1.3 collective-permute-start.1
  65.8 1.9 collective-permute-start.2
  67.8 1.8 collective-permute-start.14
  70.5 16.8 %all-gather.1 = bf16[512,512]{1,0:T(8,128)(2,1)} all-gather(bf16[64,512]{1,0:T(8,128)(2,1)S(1)} %select_select_fusion), channel_id=3, replica_groups=mesh['prow'=16,'pcol'=8] {'pcol'}, dimensions={0}, use_global_device_ids=true | all-gather | bytes 589824 | tf_op jit(solution)/shard_map/all_gather | solution.py:532
  87.4 5.9 %collective-permute-done.13.h2 = bf16[256,512]{1,0:T(8,128)(2,1)S(1)} collective-permute-done((bf16[256,512]{1,0:T(8,128)(2,1)}, bf16[256,512]{1,0:T(8,128)(2,1)S(1)}, u32[]{:S(2)}, u32[]{:S(2)}) %collective-permute-start.13) | collective-permute-done | bytes 262176 | tf_op jit(solution)/shard_map/ppermute | solution.py:483
  93.3 7.0 %all-gather.9.cloned.1.call-done = f32[8192,256]{1,0:T(8,128)} async-done(((f32[1024,256]{1,0:T(8,128)}), f32[8192,256]{1,0:T(8,128)}) %all-gather.9.cloned.1.call-update) | async-done | bytes 8388624 | tf_op jit(solution)/shard_map/all_gather | solution.py:528
  100.3 2.2 shard_map.50
  103.7 3.8 %shard_map.49 = s16[1040,256]{1,0:T(8,128)(2,1)} custom-call(s32[2,16]{1,0:T(2,128)} %map_ref.9, s32[2]{0:T(128)} %pad_add_fusion.rc_ref, f32[8,64,256]{2,1,0:T(8,128)} %get-tuple-element.46.f0, f32[8,64,256]{2,1,0:T(8,128)} %copy-done.2, f32[8,64,256]{2,1,0:T(8,128)} %copy-done.3, f32[8,64,256]{2,1,0:T(8,128)} %copy-done.4, f32[8,64,256]{2,1,0:T(8,128)} %bitcast.29, ...), custom_call_target="tpu_custom_call" | custom-call | bytes 3678344 | tf_op jit(solution)/shard_map/pallas_call | solution.py:32
  107.6 53.7 %all-gather.12 = s16[16640,256]{1,0:T(8,128)(2,1)} all-gather(s16[1040,256]{1,0:T(8,128)(2,1)} %shard_map.49), channel_id=5, replica_groups=mesh['prow'=16,'pcol'=8] {'prow'}, dimensions={0}, use_global_device_ids=true | all-gather | bytes 9052160 | tf_op jit(solution)/shard_map/all_gather | solution.py:546
  161.3 30.4 %shard_map.51 = (bf16[2,1024,1024]{2,1,0:T(8,128)(2,1)}, bf16[2,1024,1024]{2,1,0:T(8,128)(2,1)}, f32[2,256,1024]{2,1,0:T(8,128)}, bf16[1024,1024]{1,0:T(8,128)(2...) custom-call(s32[2,16]{1,0:T(2,128)} %map_ref.9, s32[2]{0:T(128)} %pad_add_fusion.rc_ref, ...), custom_call_target="tpu_custom_call" | custom-call | flops 10737418240 | bytes 33554432 | tf_op jit(solution)/shard_map/pallas_call | solution.py:331
  191.7 30.3 %shard_map.52 = f32[16384,128]{1,0:T(8,128)} custom-call(s32[2,16]{1,0:T(2,128)} %map_ref.9, s32[2]{0:T(128)} %pad_add_fusion.rc_ref, f32[16384,128]{1,0:T(8,128)} %bitcast.24, bf16[2,1024,1024]{2,1,0:T(8,128)(2,1)} %get-tuple-element.80.high_ref, bf16[2,1024,1024]{2,1,0:T(8,128)(2,1)} %get-tuple-element.81.low_ref, ...), custom_call_target="tpu_custom_call" | custom-call | flops 13958643712 | bytes 33554432 | tf_op jit(solution)/shard_map/pallas_call | solution.py:448
  (52 shorter events, 9.0 us)
Async XLA Ops:
  6.5 93.7 %all-gather.9.cloned.1.call-start = ((), (), s32[]{:S(2)}) async-start(), calls=%async_computation | async-start | bytes 9437184 | tf_op jit(solution)/shard_map/all_gather | solution.py:528
  13.7 20.8 %collective-permute-start.6 = (f32[64,256]{1,0:T(8,128)}, f32[64,256]{1,0:T(8,128)S(1)}, u32[]{:S(2)}, u32[]{:S(2)}) collective-permute-start(f32[64,256]{1,0:T(8,128)} %get-tuple-element.54), channel_id=1, source_target_pairs={{0,96},{8,104},{16,112},{24,120},{1,97},{9,105},{17,113},{25,121},... | collective-permute-start | bytes 196616 | tf_op jit(solution)/shard_map/ppermute | solution.py:488
  19.2 16.0 %collective-permute-start.7 = (f32[64,256]{1,0:T(8,128)}, f32[64,256]{1,0:T(8,128)S(1)}, u32[]{:S(2)}, u32[]{:S(2)}) collective-permute-start(f32[64,256]{1,0:T(8,128)} %get-tuple-element.55), channel_id=1, source_target_pairs={{0,64},{8,72},{16,80},{24,88},{1,65},{9,73},{17,81},{25,89},{2,66}... | collective-permute-start | bytes 196616 | tf_op jit(solution)/shard_map/ppermute | solution.py:488
  20.5 14.7 %collective-permute-start.8 = (f32[64,256]{1,0:T(8,128)}, f32[64,256]{1,0:T(8,128)S(1)}, u32[]{:S(2)}, u32[]{:S(2)}) collective-permute-start(f32[64,256]{1,0:T(8,128)} %get-tuple-element.56), channel_id=1, source_target_pairs={{0,32},{8,40},{16,48},{24,56},{1,33},{9,41},{17,49},{25,57},{2,34}... | collective-permute-start | bytes 196616 | tf_op jit(solution)/shard_map/ppermute | solution.py:488
  24.5 27.7 %collective-permute-start.3 = (bf16[256,512]{1,0:T(8,128)(2,1)}, bf16[256,512]{1,0:T(8,128)(2,1)S(1)}, u32[]{:S(2)}, u32[]{:S(2)}) collective-permute-start(bf16[256,512]{1,0:T(8,128)(2,1)} %get-tuple-element.51), channel_id=1, source_target_pairs={{0,8},{8,16},{16,24},{24,0},{32,40},{40,48},{48,56},{56,32},{64,72... | collective-permute-start | bytes 786440 | tf_op jit(solution)/shard_map/ppermute | solution.py:478
  26.2 26.0 %collective-permute-start.4 = (bf16[256,512]{1,0:T(8,128)(2,1)}, bf16[256,512]{1,0:T(8,128)(2,1)S(1)}, u32[]{:S(2)}, u32[]{:S(2)}) collective-permute-start(bf16[256,512]{1,0:T(8,128)(2,1)} %get-tuple-element.52), channel_id=1, source_target_pairs={{0,16},{8,24},{16,0},{24,8},{32,48},{40,56},{48,32},{56,40},{64,80... | collective-permute-start | bytes 786440 | tf_op jit(solution)/shard_map/ppermute | solution.py:478
  34.4 17.8 %collective-permute-start.5 = (bf16[256,512]{1,0:T(8,128)(2,1)}, bf16[256,512]{1,0:T(8,128)(2,1)S(1)}, u32[]{:S(2)}, u32[]{:S(2)}) collective-permute-start(bf16[256,512]{1,0:T(8,128)(2,1)} %get-tuple-element.53), channel_id=1, source_target_pairs={{0,24},{8,0},{16,8},{24,16},{32,56},{40,32},{48,40},{56,48},{64,88... | collective-permute-start | bytes 786440 | tf_op jit(solution)/shard_map/ppermute | solution.py:478
  52.2 0.8 copy-start.8
  52.3 109.0 %all-gather.11.cloned.1.call-start = ((), (), s32[]{:S(2)}) async-start(), calls=%async_computation.1 | async-start | bytes 9437184 | tf_op jit(solution)/shard_map/all_gather | solution.py:545
  56.0 11.9 %collective-permute-start.12 = (bf16[256,512]{1,0:T(8,128)(2,1)}, bf16[256,512]{1,0:T(8,128)(2,1)S(1)}, u32[]{:S(2)}, u32[]{:S(2)}) collective-permute-start(bf16[256,512]{1,0:T(8,128)(2,1)} %get-tuple-element.68), channel_id=1, source_target_pairs={{0,32},{8,40},{16,48},{24,56},{32,64},{40,72},{48,80},{56,88},{64,... | collective-permute-start | bytes 786440 | tf_op jit(solution)/shard_map/ppermute | solution.py:483
  56.0 8.5 %collective-permute-start.9 = (bf16[64,512]{1,0:T(8,128)(2,1)}, bf16[64,512]{1,0:T(8,128)(2,1)S(1)}, u32[]{:S(2)}, u32[]{:S(2)}) collective-permute-start(bf16[64,512]{1,0:T(8,128)(2,1)} %get-tuple-element.63), channel_id=1, source_target_pairs={{0,96},{8,104},{16,112},{24,120},{1,97},{9,105},{17,113},{25,121},... | collective-permute-start | bytes 196616 | tf_op jit(solution)/shard_map/ppermute | solution.py:488
  60.5 5.3 %collective-permute-start.10 = (bf16[64,512]{1,0:T(8,128)(2,1)}, bf16[64,512]{1,0:T(8,128)(2,1)S(1)}, u32[]{:S(2)}, u32[]{:S(2)}) collective-permute-start(bf16[64,512]{1,0:T(8,128)(2,1)} %get-tuple-element.64), channel_id=1, source_target_pairs={{0,64},{8,72},{16,80},{24,88},{1,65},{9,73},{17,81},{25,89},{2,66}... | collective-permute-start | bytes 196616 | tf_op jit(solution)/shard_map/ppermute | solution.py:488
  61.8 5.9 %collective-permute-start.11 = (bf16[64,512]{1,0:T(8,128)(2,1)}, bf16[64,512]{1,0:T(8,128)(2,1)S(1)}, u32[]{:S(2)}, u32[]{:S(2)}) collective-permute-start(bf16[64,512]{1,0:T(8,128)(2,1)} %get-tuple-element.65), channel_id=1, source_target_pairs={{0,32},{8,40},{16,48},{24,56},{1,33},{9,41},{17,49},{25,57},{2,34}... | collective-permute-start | bytes 196616 | tf_op jit(solution)/shard_map/ppermute | solution.py:488
  63.1 39.4 %collective-permute-start = (f32[8,64,256]{2,1,0:T(8,128)}, f32[8,64,256]{2,1,0:T(8,128)S(1)}, u32[]{:S(2)}, u32[]{:S(2)}) collective-permute-start(f32[8,64,256]{2,1,0:T(8,128)} %get-tuple-element.47), channel_id=1, source_target_pairs={{0,32},{8,40},{16,48},{24,56},{1,33},{9,41},{17,49},{25,57},{2,34}... | collective-permute-start | bytes 1572872 | tf_op jit(solution)/shard_map/ppermute | solution.py:488
  64.5 38.1 %collective-permute-start.1 = (f32[8,64,256]{2,1,0:T(8,128)}, f32[8,64,256]{2,1,0:T(8,128)S(1)}, u32[]{:S(2)}, u32[]{:S(2)}) collective-permute-start(f32[8,64,256]{2,1,0:T(8,128)} %get-tuple-element.48), channel_id=1, source_target_pairs={{0,64},{8,72},{16,80},{24,88},{1,65},{9,73},{17,81},{25,89},{2,66}... | collective-permute-start | bytes 1572872 | tf_op jit(solution)/shard_map/ppermute | solution.py:488
  65.8 36.7 %collective-permute-start.2 = (f32[8,64,256]{2,1,0:T(8,128)}, f32[8,64,256]{2,1,0:T(8,128)S(1)}, u32[]{:S(2)}, u32[]{:S(2)}) collective-permute-start(f32[8,64,256]{2,1,0:T(8,128)} %get-tuple-element.49), channel_id=1, source_target_pairs={{0,96},{8,104},{16,112},{24,120},{1,97},{9,105},{17,113},{25,121},... | collective-permute-start | bytes 1572872 | tf_op jit(solution)/shard_map/ppermute | solution.py:488
  67.7 25.6 %collective-permute-start.13 = (bf16[256,512]{1,0:T(8,128)(2,1)}, bf16[256,512]{1,0:T(8,128)(2,1)S(1)}, u32[]{:S(2)}, u32[]{:S(2)}) collective-permute-start(bf16[256,512]{1,0:T(8,128)(2,1)} %get-tuple-element.69), channel_id=1, source_target_pairs={{0,64},{8,72},{16,80},{24,88},{32,96},{40,104},{48,112},{56,120},{... | collective-permute-start | bytes 786440 | tf_op jit(solution)/shard_map/ppermute | solution.py:483
  67.8 32.4 %copy-start.7 = (bf16[256,512]{1,0:T(8,128)(2,1)}, bf16[256,512]{1,0:T(8,128)(2,1)S(1)}, u32[]{:S(2)}) copy-start(bf16[256,512]{1,0:T(8,128)(2,1)S(1)} %collective-permute-done.12.h1) | copy-start | bytes 786436
  67.8 25.4 %collective-permute-start.14 = (bf16[256,512]{1,0:T(8,128)(2,1)}, bf16[256,512]{1,0:T(8,128)(2,1)S(1)}, u32[]{:S(2)}, u32[]{:S(2)}) collective-permute-start(bf16[256,512]{1,0:T(8,128)(2,1)} %get-tuple-element.70), channel_id=1, source_target_pairs={{0,96},{8,104},{16,112},{24,120},{32,0},{40,8},{48,16},{56,24},{64... | collective-permute-start | bytes 786440 | tf_op jit(solution)/shard_map/ppermute | solution.py:483
  93.3 7.0 %copy-start.9 = (bf16[256,512]{1,0:T(8,128)(2,1)}, bf16[256,512]{1,0:T(8,128)(2,1)S(1)}, u32[]{:S(2)}) copy-start(bf16[256,512]{1,0:T(8,128)(2,1)S(1)} %collective-permute-done.13.h2) | copy-start | bytes 786436
  93.3 7.0 %copy-start.10 = (bf16[256,512]{1,0:T(8,128)(2,1)}, bf16[256,512]{1,0:T(8,128)(2,1)S(1)}, u32[]{:S(2)}) copy-start(bf16[256,512]{1,0:T(8,128)(2,1)S(1)} %collective-permute-done.14.h3) | copy-start | bytes 786436
  102.5 1.0 copy-start.3
  102.6 1.1 copy-start.4
  191.7 30.3 %copy-start.1 = (s32[4,256]{1,0:T(4,128)S(1)}, s32[4,256]{1,0:T(4,128)}, u32[]{:S(2)}) copy-start(s32[4,256]{1,0:T(4,128)} %param.7) | copy-start | bytes 12292
  (4 other events, 3.0 us)
Sparse Core Ops, SparseCore 0:
  52.4 47.8 all-gather.8
  107.7 49.8 all-gather.10

commit v5 on v4

--- a/solution.py
+++ b/solution.py
@@ -190,19 +190,24 @@
     n = level(jnp.max(jnp.abs(work[...])))
     for tile in range(8):
         code_ref[tile * PIECE : tile * PIECE + PIECE] = encode(work[tile], n).astype(I16)
+    z = row % 4
+    square = corner[z]
+    corner[z] = jnp.zeros((PIECE, BS), F32)
     first = level(jnp.max(jnp.abs(corner[...])))
     low = 8 * PIECE
     for k in range(NPIV):
-        code = encode(corner[k], first)
-        code_ref[low + k * PIECE : low + k * PIECE + PIECE] = code.astype(I16)
-        corner[k] = corner[k] - decode(code, first)
-    second = level(jnp.max(jnp.abs(corner[...])))
-    low = 12 * PIECE
-    for k in range(NPIV):
-        code_ref[low + k * PIECE : low + k * PIECE + PIECE] = encode(corner[k], second).astype(I16)
+        code_ref[low + k * PIECE : low + k * PIECE + PIECE] = encode(corner[k], first).astype(I16)
+    second = level(jnp.max(jnp.abs(square)))
+    code = encode(square, second)
+    code_ref[pl.ds(pl.multiple_of(low + z * PIECE, PIECE), PIECE), :] = code.astype(I16)
+    square = square - decode(code, second)
+    third = level(jnp.max(jnp.abs(square)))
+    code_ref[12 * PIECE : 13 * PIECE] = encode(square, third).astype(I16)
     line = lax.broadcasted_iota(I32, (16, BS), 0)
-    scales = jnp.where(line == 0, n[:1, :1], jnp.where(line == 1, first[:1, :1], second[:1, :1]))
-    code_ref[16 * PIECE :] = scales.astype(I32).astype(I16)
+    scales = third[:1, :1]
+    for at, n in enumerate((n, first, second)):
+        scales = jnp.where(line == at, n[:1, :1], scales)
+    code_ref[13 * PIECE :] = scales.astype(I32).astype(I16)
 
 
 def pack(rc_ref, h0, h1, h2, h3, out_ref):
@@ -211,17 +216,19 @@
         out_ref[(y - shift + 4) % 4] = source[...]
 
 
-def factor_corner(code_ref, level_ref, work, xhi, xlo):
+def factor_corner(code_ref, rest_ref, level_ref, work, xhi, xlo):
     for y in range(4):
         for z in range(4):
             low = z * BS + y * PIECE
             scale = level_ref[4 * y + z].astype(I32)
             for k in range(4):
-                rows = slice(k * PIECE, k * PIECE + PIECE)
-                rest = slice((4 + k) * PIECE, (4 + k) * PIECE + PIECE)
-                work[low : low + PIECE, block(k)] = decode(
-                    code_ref[4 * y + z, rows].astype(I32), scale[1:2]
-                ) + decode(code_ref[4 * y + z, rest].astype(I32), scale[2:3])
+                code = code_ref[4 * y + z, k * PIECE : k * PIECE + PIECE].astype(I32)
+                if k == z:
+                    value = decode(code, scale[2:3])
+                    value = value + decode(rest_ref[4 * y + z].astype(I32), scale[3:4])
+                else:
+                    value = decode(code, scale[1:2])
+                work[low : low + PIECE, block(k)] = value
     diagonal = lax.broadcasted_iota(I32, (BS, BS), 0) == lax.broadcasted_iota(I32, (BS, BS), 1)
     for k in range(NPIV):
         pivot = work[block(k), block(k)]
@@ -250,8 +257,8 @@
 
 
 def panels(
-    map_ref, rc_ref, corner_ref, code_ref, level_ref, front_ref, child_ref,
-    high_ref, low_ref, taken_ref, left_high, left_low, own_ref, block_ref,
+    map_ref, rc_ref, corner_ref, rest_ref, code_ref, level_ref, front_ref, child_ref,
+    upper_ref, taken_ref, lower_ref, own_ref, block_ref,
     work, chi, clo, xhi, xlo, raw, left,
 ):
     step = pl.program_id(0)
@@ -259,7 +266,7 @@
 
     @pl.when(step == 0)
     def _():
-        factor_corner(corner_ref, level_ref, work, xhi, xlo)
+        factor_corner(corner_ref, rest_ref, level_ref, work, xhi, xlo)
         for k in range(NPIV):
             chi[block(k)], clo[block(k)] = split(work[block(k)])
         for r in range(NPIV):
@@ -280,7 +287,8 @@
         if k:
             done = slice(0, k * BS)
             taken = dot3(
-                (chi[block(k), done], clo[block(k), done]), (high_ref[0, done], low_ref[0, done])
+                (chi[block(k), done], clo[block(k), done]),
+                (upper_ref[0, done], upper_ref[0, 4 * BS : (4 + k) * BS]),
             )
             raw[...] = raw[...] - taken
 
@@ -288,7 +296,10 @@
             def _(taken=taken):
                 taken_ref[0] = taken
 
-        high_ref[0, block(k)], low_ref[0, block(k)] = split(raw[...])
+        high, low = split(raw[...])
+        upper_ref[0, block(k)] = high
+        upper_ref[0, block(4 + k)] = low
+        upper_ref[0, block(8 + k)] = high
 
     for k in range(NPIV):
         left[:, block(k)] = front_ref[k]
@@ -313,7 +324,9 @@
     for k in range(NPIV):
         lower = dot3(split(left[:, block(k)]), (xhi[k], xlo[k]))
         pair = split(lower)
-        left_high[:, block(k)], left_low[:, block(k)] = pair
+        lower_ref[:, block(k)] = pair[0]
+        lower_ref[:, block(4 + k)] = pair[0]
+        lower_ref[:, block(8 + k)] = pair[1]
 
         @pl.when(col == k)
         def _(lower=lower):
@@ -326,27 +339,27 @@
 
 def run_panels(child_map, rc, top, front_left, child):
     once = pl.Buffered(1)
-    upper = pl.BlockSpec((1, 4 * BS, WIDE * BS), lambda s: (s, 0, 0))
-    lower = pl.BlockSpec((SPAN * BS, 4 * BS), lambda s: (s, 0))
+    upper = pl.BlockSpec((1, 12 * BS, WIDE * BS), lambda s: (s, 0, 0))
+    lower = pl.BlockSpec((SPAN * BS, 12 * BS), lambda s: (s, 0))
     return pl.pallas_call(
         panels,
         grid=(2,),
         out_shape=[
-            shape((2, 4 * BS, WIDE * BS), BF16), shape((2, 4 * BS, WIDE * BS), BF16),
-            shape((2, BS, WIDE * BS), F32),
-            shape((4 * BS, 4 * BS), BF16), shape((4 * BS, 4 * BS), BF16), shape((4 * BS, BS), F32),
+            shape((2, 12 * BS, WIDE * BS), BF16), shape((2, BS, WIDE * BS), F32),
+            shape((4 * BS, 12 * BS), BF16), shape((4 * BS, BS), F32),
             shape((BS, BS), F32),
         ],
         in_specs=[
             SMEM, SMEM,
-            pl.BlockSpec((16, 8 * PIECE, BS), lambda s: (0, 1, 0), pipeline_mode=once),
+            pl.BlockSpec((16, 4 * PIECE, BS), lambda s: (0, 2, 0), pipeline_mode=once),
+            pl.BlockSpec((16, PIECE, BS), lambda s: (0, 12, 0), pipeline_mode=once),
             pl.BlockSpec((16, WIDE * PIECE, BS), lambda s: (0, s, 0)),
-            pl.BlockSpec((16, 16, BS), lambda s: (0, PIECE, 0), pipeline_mode=once),
+            pl.BlockSpec((16, 16, BS), lambda s: (0, 13 * PIECE // 16, 0), pipeline_mode=once),
             pl.BlockSpec((4, SPAN * BS, BS), lambda s: (0, s, 0)),
             pl.BlockSpec((2, 2, BS, 2 * BS), lambda s: (0, 0, 0, 0), pipeline_mode=once),
         ],
         out_specs=[
-            upper, upper, pl.BlockSpec((1, BS, WIDE * BS), lambda s: (s, 0, 0)), lower, lower,
+            upper, pl.BlockSpec((1, BS, WIDE * BS), lambda s: (s, 0, 0)), lower,
             pl.BlockSpec((SPAN * BS, BS), lambda s: (s, 0)),
             pl.BlockSpec((BS, BS), lambda s: (0, 0)),
         ],
@@ -360,11 +373,11 @@
         cost_estimate=pl.CostEstimate(
             flops=10 * 2**30, bytes_accessed=32 * 2**20, transcendentals=0
         ),
-    )(child_map, rc, top, top, top, front_left, child)
+    )(child_map, rc, top, top, top, top, front_left, child)
 
 
 def finish(
-    map_ref, rc_ref, front_ref, high_ref, low_ref, left_high, left_low, own_ref, taken_ref,
+    map_ref, rc_ref, front_ref, upper_ref, lower_ref, own_ref, taken_ref,
     block_ref, order_ref, child_ref, out_ref, total, parts, arrived,
 ):
     step, group = pl.program_id(0), pl.program_id(1)
@@ -400,9 +413,7 @@
     def _():
         each_child(lambda copy, index, tile, s: copy.start())
 
-    total[...] = dot(left_high[...], high_ref[0])
-    total[...] += dot(left_high[...], low_ref[0])
-    total[...] += dot(left_low[...], high_ref[0])
+    total[...] = dot(lower_ref[...], upper_ref[0])
     for q in range(WIDE):
         for half in range(2):
             rows = at(WIDE * group + q, half, 0, SPAN)
@@ -443,14 +454,14 @@
         a.shape, functools.partial(lambda n, t, s: (0,) * n, a.ndim), pipeline_mode=once
     )
     rows = pl.BlockSpec((SPAN * BS * 16, HALF), lambda t, s: (t, 0))
-    lefts = pl.BlockSpec((SPAN * BS, 4 * BS), lambda t, s: (t, 0))
-    uppers = pl.BlockSpec((1, 4 * BS, WIDE * BS), lambda t, s: (s, 0, 0))
+    lefts = pl.BlockSpec((SPAN * BS, 12 * BS), lambda t, s: (t, 0))
+    uppers = pl.BlockSpec((1, 12 * BS, WIDE * BS), lambda t, s: (s, 0, 0))
     return pl.pallas_call(
         finish,
         grid=(4 // SPAN, 2),
         out_shape=shape(view.shape, F32),
         in_specs=[
-            SMEM, SMEM, rows, uppers, uppers, lefts, lefts,
+            SMEM, SMEM, rows, uppers, lefts,
             pl.BlockSpec((SPAN * BS, BS), lambda t, s: (t, 0)),
             whole(taken), whole(corner), whole(order), pl.BlockSpec(memory_space=pl.ANY),
         ],
@@ -464,7 +475,7 @@
         cost_estimate=pl.CostEstimate(
             flops=13 * 2**30, bytes_accessed=32 * 2**20, transcendentals=0
         ),
-    )(child_map, rc, view, *upper, *lower, own, taken, corner, order, child)
+    )(child_map, rc, view, upper, lower, own, taken, corner, order, child)
 
 
 def shards(front, child_update, child_map, pivots):
@@ -498,12 +509,12 @@
 
     strip = shape((BS, 2 * BS), BF16)
     zs = call(pick_z, [strip] * 4, [child_map, rc, child_update.reshape(2, BS, 2 * BS)])
-    zs = [zs[0]] + [along_z(zs[hop], hop) for hop in (1, 2, 3)]
-
     order = jnp.where(
         row < NPIV, pivots[jnp.minimum(row, NPIV - 1)], jnp.arange(BS, dtype=I32)
     )
     order = jnp.broadcast_to(order.astype(F32)[:, None], (BS, HALF))
+    order, *zs = lax.optimization_barrier((order, *zs))
+    zs = [zs[0]] + [along_z(zs[hop], hop) for hop in (1, 2, 3)]
     view = front.reshape(tiles, BS, 8, 2, HALF).transpose(0, 1, 3, 2, 4)
     view = view.reshape(tiles * BS * 16, HALF)
 
@@ -524,7 +535,7 @@
     cuts = spread(cuts[4:])
 
     front_left = front[:, :, 0, :].reshape(tiles * BS, BS)
-    zs, firsts, front_left = lax.optimization_barrier((zs, firsts, front_left))
+    zs, cuts, firsts, unused = lax.optimization_barrier((zs, cuts, firsts, front_left))
     front_left = lax.all_gather(front_left, "pcol", axis=0, tiled=False)
 
     thin = shape((PIECE, 2 * BS), BF16)
@@ -532,10 +543,9 @@
     thin = lax.all_gather(chosen(y, spread(picked[:4])), "pcol", axis=0, tiled=False)
     ys = [picked[4]] + [along_y(picked[4 + hop], hop) for hop in (1, 2, 3)]
 
-    thin, ys, front_left = lax.optimization_barrier((thin, ys, front_left))
     (code,) = call(
         assemble,
-        [shape((16 * PIECE + 16, BS), I16)],
+        [shape((13 * PIECE + 16, BS), I16)],
         [child_map, rc, *cuts, firsts, thin],
         scratch=[pltpu.VMEM((8, PIECE, BS), F32), pltpu.VMEM((NPIV, PIECE, BS), F32)],
     )
@@ -545,11 +555,11 @@
     child = lax.all_gather(child, "pcol", axis=0, tiled=False)
     top = lax.all_gather(code, "prow", axis=0, tiled=False)
 
-    *upper, taken, low_a, low_b, own, block_own = run_panels(
+    upper, taken, lower, own, block_own = run_panels(
         child_map, rc, top, front_left, child
     )
     done = run_finish(
-        child_map, rc, view, upper, (low_a, low_b), own, taken, block_own, order, child
+        child_map, rc, view, upper, lower, own, taken, block_own, order, child
     )
     done = done.reshape(tiles, BS, 2, 8, HALF).transpose(0, 1, 3, 2, 4)
     return done.reshape(front.shape)

time: 232 us -> 214 us (0.922); the launches traced: 229 us -> 213 us
  blocking collectives: 86.7 us -> 78.4 us
  waiting for transfers between devices: 13 us -> 6.24 us
    all_gather x1, blocking collectives: 53.7 us -> 44.6 us  [shards(): top = lax.all_gather(code, 'prow', axis=0, tiled=False)]
    all_gather x1, waiting for transfers between devices: 7.01 us -> 0.01 us  [shards(): front_left = lax.all_gather(front_left, 'pcol', axis=0, tiled=False)]
    all_gather x1, waiting for transfers between devices: 0.01 us -> 6.15 us  [shards(): child = lax.all_gather(child, 'pcol', axis=0, tiled=False)]
    ppermute x3, waiting for transfers between devices: 5.89 us -> 0.01 us  [along_y(): lax.ppermute(a, 'prow', [(4 * i + j, 4 * ((i + hop) % 4) + j) for i in ra...]
    ppermute x9, starting transfers between devices: 19.7 us -> 16 us  [from_plane(): return lax.ppermute(a, 'prow', [(j, 4 * hop + j) for j in range(4)])]
  transfers between devices with their start and end apart: 17 -> 17, of which waited for: 2 -> 1; matrix products, arithmetic and copies ran while one was open for 3% -> 1% of each run, Pallas kernels for 3% -> 8%
where the time goes in v5:
time: 214 us; the launch traced here: 213 us
  Pallas kernels  79.8 us (37%)
  blocking collectives  78.4 us (37%)
  starting transfers between devices  25.4 us (12%)
  between operations  13.7 us (6%)
  local copies, waits for them, and re-layouts  7.37 us (3%)
  waiting for transfers between devices  6.24 us (3%)
  other arithmetic  2.37 us (1%)
    all_gather x1, blocking collectives, shards(): top = lax.all_gather(code, 'prow', axis=0, tiled=False)  44.6 us
    pallas_call x1, Pallas kernels, run_finish(): pl.pallas_call(finish, grid=(4 // SPAN, 2), out_shape=shape(view.shape, F...  32.1 us
    pallas_call x1, Pallas kernels, run_panels(): pl.pallas_call(panels, grid=(2,), out_shape=[shape((2, 12 * BS, WIDE * BS...  31 us
    all_gather x1, blocking collectives, shards(): lax.all_gather(chosen(y, spread(cuts[:4])), 'pcol', axis=0, tiled=False)  18 us
    ppermute x9, starting transfers between devices, from_plane(): return lax.ppermute(a, 'prow', [(j, 4 * hop + j) for j in range(4)])  16 us
    all_gather x1, blocking collectives, shards(): lax.all_gather(chosen(y, spread(picked[:4])), 'pcol', axis=0, tiled=False)  15.8 us
    pallas_call x4, Pallas kernels, call(): pl.pallas_call(body, out_shape=outs, in_specs=[SMEM] * smem + [VMEM] * (l...  11 us
    ppermute x3, starting transfers between devices, along_z(): lax.ppermute(a, 'prow', [(4 * i + j, 4 * i + (j + hop) % 4) for i in rang...  6.64 us
  transfers between devices with their start and end apart: 17, of which 1 were waited for; matrix products, arithmetic and copies ran while one was open for 1% of the time, Pallas kernels for 8%

profile of v5, /device:TPU:1, one launch (start us, length us, event | category | flops | bytes accessed | tf_op | source)
XLA Modules:
  0.0 213.3 jit_solution(2898539597735779111)
XLA Ops:
  6.5 3.9 %slice.3 = f32[4,256,1,256]{3,2,1,0:T(1,128)S(1)} slice(f32[4,256,8,256]{3,2,1,0:T(8,128)} %param.4), slice={[0:4], [0:256], [0:1], [0:256]} | slice | bytes 2097152 | tf_op jit(solution)/shard_map/slice | solution.py:537
  12.2 2.1 shard_map.46
  15.2 2.5 %collective-permute-start = (bf16[256,512]{1,0:T(8,128)(2,1)}, bf16[256,512]{1,0:T(8,128)(2,1)S(1)}, u32[]{:S(2)}, u32[]{:S(2)}) collective-permute-start(bf16[256,512]{1,0:T(8,128)(2,1)} %get-tuple-element.51), channel_id=1, source_target_pairs={{0,8},{8,16},{16,24},{24,0},{32,40},{40,48},{48,56},{56,32},{64,72... | collective-permute-start | bytes 786440 | tf_op jit(solution)/shard_map/ppermute | solution.py:489
  17.6 5.6 %shard_map.47 = (f32[64,256]{1,0:T(8,128)}, f32[64,256]{1,0:T(8,128)}, f32[64,256]{1,0:T(8,128)}, f32[64,256]{1,0:T(8,128)}, f32[8,64,256]{2,1,0:T(8,128)}, /*in...) custom-call(f32[16384,128]{1,0:T(8,128)} %bitcast.23, f32[256,128]{1,0:T(8,128)} %broadcast_in_dim.2.order_ref), custom_call_target="tpu_custom_call" | custom-call | flops 1073741824 | bytes 4194304 | tf_op jit(solution)/shard_map/pallas_call | solution.py:521
  23.3 4.6 %collective-permute-start.6 = (f32[64,256]{1,0:T(8,128)}, f32[64,256]{1,0:T(8,128)S(1)}, u32[]{:S(2)}, u32[]{:S(2)}) collective-permute-start(f32[64,256]{1,0:T(8,128)} %get-tuple-element.59), channel_id=1, source_target_pairs={{0,96},{8,104},{16,112},{24,120},{1,97},{9,105},{17,113},{25,121},... | collective-permute-start | bytes 196616 | tf_op jit(solution)/shard_map/ppermute | solution.py:499
  27.9 1.3 collective-permute-start.7
  29.2 1.3 collective-permute-start.8
  30.5 1.3 collective-permute-start.3
  31.8 1.3 collective-permute-start.4
  33.2 2.3 %collective-permute-start.5 = (f32[8,64,256]{2,1,0:T(8,128)}, f32[8,64,256]{2,1,0:T(8,128)S(1)}, u32[]{:S(2)}, u32[]{:S(2)}) collective-permute-start(f32[8,64,256]{2,1,0:T(8,128)} %get-tuple-element.58), channel_id=1, source_target_pairs={{0,96},{8,104},{16,112},{24,120},{1,97},{9,105},{17,113},{25,121},... | collective-permute-start | bytes 1572872 | tf_op jit(solution)/shard_map/ppermute | solution.py:499
  35.5 3.4 %collective-permute-start.1 = (bf16[256,512]{1,0:T(8,128)(2,1)S(1)}, bf16[256,512]{1,0:T(8,128)(2,1)S(1)}, u32[]{:S(2)}, u32[]{:S(2)}) collective-permute-start(bf16[256,512]{1,0:T(8,128)(2,1)S(1)} %copy-done.12), channel_id=1, source_target_pairs={{0,16},{8,24},{16,0},{24,8},{32,48},{40,56},{48,32},{56,40},{64,80... | collective-permute-start | bytes 786440 | tf_op jit(solution)/shard_map/ppermute | solution.py:489
  40.5 18.0 %all-gather = f32[512,256]{1,0:T(8,128)} all-gather(f32[64,256]{1,0:T(8,128)S(1)} %select_select_fusion.1), channel_id=2, replica_groups=mesh['prow'=16,'pcol'=8] {'pcol'}, dimensions={0}, use_global_device_ids=true | all-gather | bytes 589824 | tf_op jit(solution)/shard_map/all_gather | solution.py:534
  59.4 3.0 %shard_map.48 = (bf16[64,512]{1,0:T(8,128)(2,1)}, bf16[64,512]{1,0:T(8,128)(2,1)}, bf16[64,512]{1,0:T(8,128)(2,1)}, bf16[64,512]{1,0:T(8,128)(2,1)}, bf16[256,51...) custom-call(s32[2,16]{1,0:T(2,128)} %map_ref.9, ...), custom_call_target="tpu_custom_call" | custom-call | bytes 2490504 | tf_op jit(solution)/shard_map/pallas_call | solution.py:32
  62.3 1.3 collective-permute-start.9
  63.6 1.3 collective-permute-start.10
  64.9 1.3 collective-permute-start.11
  66.4 2.6 %collective-permute-start.14 = (bf16[256,512]{1,0:T(8,128)(2,1)}, bf16[256,512]{1,0:T(8,128)(2,1)S(1)}, u32[]{:S(2)}, u32[]{:S(2)}) collective-permute-start(bf16[256,512]{1,0:T(8,128)(2,1)} %get-tuple-element.79), channel_id=1, source_target_pairs={{0,96},{8,104},{16,112},{24,120},{32,0},{40,8},{48,16},{56,24},{64... | collective-permute-start | bytes 786440 | tf_op jit(solution)/shard_map/ppermute | solution.py:494
  69.9 15.8 %all-gather.1 = bf16[512,512]{1,0:T(8,128)(2,1)} all-gather(bf16[64,512]{1,0:T(8,128)(2,1)S(1)} %select_select_fusion), channel_id=3, replica_groups=mesh['prow'=16,'pcol'=8] {'pcol'}, dimensions={0}, use_global_device_ids=true | all-gather | bytes 589824 | tf_op jit(solution)/shard_map/all_gather | solution.py:543
  85.7 3.7 %shard_map.49 = s16[848,256]{1,0:T(8,128)(2,1)} custom-call(s32[2,16]{1,0:T(2,128)} %map_ref.9, s32[2]{0:T(128)} %pad_add_fusion.rc_ref, f32[8,64,256]{2,1,0:T(8,128)} %get-tuple-element.63.f0, f32[8,64,256]{2,1,0:T(8,128)} %copy-done.2, f32[8,64,256]{2,1,0:T(8,128)} %copy-done.3, f32[8,64,256]{2,1,0:T(8,128)} %copy-done.4, f32[8,64,256]{2,1,0:T(8,128)} %bitcast.28, ...), custom_call_target="tpu_custom_call" | custom-call | bytes 3580040 | tf_op jit(solution)/shard_map/pallas_call | solution.py:32
  90.3 2.2 %shard_map.50 = bf16[4,256,512]{2,1,0:T(8,128)(2,1)} custom-call(s32[2]{0:T(128)} %pad_add_fusion.rc_ref, bf16[256,512]{1,0:T(8,128)(2,1)} %get-tuple-element.76.h0, bf16[256,512]{1,0:T(8,128)(2,1)} %copy-done.6, bf16[256,512]{1,0:T(8,128)(2,1)} %copy-done.7, bf16[256,512]{1,0:T(8,128)(2,1)} %copy-done.9), custom_call_target="tpu_custom_call" | custom-call | bytes 2097160 | tf_op jit(solution)/shard_map/pallas_call | solution.py:32
  92.5 44.6 %all-gather.11 = s16[13568,256]{1,0:T(8,128)(2,1)} all-gather(s16[848,256]{1,0:T(8,128)(2,1)} %shard_map.49), channel_id=4, replica_groups=mesh['prow'=16,'pcol'=8] {'prow'}, dimensions={0}, use_global_device_ids=true | all-gather | bytes 7380992 | tf_op jit(solution)/shard_map/all_gather | solution.py:556
  137.2 6.2 %all-gather.10.cloned.1.call-done = bf16[32,256,512]{2,1,0:T(8,128)(2,1)} async-done(((bf16[4,256,512]{2,1,0:T(8,128)(2,1)}), bf16[32,256,512]{2,1,0:T(8,128)(2,1)}) %all-gather.10.cloned.1.call-update) | async-done | bytes 8388624 | tf_op jit(solution)/shard_map/all_gather | solution.py:555
  143.3 31.0 %shard_map.51 = (bf16[2,3072,1024]{2,1,0:T(8,128)(2,1)}, f32[2,256,1024]{2,1,0:T(8,128)}, bf16[1024,3072]{1,0:T(8,128)(2,1)}, f32[1024,256]{1,0:T(8,128)}, f32[256,256]{1,0:T(8,128)}) custom-call(s32[2,16]{1,0:T(2,128)} %map_ref.9, s32[2]{0:T(128)} %pad_add_fusion.rc_ref, s16[16,848,256]{2,1,0:T(8,128)(2,1)} %bitcast.19, s16[16,848,256]{2,1,0:T(8,128)(2,1)} %bitcast.20, ...), custom_call_target="tpu_custom_call" | custom-call | flops 10737418240 | bytes 33554432 | tf_op jit(solution)/shard_map/pallas_call | solution.py:344
  174.4 32.1 %shard_map.52 = f32[16384,128]{1,0:T(8,128)} custom-call(s32[2,16]{1,0:T(2,128)} %map_ref.9, s32[2]{0:T(128)} %pad_add_fusion.rc_ref, f32[16384,128]{1,0:T(8,128)} %bitcast.24, bf16[2,3072,1024]{2,1,0:T(8,128)(2,1)} %get-tuple-element.82.upper_ref, bf16[1024,3072]{1,0:T(8,128)(2,1)} %get-tuple-element.83.lower_ref, f32[1024,256]{1,0:T(8,128)} %get-tuple-element.84.own_ref, ...), custom_call_target="tpu_custom_call" | custom-call | flops 13958643712 | bytes 33554432 | tf_op jit(solution)/shard_map/pallas_call | solution.py:459
  (56 shorter events, 6.9 us)
Async XLA Ops:
  6.5 130.6 %all-gather.8.cloned.1.call-start = ((), (), s32[]{:S(2)}) async-start(), calls=%async_computation | async-start | bytes 9437184 | tf_op jit(solution)/shard_map/all_gather | solution.py:539
  11.5 131.8 %all-gather.10.cloned.1.call-start = ((), (), s32[]{:S(2)}) async-start(), calls=%async_computation.1 | async-start | bytes 9437184 | tf_op jit(solution)/shard_map/all_gather | solution.py:555
  14.4 21.1 %copy-start.12 = (bf16[256,512]{1,0:T(8,128)(2,1)S(1)}, bf16[256,512]{1,0:T(8,128)(2,1)}, u32[]{:S(2)}) copy-start(bf16[256,512]{1,0:T(8,128)(2,1)} %get-tuple-element.52) | copy-start | bytes 786436
  14.4 24.5 %copy-start.11 = (bf16[256,512]{1,0:T(8,128)(2,1)S(1)}, bf16[256,512]{1,0:T(8,128)(2,1)}, u32[]{:S(2)}) copy-start(bf16[256,512]{1,0:T(8,128)(2,1)} %get-tuple-element.53) | copy-start | bytes 786436
  15.2 23.7 %collective-permute-start = (bf16[256,512]{1,0:T(8,128)(2,1)}, bf16[256,512]{1,0:T(8,128)(2,1)S(1)}, u32[]{:S(2)}, u32[]{:S(2)}) collective-permute-start(bf16[256,512]{1,0:T(8,128)(2,1)} %get-tuple-element.51), channel_id=1, source_target_pairs={{0,8},{8,16},{16,24},{24,0},{32,40},{40,48},{48,56},{56,32},{64,72... | collective-permute-start | bytes 786440 | tf_op jit(solution)/shard_map/ppermute | solution.py:489
  23.3 8.6 %collective-permute-start.6 = (f32[64,256]{1,0:T(8,128)}, f32[64,256]{1,0:T(8,128)S(1)}, u32[]{:S(2)}, u32[]{:S(2)}) collective-permute-start(f32[64,256]{1,0:T(8,128)} %get-tuple-element.59), channel_id=1, source_target_pairs={{0,96},{8,104},{16,112},{24,120},{1,97},{9,105},{17,113},{25,121},... | collective-permute-start | bytes 196616 | tf_op jit(solution)/shard_map/ppermute | solution.py:499
  27.9 5.3 %collective-permute-start.7 = (f32[64,256]{1,0:T(8,128)}, f32[64,256]{1,0:T(8,128)S(1)}, u32[]{:S(2)}, u32[]{:S(2)}) collective-permute-start(f32[64,256]{1,0:T(8,128)} %get-tuple-element.60), channel_id=1, source_target_pairs={{0,64},{8,72},{16,80},{24,88},{1,65},{9,73},{17,81},{25,89},{2,66}... | collective-permute-start | bytes 196616 | tf_op jit(solution)/shard_map/ppermute | solution.py:499
  29.2 6.3 %collective-permute-start.8 = (f32[64,256]{1,0:T(8,128)}, f32[64,256]{1,0:T(8,128)S(1)}, u32[]{:S(2)}, u32[]{:S(2)}) collective-permute-start(f32[64,256]{1,0:T(8,128)} %get-tuple-element.61), channel_id=1, source_target_pairs={{0,32},{8,40},{16,48},{24,56},{1,33},{9,41},{17,49},{25,57},{2,34}... | collective-permute-start | bytes 196616 | tf_op jit(solution)/shard_map/ppermute | solution.py:499
  30.5 28.0 %collective-permute-start.3 = (f32[8,64,256]{2,1,0:T(8,128)}, f32[8,64,256]{2,1,0:T(8,128)S(1)}, u32[]{:S(2)}, u32[]{:S(2)}) collective-permute-start(f32[8,64,256]{2,1,0:T(8,128)} %get-tuple-element.56), channel_id=1, source_target_pairs={{0,32},{8,40},{16,48},{24,56},{1,33},{9,41},{17,49},{25,57},{2,34}... | collective-permute-start | bytes 1572872 | tf_op jit(solution)/shard_map/ppermute | solution.py:499
  31.8 26.7 %collective-permute-start.4 = (f32[8,64,256]{2,1,0:T(8,128)}, f32[8,64,256]{2,1,0:T(8,128)S(1)}, u32[]{:S(2)}, u32[]{:S(2)}) collective-permute-start(f32[8,64,256]{2,1,0:T(8,128)} %get-tuple-element.57), channel_id=1, source_target_pairs={{0,64},{8,72},{16,80},{24,88},{1,65},{9,73},{17,81},{25,89},{2,66}... | collective-permute-start | bytes 1572872 | tf_op jit(solution)/shard_map/ppermute | solution.py:499
  33.2 25.4 %collective-permute-start.5 = (f32[8,64,256]{2,1,0:T(8,128)}, f32[8,64,256]{2,1,0:T(8,128)S(1)}, u32[]{:S(2)}, u32[]{:S(2)}) collective-permute-start(f32[8,64,256]{2,1,0:T(8,128)} %get-tuple-element.58), channel_id=1, source_target_pairs={{0,96},{8,104},{16,112},{24,120},{1,97},{9,105},{17,113},{25,121},... | collective-permute-start | bytes 1572872 | tf_op jit(solution)/shard_map/ppermute | solution.py:499
  35.5 23.0 %collective-permute-start.1 = (bf16[256,512]{1,0:T(8,128)(2,1)S(1)}, bf16[256,512]{1,0:T(8,128)(2,1)S(1)}, u32[]{:S(2)}, u32[]{:S(2)}) collective-permute-start(bf16[256,512]{1,0:T(8,128)(2,1)S(1)} %copy-done.12), channel_id=1, source_target_pairs={{0,16},{8,24},{16,0},{24,8},{32,48},{40,56},{48,32},{56,40},{64,80... | collective-permute-start | bytes 786440 | tf_op jit(solution)/shard_map/ppermute | solution.py:489
  38.9 19.7 %copy-start.5 = (bf16[256,512]{1,0:T(8,128)(2,1)}, bf16[256,512]{1,0:T(8,128)(2,1)S(1)}, u32[]{:S(2)}) copy-start(bf16[256,512]{1,0:T(8,128)(2,1)S(1)} %collective-permute-done.refs_1_) | copy-start | bytes 786436
  38.9 19.6 %collective-permute-start.2 = (bf16[256,512]{1,0:T(8,128)(2,1)S(1)}, bf16[256,512]{1,0:T(8,128)(2,1)S(1)}, u32[]{:S(2)}, u32[]{:S(2)}) collective-permute-start(bf16[256,512]{1,0:T(8,128)(2,1)S(1)} %copy-done.11), channel_id=1, source_target_pairs={{0,24},{8,0},{16,8},{24,16},{32,56},{40,32},{48,40},{56,48},{64,88... | collective-permute-start | bytes 786440 | tf_op jit(solution)/shard_map/ppermute | solution.py:489
  58.5 27.1 %copy-start.2 = (f32[8,64,256]{2,1,0:T(8,128)}, f32[8,64,256]{2,1,0:T(8,128)S(1)}, u32[]{:S(2)}) copy-start(f32[8,64,256]{2,1,0:T(8,128)S(1)} %collective-permute-done.3.f1) | copy-start | bytes 1572868
  58.6 27.1 %copy-start.3 = (f32[8,64,256]{2,1,0:T(8,128)}, f32[8,64,256]{2,1,0:T(8,128)S(1)}, u32[]{:S(2)}) copy-start(f32[8,64,256]{2,1,0:T(8,128)S(1)} %collective-permute-done.4.f2) | copy-start | bytes 1572868
  58.6 27.1 %copy-start.4 = (f32[8,64,256]{2,1,0:T(8,128)}, f32[8,64,256]{2,1,0:T(8,128)S(1)}, u32[]{:S(2)}) copy-start(f32[8,64,256]{2,1,0:T(8,128)S(1)} %collective-permute-done.5.f3) | copy-start | bytes 1572868
  62.3 4.1 %collective-permute-start.9 = (bf16[64,512]{1,0:T(8,128)(2,1)}, bf16[64,512]{1,0:T(8,128)(2,1)S(1)}, u32[]{:S(2)}, u32[]{:S(2)}) collective-permute-start(bf16[64,512]{1,0:T(8,128)(2,1)} %get-tuple-element.72), channel_id=1, source_target_pairs={{0,96},{8,104},{16,112},{24,120},{1,97},{9,105},{17,113},{25,121},... | collective-permute-start | bytes 196616 | tf_op jit(solution)/shard_map/ppermute | solution.py:499
  63.6 5.4 %collective-permute-start.10 = (bf16[64,512]{1,0:T(8,128)(2,1)}, bf16[64,512]{1,0:T(8,128)(2,1)S(1)}, u32[]{:S(2)}, u32[]{:S(2)}) collective-permute-start(bf16[64,512]{1,0:T(8,128)(2,1)} %get-tuple-element.73), channel_id=1, source_target_pairs={{0,64},{8,72},{16,80},{24,88},{1,65},{9,73},{17,81},{25,89},{2,66}... | collective-permute-start | bytes 196616 | tf_op jit(solution)/shard_map/ppermute | solution.py:499
  64.9 4.1 %collective-permute-start.11 = (bf16[64,512]{1,0:T(8,128)(2,1)}, bf16[64,512]{1,0:T(8,128)(2,1)S(1)}, u32[]{:S(2)}, u32[]{:S(2)}) collective-permute-start(bf16[64,512]{1,0:T(8,128)(2,1)} %get-tuple-element.74), channel_id=1, source_target_pairs={{0,32},{8,40},{16,48},{24,56},{1,33},{9,41},{17,49},{25,57},{2,34}... | collective-permute-start | bytes 196616 | tf_op jit(solution)/shard_map/ppermute | solution.py:499
  66.2 23.1 %collective-permute-start.12 = (bf16[256,512]{1,0:T(8,128)(2,1)}, bf16[256,512]{1,0:T(8,128)(2,1)S(1)}, u32[]{:S(2)}, u32[]{:S(2)}) collective-permute-start(bf16[256,512]{1,0:T(8,128)(2,1)} %get-tuple-element.77), channel_id=1, source_target_pairs={{0,32},{8,40},{16,48},{24,56},{32,64},{40,72},{48,80},{56,88},{64,... | collective-permute-start | bytes 786440 | tf_op jit(solution)/shard_map/ppermute | solution.py:494
  66.3 23.1 %collective-permute-start.13 = (bf16[256,512]{1,0:T(8,128)(2,1)}, bf16[256,512]{1,0:T(8,128)(2,1)S(1)}, u32[]{:S(2)}, u32[]{:S(2)}) collective-permute-start(bf16[256,512]{1,0:T(8,128)(2,1)} %get-tuple-element.78), channel_id=1, source_target_pairs={{0,64},{8,72},{16,80},{24,88},{32,96},{40,104},{48,112},{56,120},{... | collective-permute-start | bytes 786440 | tf_op jit(solution)/shard_map/ppermute | solution.py:494
  66.4 23.0 %collective-permute-start.14 = (bf16[256,512]{1,0:T(8,128)(2,1)}, bf16[256,512]{1,0:T(8,128)(2,1)S(1)}, u32[]{:S(2)}, u32[]{:S(2)}) collective-permute-start(bf16[256,512]{1,0:T(8,128)(2,1)} %get-tuple-element.79), channel_id=1, source_target_pairs={{0,96},{8,104},{16,112},{24,120},{32,0},{40,8},{48,16},{56,24},{64... | collective-permute-start | bytes 786440 | tf_op jit(solution)/shard_map/ppermute | solution.py:494
  174.4 32.1 %copy-start.1 = (s32[4,256]{1,0:T(4,128)S(1)}, s32[4,256]{1,0:T(4,128)}, u32[]{:S(2)}) copy-start(s32[4,256]{1,0:T(4,128)} %param.7) | copy-start | bytes 12292
  (6 other events, 11.7 us)
Sparse Core Ops, SparseCore 0:
  11.7 55.4 all-gather.7
  92.7 50.6 all-gather.9

commit v6 on v5

v6 whole, which is shorter than its diff:
```python
import functools

import jax
import jax.numpy as jnp
from jax import lax
from jax.experimental import pallas as pl
from jax.experimental.pallas import tpu as pltpu
from jax.sharding import PartitionSpec as P

NPIV = 4
NS = 2
BS = 256
HALF = 128
PIECE = 64
FULL = 32767.0
CHILD_LEVEL = 11.0
F32 = jnp.float32
BF16 = jnp.bfloat16
I16 = jnp.int16
I32 = jnp.int32
SMEM = pl.BlockSpec(memory_space=pltpu.SMEM)
VMEM = pl.BlockSpec(memory_space=pltpu.VMEM)
LIMIT = 60 * 1024 * 1024


def shape(dims, kind):
    return jax.ShapeDtypeStruct(dims, kind)


def call(body, outs, ins, smem=2, flops=0, scratch=()):
    moved = sum(a.size * a.dtype.itemsize for a in ins)
    moved += sum(o.size * o.dtype.itemsize for o in outs)
    return pl.pallas_call(
        body,
        out_shape=outs,
        in_specs=[SMEM] * smem + [VMEM] * (len(ins) - smem),
        out_specs=[VMEM] * len(outs),
        scratch_shapes=list(scratch),
        compiler_params=pltpu.CompilerParams(vmem_limit_bytes=LIMIT),
        cost_estimate=pl.CostEstimate(flops=flops, bytes_accessed=moved, transcendentals=0),
    )(*ins)


def spot(map_ref, child, low, count, test):
    found = jnp.int32(-1)
    value = jnp.int32(-1)
    for step in range(count):
        entry = map_ref[child, low + step]
        hit = test(entry)
        found = jnp.where(hit, low + step, found)
        value = jnp.where(hit, entry, value)
    return found, value


def row_of(map_ref, row, slot):
    return spot(map_ref, slot // 2, 8 * (slot % 2), 8, lambda entry: entry % 16 == row)[1]


def col_of(map_ref, child, source, col):
    return spot(map_ref, child, 4 * source, 4, lambda entry: entry % 8 == col)


def split(value):
    high = value.astype(BF16)
    low = (value - high.astype(F32)).astype(BF16)
    return high, low


def dot(left, right):
    return jnp.dot(left, right, preferred_element_type=F32)


def dot3(left, right):
    (a, b), (c, d) = left, right
    return dot(a, c) + (dot(a, d) + dot(b, c))


def block(step):
    return slice(step * BS, step * BS + BS)


def one_hot(order):
    spread = lax.broadcasted_iota(I32, (BS, BS), 1).astype(F32)
    return jnp.where(order[:, :1] == spread, 1.0, 0.0).astype(BF16)


def reorder(select, value):
    high = value.astype(BF16)
    rest = value - high.astype(F32)
    middle = rest.astype(BF16)
    last = (rest - middle.astype(F32)).astype(BF16)
    return (dot(select, high) + dot(select, middle)) + dot(select, last)


def level(peak):
    return jnp.ceil(jnp.log2(jnp.full((8, HALF), jnp.maximum(peak, 1e-30))) * 4.0)


def encode(value, n):
    scaled = jnp.abs(value) * jnp.exp2(n * -0.25)[:1, :1]
    code = jnp.minimum(jnp.floor(jnp.sqrt(scaled) * FULL + 0.5), FULL)
    return jnp.where(value < 0.0, -code, code).astype(I32)


def decode(code, n):
    code = code.astype(F32)
    return code * jnp.abs(code) * (jnp.exp2(n.astype(F32)[:1, :1] * 0.25) * (1.0 / (FULL * FULL)))


def cut_front(front_ref, order_ref, *outs):
    select = one_hot(order_ref[...])

    def one(tile, carry):
        halves = [front_ref[pl.ds(half * 8 + tile, BS, stride=16), :] for half in range(2)]
        turned = reorder(select, jnp.concatenate(halves, axis=1))
        for piece in range(4):
            outs[piece][tile] = turned[piece * PIECE : piece * PIECE + PIECE]
        return carry

    lax.fori_loop(0, 8, one, 0)


def pick_z(map_ref, rc_ref, child_ref, *outs):
    row = rc_ref[0]
    z = row % 4
    second_at = map_ref[row // 8, 2 * (row % 8) + 1] % 4
    for hop in range(4):
        outs[hop][...] = child_ref[jnp.where(second_at == (z + hop) % 4, 1, 0)]


def pick_rows(map_ref, rc_ref, order_ref, *refs):
    held, pieces, hops = refs[:4], refs[4:8], refs[8:]
    row = rc_ref[0]
    y, z = row // 4, row % 4
    found, value = spot(map_ref, 0, 0, 4, lambda entry: entry == row)
    live = (found >= 0) & (row < NPIV)
    for hop in range(4):

        @pl.when(live & (found // 2 == (z - hop + 4) % 4))
        def _(hop=hop):
            turned = dot(one_hot(order_ref[...]), held[hop][...]).astype(BF16)
            for piece in range(4):
                pieces[piece][...] = turned[piece * PIECE : piece * PIECE + PIECE]

    @pl.when(jnp.logical_not(live))
    def _():
        for piece in range(4):
            pieces[piece][...] = jnp.zeros((PIECE, 2 * BS), BF16)

    for hop in range(4):
        first = 2 * ((4 * y + (z - hop + 4) % 4) % 8)
        index, value = spot(map_ref, y // 2, first, 2, lambda entry: entry % 4 == z)
        for shift in range(4):

            @pl.when((index >= 0) & ((value // 4) % 4 == (y + shift) % 4))
            def _(hop=hop, shift=shift):
                hops[shift][...] = held[hop][...]


def mix(rc_ref, t0, t1, t2, t3, f0, f1, f2, f3, out_ref, strip, corner):
    y = rc_ref[0] // 4
    for piece, (child, source) in enumerate(((t0, f0), (t1, f1), (t2, f2), (t3, f3))):

        @pl.when(y == piece)
        def _(child=child, source=source):
            strip[...] = child[...].astype(F32)
            corner[...] = source[0]

    n = jnp.full((8, HALF), CHILD_LEVEL)
    for half in range(2):
        out_ref[half * PIECE : half * PIECE + PIECE] = encode(
            strip[:, half * BS : half * BS + BS], n
        ).astype(I16)
    value = corner[...]
    first = level(jnp.max(jnp.abs(value)))
    code = encode(value, first)
    out_ref[2 * PIECE : 3 * PIECE] = code.astype(I16)
    value = value - decode(code, first)
    second = level(jnp.max(jnp.abs(value)))
    out_ref[3 * PIECE : 4 * PIECE] = encode(value, second).astype(I16)
    line = lax.broadcasted_iota(I32, (16, BS), 0)
    scales = jnp.where(line == 0, first[:1, :1], second[:1, :1])
    out_ref[4 * PIECE :] = scales.astype(I32).astype(I16)


def assemble(map_ref, rc_ref, f0, f1, f2, f3, thin, code_ref, work, corner):
    row, col = rc_ref[0], rc_ref[1]
    y = row // 4
    for piece, source in enumerate((f0, f1, f2, f3)):

        @pl.when(y == piece)
        def _(source=source):
            work[...] = source[...]

    for k in range(NPIV):
        scales = thin[k, 4 * PIECE :].astype(I32)
        corner[k] = decode(thin[k, 2 * PIECE : 3 * PIECE].astype(I32), scales[0:1]) + decode(
            thin[k, 3 * PIECE : 4 * PIECE].astype(I32), scales[1:2]
        )
    n = jnp.full((8, HALF), CHILD_LEVEL)
    for index in range(16):
        parent = map_ref[0, index]
        low = (index % 2) * PIECE

        @pl.when(parent % 8 == col)
        def _(index=index, low=low, tile=parent // 8):
            child = decode(thin[index // 2, low : low + PIECE].astype(I32), n)
            work[tile] = work[tile] + child

        if index < NPIV:

            @pl.when(parent < NPIV)
            def _(index=index, low=low, parent=parent):
                child = decode(thin[index // 2, low : low + PIECE].astype(I32), n)
                corner[parent] = corner[parent] + child

    @pl.when(col < NPIV)
    def _():
        work[0] = jnp.zeros((PIECE, BS), F32)

    n = level(jnp.max(jnp.abs(work[...])))
    for tile in range(8):
        code_ref[tile * PIECE : tile * PIECE + PIECE] = encode(work[tile], n).astype(I16)
    z = row % 4
    square = corner[z]
    corner[z] = jnp.zeros((PIECE, BS), F32)
    first = level(jnp.max(jnp.abs(corner[...])))
    low = 8 * PIECE
    for k in range(NPIV):
        code_ref[low + k * PIECE : low + k * PIECE + PIECE] = encode(corner[k], first).astype(I16)
    second = level(jnp.max(jnp.abs(square)))
    code = encode(square, second)
    code_ref[pl.ds(pl.multiple_of(low + z * PIECE, PIECE), PIECE), :] = code.astype(I16)
    square = square - decode(code, second)
    third = level(jnp.max(jnp.abs(square)))
    code_ref[12 * PIECE : 13 * PIECE] = encode(square, third).astype(I16)
    line = lax.broadcasted_iota(I32, (16, BS), 0)
    scales = third[:1, :1]
    for at, n in enumerate((n, first, second)):
        scales = jnp.where(line == at, n[:1, :1], scales)
    code_ref[13 * PIECE :] = scales.astype(I32).astype(I16)


def pack(rc_ref, h0, h1, h2, h3, out_ref):
    y = rc_ref[0] // 4
    for shift, source in enumerate((h0, h1, h2, h3)):
        out_ref[(y - shift + 4) % 4] = source[...]


def factor_corner(code_ref, rest_ref, level_ref, work, xhi, xlo):
    for y in range(4):
        for z in range(4):
            low = z * BS + y * PIECE
            scale = level_ref[4 * y + z].astype(I32)
            for k in range(4):
                code = code_ref[4 * y + z, k * PIECE : k * PIECE + PIECE].astype(I32)
                if k == z:
                    value = decode(code, scale[2:3])
                    value = value + decode(rest_ref[4 * y + z].astype(I32), scale[3:4])
                else:
                    value = decode(code, scale[1:2])
                work[low : low + PIECE, block(k)] = value
    diagonal = lax.broadcasted_iota(I32, (BS, BS), 0) == lax.broadcasted_iota(I32, (BS, BS), 1)
    for k in range(NPIV):
        pivot = work[block(k), block(k)]
        parts = split(pivot)
        on_line = jnp.where(diagonal, pivot, 0.0)
        across = jnp.sum(on_line, axis=0, keepdims=True)
        down = jnp.sum(on_line, axis=1, keepdims=True)
        across = across / (across * across + 1.0)
        down = down / (down * down + 1.0)
        approx = 2.0 * jnp.where(diagonal, across, 0.0) - (down * pivot) * across
        for sweep_index in range(NS - 1):
            pair = split(approx)
            approx = 2.0 * approx - dot3(split(dot3(pair, parts)), pair)
        xhi[k], xlo[k] = split(approx)
        if k + 1 < NPIV:
            below = slice((k + 1) * BS, NPIV * BS)
            lower = dot3(split(work[below, block(k)]), (xhi[k], xlo[k]))
            work[below, block(k)] = lower
            work[below, below] = work[below, below] - dot3(
                split(lower), split(work[block(k), below])
            )


SPAN = 2
WIDE = 4


def finish(
    map_ref, rc_ref, corner_ref, rest_ref, level_ref, code_ref, left_ref, near_ref, order_ref,
    front_ref, f0, f1, f2, f3, child_ref, out_ref,
    work, chi, clo, xhi, xlo, uhi, ulo, lhi, llo, own_col, own_block, own_row, parts,
    arrived, own_arrived,
):
    step, group = pl.program_id(0), pl.program_id(1)
    row, col = rc_ref[0], rc_ref[1]
    top_row = row < NPIV
    low_rows = slice(0, SPAN * BS)
    high_rows = slice(SPAN * BS, 2 * SPAN * BS)

    def at(s, half, tile=0, count=1):
        return pl.ds(tile * BS * 16 + half * 8 + s, count * BS, stride=16)

    def put(s, tile, value):
        for half in range(2):
            out_ref[at(s, half, tile), :] = value[:, half * HALF : half * HALF + HALF]

    def each_child(act):
        for slot in range(4):
            parent = row_of(map_ref, row, slot)
            here = (parent >= 0) & (parent // 16 // SPAN == step)
            for source in range(4):
                found, value = col_of(map_ref, slot // 2, source, col)
                where = jnp.maximum(found, 0)
                start = pl.multiple_of((where % 2) * BS, BS)
                index = 4 * slot + source
                copy = pltpu.make_async_copy(
                    child_ref.at[where // 2, slot, :, pl.ds(start, BS)],
                    parts.at[index],
                    arrived.at[index],
                )

                @pl.when(here & (found >= 0))
                def _(copy=copy, index=index, tile=(parent // 16) % SPAN, s=value // 8):
                    act(copy, index, tile, s)

    def own_copies():
        return [
            pltpu.make_async_copy(source, own_row.at[piece], own_arrived.at[piece])
            for piece, source in enumerate((f0, f1, f2, f3))
        ]

    @pl.when(group == 0)
    def _():
        each_child(lambda copy, index, tile, s: copy.start())

    @pl.when((step == 0) & (group == 0))
    def _():
        @pl.when(top_row)
        def _():
            for copy in own_copies():
                copy.start()

        factor_corner(corner_ref, rest_ref, level_ref, work, xhi, xlo)
        for k in range(NPIV):
            chi[block(k)], clo[block(k)] = split(work[block(k)])
        for r in range(NPIV):
            for c in range(NPIV):

                @pl.when((row == r) & (col == c))
                def _(r=r, c=c):
                    own_block[...] = work[block(r), block(c)]

        @pl.when(top_row)
        def _():
            for copy in own_copies():
                copy.wait()

    @pl.when(step == 0)
    def _():
        for k in range(NPIV):
            raw = slice(0, BS)
            for piece in range(4):
                scale = level_ref[4 * piece + k].astype(I32)
                for q in range(WIDE):
                    work[piece * PIECE : piece * PIECE + PIECE, block(q)] = decode(
                        code_ref[4 * piece + k, q * PIECE : q * PIECE + PIECE].astype(I32), scale
                    )
            if k:
                done = slice(0, k * BS)
                taken = dot3(
                    (chi[block(k), done], clo[block(k), done]),
                    (uhi[group, done], ulo[group, done]),
                )
                work[raw] = work[raw] - taken

                @pl.when(row == k)
                def _(taken=taken):
                    for piece in range(4):
                        for q in range(WIDE):
                            tile = WIDE * group + q
                            own_row[piece, tile] = (
                                own_row[piece, tile]
                                - taken[piece * PIECE : piece * PIECE + PIECE, block(q)]
                            )

            uhi[group, block(k)], ulo[group, block(k)] = split(work[raw])

    @pl.when(group == 0)
    def _():
        left = work.at[high_rows]
        for k in range(NPIV):
            left[:, block(k)] = left_ref[k]
        for slot in range(2):
            parent = row_of(map_ref, row, slot)
            for index in range(4):
                target = map_ref[0, index]
                cut = slice((index % 2) * BS, (index % 2) * BS + BS)
                for tile in range(SPAN):
                    for k in range(index, NPIV):

                        @pl.when(
                            (parent >= 0) & (parent // 16 == SPAN * step + tile) & (target == k)
                        )
                        def _(slot=slot, index=index, cut=cut, tile=tile, k=k):
                            left[block(tile), block(k)] = left[block(tile), block(k)] + near_ref[
                                index // 2, slot, :, cut
                            ].astype(F32)

        @pl.when((step == 0) & top_row)
        def _():
            left[:BS] = jnp.zeros((BS, NPIV * BS), F32)

        for k in range(NPIV):
            lower = dot3(split(left[:, block(k)]), (xhi[k], xlo[k]))
            pair = split(lower)
            lhi[:, block(k)], llo[:, block(k)] = pair

            @pl.when(col == k)
            def _(lower=lower):
                own_col[...] = lower

            if k + 1 < NPIV:
                rest = slice((k + 1) * BS, NPIV * BS)
                left[:, rest] = left[:, rest] - dot3(pair, (chi[block(k), rest], clo[block(k), rest]))

    total = work.at[low_rows]
    total[...] = dot(lhi[...], uhi[group])
    total[...] += dot(lhi[...], ulo[group])
    total[...] += dot(llo[...], uhi[group])
    for q in range(WIDE):
        for half in range(2):
            rows = at(WIDE * group + q, half, 0, SPAN)
            low = q * BS + half * HALF
            out_ref[rows, :] = front_ref[rows, :] - total[:, low : low + HALF]

    @pl.when(group == 1)
    def _():
        top_tile = (step == 0) & top_row

        @pl.when(top_tile)
        def _():
            for s in range(2 * WIDE):
                put(s, 0, jnp.concatenate([own_row[piece, s] for piece in range(4)], axis=0))

        def add(copy, index, tile, s):
            copy.wait()
            turn = top_tile & (tile == 0)

            @pl.when(turn)
            def _():
                turned = dot(one_hot(order_ref[...]), parts[index])
                for half in range(2):
                    rows = at(s, half)
                    lanes = slice(half * HALF, half * HALF + HALF)
                    out_ref[rows, :] = out_ref[rows, :] + turned[:, lanes]

            @pl.when(jnp.logical_not(turn))
            def _():
                for half in range(2):
                    rows = at(s, half, tile)
                    lanes = slice(half * HALF, half * HALF + HALF)
                    out_ref[rows, :] = out_ref[rows, :] + parts[index, :, lanes].astype(F32)

        each_child(add)

        @pl.when(col < NPIV)
        def _():
            @pl.when(jnp.logical_not(top_tile))
            def _():
                put(0, 0, own_col[:BS])

            put(0, 1, own_col[BS:])

            @pl.when(top_tile)
            def _():
                put(0, 0, own_block[...])


def run_finish(child_map, rc, top, front_left, order, view, cuts, child):
    once = pl.Buffered(1)
    rows = pl.BlockSpec((SPAN * BS * 16, HALF), lambda t, g: (t, 0))
    away = pl.BlockSpec(memory_space=pl.ANY)
    return pl.pallas_call(
        finish,
        grid=(4 // SPAN, 2),
        out_shape=shape(view.shape, F32),
        in_specs=[
            SMEM, SMEM,
            pl.BlockSpec((16, 4 * PIECE, BS), lambda t, g: (0, 2, 0), pipeline_mode=once),
            pl.BlockSpec((16, PIECE, BS), lambda t, g: (0, 12, 0), pipeline_mode=once),
            pl.BlockSpec((16, 16, BS), lambda t, g: (0, 13 * PIECE // 16, 0), pipeline_mode=once),
            pl.BlockSpec((16, WIDE * PIECE, BS), lambda t, g: (0, jnp.maximum(t, g), 0)),
            pl.BlockSpec((4, SPAN * BS, BS), lambda t, g: (0, t, 0)),
            pl.BlockSpec((2, 2, BS, 2 * BS), lambda t, g: (0, 0, 0, 0), pipeline_mode=once),
            pl.BlockSpec((BS, HALF), lambda t, g: (0, 0), pipeline_mode=once),
            rows, away, away, away, away, away,
        ],
        out_specs=rows,
        scratch_shapes=[
            pltpu.VMEM((4 * BS, 4 * BS), F32),
            pltpu.VMEM((4 * BS, 4 * BS), BF16), pltpu.VMEM((4 * BS, 4 * BS), BF16),
            pltpu.VMEM((NPIV, BS, BS), BF16), pltpu.VMEM((NPIV, BS, BS), BF16),
            pltpu.VMEM((2, 4 * BS, WIDE * BS), BF16), pltpu.VMEM((2, 4 * BS, WIDE * BS), BF16),
            pltpu.VMEM((SPAN * BS, 4 * BS), BF16), pltpu.VMEM((SPAN * BS, 4 * BS), BF16),
            pltpu.VMEM((SPAN * BS, BS), F32), pltpu.VMEM((BS, BS), F32),
            pltpu.VMEM((4, 8, PIECE, BS), F32),
            pltpu.VMEM((16, BS, BS), BF16),
            pltpu.SemaphoreType.DMA((16,)), pltpu.SemaphoreType.DMA((4,)),
        ],
        compiler_params=pltpu.CompilerParams(vmem_limit_bytes=LIMIT),
        cost_estimate=pl.CostEstimate(
            flops=23 * 2**30, bytes_accessed=32 * 2**20, transcendentals=0
        ),
    )(child_map, rc, top, top, top, top, front_left, child, order, view, *cuts, child)


def shards(front, child_update, child_map, pivots):
    row = lax.axis_index("prow")
    col = lax.axis_index("pcol")
    rc = jnp.stack([row, col]).astype(I32)
    tiles = front.shape[0]

    def along_z(a, hop):
        return lax.ppermute(
            a, "prow", [(4 * i + j, 4 * i + (j + hop) % 4) for i in range(4) for j in range(4)]
        )

    def along_y(a, hop):
        return lax.ppermute(
            a, "prow", [(4 * i + j, 4 * ((i + hop) % 4) + j) for i in range(4) for j in range(4)]
        )

    def from_plane(a, hop):
        return lax.ppermute(a, "prow", [(j, 4 * hop + j) for j in range(4)])

    def spread(pieces):
        return [pieces[0]] + [from_plane(pieces[hop], hop) for hop in (1, 2, 3)]

    strip = shape((BS, 2 * BS), BF16)
    zs = call(pick_z, [strip] * 4, [child_map, rc, child_update.reshape(2, BS, 2 * BS)])
    order = jnp.where(
        row < NPIV, pivots[jnp.minimum(row, NPIV - 1)], jnp.arange(BS, dtype=I32)
    )
    order = jnp.broadcast_to(order.astype(F32)[:, None], (BS, HALF))
    order, *zs = lax.optimization_barrier((order, *zs))
    zs = [zs[0]] + [along_z(zs[hop], hop) for hop in (1, 2, 3)]
    view = front.reshape(tiles, BS, 8, 2, HALF).transpose(0, 1, 3, 2, 4)
    view = view.reshape(tiles * BS * 16, HALF)

    cuts = pl.pallas_call(
        cut_front,
        grid=(1,),
        out_shape=[shape((8, PIECE, BS), F32)] * 4,
        in_specs=[
            pl.BlockSpec((BS * 16, HALF), lambda t: (0, 0)),
            pl.BlockSpec((BS, HALF), lambda t: (0, 0)),
        ],
        out_specs=[pl.BlockSpec((8, PIECE, BS), lambda t: (0, 0, 0))] * 4,
        compiler_params=pltpu.CompilerParams(vmem_limit_bytes=LIMIT),
        cost_estimate=pl.CostEstimate(flops=2**30, bytes_accessed=4 * 2**20, transcendentals=0),
    )(view, order)
    moved = spread(cuts)

    front_left = front[:, :, 0, :].reshape(tiles * BS, BS)
    zs, unused, unused = lax.optimization_barrier((zs, front_left, moved[0]))
    front_left = lax.all_gather(front_left, "pcol", axis=0, tiled=False)

    thin = shape((PIECE, 2 * BS), BF16)
    picked = call(pick_rows, [thin] * 4 + [strip] * 4, [child_map, rc, order, *zs])
    thin = spread(picked[:4])
    ys = [picked[4]] + [along_y(picked[4 + hop], hop) for hop in (1, 2, 3)]

    (thin,) = call(
        mix,
        [shape((4 * PIECE + 16, BS), I16)],
        [rc, *thin, *moved],
        smem=1,
        scratch=[pltpu.VMEM((PIECE, 2 * BS), F32), pltpu.VMEM((PIECE, BS), F32)],
    )
    thin = lax.all_gather(thin, "pcol", axis=0, tiled=False)
    (code,) = call(
        assemble,
        [shape((13 * PIECE + 16, BS), I16)],
        [child_map, rc, *moved, thin],
        scratch=[pltpu.VMEM((8, PIECE, BS), F32), pltpu.VMEM((NPIV, PIECE, BS), F32)],
    )

    (child,) = call(pack, [shape((4, BS, 2 * BS), BF16)], [rc, *ys], smem=1)
    code, child = lax.optimization_barrier((code, child))
    child = lax.all_gather(child, "pcol", axis=0, tiled=False)
    top = lax.all_gather(code, "prow", axis=0, tiled=False)

    done = run_finish(child_map, rc, top, front_left, order, view, cuts, child)
    done = done.reshape(tiles, BS, 2, 8, HALF).transpose(0, 1, 3, 2, 4)
    return done.reshape(front.shape)


def solution(mesh):
    return jax.shard_map(
        shards,
        mesh=mesh,
        in_specs=(P(None, "prow", None, "pcol"), P("prow", "pcol"), P(), P()),
        out_specs=P(None, "prow", None, "pcol"),
        check_vma=False,
    )
```

time: 214 us -> 195 us (0.911)
  blocking collectives: 78.4 us -> 61.2 us
  waiting for transfers between devices: 6.24 us -> 16.5 us
  Pallas kernels: 79.8 us -> 71.5 us
  starting transfers between devices: 25.4 us -> 23.1 us
    pallas_call x2 -> x1, Pallas kernels: 36.7 us -> 5.59 us  [shards(): pl.pallas_call(cut_front, grid=(1,), out_shape=[shape((8, PIECE, BS), F32...]
    pallas_call x1, Pallas kernels: 32.1 us -> 52 us  [run_finish(): pl.pallas_call(finish, grid=(4 // SPAN, 2), out_shape=shape(view.shape, F...]
    all_gather x2 -> x1, blocking collectives: 33.8 us -> 17.8 us  [shards(): thin = lax.all_gather(thin, 'pcol', axis=0, tiled=False)]
    ppermute x3, waiting for transfers between devices: 0.01 us -> 9.96 us  [along_z(): lax.ppermute(a, 'prow', [(4 * i + j, 4 * i + (j + hop) % 4) for i in rang...]
    ppermute x9 -> x6, starting transfers between devices: 16 us -> 10.7 us  [from_plane(): return lax.ppermute(a, 'prow', [(j, 4 * hop + j) for j in range(4)])]
    ppermute x3, starting transfers between devices: 2.73 us -> 5.69 us  [along_y(): lax.ppermute(a, 'prow', [(4 * i + j, 4 * ((i + hop) % 4) + j) for i in ra...]
    pallas_call x4 -> x5, Pallas kernels: 11 us -> 13.9 us  [call(): pl.pallas_call(body, out_shape=outs, in_specs=[SMEM] * smem + [VMEM] * (l...]
  transfers between devices with their start and end apart: 17 -> 14, of which waited for: 1 -> 6; matrix products, arithmetic and copies ran while one was open for 1% -> 1% of each run, Pallas kernels for 8% -> 10%
where the time goes in v6:
time: 195 us
  Pallas kernels  71.5 us (37%)
  blocking collectives  61.2 us (31%)
  starting transfers between devices  23.1 us (12%)
  waiting for transfers between devices  16.5 us (8%)
  between operations  13.6 us (7%)
  local copies, waits for them, and re-layouts  8.3 us (4%)
    pallas_call x1, Pallas kernels, run_finish(): pl.pallas_call(finish, grid=(4 // SPAN, 2), out_shape=shape(view.shape, F...  52 us
    all_gather x1, blocking collectives, shards(): top = lax.all_gather(code, 'prow', axis=0, tiled=False)  43.4 us
    all_gather x1, blocking collectives, shards(): thin = lax.all_gather(thin, 'pcol', axis=0, tiled=False)  17.8 us
    pallas_call x5, Pallas kernels, call(): pl.pallas_call(body, out_shape=outs, in_specs=[SMEM] * smem + [VMEM] * (l...  13.9 us
    ppermute x6, starting transfers between devices, from_plane(): return lax.ppermute(a, 'prow', [(j, 4 * hop + j) for j in range(4)])  10.7 us
    ppermute x3, waiting for transfers between devices, along_z(): lax.ppermute(a, 'prow', [(4 * i + j, 4 * i + (j + hop) % 4) for i in rang...  9.96 us
    ppermute x3, starting transfers between devices, along_z(): lax.ppermute(a, 'prow', [(4 * i + j, 4 * i + (j + hop) % 4) for i in rang...  6.64 us
    all_gather x1, waiting for transfers between devices, shards(): child = lax.all_gather(child, 'pcol', axis=0, tiled=False)  5.88 us
  transfers between devices with their start and end apart: 14, of which 6 were waited for; matrix products, arithmetic and copies ran while one was open for 1% of the time, Pallas kernels for 10%

profile of v6, /device:TPU:1, one launch (start us, length us, event | category | flops | bytes accessed | tf_op | source)
XLA Modules:
  0.0 194.8 jit_solution(3896245005730900637)
XLA Ops:
  6.5 3.9 %slice.3 = f32[4,256,1,256]{3,2,1,0:T(1,128)S(1)} slice(f32[4,256,8,256]{3,2,1,0:T(8,128)} %param.4), slice={[0:4], [0:256], [0:1], [0:256]} | slice | bytes 2097152 | tf_op jit(solution)/shard_map/slice | solution.py:566
  12.2 2.2 %shard_map.46 = (bf16[256,512]{1,0:T(8,128)(2,1)}, bf16[256,512]{1,0:T(8,128)(2,1)}, bf16[256,512]{1,0:T(8,128)(2,1)}, bf16[256,512]{1,0:T(8,128)(2,1)}) custom-call(s32[2,16]{1,0:T(2,128)} %map_ref.7, s32[2]{0:T(128)} %pad_add_fusion.rc_ref, bf16[2,256,512]{2,1,0:T(8,128)(2,1)} %bitcast.26), custom_call_target="tpu_custom_call" | custom-call | bytes 1573000 | tf_op jit(solution)/shard_map/pallas_call | solution.py:33
  15.2 2.5 %collective-permute-start.3 = (bf16[256,512]{1,0:T(8,128)(2,1)}, bf16[256,512]{1,0:T(8,128)(2,1)S(1)}, u32[]{:S(2)}, u32[]{:S(2)}) collective-permute-start(bf16[256,512]{1,0:T(8,128)(2,1)} %get-tuple-element.42), channel_id=1, source_target_pairs={{0,8},{8,16},{16,24},{24,0},{32,40},{40,48},{48,56},{56,32},{64,72... | collective-permute-start | bytes 786440 | tf_op jit(solution)/shard_map/ppermute | solution.py:526
  17.7 5.6 %shard_map.47 = (f32[8,64,256]{2,1,0:T(8,128)}, f32[8,64,256]{2,1,0:T(8,128)}, f32[8,64,256]{2,1,0:T(8,128)}, f32[8,64,256]{2,1,0:T(8,128)}) custom-call(f32[16384,128]{1,0:T(8,128)} %bitcast.18, f32[256,128]{1,0:T(8,128)} %broadcast_in_dim.2.order_ref), custom_call_target="tpu_custom_call" | custom-call | flops 1073741824 | bytes 4194304 | tf_op jit(solution)/shard_map/pallas_call | solution.py:552
  23.3 3.2 %collective-permute-start = (f32[8,64,256]{2,1,0:T(8,128)}, f32[8,64,256]{2,1,0:T(8,128)S(1)}, u32[]{:S(2)}, u32[]{:S(2)}) collective-permute-start(f32[8,64,256]{2,1,0:T(8,128)} %get-tuple-element.38.f1), channel_id=1, source_target_pairs={{0,32},{8,40},{16,48},{24,56},{1,33},{9,41},{17,49},{25,57},{2,34}... | collective-permute-start | bytes 1572872 | tf_op jit(solution)/shard_map/ppermute | solution.py:536
  26.5 2.3 %collective-permute-start.1 = (f32[8,64,256]{2,1,0:T(8,128)}, f32[8,64,256]{2,1,0:T(8,128)S(1)}, u32[]{:S(2)}, u32[]{:S(2)}) collective-permute-start(f32[8,64,256]{2,1,0:T(8,128)} %get-tuple-element.39.f2), channel_id=1, source_target_pairs={{0,64},{8,72},{16,80},{24,88},{1,65},{9,73},{17,81},{25,89},{2,66}... | collective-permute-start | bytes 1572872 | tf_op jit(solution)/shard_map/ppermute | solution.py:536
  28.8 1.3 collective-permute-start.2
  30.1 3.4 %collective-permute-start.4 = (bf16[256,512]{1,0:T(8,128)(2,1)S(1)}, bf16[256,512]{1,0:T(8,128)(2,1)S(1)}, u32[]{:S(2)}, u32[]{:S(2)}) collective-permute-start(bf16[256,512]{1,0:T(8,128)(2,1)S(1)} %copy-done.14), channel_id=1, source_target_pairs={{0,16},{8,24},{16,0},{24,8},{32,48},{40,56},{48,32},{56,40},{64,80... | collective-permute-start | bytes 786440 | tf_op jit(solution)/shard_map/ppermute | solution.py:526
  34.3 4.6 %collective-permute-done.4.refs_2_ = bf16[256,512]{1,0:T(8,128)(2,1)S(1)} collective-permute-done((bf16[256,512]{1,0:T(8,128)(2,1)S(1)}, bf16[256,512]{1,0:T(8,128)(2,1)S(1)}, u32[]{:S(2)}, u32[]{:S(2)}) %collective-permute-start.4) | collective-permute-done | bytes 262176 | tf_op jit(solution)/shard_map/ppermute | solution.py:526
  38.9 5.4 %collective-permute-done.5.refs_3_ = bf16[256,512]{1,0:T(8,128)(2,1)S(1)} collective-permute-done((bf16[256,512]{1,0:T(8,128)(2,1)S(1)}, bf16[256,512]{1,0:T(8,128)(2,1)S(1)}, u32[]{:S(2)}, u32[]{:S(2)}) %collective-permute-start.5) | collective-permute-done | bytes 262176 | tf_op jit(solution)/shard_map/ppermute | solution.py:526
  45.0 2.9 %shard_map.48 = (bf16[64,512]{1,0:T(8,128)(2,1)}, bf16[64,512]{1,0:T(8,128)(2,1)}, bf16[64,512]{1,0:T(8,128)(2,1)}, bf16[64,512]{1,0:T(8,128)(2,1)}, bf16[256,51...) custom-call(s32[2,16]{1,0:T(2,128)} %map_ref.7, ...), custom_call_target="tpu_custom_call" | custom-call | bytes 2490504 | tf_op jit(solution)/shard_map/pallas_call | solution.py:33
  47.9 1.3 collective-permute-start.6
  49.1 1.3 collective-permute-start.7
  50.8 1.3 collective-permute-start.8
  52.3 1.3 collective-permute-start.9
  53.7 2.4 %collective-permute-start.10 = (bf16[256,512]{1,0:T(8,128)(2,1)}, bf16[256,512]{1,0:T(8,128)(2,1)S(1)}, u32[]{:S(2)}, u32[]{:S(2)}) collective-permute-start(bf16[256,512]{1,0:T(8,128)(2,1)} %get-tuple-element.55), channel_id=1, source_target_pairs={{0,64},{8,72},{16,80},{24,88},{32,96},{40,104},{48,112},{56,120},{... | collective-permute-start | bytes 786440 | tf_op jit(solution)/shard_map/ppermute | solution.py:531
  56.1 2.0 %collective-permute-start.11 = (bf16[256,512]{1,0:T(8,128)(2,1)}, bf16[256,512]{1,0:T(8,128)(2,1)S(1)}, u32[]{:S(2)}, u32[]{:S(2)}) collective-permute-start(bf16[256,512]{1,0:T(8,128)(2,1)} %get-tuple-element.56), channel_id=1, source_target_pairs={{0,96},{8,104},{16,112},{24,120},{32,0},{40,8},{48,16},{56,24},{64... | collective-permute-start | bytes 786440 | tf_op jit(solution)/shard_map/ppermute | solution.py:531
  59.1 2.7 %shard_map.49 = s16[272,256]{1,0:T(8,128)(2,1)} custom-call(s32[2]{0:T(128)} %pad_add_fusion.rc_ref, bf16[64,512]{1,0:T(8,128)(2,1)} %get-tuple-element.49.t0, bf16[64,512]{1,0:T(8,128)(2,1)} %copy-done.10, bf16[64,512]{1,0:T(8,128)(2,1)} %copy-done.11, bf16[64,512]{1,0:T(8,128)(2,1)} %copy-done.12, f32[8,64,256]{2,1,0:T(8,128)} %get-tuple-element.37.f0, ...), custom_call_target="tpu_custom_call" | custom-call | bytes 2498568 | tf_op jit(solution)/shard_map/pallas_call | solution.py:33
  61.8 17.8 %all-gather.11 = s16[2176,256]{1,0:T(8,128)(2,1)} all-gather(s16[272,256]{1,0:T(8,128)(2,1)} %shard_map.49), channel_id=2, replica_groups=mesh['prow'=16,'pcol'=8] {'pcol'}, dimensions={0}, use_global_device_ids=true | all-gather | bytes 1253376 | tf_op jit(solution)/shard_map/all_gather | solution.py:582
  79.5 3.9 %shard_map.50 = s16[848,256]{1,0:T(8,128)(2,1)} custom-call(s32[2,16]{1,0:T(2,128)} %map_ref.7, s32[2]{0:T(128)} %pad_add_fusion.rc_ref, f32[8,64,256]{2,1,0:T(8,128)} %get-tuple-element.37.f0, f32[8,64,256]{2,1,0:T(8,128)} %copy-done.1, f32[8,64,256]{2,1,0:T(8,128)} %copy-done.2, f32[8,64,256]{2,1,0:T(8,128)} %copy-done.3, s16[8,272,256]{2,1,0:T(8,128)(2,1)} %bitcast.24), custom_call_target="tpu_custom_call" | custom-call | bytes 3645576 | tf_op jit(solution)/shard_map/pallas_call | solution.py:33
  84.4 2.3 %shard_map.51 = bf16[4,256,512]{2,1,0:T(8,128)(2,1)} custom-call(s32[2]{0:T(128)} %pad_add_fusion.rc_ref, bf16[256,512]{1,0:T(8,128)(2,1)} %get-tuple-element.53.h0, bf16[256,512]{1,0:T(8,128)(2,1)} %copy-done.5, bf16[256,512]{1,0:T(8,128)(2,1)} %copy-done.6, bf16[256,512]{1,0:T(8,128)(2,1)} %copy-done.7), custom_call_target="tpu_custom_call" | custom-call | bytes 2097160 | tf_op jit(solution)/shard_map/pallas_call | solution.py:33
  86.7 43.4 %all-gather.12 = s16[13568,256]{1,0:T(8,128)(2,1)} all-gather(s16[848,256]{1,0:T(8,128)(2,1)} %shard_map.50), channel_id=3, replica_groups=mesh['prow'=16,'pcol'=8] {'prow'}, dimensions={0}, use_global_device_ids=true | all-gather | bytes 7380992 | tf_op jit(solution)/shard_map/all_gather | solution.py:593
  130.1 5.9 %all-gather.10.cloned.1.call-done = bf16[32,256,512]{2,1,0:T(8,128)(2,1)} async-done(((bf16[4,256,512]{2,1,0:T(8,128)(2,1)}), bf16[32,256,512]{2,1,0:T(8,128)(2,1)}) %all-gather.10.cloned.1.call-update) | async-done | bytes 8388624 | tf_op jit(solution)/shard_map/all_gather | solution.py:592
  136.0 52.0 %shard_map.52 = f32[16384,128]{1,0:T(8,128)} custom-call(s32[2,16]{1,0:T(2,128)} %map_ref.7, s32[2]{0:T(128)} %pad_add_fusion.rc_ref, s16[16,848,256]{2,1,0:T(8,128)(2,1)} %bitcast.20, s16[16,848,256]{2,1,0:T(8,128)(2,1)} %bitcast.21, s16[16,848,256]{2,1,0:T(8,128)(2,1)} %bitcast.22, s16[16,848,256]{2,1,0:T(8,128)(2,1)} %bitcast.23, ...), custom_call_target="tpu_custom_call" | custom-call | flops 24696061952 | bytes 33554432 | tf_op jit(solution)/shard_map/pallas_call | solution.py:485
  (51 shorter events, 6.5 us)
Async XLA Ops:
  6.5 7.9 %copy-start = (s32[4,256]{1,0:T(4,128)S(1)}, s32[4,256]{1,0:T(4,128)}, u32[]{:S(2)}) copy-start(s32[4,256]{1,0:T(4,128)} %param.7) | copy-start | bytes 12292
  6.5 123.6 %all-gather.8.cloned.1.call-start = ((), (), s32[]{:S(2)}) async-start(), calls=%async_computation | async-start | bytes 9437184 | tf_op jit(solution)/shard_map/all_gather | solution.py:568
  11.5 124.5 %all-gather.10.cloned.1.call-start = ((), (), s32[]{:S(2)}) async-start(), calls=%async_computation.1 | async-start | bytes 9437184 | tf_op jit(solution)/shard_map/all_gather | solution.py:592
  14.4 15.7 %copy-start.14 = (bf16[256,512]{1,0:T(8,128)(2,1)S(1)}, bf16[256,512]{1,0:T(8,128)(2,1)}, u32[]{:S(2)}) copy-start(bf16[256,512]{1,0:T(8,128)(2,1)} %get-tuple-element.43) | copy-start | bytes 786436
  14.4 19.1 %copy-start.13 = (bf16[256,512]{1,0:T(8,128)(2,1)S(1)}, bf16[256,512]{1,0:T(8,128)(2,1)}, u32[]{:S(2)}) copy-start(bf16[256,512]{1,0:T(8,128)(2,1)} %get-tuple-element.44) | copy-start | bytes 786436
  15.2 18.3 %collective-permute-start.3 = (bf16[256,512]{1,0:T(8,128)(2,1)}, bf16[256,512]{1,0:T(8,128)(2,1)S(1)}, u32[]{:S(2)}, u32[]{:S(2)}) collective-permute-start(bf16[256,512]{1,0:T(8,128)(2,1)} %get-tuple-element.42), channel_id=1, source_target_pairs={{0,8},{8,16},{16,24},{24,0},{32,40},{40,48},{48,56},{56,32},{64,72... | collective-permute-start | bytes 786440 | tf_op jit(solution)/shard_map/ppermute | solution.py:526
  23.3 32.9 %collective-permute-start = (f32[8,64,256]{2,1,0:T(8,128)}, f32[8,64,256]{2,1,0:T(8,128)S(1)}, u32[]{:S(2)}, u32[]{:S(2)}) collective-permute-start(f32[8,64,256]{2,1,0:T(8,128)} %get-tuple-element.38.f1), channel_id=1, source_target_pairs={{0,32},{8,40},{16,48},{24,56},{1,33},{9,41},{17,49},{25,57},{2,34}... | collective-permute-start | bytes 1572872 | tf_op jit(solution)/shard_map/ppermute | solution.py:536
  26.5 31.6 %collective-permute-start.1 = (f32[8,64,256]{2,1,0:T(8,128)}, f32[8,64,256]{2,1,0:T(8,128)S(1)}, u32[]{:S(2)}, u32[]{:S(2)}) collective-permute-start(f32[8,64,256]{2,1,0:T(8,128)} %get-tuple-element.39.f2), channel_id=1, source_target_pairs={{0,64},{8,72},{16,80},{24,88},{1,65},{9,73},{17,81},{25,89},{2,66}... | collective-permute-start | bytes 1572872 | tf_op jit(solution)/shard_map/ppermute | solution.py:536
  28.8 29.3 %collective-permute-start.2 = (f32[8,64,256]{2,1,0:T(8,128)}, f32[8,64,256]{2,1,0:T(8,128)S(1)}, u32[]{:S(2)}, u32[]{:S(2)}) collective-permute-start(f32[8,64,256]{2,1,0:T(8,128)} %get-tuple-element.40.f3), channel_id=1, source_target_pairs={{0,96},{8,104},{16,112},{24,120},{1,97},{9,105},{17,113},{25,121},... | collective-permute-start | bytes 1572872 | tf_op jit(solution)/shard_map/ppermute | solution.py:536
  30.1 8.8 %collective-permute-start.4 = (bf16[256,512]{1,0:T(8,128)(2,1)S(1)}, bf16[256,512]{1,0:T(8,128)(2,1)S(1)}, u32[]{:S(2)}, u32[]{:S(2)}) collective-permute-start(bf16[256,512]{1,0:T(8,128)(2,1)S(1)} %copy-done.14), channel_id=1, source_target_pairs={{0,16},{8,24},{16,0},{24,8},{32,48},{40,56},{48,32},{56,40},{64,80... | collective-permute-start | bytes 786440 | tf_op jit(solution)/shard_map/ppermute | solution.py:526
  33.5 10.8 %copy-start.4 = (bf16[256,512]{1,0:T(8,128)(2,1)}, bf16[256,512]{1,0:T(8,128)(2,1)S(1)}, u32[]{:S(2)}) copy-start(bf16[256,512]{1,0:T(8,128)(2,1)S(1)} %collective-permute-done.3.refs_1_) | copy-start | bytes 786436
  33.5 10.7 %collective-permute-start.5 = (bf16[256,512]{1,0:T(8,128)(2,1)S(1)}, bf16[256,512]{1,0:T(8,128)(2,1)S(1)}, u32[]{:S(2)}, u32[]{:S(2)}) collective-permute-start(bf16[256,512]{1,0:T(8,128)(2,1)S(1)} %copy-done.13), channel_id=1, source_target_pairs={{0,24},{8,0},{16,8},{24,16},{32,56},{40,32},{48,40},{56,48},{64,88... | collective-permute-start | bytes 786440 | tf_op jit(solution)/shard_map/ppermute | solution.py:526
  38.9 5.4 %copy-start.8 = (bf16[256,512]{1,0:T(8,128)(2,1)}, bf16[256,512]{1,0:T(8,128)(2,1)S(1)}, u32[]{:S(2)}) copy-start(bf16[256,512]{1,0:T(8,128)(2,1)S(1)} %collective-permute-done.4.refs_2_) | copy-start | bytes 786436
  47.9 2.9 %collective-permute-start.6 = (bf16[64,512]{1,0:T(8,128)(2,1)}, bf16[64,512]{1,0:T(8,128)(2,1)S(1)}, u32[]{:S(2)}, u32[]{:S(2)}) collective-permute-start(bf16[64,512]{1,0:T(8,128)(2,1)} %get-tuple-element.50), channel_id=1, source_target_pairs={{0,32},{8,40},{16,48},{24,56},{1,33},{9,41},{17,49},{25,57},{2,34}... | collective-permute-start | bytes 196616 | tf_op jit(solution)/shard_map/ppermute | solution.py:536
  49.1 3.2 %collective-permute-start.7 = (bf16[64,512]{1,0:T(8,128)(2,1)}, bf16[64,512]{1,0:T(8,128)(2,1)S(1)}, u32[]{:S(2)}, u32[]{:S(2)}) collective-permute-start(bf16[64,512]{1,0:T(8,128)(2,1)} %get-tuple-element.51), channel_id=1, source_target_pairs={{0,64},{8,72},{16,80},{24,88},{1,65},{9,73},{17,81},{25,89},{2,66}... | collective-permute-start | bytes 196616 | tf_op jit(solution)/shard_map/ppermute | solution.py:536
  50.8 7.3 %copy-start.10 = (bf16[64,512]{1,0:T(8,128)(2,1)}, bf16[64,512]{1,0:T(8,128)(2,1)S(1)}, u32[]{:S(2)}) copy-start(bf16[64,512]{1,0:T(8,128)(2,1)S(1)} %collective-permute-done.6.t1) | copy-start | bytes 196612
  50.8 2.9 %collective-permute-start.8 = (bf16[64,512]{1,0:T(8,128)(2,1)}, bf16[64,512]{1,0:T(8,128)(2,1)S(1)}, u32[]{:S(2)}, u32[]{:S(2)}) collective-permute-start(bf16[64,512]{1,0:T(8,128)(2,1)} %get-tuple-element.52), channel_id=1, source_target_pairs={{0,96},{8,104},{16,112},{24,120},{1,97},{9,105},{17,113},{25,121},... | collective-permute-start | bytes 196616 | tf_op jit(solution)/shard_map/ppermute | solution.py:536
  52.3 5.8 %copy-start.11 = (bf16[64,512]{1,0:T(8,128)(2,1)}, bf16[64,512]{1,0:T(8,128)(2,1)S(1)}, u32[]{:S(2)}) copy-start(bf16[64,512]{1,0:T(8,128)(2,1)S(1)} %collective-permute-done.7.t2) | copy-start | bytes 196612
  52.3 31.1 %collective-permute-start.9 = (bf16[256,512]{1,0:T(8,128)(2,1)}, bf16[256,512]{1,0:T(8,128)(2,1)S(1)}, u32[]{:S(2)}, u32[]{:S(2)}) collective-permute-start(bf16[256,512]{1,0:T(8,128)(2,1)} %get-tuple-element.54), channel_id=1, source_target_pairs={{0,32},{8,40},{16,48},{24,56},{32,64},{40,72},{48,80},{56,88},{64,... | collective-permute-start | bytes 786440 | tf_op jit(solution)/shard_map/ppermute | solution.py:531
  53.7 4.4 %copy-start.12 = (bf16[64,512]{1,0:T(8,128)(2,1)}, bf16[64,512]{1,0:T(8,128)(2,1)S(1)}, u32[]{:S(2)}) copy-start(bf16[64,512]{1,0:T(8,128)(2,1)S(1)} %collective-permute-done.8.t3) | copy-start | bytes 196612
  53.7 29.7 %collective-permute-start.10 = (bf16[256,512]{1,0:T(8,128)(2,1)}, bf16[256,512]{1,0:T(8,128)(2,1)S(1)}, u32[]{:S(2)}, u32[]{:S(2)}) collective-permute-start(bf16[256,512]{1,0:T(8,128)(2,1)} %get-tuple-element.55), channel_id=1, source_target_pairs={{0,64},{8,72},{16,80},{24,88},{32,96},{40,104},{48,112},{56,120},{... | collective-permute-start | bytes 786440 | tf_op jit(solution)/shard_map/ppermute | solution.py:531
  56.1 2.0 %copy-start.1 = (f32[8,64,256]{2,1,0:T(8,128)}, f32[8,64,256]{2,1,0:T(8,128)S(1)}, u32[]{:S(2)}) copy-start(f32[8,64,256]{2,1,0:T(8,128)S(1)} %collective-permute-done.f1) | copy-start | bytes 1572868
  56.1 27.3 %collective-permute-start.11 = (bf16[256,512]{1,0:T(8,128)(2,1)}, bf16[256,512]{1,0:T(8,128)(2,1)S(1)}, u32[]{:S(2)}, u32[]{:S(2)}) collective-permute-start(bf16[256,512]{1,0:T(8,128)(2,1)} %get-tuple-element.56), channel_id=1, source_target_pairs={{0,96},{8,104},{16,112},{24,120},{32,0},{40,8},{48,16},{56,24},{64... | collective-permute-start | bytes 786440 | tf_op jit(solution)/shard_map/ppermute | solution.py:531
  58.1 1.0 copy-start.3
  (5 other events, 4.0 us)
Sparse Core Ops, SparseCore 0:
  11.7 53.3 all-gather.7
  86.8 49.1 all-gather.9

commit v7 on v6

--- a/solution.py
+++ b/solution.py
@@ -75,6 +75,13 @@
     return dot(a, c) + (dot(a, d) + dot(b, c))
 
 
+CHUNK = 128
+
+
+def chunk(step):
+    return pl.ds(pl.multiple_of(step * CHUNK, CHUNK), CHUNK)
+
+
 def block(step):
     return slice(step * BS, step * BS + BS)
 
@@ -120,12 +127,24 @@
     lax.fori_loop(0, 8, one, 0)
 
 
-def pick_z(map_ref, rc_ref, child_ref, *outs):
+def begin(map_ref, rc_ref, child_ref, view_ref, o0, o1, o2, o3, left_ref, arrived):
+    copies = [
+        pltpu.make_async_copy(
+            view_ref.at[:, half, 0, :],
+            left_ref.at[:, half * HALF : half * HALF + HALF],
+            arrived.at[half],
+        )
+        for half in range(2)
+    ]
+    for copy in copies:
+        copy.start()
     row = rc_ref[0]
     z = row % 4
     second_at = map_ref[row // 8, 2 * (row % 8) + 1] % 4
-    for hop in range(4):
-        outs[hop][...] = child_ref[jnp.where(second_at == (z + hop) % 4, 1, 0)]
+    for hop, out in enumerate((o0, o1, o2, o3)):
+        out[...] = child_ref[jnp.where(second_at == (z + hop) % 4, 1, 0)]
+    for copy in copies:
+        copy.wait()
 
 
 def pick_rows(map_ref, rc_ref, order_ref, *refs):
@@ -247,7 +266,7 @@
         out_ref[(y - shift + 4) % 4] = source[...]
 
 
-def factor_corner(code_ref, rest_ref, level_ref, work, xhi, xlo):
+def factor_corner(code_ref, rest_ref, level_ref, work, chi, clo, xhi, xlo):
     for y in range(4):
         for z in range(4):
             low = z * BS + y * PIECE
@@ -272,15 +291,26 @@
         approx = 2.0 * jnp.where(diagonal, across, 0.0) - (down * pivot) * across
         for sweep_index in range(NS - 1):
             pair = split(approx)
-            approx = 2.0 * approx - dot3(split(dot3(pair, parts)), pair)
+            halves = []
+            for half in range(2):
+                rows = slice(half * CHUNK, half * CHUNK + CHUNK)
+                left = split(dot3((pair[0][rows], pair[1][rows]), parts))
+                halves.append(2.0 * approx[rows] - dot3(left, pair))
+            approx = jnp.concatenate(halves, axis=0)
         xhi[k], xlo[k] = split(approx)
-        if k + 1 < NPIV:
-            below = slice((k + 1) * BS, NPIV * BS)
-            lower = dot3(split(work[below, block(k)]), (xhi[k], xlo[k]))
-            work[below, block(k)] = lower
-            work[below, below] = work[below, below] - dot3(
-                split(lower), split(work[block(k), below])
-            )
+        chi[block(k)], clo[block(k)] = split(work[block(k)])
+
+        def below(step, carry, k=k):
+            rows = chunk(step)
+            pair = split(dot3(split(work[rows, block(k)]), (xhi[k], xlo[k])))
+            work[rows, block(k)] = pair[0].astype(F32) + pair[1].astype(F32)
+            for j in range(k + 1, NPIV):
+                work[rows, block(j)] = work[rows, block(j)] - dot3(
+                    pair, (chi[block(k), block(j)], clo[block(k), block(j)])
+                )
+            return carry
+
+        lax.fori_loop(2 * (k + 1), 2 * NPIV, below, 0)
 
 
 SPAN = 2
@@ -296,7 +326,6 @@
     step, group = pl.program_id(0), pl.program_id(1)
     row, col = rc_ref[0], rc_ref[1]
     top_row = row < NPIV
-    low_rows = slice(0, SPAN * BS)
     high_rows = slice(SPAN * BS, 2 * SPAN * BS)
 
     def at(s, half, tile=0, count=1):
@@ -342,9 +371,7 @@
             for copy in own_copies():
                 copy.start()
 
-        factor_corner(corner_ref, rest_ref, level_ref, work, xhi, xlo)
-        for k in range(NPIV):
-            chi[block(k)], clo[block(k)] = split(work[block(k)])
+        factor_corner(corner_ref, rest_ref, level_ref, work, chi, clo, xhi, xlo)
         for r in range(NPIV):
             for c in range(NPIV):
 
@@ -360,32 +387,41 @@
     @pl.when(step == 0)
     def _():
         for k in range(NPIV):
-            raw = slice(0, BS)
             for piece in range(4):
                 scale = level_ref[4 * piece + k].astype(I32)
                 for q in range(WIDE):
                     work[piece * PIECE : piece * PIECE + PIECE, block(q)] = decode(
                         code_ref[4 * piece + k, q * PIECE : q * PIECE + PIECE].astype(I32), scale
                     )
-            if k:
-                done = slice(0, k * BS)
-                taken = dot3(
-                    (chi[block(k), done], clo[block(k), done]),
-                    (uhi[group, done], ulo[group, done]),
-                )
-                work[raw] = work[raw] - taken
-
-                @pl.when(row == k)
-                def _(taken=taken):
-                    for piece in range(4):
-                        for q in range(WIDE):
+
+            def upper(half, carry, k=k):
+                rows = chunk(half)
+                put_rows = chunk(2 * k + half)
+                for q in range(WIDE):
+                    value = work[rows, block(q)]
+                    if k:
+                        done = slice(0, k * BS)
+                        taken = dot3(
+                            (chi[put_rows, done], clo[put_rows, done]),
+                            (uhi[group, done, block(q)], ulo[group, done, block(q)]),
+                        )
+                        value = value - taken
+
+                        @pl.when(row == k)
+                        def _(taken=taken, q=q):
                             tile = WIDE * group + q
-                            own_row[piece, tile] = (
-                                own_row[piece, tile]
-                                - taken[piece * PIECE : piece * PIECE + PIECE, block(q)]
-                            )
-
-            uhi[group, block(k)], ulo[group, block(k)] = split(work[raw])
+                            for part in range(2):
+                                low = part * PIECE
+                                own_row[2 * half + part, tile] = (
+                                    own_row[2 * half + part, tile] - taken[low : low + PIECE]
+                                )
+
+                    high, low = split(value)
+                    uhi[group, put_rows, block(q)] = high
+                    ulo[group, put_rows, block(q)] = low
+                return carry
+
+            lax.fori_loop(0, 2, upper, 0)
 
     @pl.when(group == 0)
     def _():
@@ -412,28 +448,40 @@
         def _():
             left[:BS] = jnp.zeros((BS, NPIV * BS), F32)
 
-        for k in range(NPIV):
-            lower = dot3(split(left[:, block(k)]), (xhi[k], xlo[k]))
-            pair = split(lower)
-            lhi[:, block(k)], llo[:, block(k)] = pair
-
-            @pl.when(col == k)
-            def _(lower=lower):
-                own_col[...] = lower
-
-            if k + 1 < NPIV:
-                rest = slice((k + 1) * BS, NPIV * BS)
-                left[:, rest] = left[:, rest] - dot3(pair, (chi[block(k), rest], clo[block(k), rest]))
-
-    total = work.at[low_rows]
-    total[...] = dot(lhi[...], uhi[group])
-    total[...] += dot(lhi[...], ulo[group])
-    total[...] += dot(llo[...], uhi[group])
-    for q in range(WIDE):
-        for half in range(2):
-            rows = at(WIDE * group + q, half, 0, SPAN)
-            low = q * BS + half * HALF
-            out_ref[rows, :] = front_ref[rows, :] - total[:, low : low + HALF]
+        def lower(step, carry):
+            lines = [chunk(2 * step + half) for half in range(2)]
+            for k in range(NPIV):
+                for rows in lines:
+                    value = dot3(split(left[rows, block(k)]), (xhi[k], xlo[k]))
+                    pair = split(value)
+                    lhi[rows, block(k)], llo[rows, block(k)] = pair
+
+                    @pl.when(col == k)
+                    def _(value=value, rows=rows):
+                        own_col[rows, :] = value
+
+                    for j in range(k + 1, NPIV):
+                        left[rows, block(j)] = left[rows, block(j)] - dot3(
+                            pair, (chi[block(k), block(j)], clo[block(k), block(j)])
+                        )
+            return carry
+
+        lax.fori_loop(0, SPAN * BS // (2 * CHUNK), lower, 0)
+
+    def update(step, carry):
+        rows = chunk(step)
+        for q in range(WIDE):
+            upper = (uhi[group, :, block(q)], ulo[group, :, block(q)])
+            total = dot3((lhi[rows, :], llo[rows, :]), upper)
+            for half in range(2):
+                first = step * (CHUNK * 16) + half * 8 + WIDE * group + q
+                lines = pl.ds(first, CHUNK, stride=16)
+                out_ref[lines, :] = (
+                    front_ref[lines, :] - total[:, half * HALF : half * HALF + HALF]
+                )
+        return carry
+
+    lax.fori_loop(0, SPAN * BS // CHUNK, update, 0)
 
     @pl.when(group == 1)
     def _():
@@ -539,16 +587,23 @@
         return [pieces[0]] + [from_plane(pieces[hop], hop) for hop in (1, 2, 3)]
 
     strip = shape((BS, 2 * BS), BF16)
-    zs = call(pick_z, [strip] * 4, [child_map, rc, child_update.reshape(2, BS, 2 * BS)])
+    view = front.reshape(tiles, BS, 8, 2, HALF).transpose(0, 1, 3, 2, 4)
+    *zs, front_left = pl.pallas_call(
+        begin,
+        out_shape=[strip] * 4 + [shape((tiles * BS, BS), F32)],
+        in_specs=[SMEM, SMEM, VMEM, pl.BlockSpec(memory_space=pl.ANY)],
+        out_specs=[VMEM] * 5,
+        scratch_shapes=[pltpu.SemaphoreType.DMA((2,))],
+        compiler_params=pltpu.CompilerParams(vmem_limit_bytes=LIMIT),
+        cost_estimate=pl.CostEstimate(flops=0, bytes_accessed=4 * 2**20, transcendentals=0),
+    )(child_map, rc, child_update.reshape(2, BS, 2 * BS), view.reshape(tiles * BS, 2, 8, HALF))
+    view = view.reshape(tiles * BS * 16, HALF)
     order = jnp.where(
         row < NPIV, pivots[jnp.minimum(row, NPIV - 1)], jnp.arange(BS, dtype=I32)
     )
     order = jnp.broadcast_to(order.astype(F32)[:, None], (BS, HALF))
     order, *zs = lax.optimization_barrier((order, *zs))
     zs = [zs[0]] + [along_z(zs[hop], hop) for hop in (1, 2, 3)]
-    view = front.reshape(tiles, BS, 8, 2, HALF).transpose(0, 1, 3, 2, 4)
-    view = view.reshape(tiles * BS * 16, HALF)
-
     cuts = pl.pallas_call(
         cut_front,
         grid=(1,),
@@ -563,12 +618,13 @@
     )(view, order)
     moved = spread(cuts)
 
-    front_left = front[:, :, 0, :].reshape(tiles * BS, BS)
-    zs, unused, unused = lax.optimization_barrier((zs, front_left, moved[0]))
     front_left = lax.all_gather(front_left, "pcol", axis=0, tiled=False)
 
     thin = shape((PIECE, 2 * BS), BF16)
-    picked = call(pick_rows, [thin] * 4 + [strip] * 4, [child_map, rc, order, *zs])
+    zs, unused = lax.optimization_barrier((zs, moved[1]))
+    picked = call(
+        pick_rows, [thin] * 4 + [strip] * 4, [child_map, rc, order, *zs], flops=20 * 2**30
+    )
     thin = spread(picked[:4])
     ys = [picked[4]] + [along_y(picked[4 + hop], hop) for hop in (1, 2, 3)]
 
@@ -580,6 +636,8 @@
         scratch=[pltpu.VMEM((PIECE, 2 * BS), F32), pltpu.VMEM((PIECE, BS), F32)],
     )
     thin = lax.all_gather(thin, "pcol", axis=0, tiled=False)
+    (child,) = call(pack, [shape((4, BS, 2 * BS), BF16)], [rc, *ys], smem=1)
+    thin, child = lax.optimization_barrier((thin, child))
     (code,) = call(
         assemble,
         [shape((13 * PIECE + 16, BS), I16)],
@@ -587,8 +645,6 @@
         scratch=[pltpu.VMEM((8, PIECE, BS), F32), pltpu.VMEM((NPIV, PIECE, BS), F32)],
     )
 
-    (child,) = call(pack, [shape((4, BS, 2 * BS), BF16)], [rc, *ys], smem=1)
-    code, child = lax.optimization_barrier((code, child))
     child = lax.all_gather(child, "pcol", axis=0, tiled=False)
     top = lax.all_gather(code, "prow", axis=0, tiled=False)
 

time: 195 us -> 211 us (1.082)
  Pallas kernels: 71.5 us -> 98.5 us
  waiting for transfers between devices: 16.5 us -> 5.72 us
  local copies, waits for them, and re-layouts: 8.3 us -> 3.06 us
  blocking collectives: 61.2 us -> 65.4 us
    pallas_call x1, Pallas kernels: 52 us -> 77.3 us  [run_finish(): pl.pallas_call(finish, grid=(4 // SPAN, 2), out_shape=shape(view.shape, F...]
    all_gather x1, waiting for transfers between devices: 5.88 us -> 0.05 us  [shards(): child = lax.all_gather(child, 'pcol', axis=0, tiled=False)]
    ppermute x3, waiting for transfers between devices: 9.96 us -> 5.61 us  [along_z(): lax.ppermute(a, 'prow', [(4 * i + j, 4 * i + (j + hop) % 4) for i in rang...]
    slice x1 -> x0, local copies, waits for them, and re-layouts: 3.93 us -> none  [shards(): front_left = front[:, :, 0, :].reshape(tiles * BS, BS)]
    pallas_call x0 -> x1, Pallas kernels: none -> 3.64 us  [shards(): pl.pallas_call(begin, out_shape=[strip] * 4 + [shape((tiles * BS, BS), F3...]
    all_gather x1, blocking collectives: 17.8 us -> 20.3 us  [shards(): thin = lax.all_gather(thin, 'pcol', axis=0, tiled=False)]
    ppermute x6, starting transfers between devices: 10.7 us -> 13 us  [from_plane(): return lax.ppermute(a, 'prow', [(j, 4 * hop + j) for j in range(4)])]
    pallas_call x5 -> x4, Pallas kernels: 13.9 us -> 11.9 us  [call(): pl.pallas_call(body, out_shape=outs, in_specs=[SMEM] * smem + [VMEM] * (l...]
  transfers between devices with their start and end apart: 14 -> 14, of which waited for: 6 -> 2; matrix products, arithmetic and copies ran while one was open for 1% -> 0% of each run, Pallas kernels for 10% -> 8%
where the time goes in v7:
time: 211 us; the launch traced here: 209 us
  Pallas kernels  98.5 us (47%)
  blocking collectives  65.4 us (31%)
  starting transfers between devices  22.4 us (11%)
  between operations  13.7 us (6%)
  waiting for transfers between devices  5.72 us (3%)
  local copies, waits for them, and re-layouts  3.06 us (1%)
    pallas_call x1, Pallas kernels, run_finish(): pl.pallas_call(finish, grid=(4 // SPAN, 2), out_shape=shape(view.shape, F...  77.3 us
    all_gather x1, blocking collectives, shards(): top = lax.all_gather(code, 'prow', axis=0, tiled=False)  45 us
    all_gather x1, blocking collectives, shards(): thin = lax.all_gather(thin, 'pcol', axis=0, tiled=False)  20.3 us
    ppermute x6, starting transfers between devices, from_plane(): return lax.ppermute(a, 'prow', [(j, 4 * hop + j) for j in range(4)])  13 us
    pallas_call x4, Pallas kernels, call(): pl.pallas_call(body, out_shape=outs, in_specs=[SMEM] * smem + [VMEM] * (l...  11.9 us
    ppermute x3, starting transfers between devices, along_z(): lax.ppermute(a, 'prow', [(4 * i + j, 4 * i + (j + hop) % 4) for i in rang...  5.74 us
    ppermute x3, waiting for transfers between devices, along_z(): lax.ppermute(a, 'prow', [(4 * i + j, 4 * i + (j + hop) % 4) for i in rang...  5.61 us
    pallas_call x1, Pallas kernels, shards(): pl.pallas_call(cut_front, grid=(1,), out_shape=[shape((8, PIECE, BS), F32...  5.59 us
  transfers between devices with their start and end apart: 14, of which 2 were waited for; matrix products, arithmetic and copies ran while one was open for 0% of the time, Pallas kernels for 8%

profile of v7, /device:TPU:1, one launch (start us, length us, event | category | flops | bytes accessed | tf_op | source)
XLA Modules:
  0.0 209.4 jit_solution(17350601906645209156)
XLA Ops:
  7.2 3.6 %shard_map.46 = (bf16[256,512]{1,0:T(8,128)(2,1)}, bf16[256,512]{1,0:T(8,128)(2,1)}, bf16[256,512]{1,0:T(8,128)(2,1)}, bf16[256,512]{1,0:T(8,128)(2,1)}, f32[1024,256]{1,0:T(8,128)}) custom-call(s32[2,16]{1,0:T(2,128)} %map_ref.7, s32[2]{0:T(128)} %pad_add_fusion.rc_ref, bf16[2,256,512]{2,1,0:T(8,128)(2,1)} %bitcast.28, f32[1024,2,8,128]{3,2,1,0:T(8,128)} %bitcast.20), custom_call_target="tpu_custom_call" | custom-call | bytes 4194304 | tf_op jit(solution)/shard_map/pallas_call | solution.py:591
  11.0 0.8 broadcast_in_dim.2.order_ref
  11.7 5.6 %shard_map.47 = (f32[8,64,256]{2,1,0:T(8,128)}, f32[8,64,256]{2,1,0:T(8,128)}, f32[8,64,256]{2,1,0:T(8,128)}, f32[8,64,256]{2,1,0:T(8,128)}) custom-call(f32[16384,128]{1,0:T(8,128)} %bitcast.21, f32[256,128]{1,0:T(8,128)} %broadcast_in_dim.2.order_ref), custom_call_target="tpu_custom_call" | custom-call | flops 1073741824 | bytes 4194304 | tf_op jit(solution)/shard_map/pallas_call | solution.py:607
  17.3 4.1 %collective-permute-start = (f32[8,64,256]{2,1,0:T(8,128)}, f32[8,64,256]{2,1,0:T(8,128)S(1)}, u32[]{:S(2)}, u32[]{:S(2)}) collective-permute-start(f32[8,64,256]{2,1,0:T(8,128)} %get-tuple-element.39.f1), channel_id=1, source_target_pairs={{0,32},{8,40},{16,48},{24,56},{1,33},{9,41},{17,49},{25,57},{2,34}... | collective-permute-start | bytes 1572872 | tf_op jit(solution)/shard_map/ppermute | solution.py:584
  21.4 1.7 collective-permute-start.3
  23.1 3.3 %collective-permute-start.4 = (bf16[256,512]{1,0:T(8,128)(2,1)S(1)}, bf16[256,512]{1,0:T(8,128)(2,1)S(1)}, u32[]{:S(2)}, u32[]{:S(2)}) collective-permute-start(bf16[256,512]{1,0:T(8,128)(2,1)S(1)} %copy-done.11), channel_id=1, source_target_pairs={{0,16},{8,24},{16,0},{24,8},{32,48},{40,56},{48,32},{56,40},{64,80... | collective-permute-start | bytes 786440 | tf_op jit(solution)/shard_map/ppermute | solution.py:574
  26.4 0.7 collective-permute-start.5
  27.1 2.3 %collective-permute-start.1 = (f32[8,64,256]{2,1,0:T(8,128)}, f32[8,64,256]{2,1,0:T(8,128)S(1)}, u32[]{:S(2)}, u32[]{:S(2)}) collective-permute-start(f32[8,64,256]{2,1,0:T(8,128)} %get-tuple-element.40.f2), channel_id=1, source_target_pairs={{0,64},{8,72},{16,80},{24,88},{1,65},{9,73},{17,81},{25,89},{2,66}... | collective-permute-start | bytes 1572872 | tf_op jit(solution)/shard_map/ppermute | solution.py:584
  29.4 1.6 collective-permute-done.3.refs_1_
  31.0 2.3 %collective-permute-start.2 = (f32[8,64,256]{2,1,0:T(8,128)}, f32[8,64,256]{2,1,0:T(8,128)S(1)}, u32[]{:S(2)}, u32[]{:S(2)}) collective-permute-start(f32[8,64,256]{2,1,0:T(8,128)} %get-tuple-element.41.f3), channel_id=1, source_target_pairs={{0,96},{8,104},{16,112},{24,120},{1,97},{9,105},{17,113},{25,121},... | collective-permute-start | bytes 1572872 | tf_op jit(solution)/shard_map/ppermute | solution.py:584
  33.4 4.0 %collective-permute-done.4.refs_2_ = bf16[256,512]{1,0:T(8,128)(2,1)S(1)} collective-permute-done((bf16[256,512]{1,0:T(8,128)(2,1)S(1)}, bf16[256,512]{1,0:T(8,128)(2,1)S(1)}, u32[]{:S(2)}, u32[]{:S(2)}) %collective-permute-start.4) | collective-permute-done | bytes 262176 | tf_op jit(solution)/shard_map/ppermute | solution.py:574
  37.4 0.7 copy-done.14
  38.2 3.1 %shard_map.48 = (bf16[64,512]{1,0:T(8,128)(2,1)}, bf16[64,512]{1,0:T(8,128)(2,1)}, bf16[64,512]{1,0:T(8,128)(2,1)}, bf16[64,512]{1,0:T(8,128)(2,1)}, bf16[256,51...) custom-call(s32[2,16]{1,0:T(2,128)} %map_ref.7, ...), custom_call_target="tpu_custom_call" | custom-call | flops 21474836480 | bytes 2490504 | tf_op jit(solution)/shard_map/pallas_call | solution.py:33
  41.3 1.3 collective-permute-start.6
  42.6 1.7 collective-permute-start.7
  44.3 1.3 collective-permute-start.8
  45.7 1.6 collective-permute-start.10
  47.3 2.0 collective-permute-start.11
  49.9 2.7 %shard_map.49 = s16[272,256]{1,0:T(8,128)(2,1)} custom-call(s32[2]{0:T(128)} %pad_add_fusion.rc_ref, bf16[64,512]{1,0:T(8,128)(2,1)} %get-tuple-element.50.t0, bf16[64,512]{1,0:T(8,128)(2,1)} %copy-done.7, bf16[64,512]{1,0:T(8,128)(2,1)} %copy-done.8, bf16[64,512]{1,0:T(8,128)(2,1)} %copy-done.9, f32[8,64,256]{2,1,0:T(8,128)} %get-tuple-element.38.f0, ...), custom_call_target="tpu_custom_call" | custom-call | bytes 2498568 | tf_op jit(solution)/shard_map/pallas_call | solution.py:33
  52.6 20.3 %all-gather.12 = s16[2176,256]{1,0:T(8,128)(2,1)} all-gather(s16[272,256]{1,0:T(8,128)(2,1)} %shard_map.49), channel_id=2, replica_groups=mesh['prow'=16,'pcol'=8] {'pcol'}, dimensions={0}, use_global_device_ids=true | all-gather | bytes 1253376 | tf_op jit(solution)/shard_map/all_gather | solution.py:638
  73.9 2.3 %shard_map.50 = bf16[4,256,512]{2,1,0:T(8,128)(2,1)} custom-call(s32[2]{0:T(128)} %pad_add_fusion.rc_ref, bf16[256,512]{1,0:T(8,128)(2,1)} %get-tuple-element.54.h0, bf16[256,512]{1,0:T(8,128)(2,1)} %copy-done.4, bf16[256,512]{1,0:T(8,128)(2,1)} %copy-done.5, bf16[256,512]{1,0:T(8,128)(2,1)} %copy-done.6), custom_call_target="tpu_custom_call" | custom-call | bytes 2097160 | tf_op jit(solution)/shard_map/pallas_call | solution.py:33
  76.2 3.9 %shard_map.51 = s16[848,256]{1,0:T(8,128)(2,1)} custom-call(s32[2,16]{1,0:T(2,128)} %map_ref.7, s32[2]{0:T(128)} %pad_add_fusion.rc_ref, f32[8,64,256]{2,1,0:T(8,128)} %get-tuple-element.38.f0, f32[8,64,256]{2,1,0:T(8,128)} %copy-done.1, f32[8,64,256]{2,1,0:T(8,128)} %copy-done.2, f32[8,64,256]{2,1,0:T(8,128)} %copy-done.3, s16[8,272,256]{2,1,0:T(8,128)(2,1)} %bitcast.27), custom_call_target="tpu_custom_call" | custom-call | bytes 3645576 | tf_op jit(solution)/shard_map/pallas_call | solution.py:33
  80.1 45.0 %all-gather.13 = s16[13568,256]{1,0:T(8,128)(2,1)} all-gather(s16[848,256]{1,0:T(8,128)(2,1)} %shard_map.51), channel_id=3, replica_groups=mesh['prow'=16,'pcol'=8] {'prow'}, dimensions={0}, use_global_device_ids=true | all-gather | bytes 7380992 | tf_op jit(solution)/shard_map/all_gather | solution.py:649
  125.2 77.3 %shard_map.52 = f32[16384,128]{1,0:T(8,128)} custom-call(s32[2,16]{1,0:T(2,128)} %map_ref.7, s32[2]{0:T(128)} %pad_add_fusion.rc_ref, s16[16,848,256]{2,1,0:T(8,128)(2,1)} %bitcast.23, s16[16,848,256]{2,1,0:T(8,128)(2,1)} %bitcast.24, s16[16,848,256]{2,1,0:T(8,128)(2,1)} %bitcast.25, s16[16,848,256]{2,1,0:T(8,128)(2,1)} %bitcast.26, ...), custom_call_target="tpu_custom_call" | custom-call | flops 24696061952 | bytes 33554432 | tf_op jit(solution)/shard_map/pallas_call | solution.py:533
  (51 shorter events, 2.5 us)
Async XLA Ops:
  6.5 4.4 %copy-start = (s32[4,256]{1,0:T(4,128)S(1)}, s32[4,256]{1,0:T(4,128)}, u32[]{:S(2)}) copy-start(s32[4,256]{1,0:T(4,128)} %param.7) | copy-start | bytes 12292
  6.5 118.6 %all-gather.9.cloned.1.call-start = ((), (), s32[]{:S(2)}) async-start(), calls=%async_computation | async-start | bytes 9437184 | tf_op jit(solution)/shard_map/all_gather | solution.py:621
  10.8 10.5 %copy-start.12 = (bf16[256,512]{1,0:T(8,128)(2,1)S(1)}, bf16[256,512]{1,0:T(8,128)(2,1)}, u32[]{:S(2)}) copy-start(bf16[256,512]{1,0:T(8,128)(2,1)} %get-tuple-element.43) | copy-start | bytes 786436
  10.8 12.3 %copy-start.11 = (bf16[256,512]{1,0:T(8,128)(2,1)S(1)}, bf16[256,512]{1,0:T(8,128)(2,1)}, u32[]{:S(2)}) copy-start(bf16[256,512]{1,0:T(8,128)(2,1)} %get-tuple-element.44) | copy-start | bytes 786436
  10.9 15.5 %copy-start.10 = (bf16[256,512]{1,0:T(8,128)(2,1)S(1)}, bf16[256,512]{1,0:T(8,128)(2,1)}, u32[]{:S(2)}) copy-start(bf16[256,512]{1,0:T(8,128)(2,1)} %get-tuple-element.45) | copy-start | bytes 786436
  10.9 114.3 %all-gather.11.cloned.1.call-start = ((), (), s32[]{:S(2)}) async-start(), calls=%async_computation.1 | async-start | bytes 9437184 | tf_op jit(solution)/shard_map/all_gather | solution.py:648
  17.3 20.1 %collective-permute-start = (f32[8,64,256]{2,1,0:T(8,128)}, f32[8,64,256]{2,1,0:T(8,128)S(1)}, u32[]{:S(2)}, u32[]{:S(2)}) collective-permute-start(f32[8,64,256]{2,1,0:T(8,128)} %get-tuple-element.39.f1), channel_id=1, source_target_pairs={{0,32},{8,40},{16,48},{24,56},{1,33},{9,41},{17,49},{25,57},{2,34}... | collective-permute-start | bytes 1572872 | tf_op jit(solution)/shard_map/ppermute | solution.py:584
  21.4 9.6 %collective-permute-start.3 = (bf16[256,512]{1,0:T(8,128)(2,1)S(1)}, bf16[256,512]{1,0:T(8,128)(2,1)S(1)}, u32[]{:S(2)}, u32[]{:S(2)}) collective-permute-start(bf16[256,512]{1,0:T(8,128)(2,1)S(1)} %copy-done.12), channel_id=1, source_target_pairs={{0,8},{8,16},{16,24},{24,0},{32,40},{40,48},{48,56},{56,32},{64,72... | collective-permute-start | bytes 786440 | tf_op jit(solution)/shard_map/ppermute | solution.py:574
  23.1 14.3 %collective-permute-start.4 = (bf16[256,512]{1,0:T(8,128)(2,1)S(1)}, bf16[256,512]{1,0:T(8,128)(2,1)S(1)}, u32[]{:S(2)}, u32[]{:S(2)}) collective-permute-start(bf16[256,512]{1,0:T(8,128)(2,1)S(1)} %copy-done.11), channel_id=1, source_target_pairs={{0,16},{8,24},{16,0},{24,8},{32,48},{40,56},{48,32},{56,40},{64,80... | collective-permute-start | bytes 786440 | tf_op jit(solution)/shard_map/ppermute | solution.py:574
  26.4 11.0 %collective-permute-start.5 = (bf16[256,512]{1,0:T(8,128)(2,1)S(1)}, bf16[256,512]{1,0:T(8,128)(2,1)S(1)}, u32[]{:S(2)}, u32[]{:S(2)}) collective-permute-start(bf16[256,512]{1,0:T(8,128)(2,1)S(1)} %copy-done.10), channel_id=1, source_target_pairs={{0,24},{8,0},{16,8},{24,16},{32,56},{40,32},{48,40},{56,48},{64,88... | collective-permute-start | bytes 786440 | tf_op jit(solution)/shard_map/ppermute | solution.py:574
  27.1 18.4 %collective-permute-start.1 = (f32[8,64,256]{2,1,0:T(8,128)}, f32[8,64,256]{2,1,0:T(8,128)S(1)}, u32[]{:S(2)}, u32[]{:S(2)}) collective-permute-start(f32[8,64,256]{2,1,0:T(8,128)} %get-tuple-element.40.f2), channel_id=1, source_target_pairs={{0,64},{8,72},{16,80},{24,88},{1,65},{9,73},{17,81},{25,89},{2,66}... | collective-permute-start | bytes 1572872 | tf_op jit(solution)/shard_map/ppermute | solution.py:584
  31.0 6.4 %copy-start.13 = (bf16[256,512]{1,0:T(8,128)(2,1)}, bf16[256,512]{1,0:T(8,128)(2,1)S(1)}, u32[]{:S(2)}) copy-start(bf16[256,512]{1,0:T(8,128)(2,1)S(1)} %collective-permute-done.3.refs_1_) | copy-start | bytes 786436
  31.0 14.6 %collective-permute-start.2 = (f32[8,64,256]{2,1,0:T(8,128)}, f32[8,64,256]{2,1,0:T(8,128)S(1)}, u32[]{:S(2)}, u32[]{:S(2)}) collective-permute-start(f32[8,64,256]{2,1,0:T(8,128)} %get-tuple-element.41.f3), channel_id=1, source_target_pairs={{0,96},{8,104},{16,112},{24,120},{1,97},{9,105},{17,113},{25,121},... | collective-permute-start | bytes 1572872 | tf_op jit(solution)/shard_map/ppermute | solution.py:584
  38.2 3.1 %copy-start.1 = (f32[8,64,256]{2,1,0:T(8,128)}, f32[8,64,256]{2,1,0:T(8,128)S(1)}, u32[]{:S(2)}) copy-start(f32[8,64,256]{2,1,0:T(8,128)S(1)} %collective-permute-done.f1) | copy-start | bytes 1572868
  41.3 6.0 %collective-permute-start.6 = (bf16[64,512]{1,0:T(8,128)(2,1)}, bf16[64,512]{1,0:T(8,128)(2,1)S(1)}, u32[]{:S(2)}, u32[]{:S(2)}) collective-permute-start(bf16[64,512]{1,0:T(8,128)(2,1)} %get-tuple-element.51), channel_id=1, source_target_pairs={{0,32},{8,40},{16,48},{24,56},{1,33},{9,41},{17,49},{25,57},{2,34}... | collective-permute-start | bytes 196616 | tf_op jit(solution)/shard_map/ppermute | solution.py:584
  42.6 6.7 %collective-permute-start.7 = (bf16[64,512]{1,0:T(8,128)(2,1)}, bf16[64,512]{1,0:T(8,128)(2,1)S(1)}, u32[]{:S(2)}, u32[]{:S(2)}) collective-permute-start(bf16[64,512]{1,0:T(8,128)(2,1)} %get-tuple-element.52), channel_id=1, source_target_pairs={{0,64},{8,72},{16,80},{24,88},{1,65},{9,73},{17,81},{25,89},{2,66}... | collective-permute-start | bytes 196616 | tf_op jit(solution)/shard_map/ppermute | solution.py:584
  44.3 5.0 %collective-permute-start.8 = (bf16[64,512]{1,0:T(8,128)(2,1)}, bf16[64,512]{1,0:T(8,128)(2,1)S(1)}, u32[]{:S(2)}, u32[]{:S(2)}) collective-permute-start(bf16[64,512]{1,0:T(8,128)(2,1)} %get-tuple-element.53), channel_id=1, source_target_pairs={{0,96},{8,104},{16,112},{24,120},{1,97},{9,105},{17,113},{25,121},... | collective-permute-start | bytes 196616 | tf_op jit(solution)/shard_map/ppermute | solution.py:584
  45.6 3.7 %copy-start.2 = (f32[8,64,256]{2,1,0:T(8,128)}, f32[8,64,256]{2,1,0:T(8,128)S(1)}, u32[]{:S(2)}) copy-start(f32[8,64,256]{2,1,0:T(8,128)S(1)} %collective-permute-done.1.f2) | copy-start | bytes 1572868
  45.6 27.4 %collective-permute-start.9 = (bf16[256,512]{1,0:T(8,128)(2,1)}, bf16[256,512]{1,0:T(8,128)(2,1)S(1)}, u32[]{:S(2)}, u32[]{:S(2)}) collective-permute-start(bf16[256,512]{1,0:T(8,128)(2,1)} %get-tuple-element.55), channel_id=1, source_target_pairs={{0,32},{8,40},{16,48},{24,56},{32,64},{40,72},{48,80},{56,88},{64,... | collective-permute-start | bytes 786440 | tf_op jit(solution)/shard_map/ppermute | solution.py:579
  45.7 3.6 %copy-start.3 = (f32[8,64,256]{2,1,0:T(8,128)}, f32[8,64,256]{2,1,0:T(8,128)S(1)}, u32[]{:S(2)}) copy-start(f32[8,64,256]{2,1,0:T(8,128)S(1)} %collective-permute-done.2.f3) | copy-start | bytes 1572868
  45.7 27.3 %collective-permute-start.10 = (bf16[256,512]{1,0:T(8,128)(2,1)}, bf16[256,512]{1,0:T(8,128)(2,1)S(1)}, u32[]{:S(2)}, u32[]{:S(2)}) collective-permute-start(bf16[256,512]{1,0:T(8,128)(2,1)} %get-tuple-element.56), channel_id=1, source_target_pairs={{0,64},{8,72},{16,80},{24,88},{32,96},{40,104},{48,112},{56,120},{... | collective-permute-start | bytes 786440 | tf_op jit(solution)/shard_map/ppermute | solution.py:579
  47.3 2.0 copy-start.7
  47.3 25.7 %collective-permute-start.11 = (bf16[256,512]{1,0:T(8,128)(2,1)}, bf16[256,512]{1,0:T(8,128)(2,1)S(1)}, u32[]{:S(2)}, u32[]{:S(2)}) collective-permute-start(bf16[256,512]{1,0:T(8,128)(2,1)} %get-tuple-element.57), channel_id=1, source_target_pairs={{0,96},{8,104},{16,112},{24,120},{32,0},{40,8},{48,16},{56,24},{64... | collective-permute-start | bytes 786440 | tf_op jit(solution)/shard_map/ppermute | solution.py:579
  73.0 0.9 copy-start.6
  (6 other events, 4.3 us)
Sparse Core Ops, SparseCore 0:
  11.0 55.1 all-gather.8
  76.3 48.8 all-gather.10

commit v8 on v7

--- a/solution.py
+++ b/solution.py
@@ -72,14 +72,9 @@
 
 def dot3(left, right):
     (a, b), (c, d) = left, right
-    return dot(a, c) + (dot(a, d) + dot(b, c))
-
-
-CHUNK = 128
-
-
-def chunk(step):
-    return pl.ds(pl.multiple_of(step * CHUNK, CHUNK), CHUNK)
+    rows = a.shape[0]
+    both = dot(jnp.concatenate([a, b], axis=0), c)
+    return both[:rows] + (both[rows:] + dot(a, d))
 
 
 def block(step):
@@ -291,26 +286,16 @@
         approx = 2.0 * jnp.where(diagonal, across, 0.0) - (down * pivot) * across
         for sweep_index in range(NS - 1):
             pair = split(approx)
-            halves = []
-            for half in range(2):
-                rows = slice(half * CHUNK, half * CHUNK + CHUNK)
-                left = split(dot3((pair[0][rows], pair[1][rows]), parts))
-                halves.append(2.0 * approx[rows] - dot3(left, pair))
-            approx = jnp.concatenate(halves, axis=0)
+            approx = 2.0 * approx - dot3(split(dot3(pair, parts)), pair)
         xhi[k], xlo[k] = split(approx)
         chi[block(k)], clo[block(k)] = split(work[block(k)])
-
-        def below(step, carry, k=k):
-            rows = chunk(step)
-            pair = split(dot3(split(work[rows, block(k)]), (xhi[k], xlo[k])))
-            work[rows, block(k)] = pair[0].astype(F32) + pair[1].astype(F32)
-            for j in range(k + 1, NPIV):
-                work[rows, block(j)] = work[rows, block(j)] - dot3(
-                    pair, (chi[block(k), block(j)], clo[block(k), block(j)])
-                )
-            return carry
-
-        lax.fori_loop(2 * (k + 1), 2 * NPIV, below, 0)
+        if k + 1 < NPIV:
+            below = slice((k + 1) * BS, NPIV * BS)
+            pair = split(dot3(split(work[below, block(k)]), (xhi[k], xlo[k])))
+            work[below, block(k)] = pair[0].astype(F32) + pair[1].astype(F32)
+            work[below, below] = work[below, below] - dot3(
+                pair, (chi[block(k), below], clo[block(k), below])
+            )
 
 
 SPAN = 2
@@ -320,7 +305,7 @@
 def finish(
     map_ref, rc_ref, corner_ref, rest_ref, level_ref, code_ref, left_ref, near_ref, order_ref,
     front_ref, f0, f1, f2, f3, child_ref, out_ref,
-    work, chi, clo, xhi, xlo, uhi, ulo, lhi, llo, own_col, own_block, own_row, parts,
+    work, chi, clo, xhi, xlo, uhi, ulo, lower, own_col, own_block, own_row, parts,
     arrived, own_arrived,
 ):
     step, group = pl.program_id(0), pl.program_id(1)
@@ -388,40 +373,35 @@
     def _():
         for k in range(NPIV):
             for piece in range(4):
+                low = k * BS + piece * PIECE
                 scale = level_ref[4 * piece + k].astype(I32)
                 for q in range(WIDE):
-                    work[piece * PIECE : piece * PIECE + PIECE, block(q)] = decode(
+                    work[low : low + PIECE, block(q)] = decode(
                         code_ref[4 * piece + k, q * PIECE : q * PIECE + PIECE].astype(I32), scale
                     )
-
-            def upper(half, carry, k=k):
-                rows = chunk(half)
-                put_rows = chunk(2 * k + half)
-                for q in range(WIDE):
-                    value = work[rows, block(q)]
-                    if k:
-                        done = slice(0, k * BS)
-                        taken = dot3(
-                            (chi[put_rows, done], clo[put_rows, done]),
-                            (uhi[group, done, block(q)], ulo[group, done, block(q)]),
-                        )
-                        value = value - taken
-
-                        @pl.when(row == k)
-                        def _(taken=taken, q=q):
-                            tile = WIDE * group + q
-                            for part in range(2):
-                                low = part * PIECE
-                                own_row[2 * half + part, tile] = (
-                                    own_row[2 * half + part, tile] - taken[low : low + PIECE]
+        for k in range(NPIV):
+            uhi[group, block(k)], ulo[group, block(k)] = split(work[block(k)])
+            if k + 1 == NPIV:
+                break
+            below = slice((k + 1) * BS, NPIV * BS)
+            for pair in range(WIDE // 2):
+                wide = slice(2 * pair * BS, 2 * (pair + 1) * BS)
+                taken = dot3(
+                    (chi[below, block(k)], clo[below, block(k)]),
+                    (uhi[group, block(k), wide], ulo[group, block(k), wide]),
+                )
+                work[below, wide] = work[below, wide] - taken
+                for j in range(k + 1, NPIV):
+
+                    @pl.when(row == j)
+                    def _(taken=taken, pair=pair, j=j, k=k):
+                        for piece in range(4):
+                            low = (j - k - 1) * BS + piece * PIECE
+                            for q in range(2):
+                                tile = WIDE * group + 2 * pair + q
+                                own_row[piece, tile] = (
+                                    own_row[piece, tile] - taken[low : low + PIECE, block(q)]
                                 )
-
-                    high, low = split(value)
-                    uhi[group, put_rows, block(q)] = high
-                    ulo[group, put_rows, block(q)] = low
-                return carry
-
-            lax.fori_loop(0, 2, upper, 0)
 
     @pl.when(group == 0)
     def _():
@@ -448,40 +428,32 @@
         def _():
             left[:BS] = jnp.zeros((BS, NPIV * BS), F32)
 
-        def lower(step, carry):
-            lines = [chunk(2 * step + half) for half in range(2)]
-            for k in range(NPIV):
-                for rows in lines:
-                    value = dot3(split(left[rows, block(k)]), (xhi[k], xlo[k]))
-                    pair = split(value)
-                    lhi[rows, block(k)], llo[rows, block(k)] = pair
-
-                    @pl.when(col == k)
-                    def _(value=value, rows=rows):
-                        own_col[rows, :] = value
-
-                    for j in range(k + 1, NPIV):
-                        left[rows, block(j)] = left[rows, block(j)] - dot3(
-                            pair, (chi[block(k), block(j)], clo[block(k), block(j)])
-                        )
-            return carry
-
-        lax.fori_loop(0, SPAN * BS // (2 * CHUNK), lower, 0)
-
-    def update(step, carry):
-        rows = chunk(step)
-        for q in range(WIDE):
-            upper = (uhi[group, :, block(q)], ulo[group, :, block(q)])
-            total = dot3((lhi[rows, :], llo[rows, :]), upper)
+        for k in range(NPIV):
+            value = dot3(split(left[:, block(k)]), (xhi[k], xlo[k]))
+            lower[: SPAN * BS, block(k)], lower[SPAN * BS :, block(k)] = split(value)
+
+            @pl.when(col == k)
+            def _(value=value):
+                own_col[...] = value
+
+            if k + 1 < NPIV:
+                rest = slice((k + 1) * BS, NPIV * BS)
+                both = dot(lower[:, block(k)], chi[block(k), rest])
+                both = both[: SPAN * BS] + both[SPAN * BS :]
+                both = both + dot(lower[: SPAN * BS, block(k)], clo[block(k), rest])
+                left[:, rest] = left[:, rest] - both
+
+    for pair in range(WIDE // 2):
+        wide = slice(2 * pair * BS, 2 * (pair + 1) * BS)
+        both = dot(lower[...], uhi[group, :, wide])
+        total = both[: SPAN * BS] + (
+            both[SPAN * BS :] + dot(lower[: SPAN * BS], ulo[group, :, wide])
+        )
+        for q in range(2):
             for half in range(2):
-                first = step * (CHUNK * 16) + half * 8 + WIDE * group + q
-                lines = pl.ds(first, CHUNK, stride=16)
-                out_ref[lines, :] = (
-                    front_ref[lines, :] - total[:, half * HALF : half * HALF + HALF]
-                )
-        return carry
-
-    lax.fori_loop(0, SPAN * BS // CHUNK, update, 0)
+                rows = at(WIDE * group + 2 * pair + q, half, 0, SPAN)
+                low = q * BS + half * HALF
+                out_ref[rows, :] = front_ref[rows, :] - total[:, low : low + HALF]
 
     @pl.when(group == 1)
     def _():
@@ -551,7 +523,7 @@
             pltpu.VMEM((4 * BS, 4 * BS), BF16), pltpu.VMEM((4 * BS, 4 * BS), BF16),
             pltpu.VMEM((NPIV, BS, BS), BF16), pltpu.VMEM((NPIV, BS, BS), BF16),
             pltpu.VMEM((2, 4 * BS, WIDE * BS), BF16), pltpu.VMEM((2, 4 * BS, WIDE * BS), BF16),
-            pltpu.VMEM((SPAN * BS, 4 * BS), BF16), pltpu.VMEM((SPAN * BS, 4 * BS), BF16),
+            pltpu.VMEM((2 * SPAN * BS, 4 * BS), BF16),
             pltpu.VMEM((SPAN * BS, BS), F32), pltpu.VMEM((BS, BS), F32),
             pltpu.VMEM((4, 8, PIECE, BS), F32),
             pltpu.VMEM((16, BS, BS), BF16),

time: 211 us -> 186 us (0.88)
  Pallas kernels: 98.5 us -> 74.3 us
    pallas_call x1, Pallas kernels: 77.3 us -> 53.1 us  [run_finish(): pl.pallas_call(finish, grid=(4 // SPAN, 2), out_shape=shape(view.shape, F...]
  transfers between devices with their start and end apart: 14 -> 14, of which waited for: 2 -> 2; matrix products, arithmetic and copies ran while one was open for 0% -> 0% of each run, Pallas kernels for 8% -> 9%
where the time goes in v8:
time: 186 us; the launch traced here: 185 us
  Pallas kernels  74.3 us (40%)
  blocking collectives  65.3 us (35%)
  starting transfers between devices  22.4 us (12%)
  between operations  13.7 us (7%)
  waiting for transfers between devices  5.69 us (3%)
  local copies, waits for them, and re-layouts  3.06 us (2%)
    pallas_call x1, Pallas kernels, run_finish(): pl.pallas_call(finish, grid=(4 // SPAN, 2), out_shape=shape(view.shape, F...  53.1 us
    all_gather x1, blocking collectives, shards(): top = lax.all_gather(code, 'prow', axis=0, tiled=False)  45 us
    all_gather x1, blocking collectives, shards(): thin = lax.all_gather(thin, 'pcol', axis=0, tiled=False)  20.3 us
    ppermute x6, starting transfers between devices, from_plane(): return lax.ppermute(a, 'prow', [(j, 4 * hop + j) for j in range(4)])  13 us
    pallas_call x4, Pallas kernels, call(): pl.pallas_call(body, out_shape=outs, in_specs=[SMEM] * smem + [VMEM] * (l...  12 us
    ppermute x3, starting transfers between devices, along_z(): lax.ppermute(a, 'prow', [(4 * i + j, 4 * i + (j + hop) % 4) for i in rang...  5.74 us
    ppermute x3, waiting for transfers between devices, along_z(): lax.ppermute(a, 'prow', [(4 * i + j, 4 * i + (j + hop) % 4) for i in rang...  5.61 us
    pallas_call x1, Pallas kernels, shards(): pl.pallas_call(cut_front, grid=(1,), out_shape=[shape((8, PIECE, BS), F32...  5.59 us
  transfers between devices with their start and end apart: 14, of which 2 were waited for; matrix products, arithmetic and copies ran while one was open for 0% of the time, Pallas kernels for 9%

profile of v8, /device:TPU:1, one launch (start us, length us, event | category | flops | bytes accessed | tf_op | source)
XLA Modules:
  0.0 185.1 jit_solution(1242256877837699319)
XLA Ops:
  7.2 3.6 %shard_map.46 = (bf16[256,512]{1,0:T(8,128)(2,1)}, bf16[256,512]{1,0:T(8,128)(2,1)}, bf16[256,512]{1,0:T(8,128)(2,1)}, bf16[256,512]{1,0:T(8,128)(2,1)}, f32[1024,256]{1,0:T(8,128)}) custom-call(s32[2,16]{1,0:T(2,128)} %map_ref.7, s32[2]{0:T(128)} %pad_add_fusion.rc_ref, bf16[2,256,512]{2,1,0:T(8,128)(2,1)} %bitcast.28, f32[1024,2,8,128]{3,2,1,0:T(8,128)} %bitcast.20), custom_call_target="tpu_custom_call" | custom-call | bytes 4194304 | tf_op jit(solution)/shard_map/pallas_call | solution.py:563
  11.0 0.8 broadcast_in_dim.2.order_ref
  11.7 5.6 %shard_map.47 = (f32[8,64,256]{2,1,0:T(8,128)}, f32[8,64,256]{2,1,0:T(8,128)}, f32[8,64,256]{2,1,0:T(8,128)}, f32[8,64,256]{2,1,0:T(8,128)}) custom-call(f32[16384,128]{1,0:T(8,128)} %bitcast.21, f32[256,128]{1,0:T(8,128)} %broadcast_in_dim.2.order_ref), custom_call_target="tpu_custom_call" | custom-call | flops 1073741824 | bytes 4194304 | tf_op jit(solution)/shard_map/pallas_call | solution.py:579
  17.3 4.1 %collective-permute-start = (f32[8,64,256]{2,1,0:T(8,128)}, f32[8,64,256]{2,1,0:T(8,128)S(1)}, u32[]{:S(2)}, u32[]{:S(2)}) collective-permute-start(f32[8,64,256]{2,1,0:T(8,128)} %get-tuple-element.39.f1), channel_id=1, source_target_pairs={{0,32},{8,40},{16,48},{24,56},{1,33},{9,41},{17,49},{25,57},{2,34}... | collective-permute-start | bytes 1572872 | tf_op jit(solution)/shard_map/ppermute | solution.py:556
  21.4 1.7 collective-permute-start.3
  23.1 3.3 %collective-permute-start.4 = (bf16[256,512]{1,0:T(8,128)(2,1)S(1)}, bf16[256,512]{1,0:T(8,128)(2,1)S(1)}, u32[]{:S(2)}, u32[]{:S(2)}) collective-permute-start(bf16[256,512]{1,0:T(8,128)(2,1)S(1)} %copy-done.11), channel_id=1, source_target_pairs={{0,16},{8,24},{16,0},{24,8},{32,48},{40,56},{48,32},{56,40},{64,80... | collective-permute-start | bytes 786440 | tf_op jit(solution)/shard_map/ppermute | solution.py:546
  26.4 0.7 collective-permute-start.5
  27.1 2.3 %collective-permute-start.1 = (f32[8,64,256]{2,1,0:T(8,128)}, f32[8,64,256]{2,1,0:T(8,128)S(1)}, u32[]{:S(2)}, u32[]{:S(2)}) collective-permute-start(f32[8,64,256]{2,1,0:T(8,128)} %get-tuple-element.40.f2), channel_id=1, source_target_pairs={{0,64},{8,72},{16,80},{24,88},{1,65},{9,73},{17,81},{25,89},{2,66}... | collective-permute-start | bytes 1572872 | tf_op jit(solution)/shard_map/ppermute | solution.py:556
  29.4 1.6 collective-permute-done.3.refs_1_
  31.0 2.3 %collective-permute-start.2 = (f32[8,64,256]{2,1,0:T(8,128)}, f32[8,64,256]{2,1,0:T(8,128)S(1)}, u32[]{:S(2)}, u32[]{:S(2)}) collective-permute-start(f32[8,64,256]{2,1,0:T(8,128)} %get-tuple-element.41.f3), channel_id=1, source_target_pairs={{0,96},{8,104},{16,112},{24,120},{1,97},{9,105},{17,113},{25,121},... | collective-permute-start | bytes 1572872 | tf_op jit(solution)/shard_map/ppermute | solution.py:556
  33.4 4.0 %collective-permute-done.4.refs_2_ = bf16[256,512]{1,0:T(8,128)(2,1)S(1)} collective-permute-done((bf16[256,512]{1,0:T(8,128)(2,1)S(1)}, bf16[256,512]{1,0:T(8,128)(2,1)S(1)}, u32[]{:S(2)}, u32[]{:S(2)}) %collective-permute-start.4) | collective-permute-done | bytes 262176 | tf_op jit(solution)/shard_map/ppermute | solution.py:546
  37.4 0.7 copy-done.14
  38.2 3.1 %shard_map.48 = (bf16[64,512]{1,0:T(8,128)(2,1)}, bf16[64,512]{1,0:T(8,128)(2,1)}, bf16[64,512]{1,0:T(8,128)(2,1)}, bf16[64,512]{1,0:T(8,128)(2,1)}, bf16[256,51...) custom-call(s32[2,16]{1,0:T(2,128)} %map_ref.7, ...), custom_call_target="tpu_custom_call" | custom-call | flops 21474836480 | bytes 2490504 | tf_op jit(solution)/shard_map/pallas_call | solution.py:33
  41.3 1.3 collective-permute-start.6
  42.6 1.7 collective-permute-start.7
  44.3 1.3 collective-permute-start.8
  45.7 1.6 collective-permute-start.10
  47.3 2.0 %collective-permute-start.11 = (bf16[256,512]{1,0:T(8,128)(2,1)}, bf16[256,512]{1,0:T(8,128)(2,1)S(1)}, u32[]{:S(2)}, u32[]{:S(2)}) collective-permute-start(bf16[256,512]{1,0:T(8,128)(2,1)} %get-tuple-element.57), channel_id=1, source_target_pairs={{0,96},{8,104},{16,112},{24,120},{32,0},{40,8},{48,16},{56,24},{64... | collective-permute-start | bytes 786440 | tf_op jit(solution)/shard_map/ppermute | solution.py:551
  49.9 2.7 %shard_map.49 = s16[272,256]{1,0:T(8,128)(2,1)} custom-call(s32[2]{0:T(128)} %pad_add_fusion.rc_ref, bf16[64,512]{1,0:T(8,128)(2,1)} %get-tuple-element.50.t0, bf16[64,512]{1,0:T(8,128)(2,1)} %copy-done.7, bf16[64,512]{1,0:T(8,128)(2,1)} %copy-done.8, bf16[64,512]{1,0:T(8,128)(2,1)} %copy-done.9, f32[8,64,256]{2,1,0:T(8,128)} %get-tuple-element.38.f0, ...), custom_call_target="tpu_custom_call" | custom-call | bytes 2498568 | tf_op jit(solution)/shard_map/pallas_call | solution.py:33
  52.6 20.3 %all-gather.12 = s16[2176,256]{1,0:T(8,128)(2,1)} all-gather(s16[272,256]{1,0:T(8,128)(2,1)} %shard_map.49), channel_id=2, replica_groups=mesh['prow'=16,'pcol'=8] {'pcol'}, dimensions={0}, use_global_device_ids=true | all-gather | bytes 1253376 | tf_op jit(solution)/shard_map/all_gather | solution.py:610
  73.9 2.3 %shard_map.50 = bf16[4,256,512]{2,1,0:T(8,128)(2,1)} custom-call(s32[2]{0:T(128)} %pad_add_fusion.rc_ref, bf16[256,512]{1,0:T(8,128)(2,1)} %get-tuple-element.54.h0, bf16[256,512]{1,0:T(8,128)(2,1)} %copy-done.4, bf16[256,512]{1,0:T(8,128)(2,1)} %copy-done.5, bf16[256,512]{1,0:T(8,128)(2,1)} %copy-done.6), custom_call_target="tpu_custom_call" | custom-call | bytes 2097160 | tf_op jit(solution)/shard_map/pallas_call | solution.py:33
  76.2 3.9 %shard_map.51 = s16[848,256]{1,0:T(8,128)(2,1)} custom-call(s32[2,16]{1,0:T(2,128)} %map_ref.7, s32[2]{0:T(128)} %pad_add_fusion.rc_ref, f32[8,64,256]{2,1,0:T(8,128)} %get-tuple-element.38.f0, f32[8,64,256]{2,1,0:T(8,128)} %copy-done.1, f32[8,64,256]{2,1,0:T(8,128)} %copy-done.2, f32[8,64,256]{2,1,0:T(8,128)} %copy-done.3, s16[8,272,256]{2,1,0:T(8,128)(2,1)} %bitcast.27), custom_call_target="tpu_custom_call" | custom-call | bytes 3645576 | tf_op jit(solution)/shard_map/pallas_call | solution.py:33
  80.1 45.0 %all-gather.13 = s16[13568,256]{1,0:T(8,128)(2,1)} all-gather(s16[848,256]{1,0:T(8,128)(2,1)} %shard_map.51), channel_id=3, replica_groups=mesh['prow'=16,'pcol'=8] {'prow'}, dimensions={0}, use_global_device_ids=true | all-gather | bytes 7380992 | tf_op jit(solution)/shard_map/all_gather | solution.py:621
  125.1 53.1 %shard_map.52 = f32[16384,128]{1,0:T(8,128)} custom-call(s32[2,16]{1,0:T(2,128)} %map_ref.7, s32[2]{0:T(128)} %pad_add_fusion.rc_ref, s16[16,848,256]{2,1,0:T(8,128)(2,1)} %bitcast.23, s16[16,848,256]{2,1,0:T(8,128)(2,1)} %bitcast.24, s16[16,848,256]{2,1,0:T(8,128)(2,1)} %bitcast.25, s16[16,848,256]{2,1,0:T(8,128)(2,1)} %bitcast.26, ...), custom_call_target="tpu_custom_call" | custom-call | flops 24696061952 | bytes 33554432 | tf_op jit(solution)/shard_map/pallas_call | solution.py:505
  (51 shorter events, 2.5 us)
Async XLA Ops:
  6.5 4.4 %copy-start = (s32[4,256]{1,0:T(4,128)S(1)}, s32[4,256]{1,0:T(4,128)}, u32[]{:S(2)}) copy-start(s32[4,256]{1,0:T(4,128)} %param.7) | copy-start | bytes 12292
  6.5 118.5 %all-gather.9.cloned.1.call-start = ((), (), s32[]{:S(2)}) async-start(), calls=%async_computation | async-start | bytes 9437184 | tf_op jit(solution)/shard_map/all_gather | solution.py:593
  10.8 10.5 %copy-start.12 = (bf16[256,512]{1,0:T(8,128)(2,1)S(1)}, bf16[256,512]{1,0:T(8,128)(2,1)}, u32[]{:S(2)}) copy-start(bf16[256,512]{1,0:T(8,128)(2,1)} %get-tuple-element.43) | copy-start | bytes 786436
  10.8 12.3 %copy-start.11 = (bf16[256,512]{1,0:T(8,128)(2,1)S(1)}, bf16[256,512]{1,0:T(8,128)(2,1)}, u32[]{:S(2)}) copy-start(bf16[256,512]{1,0:T(8,128)(2,1)} %get-tuple-element.44) | copy-start | bytes 786436
  10.9 15.5 %copy-start.10 = (bf16[256,512]{1,0:T(8,128)(2,1)S(1)}, bf16[256,512]{1,0:T(8,128)(2,1)}, u32[]{:S(2)}) copy-start(bf16[256,512]{1,0:T(8,128)(2,1)} %get-tuple-element.45) | copy-start | bytes 786436
  10.9 114.2 %all-gather.11.cloned.1.call-start = ((), (), s32[]{:S(2)}) async-start(), calls=%async_computation.1 | async-start | bytes 9437184 | tf_op jit(solution)/shard_map/all_gather | solution.py:620
  17.3 20.1 %collective-permute-start = (f32[8,64,256]{2,1,0:T(8,128)}, f32[8,64,256]{2,1,0:T(8,128)S(1)}, u32[]{:S(2)}, u32[]{:S(2)}) collective-permute-start(f32[8,64,256]{2,1,0:T(8,128)} %get-tuple-element.39.f1), channel_id=1, source_target_pairs={{0,32},{8,40},{16,48},{24,56},{1,33},{9,41},{17,49},{25,57},{2,34}... | collective-permute-start | bytes 1572872 | tf_op jit(solution)/shard_map/ppermute | solution.py:556
  21.4 9.6 %collective-permute-start.3 = (bf16[256,512]{1,0:T(8,128)(2,1)S(1)}, bf16[256,512]{1,0:T(8,128)(2,1)S(1)}, u32[]{:S(2)}, u32[]{:S(2)}) collective-permute-start(bf16[256,512]{1,0:T(8,128)(2,1)S(1)} %copy-done.12), channel_id=1, source_target_pairs={{0,8},{8,16},{16,24},{24,0},{32,40},{40,48},{48,56},{56,32},{64,72... | collective-permute-start | bytes 786440 | tf_op jit(solution)/shard_map/ppermute | solution.py:546
  23.1 14.3 %collective-permute-start.4 = (bf16[256,512]{1,0:T(8,128)(2,1)S(1)}, bf16[256,512]{1,0:T(8,128)(2,1)S(1)}, u32[]{:S(2)}, u32[]{:S(2)}) collective-permute-start(bf16[256,512]{1,0:T(8,128)(2,1)S(1)} %copy-done.11), channel_id=1, source_target_pairs={{0,16},{8,24},{16,0},{24,8},{32,48},{40,56},{48,32},{56,40},{64,80... | collective-permute-start | bytes 786440 | tf_op jit(solution)/shard_map/ppermute | solution.py:546
  26.4 11.0 %collective-permute-start.5 = (bf16[256,512]{1,0:T(8,128)(2,1)S(1)}, bf16[256,512]{1,0:T(8,128)(2,1)S(1)}, u32[]{:S(2)}, u32[]{:S(2)}) collective-permute-start(bf16[256,512]{1,0:T(8,128)(2,1)S(1)} %copy-done.10), channel_id=1, source_target_pairs={{0,24},{8,0},{16,8},{24,16},{32,56},{40,32},{48,40},{56,48},{64,88... | collective-permute-start | bytes 786440 | tf_op jit(solution)/shard_map/ppermute | solution.py:546
  27.1 18.5 %collective-permute-start.1 = (f32[8,64,256]{2,1,0:T(8,128)}, f32[8,64,256]{2,1,0:T(8,128)S(1)}, u32[]{:S(2)}, u32[]{:S(2)}) collective-permute-start(f32[8,64,256]{2,1,0:T(8,128)} %get-tuple-element.40.f2), channel_id=1, source_target_pairs={{0,64},{8,72},{16,80},{24,88},{1,65},{9,73},{17,81},{25,89},{2,66}... | collective-permute-start | bytes 1572872 | tf_op jit(solution)/shard_map/ppermute | solution.py:556
  31.0 6.4 %copy-start.13 = (bf16[256,512]{1,0:T(8,128)(2,1)}, bf16[256,512]{1,0:T(8,128)(2,1)S(1)}, u32[]{:S(2)}) copy-start(bf16[256,512]{1,0:T(8,128)(2,1)S(1)} %collective-permute-done.3.refs_1_) | copy-start | bytes 786436
  31.0 14.7 %collective-permute-start.2 = (f32[8,64,256]{2,1,0:T(8,128)}, f32[8,64,256]{2,1,0:T(8,128)S(1)}, u32[]{:S(2)}, u32[]{:S(2)}) collective-permute-start(f32[8,64,256]{2,1,0:T(8,128)} %get-tuple-element.41.f3), channel_id=1, source_target_pairs={{0,96},{8,104},{16,112},{24,120},{1,97},{9,105},{17,113},{25,121},... | collective-permute-start | bytes 1572872 | tf_op jit(solution)/shard_map/ppermute | solution.py:556
  38.2 3.1 %copy-start.1 = (f32[8,64,256]{2,1,0:T(8,128)}, f32[8,64,256]{2,1,0:T(8,128)S(1)}, u32[]{:S(2)}) copy-start(f32[8,64,256]{2,1,0:T(8,128)S(1)} %collective-permute-done.f1) | copy-start | bytes 1572868
  41.3 6.0 %collective-permute-start.6 = (bf16[64,512]{1,0:T(8,128)(2,1)}, bf16[64,512]{1,0:T(8,128)(2,1)S(1)}, u32[]{:S(2)}, u32[]{:S(2)}) collective-permute-start(bf16[64,512]{1,0:T(8,128)(2,1)} %get-tuple-element.51), channel_id=1, source_target_pairs={{0,32},{8,40},{16,48},{24,56},{1,33},{9,41},{17,49},{25,57},{2,34}... | collective-permute-start | bytes 196616 | tf_op jit(solution)/shard_map/ppermute | solution.py:556
  42.6 6.7 %collective-permute-start.7 = (bf16[64,512]{1,0:T(8,128)(2,1)}, bf16[64,512]{1,0:T(8,128)(2,1)S(1)}, u32[]{:S(2)}, u32[]{:S(2)}) collective-permute-start(bf16[64,512]{1,0:T(8,128)(2,1)} %get-tuple-element.52), channel_id=1, source_target_pairs={{0,64},{8,72},{16,80},{24,88},{1,65},{9,73},{17,81},{25,89},{2,66}... | collective-permute-start | bytes 196616 | tf_op jit(solution)/shard_map/ppermute | solution.py:556
  44.3 5.0 %collective-permute-start.8 = (bf16[64,512]{1,0:T(8,128)(2,1)}, bf16[64,512]{1,0:T(8,128)(2,1)S(1)}, u32[]{:S(2)}, u32[]{:S(2)}) collective-permute-start(bf16[64,512]{1,0:T(8,128)(2,1)} %get-tuple-element.53), channel_id=1, source_target_pairs={{0,96},{8,104},{16,112},{24,120},{1,97},{9,105},{17,113},{25,121},... | collective-permute-start | bytes 196616 | tf_op jit(solution)/shard_map/ppermute | solution.py:556
  45.6 3.7 %copy-start.2 = (f32[8,64,256]{2,1,0:T(8,128)}, f32[8,64,256]{2,1,0:T(8,128)S(1)}, u32[]{:S(2)}) copy-start(f32[8,64,256]{2,1,0:T(8,128)S(1)} %collective-permute-done.1.f2) | copy-start | bytes 1572868
  45.6 27.4 %collective-permute-start.9 = (bf16[256,512]{1,0:T(8,128)(2,1)}, bf16[256,512]{1,0:T(8,128)(2,1)S(1)}, u32[]{:S(2)}, u32[]{:S(2)}) collective-permute-start(bf16[256,512]{1,0:T(8,128)(2,1)} %get-tuple-element.55), channel_id=1, source_target_pairs={{0,32},{8,40},{16,48},{24,56},{32,64},{40,72},{48,80},{56,88},{64,... | collective-permute-start | bytes 786440 | tf_op jit(solution)/shard_map/ppermute | solution.py:551
  45.7 3.6 %copy-start.3 = (f32[8,64,256]{2,1,0:T(8,128)}, f32[8,64,256]{2,1,0:T(8,128)S(1)}, u32[]{:S(2)}) copy-start(f32[8,64,256]{2,1,0:T(8,128)S(1)} %collective-permute-done.2.f3) | copy-start | bytes 1572868
  45.7 27.3 %collective-permute-start.10 = (bf16[256,512]{1,0:T(8,128)(2,1)}, bf16[256,512]{1,0:T(8,128)(2,1)S(1)}, u32[]{:S(2)}, u32[]{:S(2)}) collective-permute-start(bf16[256,512]{1,0:T(8,128)(2,1)} %get-tuple-element.56), channel_id=1, source_target_pairs={{0,64},{8,72},{16,80},{24,88},{32,96},{40,104},{48,112},{56,120},{... | collective-permute-start | bytes 786440 | tf_op jit(solution)/shard_map/ppermute | solution.py:551
  47.3 2.0 %copy-start.7 = (bf16[64,512]{1,0:T(8,128)(2,1)}, bf16[64,512]{1,0:T(8,128)(2,1)S(1)}, u32[]{:S(2)}) copy-start(bf16[64,512]{1,0:T(8,128)(2,1)S(1)} %collective-permute-done.6.t1) | copy-start | bytes 196612
  47.3 25.7 %collective-permute-start.11 = (bf16[256,512]{1,0:T(8,128)(2,1)}, bf16[256,512]{1,0:T(8,128)(2,1)S(1)}, u32[]{:S(2)}, u32[]{:S(2)}) collective-permute-start(bf16[256,512]{1,0:T(8,128)(2,1)} %get-tuple-element.57), channel_id=1, source_target_pairs={{0,96},{8,104},{16,112},{24,120},{32,0},{40,8},{48,16},{56,24},{64... | collective-permute-start | bytes 786440 | tf_op jit(solution)/shard_map/ppermute | solution.py:551
  73.0 0.9 copy-start.6
  (6 other events, 4.3 us)
Sparse Core Ops, SparseCore 0:
  11.0 55.1 all-gather.8
  76.3 48.4 all-gather.10

commit v9 on v8

--- a/solution.py
+++ b/solution.py
@@ -273,10 +273,10 @@
                     value = value + decode(rest_ref[4 * y + z].astype(I32), scale[3:4])
                 else:
                     value = decode(code, scale[1:2])
-                work[low : low + PIECE, block(k)] = value
+                work[k, low : low + PIECE] = value
     diagonal = lax.broadcasted_iota(I32, (BS, BS), 0) == lax.broadcasted_iota(I32, (BS, BS), 1)
     for k in range(NPIV):
-        pivot = work[block(k), block(k)]
+        pivot = work[k, block(k)]
         parts = split(pivot)
         on_line = jnp.where(diagonal, pivot, 0.0)
         across = jnp.sum(on_line, axis=0, keepdims=True)
@@ -288,14 +288,15 @@
             pair = split(approx)
             approx = 2.0 * approx - dot3(split(dot3(pair, parts)), pair)
         xhi[k], xlo[k] = split(approx)
-        chi[block(k)], clo[block(k)] = split(work[block(k)])
+        for j in range(NPIV):
+            chi[block(k), block(j)], clo[block(k), block(j)] = split(work[j, block(k)])
         if k + 1 < NPIV:
             below = slice((k + 1) * BS, NPIV * BS)
-            pair = split(dot3(split(work[below, block(k)]), (xhi[k], xlo[k])))
-            work[below, block(k)] = pair[0].astype(F32) + pair[1].astype(F32)
-            work[below, below] = work[below, below] - dot3(
-                pair, (chi[block(k), below], clo[block(k), below])
-            )
+            pair = split(dot3(split(work[k, below]), (xhi[k], xlo[k])))
+            work[k, below] = pair[0].astype(F32) + pair[1].astype(F32)
+            taken = dot3(pair, (chi[block(k), below], clo[block(k), below]))
+            for j in range(k + 1, NPIV):
+                work[j, below] = work[j, below] - taken[:, block(j - k - 1)]
 
 
 SPAN = 2
@@ -308,17 +309,13 @@
     work, chi, clo, xhi, xlo, uhi, ulo, lower, own_col, own_block, own_row, parts,
     arrived, own_arrived,
 ):
-    step, group = pl.program_id(0), pl.program_id(1)
+    step = pl.program_id(0)
     row, col = rc_ref[0], rc_ref[1]
     top_row = row < NPIV
-    high_rows = slice(SPAN * BS, 2 * SPAN * BS)
-
-    def at(s, half, tile=0, count=1):
-        return pl.ds(tile * BS * 16 + half * 8 + s, count * BS, stride=16)
-
-    def put(s, tile, value):
-        for half in range(2):
-            out_ref[at(s, half, tile), :] = value[:, half * HALF : half * HALF + HALF]
+    height = SPAN * BS
+
+    def lost(s, first, count):
+        return work.at[s // 2, pl.ds((s % 2) * height + first, count)]
 
     def each_child(act):
         for slot in range(4):
@@ -345,11 +342,9 @@
             for piece, source in enumerate((f0, f1, f2, f3))
         ]
 
-    @pl.when(group == 0)
-    def _():
-        each_child(lambda copy, index, tile, s: copy.start())
-
-    @pl.when((step == 0) & (group == 0))
+    each_child(lambda copy, index, tile, s: copy.start())
+
+    @pl.when(step == 0)
     def _():
         @pl.when(top_row)
         def _():
@@ -362,164 +357,173 @@
 
                 @pl.when((row == r) & (col == c))
                 def _(r=r, c=c):
-                    own_block[...] = work[block(r), block(c)]
+                    own_block[...] = work[c, block(r)]
 
         @pl.when(top_row)
         def _():
             for copy in own_copies():
                 copy.wait()
 
-    @pl.when(step == 0)
+        for group in range(2):
+            for k in range(NPIV):
+                for piece in range(4):
+                    low = k * BS + piece * PIECE
+                    scale = level_ref[4 * piece + k].astype(I32)
+                    for q in range(WIDE):
+                        first = (WIDE * group + q) * PIECE
+                        work[q, low : low + PIECE] = decode(
+                            code_ref[4 * piece + k, first : first + PIECE].astype(I32), scale
+                        )
+            for k in range(NPIV):
+                for q in range(WIDE):
+                    uhi[group, block(k), block(q)], ulo[group, block(k), block(q)] = split(
+                        work[q, block(k)]
+                    )
+                if k + 1 == NPIV:
+                    break
+                below = slice((k + 1) * BS, NPIV * BS)
+                for pair in range(WIDE // 2):
+                    wide = slice(2 * pair * BS, 2 * (pair + 1) * BS)
+                    taken = dot3(
+                        (chi[below, block(k)], clo[below, block(k)]),
+                        (uhi[group, block(k), wide], ulo[group, block(k), wide]),
+                    )
+                    for q in range(2):
+                        at = 2 * pair + q
+                        work[at, below] = work[at, below] - taken[:, block(q)]
+                    for j in range(k + 1, NPIV):
+
+                        @pl.when(row == j)
+                        def _(taken=taken, pair=pair, j=j, k=k, group=group):
+                            for piece in range(4):
+                                low = (j - k - 1) * BS + piece * PIECE
+                                for q in range(2):
+                                    tile = WIDE * group + 2 * pair + q
+                                    own_row[piece, tile] = (
+                                        own_row[piece, tile] - taken[low : low + PIECE, block(q)]
+                                    )
+
+    left = work.at[:, pl.ds(height, height)]
+    left[...] = left_ref[...]
+    for slot in range(2):
+        parent = row_of(map_ref, row, slot)
+        for index in range(4):
+            target = map_ref[0, index]
+            cut = slice((index % 2) * BS, (index % 2) * BS + BS)
+            for tile in range(SPAN):
+
+                @pl.when(
+                    (parent >= 0) & (parent // 16 == SPAN * step + tile) & (target < NPIV)
+                )
+                def _(slot=slot, index=index, cut=cut, tile=tile, target=target):
+                    left[target, block(tile)] = left[target, block(tile)] + near_ref[
+                        index // 2, slot, :, cut
+                    ].astype(F32)
+
+    @pl.when((step == 0) & top_row)
     def _():
-        for k in range(NPIV):
+        left[:, :BS] = jnp.zeros((NPIV, BS, BS), F32)
+
+    for k in range(NPIV):
+        value = dot3(split(left[k]), (xhi[k], xlo[k]))
+        lower[:height, block(k)], lower[height:, block(k)] = split(value)
+
+        @pl.when(col == k)
+        def _(value=value):
+            own_col[...] = value
+
+        if k + 1 < NPIV:
+            rest = slice((k + 1) * BS, NPIV * BS)
+            both = dot(lower[:, block(k)], chi[block(k), rest])
+            both = both[:height] + both[height:]
+            both = both + dot(lower[:height, block(k)], clo[block(k), rest])
+            for j in range(k + 1, NPIV):
+                left[j] = left[j] - both[:, block(j - k - 1)]
+
+    for group in range(2):
+        for pair in range(WIDE // 2):
+            wide = slice(2 * pair * BS, 2 * (pair + 1) * BS)
+            both = dot(lower[...], uhi[group, :, wide])
+            total = both[:height] + (
+                both[height:] + dot(lower[:height], ulo[group, :, wide])
+            )
+            for q in range(2):
+                lost(WIDE * group + 2 * pair + q, 0, height)[...] = total[:, block(q)]
+
+    top_tile = (step == 0) & top_row
+
+    @pl.when(top_tile)
+    def _():
+        for s in range(2 * WIDE):
             for piece in range(4):
-                low = k * BS + piece * PIECE
-                scale = level_ref[4 * piece + k].astype(I32)
-                for q in range(WIDE):
-                    work[low : low + PIECE, block(q)] = decode(
-                        code_ref[4 * piece + k, q * PIECE : q * PIECE + PIECE].astype(I32), scale
-                    )
-        for k in range(NPIV):
-            uhi[group, block(k)], ulo[group, block(k)] = split(work[block(k)])
-            if k + 1 == NPIV:
-                break
-            below = slice((k + 1) * BS, NPIV * BS)
-            for pair in range(WIDE // 2):
-                wide = slice(2 * pair * BS, 2 * (pair + 1) * BS)
-                taken = dot3(
-                    (chi[below, block(k)], clo[below, block(k)]),
-                    (uhi[group, block(k), wide], ulo[group, block(k), wide]),
-                )
-                work[below, wide] = work[below, wide] - taken
-                for j in range(k + 1, NPIV):
-
-                    @pl.when(row == j)
-                    def _(taken=taken, pair=pair, j=j, k=k):
-                        for piece in range(4):
-                            low = (j - k - 1) * BS + piece * PIECE
-                            for q in range(2):
-                                tile = WIDE * group + 2 * pair + q
-                                own_row[piece, tile] = (
-                                    own_row[piece, tile] - taken[low : low + PIECE, block(q)]
-                                )
-
-    @pl.when(group == 0)
+                lost(s, piece * PIECE, PIECE)[...] = -own_row[piece, s]
+
+    def add(copy, index, tile, s):
+        copy.wait()
+        place = lost(s, pl.multiple_of(tile * BS, BS), BS)
+        turn = top_tile & (tile == 0)
+
+        @pl.when(turn)
+        def _():
+            place[...] = place[...] - dot(one_hot(order_ref[...]), parts[index])
+
+        @pl.when(jnp.logical_not(turn))
+        def _():
+            place[...] = place[...] - parts[index].astype(F32)
+
+    each_child(add)
+
+    @pl.when(col < NPIV)
     def _():
-        left = work.at[high_rows]
-        for k in range(NPIV):
-            left[:, block(k)] = left_ref[k]
-        for slot in range(2):
-            parent = row_of(map_ref, row, slot)
-            for index in range(4):
-                target = map_ref[0, index]
-                cut = slice((index % 2) * BS, (index % 2) * BS + BS)
-                for tile in range(SPAN):
-                    for k in range(index, NPIV):
-
-                        @pl.when(
-                            (parent >= 0) & (parent // 16 == SPAN * step + tile) & (target == k)
-                        )
-                        def _(slot=slot, index=index, cut=cut, tile=tile, k=k):
-                            left[block(tile), block(k)] = left[block(tile), block(k)] + near_ref[
-                                index // 2, slot, :, cut
-                            ].astype(F32)
-
-        @pl.when((step == 0) & top_row)
-        def _():
-            left[:BS] = jnp.zeros((BS, NPIV * BS), F32)
-
-        for k in range(NPIV):
-            value = dot3(split(left[:, block(k)]), (xhi[k], xlo[k]))
-            lower[: SPAN * BS, block(k)], lower[SPAN * BS :, block(k)] = split(value)
-
-            @pl.when(col == k)
-            def _(value=value):
-                own_col[...] = value
-
-            if k + 1 < NPIV:
-                rest = slice((k + 1) * BS, NPIV * BS)
-                both = dot(lower[:, block(k)], chi[block(k), rest])
-                both = both[: SPAN * BS] + both[SPAN * BS :]
-                both = both + dot(lower[: SPAN * BS, block(k)], clo[block(k), rest])
-                left[:, rest] = left[:, rest] - both
-
-    for pair in range(WIDE // 2):
-        wide = slice(2 * pair * BS, 2 * (pair + 1) * BS)
-        both = dot(lower[...], uhi[group, :, wide])
-        total = both[: SPAN * BS] + (
-            both[SPAN * BS :] + dot(lower[: SPAN * BS], ulo[group, :, wide])
-        )
-        for q in range(2):
-            for half in range(2):
-                rows = at(WIDE * group + 2 * pair + q, half, 0, SPAN)
-                low = q * BS + half * HALF
-                out_ref[rows, :] = front_ref[rows, :] - total[:, low : low + HALF]
-
-    @pl.when(group == 1)
-    def _():
-        top_tile = (step == 0) & top_row
+        lost(0, 0, height)[...] = -own_col[...]
 
         @pl.when(top_tile)
         def _():
-            for s in range(2 * WIDE):
-                put(s, 0, jnp.concatenate([own_row[piece, s] for piece in range(4)], axis=0))
-
-        def add(copy, index, tile, s):
-            copy.wait()
-            turn = top_tile & (tile == 0)
-
-            @pl.when(turn)
-            def _():
-                turned = dot(one_hot(order_ref[...]), parts[index])
-                for half in range(2):
-                    rows = at(s, half)
-                    lanes = slice(half * HALF, half * HALF + HALF)
-                    out_ref[rows, :] = out_ref[rows, :] + turned[:, lanes]
-
-            @pl.when(jnp.logical_not(turn))
-            def _():
-                for half in range(2):
-                    rows = at(s, half, tile)
-                    lanes = slice(half * HALF, half * HALF + HALF)
-                    out_ref[rows, :] = out_ref[rows, :] + parts[index, :, lanes].astype(F32)
-
-        each_child(add)
-
-        @pl.when(col < NPIV)
-        def _():
-            @pl.when(jnp.logical_not(top_tile))
-            def _():
-                put(0, 0, own_col[:BS])
-
-            put(0, 1, own_col[BS:])
-
-            @pl.when(top_tile)
-            def _():
-                put(0, 0, own_block[...])
+            lost(0, 0, BS)[...] = -own_block[...]
+
+    first_tile = lax.broadcasted_iota(I32, (LINES, 2 * WIDE, HALF), 1) == 0
+
+    def turn(index, carry):
+        low = pl.multiple_of(index * LINES, LINES)
+        keep = jnp.where(top_tile & (low < BS), 0.0, 1.0)
+        keep_first = jnp.where(col < NPIV, 0.0, keep)
+        mask = jnp.where(first_tile, keep_first, keep)
+        for half in range(2):
+            lanes = slice(half * HALF, half * HALF + HALF)
+            tiles = [lost(s, low, LINES)[:, lanes] for s in range(2 * WIDE)]
+            turned = jnp.swapaxes(jnp.stack(tiles, axis=0), 0, 1)
+            rows = pl.ds(low, LINES)
+            out_ref[rows, half] = jnp.where(mask > 0.0, front_ref[rows, half], 0.0) - turned
+        return carry
+
+    lax.fori_loop(0, height // LINES, turn, 0)
+
+
+LINES = 32
 
 
 def run_finish(child_map, rc, top, front_left, order, view, cuts, child):
     once = pl.Buffered(1)
-    rows = pl.BlockSpec((SPAN * BS * 16, HALF), lambda t, g: (t, 0))
+    rows = pl.BlockSpec((SPAN * BS,) + view.shape[1:], lambda t: (t, 0, 0, 0))
     away = pl.BlockSpec(memory_space=pl.ANY)
     return pl.pallas_call(
         finish,
-        grid=(4 // SPAN, 2),
+        grid=(4 // SPAN,),
         out_shape=shape(view.shape, F32),
         in_specs=[
             SMEM, SMEM,
-            pl.BlockSpec((16, 4 * PIECE, BS), lambda t, g: (0, 2, 0), pipeline_mode=once),
-            pl.BlockSpec((16, PIECE, BS), lambda t, g: (0, 12, 0), pipeline_mode=once),
-            pl.BlockSpec((16, 16, BS), lambda t, g: (0, 13 * PIECE // 16, 0), pipeline_mode=once),
-            pl.BlockSpec((16, WIDE * PIECE, BS), lambda t, g: (0, jnp.maximum(t, g), 0)),
-            pl.BlockSpec((4, SPAN * BS, BS), lambda t, g: (0, t, 0)),
-            pl.BlockSpec((2, 2, BS, 2 * BS), lambda t, g: (0, 0, 0, 0), pipeline_mode=once),
-            pl.BlockSpec((BS, HALF), lambda t, g: (0, 0), pipeline_mode=once),
+            pl.BlockSpec((16, 4 * PIECE, BS), lambda t: (0, 2, 0), pipeline_mode=once),
+            pl.BlockSpec((16, PIECE, BS), lambda t: (0, 12, 0), pipeline_mode=once),
+            pl.BlockSpec((16, 16, BS), lambda t: (0, 13 * PIECE // 16, 0), pipeline_mode=once),
+            pl.BlockSpec((16, 8 * PIECE, BS), lambda t: (0, 0, 0), pipeline_mode=once),
+            pl.BlockSpec((4, SPAN * BS, BS), lambda t: (0, t, 0)),
+            pl.BlockSpec((2, 2, BS, 2 * BS), lambda t: (0, 0, 0, 0), pipeline_mode=once),
+            pl.BlockSpec((BS, HALF), lambda t: (0, 0), pipeline_mode=once),
             rows, away, away, away, away, away,
         ],
         out_specs=rows,
         scratch_shapes=[
-            pltpu.VMEM((4 * BS, 4 * BS), F32),
+            pltpu.VMEM((4, 4 * BS, BS), F32),
             pltpu.VMEM((4 * BS, 4 * BS), BF16), pltpu.VMEM((4 * BS, 4 * BS), BF16),
             pltpu.VMEM((NPIV, BS, BS), BF16), pltpu.VMEM((NPIV, BS, BS), BF16),
             pltpu.VMEM((2, 4 * BS, WIDE * BS), BF16), pltpu.VMEM((2, 4 * BS, WIDE * BS), BF16),
@@ -560,6 +564,7 @@
 
     strip = shape((BS, 2 * BS), BF16)
     view = front.reshape(tiles, BS, 8, 2, HALF).transpose(0, 1, 3, 2, 4)
+    view = view.reshape(tiles * BS, 2, 8, HALF)
     *zs, front_left = pl.pallas_call(
         begin,
         out_shape=[strip] * 4 + [shape((tiles * BS, BS), F32)],
@@ -568,8 +573,7 @@
         scratch_shapes=[pltpu.SemaphoreType.DMA((2,))],
         compiler_params=pltpu.CompilerParams(vmem_limit_bytes=LIMIT),
         cost_estimate=pl.CostEstimate(flops=0, bytes_accessed=4 * 2**20, transcendentals=0),
-    )(child_map, rc, child_update.reshape(2, BS, 2 * BS), view.reshape(tiles * BS, 2, 8, HALF))
-    view = view.reshape(tiles * BS * 16, HALF)
+    )(child_map, rc, child_update.reshape(2, BS, 2 * BS), view)
     order = jnp.where(
         row < NPIV, pivots[jnp.minimum(row, NPIV - 1)], jnp.arange(BS, dtype=I32)
     )
@@ -587,7 +591,7 @@
         out_specs=[pl.BlockSpec((8, PIECE, BS), lambda t: (0, 0, 0))] * 4,
         compiler_params=pltpu.CompilerParams(vmem_limit_bytes=LIMIT),
         cost_estimate=pl.CostEstimate(flops=2**30, bytes_accessed=4 * 2**20, transcendentals=0),
-    )(view, order)
+    )(view.reshape(tiles * BS * 16, HALF), order)
     moved = spread(cuts)
 
     front_left = lax.all_gather(front_left, "pcol", axis=0, tiled=False)

time: 186 us -> 183 us (0.984)
  Pallas kernels: 74.3 us -> 70.7 us
    pallas_call x1, Pallas kernels: 53.1 us -> 49.5 us  [run_finish(): pl.pallas_call(finish, grid=(4 // SPAN,), out_shape=shape(view.shape, F32...]
  transfers between devices with their start and end apart: 14 -> 14, of which waited for: 2 -> 2; matrix products, arithmetic and copies ran while one was open for 0% -> 0% of each run, Pallas kernels for 9% -> 10%
where the time goes in v9:
time: 183 us; the launch traced here: 182 us
  Pallas kernels  70.7 us (39%)
  blocking collectives  65.5 us (36%)
  starting transfers between devices  22.4 us (12%)
  between operations  13.7 us (7%)
  waiting for transfers between devices  5.69 us (3%)
  local copies, waits for them, and re-layouts  3.06 us (2%)
    pallas_call x1, Pallas kernels, run_finish(): pl.pallas_call(finish, grid=(4 // SPAN,), out_shape=shape(view.shape, F32...  49.5 us
    all_gather x1, blocking collectives, shards(): top = lax.all_gather(code, 'prow', axis=0, tiled=False)  45.1 us
    all_gather x1, blocking collectives, shards(): thin = lax.all_gather(thin, 'pcol', axis=0, tiled=False)  20.3 us
    ppermute x6, starting transfers between devices, from_plane(): return lax.ppermute(a, 'prow', [(j, 4 * hop + j) for j in range(4)])  13 us
    pallas_call x4, Pallas kernels, call(): pl.pallas_call(body, out_shape=outs, in_specs=[SMEM] * smem + [VMEM] * (l...  12 us
    ppermute x3, starting transfers between devices, along_z(): lax.ppermute(a, 'prow', [(4 * i + j, 4 * i + (j + hop) % 4) for i in rang...  5.74 us
    ppermute x3, waiting for transfers between devices, along_z(): lax.ppermute(a, 'prow', [(4 * i + j, 4 * i + (j + hop) % 4) for i in rang...  5.61 us
    pallas_call x1, Pallas kernels, shards(): pl.pallas_call(cut_front, grid=(1,), out_shape=[shape((8, PIECE, BS), F32...  5.59 us
  transfers between devices with their start and end apart: 14, of which 2 were waited for; matrix products, arithmetic and copies ran while one was open for 0% of the time, Pallas kernels for 10%

profile of v9, /device:TPU:1, one launch (start us, length us, event | category | flops | bytes accessed | tf_op | source)
XLA Modules:
  0.0 181.6 jit_solution(5852995953892507658)
XLA Ops:
  7.2 3.6 %shard_map.46 = (bf16[256,512]{1,0:T(8,128)(2,1)}, bf16[256,512]{1,0:T(8,128)(2,1)}, bf16[256,512]{1,0:T(8,128)(2,1)}, bf16[256,512]{1,0:T(8,128)(2,1)}, f32[1024,256]{1,0:T(8,128)}) custom-call(s32[2,16]{1,0:T(2,128)} %map_ref.7, s32[2]{0:T(128)} %pad_add_fusion.rc_ref, bf16[2,256,512]{2,1,0:T(8,128)(2,1)} %bitcast.28, f32[1024,2,8,128]{3,2,1,0:T(8,128)} %bitcast.20), custom_call_target="tpu_custom_call" | custom-call | bytes 4194304 | tf_op jit(solution)/shard_map/pallas_call | solution.py:568
  11.0 0.8 broadcast_in_dim.2.order_ref
  11.7 5.6 %shard_map.47 = (f32[8,64,256]{2,1,0:T(8,128)}, f32[8,64,256]{2,1,0:T(8,128)}, f32[8,64,256]{2,1,0:T(8,128)}, f32[8,64,256]{2,1,0:T(8,128)}) custom-call(f32[16384,128]{1,0:T(8,128)} %bitcast.21, f32[256,128]{1,0:T(8,128)} %broadcast_in_dim.2.order_ref), custom_call_target="tpu_custom_call" | custom-call | flops 1073741824 | bytes 4194304 | tf_op jit(solution)/shard_map/pallas_call | solution.py:583
  17.3 4.1 %collective-permute-start = (f32[8,64,256]{2,1,0:T(8,128)}, f32[8,64,256]{2,1,0:T(8,128)S(1)}, u32[]{:S(2)}, u32[]{:S(2)}) collective-permute-start(f32[8,64,256]{2,1,0:T(8,128)} %get-tuple-element.39.f1), channel_id=1, source_target_pairs={{0,32},{8,40},{16,48},{24,56},{1,33},{9,41},{17,49},{25,57},{2,34}... | collective-permute-start | bytes 1572872 | tf_op jit(solution)/shard_map/ppermute | solution.py:560
  21.4 1.7 collective-permute-start.3
  23.1 3.3 %collective-permute-start.4 = (bf16[256,512]{1,0:T(8,128)(2,1)S(1)}, bf16[256,512]{1,0:T(8,128)(2,1)S(1)}, u32[]{:S(2)}, u32[]{:S(2)}) collective-permute-start(bf16[256,512]{1,0:T(8,128)(2,1)S(1)} %copy-done.11), channel_id=1, source_target_pairs={{0,16},{8,24},{16,0},{24,8},{32,48},{40,56},{48,32},{56,40},{64,80... | collective-permute-start | bytes 786440 | tf_op jit(solution)/shard_map/ppermute | solution.py:550
  26.4 0.7 collective-permute-start.5
  27.1 2.3 %collective-permute-start.1 = (f32[8,64,256]{2,1,0:T(8,128)}, f32[8,64,256]{2,1,0:T(8,128)S(1)}, u32[]{:S(2)}, u32[]{:S(2)}) collective-permute-start(f32[8,64,256]{2,1,0:T(8,128)} %get-tuple-element.40.f2), channel_id=1, source_target_pairs={{0,64},{8,72},{16,80},{24,88},{1,65},{9,73},{17,81},{25,89},{2,66}... | collective-permute-start | bytes 1572872 | tf_op jit(solution)/shard_map/ppermute | solution.py:560
  29.4 1.6 collective-permute-done.3.refs_1_
  31.0 2.3 %collective-permute-start.2 = (f32[8,64,256]{2,1,0:T(8,128)}, f32[8,64,256]{2,1,0:T(8,128)S(1)}, u32[]{:S(2)}, u32[]{:S(2)}) collective-permute-start(f32[8,64,256]{2,1,0:T(8,128)} %get-tuple-element.41.f3), channel_id=1, source_target_pairs={{0,96},{8,104},{16,112},{24,120},{1,97},{9,105},{17,113},{25,121},... | collective-permute-start | bytes 1572872 | tf_op jit(solution)/shard_map/ppermute | solution.py:560
  33.4 4.0 %collective-permute-done.4.refs_2_ = bf16[256,512]{1,0:T(8,128)(2,1)S(1)} collective-permute-done((bf16[256,512]{1,0:T(8,128)(2,1)S(1)}, bf16[256,512]{1,0:T(8,128)(2,1)S(1)}, u32[]{:S(2)}, u32[]{:S(2)}) %collective-permute-start.4) | collective-permute-done | bytes 262176 | tf_op jit(solution)/shard_map/ppermute | solution.py:550
  37.4 0.7 copy-done.14
  38.2 3.1 %shard_map.48 = (bf16[64,512]{1,0:T(8,128)(2,1)}, bf16[64,512]{1,0:T(8,128)(2,1)}, bf16[64,512]{1,0:T(8,128)(2,1)}, bf16[64,512]{1,0:T(8,128)(2,1)}, bf16[256,51...) custom-call(s32[2,16]{1,0:T(2,128)} %map_ref.7, ...), custom_call_target="tpu_custom_call" | custom-call | flops 21474836480 | bytes 2490504 | tf_op jit(solution)/shard_map/pallas_call | solution.py:33
  41.3 1.3 collective-permute-start.6
  42.6 1.7 collective-permute-start.7
  44.3 1.3 collective-permute-start.8
  45.7 1.6 collective-permute-start.10
  47.3 2.0 %collective-permute-start.11 = (bf16[256,512]{1,0:T(8,128)(2,1)}, bf16[256,512]{1,0:T(8,128)(2,1)S(1)}, u32[]{:S(2)}, u32[]{:S(2)}) collective-permute-start(bf16[256,512]{1,0:T(8,128)(2,1)} %get-tuple-element.57), channel_id=1, source_target_pairs={{0,96},{8,104},{16,112},{24,120},{32,0},{40,8},{48,16},{56,24},{64... | collective-permute-start | bytes 786440 | tf_op jit(solution)/shard_map/ppermute | solution.py:555
  49.9 2.7 %shard_map.49 = s16[272,256]{1,0:T(8,128)(2,1)} custom-call(s32[2]{0:T(128)} %pad_add_fusion.rc_ref, bf16[64,512]{1,0:T(8,128)(2,1)} %get-tuple-element.50.t0, bf16[64,512]{1,0:T(8,128)(2,1)} %copy-done.7, bf16[64,512]{1,0:T(8,128)(2,1)} %copy-done.8, bf16[64,512]{1,0:T(8,128)(2,1)} %copy-done.9, f32[8,64,256]{2,1,0:T(8,128)} %get-tuple-element.38.f0, ...), custom_call_target="tpu_custom_call" | custom-call | bytes 2498568 | tf_op jit(solution)/shard_map/pallas_call | solution.py:33
  52.6 20.3 %all-gather.12 = s16[2176,256]{1,0:T(8,128)(2,1)} all-gather(s16[272,256]{1,0:T(8,128)(2,1)} %shard_map.49), channel_id=2, replica_groups=mesh['prow'=16,'pcol'=8] {'pcol'}, dimensions={0}, use_global_device_ids=true | all-gather | bytes 1253376 | tf_op jit(solution)/shard_map/all_gather | solution.py:614
  73.9 2.3 %shard_map.50 = bf16[4,256,512]{2,1,0:T(8,128)(2,1)} custom-call(s32[2]{0:T(128)} %pad_add_fusion.rc_ref, bf16[256,512]{1,0:T(8,128)(2,1)} %get-tuple-element.54.h0, bf16[256,512]{1,0:T(8,128)(2,1)} %copy-done.4, bf16[256,512]{1,0:T(8,128)(2,1)} %copy-done.5, bf16[256,512]{1,0:T(8,128)(2,1)} %copy-done.6), custom_call_target="tpu_custom_call" | custom-call | bytes 2097160 | tf_op jit(solution)/shard_map/pallas_call | solution.py:33
  76.2 3.9 %shard_map.51 = s16[848,256]{1,0:T(8,128)(2,1)} custom-call(s32[2,16]{1,0:T(2,128)} %map_ref.7, s32[2]{0:T(128)} %pad_add_fusion.rc_ref, f32[8,64,256]{2,1,0:T(8,128)} %get-tuple-element.38.f0, f32[8,64,256]{2,1,0:T(8,128)} %copy-done.1, f32[8,64,256]{2,1,0:T(8,128)} %copy-done.2, f32[8,64,256]{2,1,0:T(8,128)} %copy-done.3, s16[8,272,256]{2,1,0:T(8,128)(2,1)} %bitcast.27), custom_call_target="tpu_custom_call" | custom-call | bytes 3645576 | tf_op jit(solution)/shard_map/pallas_call | solution.py:33
  80.1 45.1 %all-gather.13 = s16[13568,256]{1,0:T(8,128)(2,1)} all-gather(s16[848,256]{1,0:T(8,128)(2,1)} %shard_map.51), channel_id=3, replica_groups=mesh['prow'=16,'pcol'=8] {'prow'}, dimensions={0}, use_global_device_ids=true | all-gather | bytes 7380992 | tf_op jit(solution)/shard_map/all_gather | solution.py:625
  125.3 49.5 %shard_map.52 = f32[1024,2,8,128]{3,2,1,0:T(8,128)} custom-call(s32[2,16]{1,0:T(2,128)} %map_ref.7, s32[2]{0:T(128)} %pad_add_fusion.rc_ref, s16[16,848,256]{2,1,0:T(8,128)(2,1)} %bitcast.23, s16[16,848,256]{2,1,0:T(8,128)(2,1)} %bitcast.24, s16[16,848,256]{2,1,0:T(8,128)(2,1)} %bitcast.25, s16[16,848,256]{2,1,0:T(8,128)(2,1)} %bitcast.26, ...), custom_call_target="tpu_custom_call" | custom-call | flops 24696061952 | bytes 33554432 | tf_op jit(solution)/shard_map/pallas_call | solution.py:509
  (51 shorter events, 2.5 us)
Async XLA Ops:
  6.5 4.4 %copy-start = (s32[4,256]{1,0:T(4,128)S(1)}, s32[4,256]{1,0:T(4,128)}, u32[]{:S(2)}) copy-start(s32[4,256]{1,0:T(4,128)} %param.7) | copy-start | bytes 12292
  6.5 118.7 %all-gather.9.cloned.1.call-start = ((), (), s32[]{:S(2)}) async-start(), calls=%async_computation | async-start | bytes 9437184 | tf_op jit(solution)/shard_map/all_gather | solution.py:597
  10.8 10.5 %copy-start.12 = (bf16[256,512]{1,0:T(8,128)(2,1)S(1)}, bf16[256,512]{1,0:T(8,128)(2,1)}, u32[]{:S(2)}) copy-start(bf16[256,512]{1,0:T(8,128)(2,1)} %get-tuple-element.43) | copy-start | bytes 786436
  10.8 12.3 %copy-start.11 = (bf16[256,512]{1,0:T(8,128)(2,1)S(1)}, bf16[256,512]{1,0:T(8,128)(2,1)}, u32[]{:S(2)}) copy-start(bf16[256,512]{1,0:T(8,128)(2,1)} %get-tuple-element.44) | copy-start | bytes 786436
  10.9 15.5 %copy-start.10 = (bf16[256,512]{1,0:T(8,128)(2,1)S(1)}, bf16[256,512]{1,0:T(8,128)(2,1)}, u32[]{:S(2)}) copy-start(bf16[256,512]{1,0:T(8,128)(2,1)} %get-tuple-element.45) | copy-start | bytes 786436
  10.9 114.4 %all-gather.11.cloned.1.call-start = ((), (), s32[]{:S(2)}) async-start(), calls=%async_computation.1 | async-start | bytes 9437184 | tf_op jit(solution)/shard_map/all_gather | solution.py:624
  17.3 20.1 %collective-permute-start = (f32[8,64,256]{2,1,0:T(8,128)}, f32[8,64,256]{2,1,0:T(8,128)S(1)}, u32[]{:S(2)}, u32[]{:S(2)}) collective-permute-start(f32[8,64,256]{2,1,0:T(8,128)} %get-tuple-element.39.f1), channel_id=1, source_target_pairs={{0,32},{8,40},{16,48},{24,56},{1,33},{9,41},{17,49},{25,57},{2,34}... | collective-permute-start | bytes 1572872 | tf_op jit(solution)/shard_map/ppermute | solution.py:560
  21.4 9.6 %collective-permute-start.3 = (bf16[256,512]{1,0:T(8,128)(2,1)S(1)}, bf16[256,512]{1,0:T(8,128)(2,1)S(1)}, u32[]{:S(2)}, u32[]{:S(2)}) collective-permute-start(bf16[256,512]{1,0:T(8,128)(2,1)S(1)} %copy-done.12), channel_id=1, source_target_pairs={{0,8},{8,16},{16,24},{24,0},{32,40},{40,48},{48,56},{56,32},{64,72... | collective-permute-start | bytes 786440 | tf_op jit(solution)/shard_map/ppermute | solution.py:550
  23.1 14.3 %collective-permute-start.4 = (bf16[256,512]{1,0:T(8,128)(2,1)S(1)}, bf16[256,512]{1,0:T(8,128)(2,1)S(1)}, u32[]{:S(2)}, u32[]{:S(2)}) collective-permute-start(bf16[256,512]{1,0:T(8,128)(2,1)S(1)} %copy-done.11), channel_id=1, source_target_pairs={{0,16},{8,24},{16,0},{24,8},{32,48},{40,56},{48,32},{56,40},{64,80... | collective-permute-start | bytes 786440 | tf_op jit(solution)/shard_map/ppermute | solution.py:550
  26.4 11.0 %collective-permute-start.5 = (bf16[256,512]{1,0:T(8,128)(2,1)S(1)}, bf16[256,512]{1,0:T(8,128)(2,1)S(1)}, u32[]{:S(2)}, u32[]{:S(2)}) collective-permute-start(bf16[256,512]{1,0:T(8,128)(2,1)S(1)} %copy-done.10), channel_id=1, source_target_pairs={{0,24},{8,0},{16,8},{24,16},{32,56},{40,32},{48,40},{56,48},{64,88... | collective-permute-start | bytes 786440 | tf_op jit(solution)/shard_map/ppermute | solution.py:550
  27.1 18.4 %collective-permute-start.1 = (f32[8,64,256]{2,1,0:T(8,128)}, f32[8,64,256]{2,1,0:T(8,128)S(1)}, u32[]{:S(2)}, u32[]{:S(2)}) collective-permute-start(f32[8,64,256]{2,1,0:T(8,128)} %get-tuple-element.40.f2), channel_id=1, source_target_pairs={{0,64},{8,72},{16,80},{24,88},{1,65},{9,73},{17,81},{25,89},{2,66}... | collective-permute-start | bytes 1572872 | tf_op jit(solution)/shard_map/ppermute | solution.py:560
  31.0 6.4 %copy-start.13 = (bf16[256,512]{1,0:T(8,128)(2,1)}, bf16[256,512]{1,0:T(8,128)(2,1)S(1)}, u32[]{:S(2)}) copy-start(bf16[256,512]{1,0:T(8,128)(2,1)S(1)} %collective-permute-done.3.refs_1_) | copy-start | bytes 786436
  31.0 14.6 %collective-permute-start.2 = (f32[8,64,256]{2,1,0:T(8,128)}, f32[8,64,256]{2,1,0:T(8,128)S(1)}, u32[]{:S(2)}, u32[]{:S(2)}) collective-permute-start(f32[8,64,256]{2,1,0:T(8,128)} %get-tuple-element.41.f3), channel_id=1, source_target_pairs={{0,96},{8,104},{16,112},{24,120},{1,97},{9,105},{17,113},{25,121},... | collective-permute-start | bytes 1572872 | tf_op jit(solution)/shard_map/ppermute | solution.py:560
  38.2 3.1 %copy-start.1 = (f32[8,64,256]{2,1,0:T(8,128)}, f32[8,64,256]{2,1,0:T(8,128)S(1)}, u32[]{:S(2)}) copy-start(f32[8,64,256]{2,1,0:T(8,128)S(1)} %collective-permute-done.f1) | copy-start | bytes 1572868
  41.3 6.0 %collective-permute-start.6 = (bf16[64,512]{1,0:T(8,128)(2,1)}, bf16[64,512]{1,0:T(8,128)(2,1)S(1)}, u32[]{:S(2)}, u32[]{:S(2)}) collective-permute-start(bf16[64,512]{1,0:T(8,128)(2,1)} %get-tuple-element.51), channel_id=1, source_target_pairs={{0,32},{8,40},{16,48},{24,56},{1,33},{9,41},{17,49},{25,57},{2,34}... | collective-permute-start | bytes 196616 | tf_op jit(solution)/shard_map/ppermute | solution.py:560
  42.6 6.7 %collective-permute-start.7 = (bf16[64,512]{1,0:T(8,128)(2,1)}, bf16[64,512]{1,0:T(8,128)(2,1)S(1)}, u32[]{:S(2)}, u32[]{:S(2)}) collective-permute-start(bf16[64,512]{1,0:T(8,128)(2,1)} %get-tuple-element.52), channel_id=1, source_target_pairs={{0,64},{8,72},{16,80},{24,88},{1,65},{9,73},{17,81},{25,89},{2,66}... | collective-permute-start | bytes 196616 | tf_op jit(solution)/shard_map/ppermute | solution.py:560
  44.3 5.0 %collective-permute-start.8 = (bf16[64,512]{1,0:T(8,128)(2,1)}, bf16[64,512]{1,0:T(8,128)(2,1)S(1)}, u32[]{:S(2)}, u32[]{:S(2)}) collective-permute-start(bf16[64,512]{1,0:T(8,128)(2,1)} %get-tuple-element.53), channel_id=1, source_target_pairs={{0,96},{8,104},{16,112},{24,120},{1,97},{9,105},{17,113},{25,121},... | collective-permute-start | bytes 196616 | tf_op jit(solution)/shard_map/ppermute | solution.py:560
  45.6 3.7 %copy-start.2 = (f32[8,64,256]{2,1,0:T(8,128)}, f32[8,64,256]{2,1,0:T(8,128)S(1)}, u32[]{:S(2)}) copy-start(f32[8,64,256]{2,1,0:T(8,128)S(1)} %collective-permute-done.1.f2) | copy-start | bytes 1572868
  45.6 27.4 %collective-permute-start.9 = (bf16[256,512]{1,0:T(8,128)(2,1)}, bf16[256,512]{1,0:T(8,128)(2,1)S(1)}, u32[]{:S(2)}, u32[]{:S(2)}) collective-permute-start(bf16[256,512]{1,0:T(8,128)(2,1)} %get-tuple-element.55), channel_id=1, source_target_pairs={{0,32},{8,40},{16,48},{24,56},{32,64},{40,72},{48,80},{56,88},{64,... | collective-permute-start | bytes 786440 | tf_op jit(solution)/shard_map/ppermute | solution.py:555
  45.7 3.6 %copy-start.3 = (f32[8,64,256]{2,1,0:T(8,128)}, f32[8,64,256]{2,1,0:T(8,128)S(1)}, u32[]{:S(2)}) copy-start(f32[8,64,256]{2,1,0:T(8,128)S(1)} %collective-permute-done.2.f3) | copy-start | bytes 1572868
  45.7 27.3 %collective-permute-start.10 = (bf16[256,512]{1,0:T(8,128)(2,1)}, bf16[256,512]{1,0:T(8,128)(2,1)S(1)}, u32[]{:S(2)}, u32[]{:S(2)}) collective-permute-start(bf16[256,512]{1,0:T(8,128)(2,1)} %get-tuple-element.56), channel_id=1, source_target_pairs={{0,64},{8,72},{16,80},{24,88},{32,96},{40,104},{48,112},{56,120},{... | collective-permute-start | bytes 786440 | tf_op jit(solution)/shard_map/ppermute | solution.py:555
  47.3 2.0 %copy-start.7 = (bf16[64,512]{1,0:T(8,128)(2,1)}, bf16[64,512]{1,0:T(8,128)(2,1)S(1)}, u32[]{:S(2)}) copy-start(bf16[64,512]{1,0:T(8,128)(2,1)S(1)} %collective-permute-done.6.t1) | copy-start | bytes 196612
  47.3 25.7 %collective-permute-start.11 = (bf16[256,512]{1,0:T(8,128)(2,1)}, bf16[256,512]{1,0:T(8,128)(2,1)S(1)}, u32[]{:S(2)}, u32[]{:S(2)}) collective-permute-start(bf16[256,512]{1,0:T(8,128)(2,1)} %get-tuple-element.57), channel_id=1, source_target_pairs={{0,96},{8,104},{16,112},{24,120},{32,0},{40,8},{48,16},{56,24},{64... | collective-permute-start | bytes 786440 | tf_op jit(solution)/shard_map/ppermute | solution.py:555
  73.0 0.9 copy-start.6
  (6 other events, 4.3 us)
Sparse Core Ops, SparseCore 0:
  11.0 55.1 all-gather.8
  76.3 48.8 all-gather.10

commit v10 on v9

--- a/solution.py
+++ b/solution.py
@@ -16,11 +16,12 @@
 CHILD_LEVEL = 11.0
 F32 = jnp.float32
 BF16 = jnp.bfloat16
+F8 = jnp.float8_e4m3fn
 I16 = jnp.int16
 I32 = jnp.int32
 SMEM = pl.BlockSpec(memory_space=pltpu.SMEM)
 VMEM = pl.BlockSpec(memory_space=pltpu.VMEM)
-LIMIT = 60 * 1024 * 1024
+LIMIT = 62 * 1024 * 1024
 
 
 def shape(dims, kind):
@@ -245,14 +246,11 @@
     second = level(jnp.max(jnp.abs(square)))
     code = encode(square, second)
     code_ref[pl.ds(pl.multiple_of(low + z * PIECE, PIECE), PIECE), :] = code.astype(I16)
-    square = square - decode(code, second)
-    third = level(jnp.max(jnp.abs(square)))
-    code_ref[12 * PIECE : 13 * PIECE] = encode(square, third).astype(I16)
     line = lax.broadcasted_iota(I32, (16, BS), 0)
-    scales = third[:1, :1]
-    for at, n in enumerate((n, first, second)):
+    scales = second[:1, :1]
+    for at, n in enumerate((n, first)):
         scales = jnp.where(line == at, n[:1, :1], scales)
-    code_ref[13 * PIECE :] = scales.astype(I32).astype(I16)
+    code_ref[12 * PIECE :] = scales.astype(I32).astype(I16)
 
 
 def pack(rc_ref, h0, h1, h2, h3, out_ref):
@@ -261,19 +259,14 @@
         out_ref[(y - shift + 4) % 4] = source[...]
 
 
-def factor_corner(code_ref, rest_ref, level_ref, work, chi, clo, xhi, xlo):
+def factor_corner(code_ref, level_ref, work, chi, clo, xhi, xlo):
     for y in range(4):
         for z in range(4):
             low = z * BS + y * PIECE
             scale = level_ref[4 * y + z].astype(I32)
             for k in range(4):
                 code = code_ref[4 * y + z, k * PIECE : k * PIECE + PIECE].astype(I32)
-                if k == z:
-                    value = decode(code, scale[2:3])
-                    value = value + decode(rest_ref[4 * y + z].astype(I32), scale[3:4])
-                else:
-                    value = decode(code, scale[1:2])
-                work[k, low : low + PIECE] = value
+                work[k, low : low + PIECE] = decode(code, scale[2:3] if k == z else scale[1:2])
     diagonal = lax.broadcasted_iota(I32, (BS, BS), 0) == lax.broadcasted_iota(I32, (BS, BS), 1)
     for k in range(NPIV):
         pivot = work[k, block(k)]
@@ -304,10 +297,10 @@
 
 
 def finish(
-    map_ref, rc_ref, corner_ref, rest_ref, level_ref, code_ref, left_ref, near_ref, order_ref,
+    map_ref, rc_ref, corner_ref, level_ref, code_ref, left_ref, near_ref, order_ref,
     front_ref, f0, f1, f2, f3, child_ref, out_ref,
-    work, chi, clo, xhi, xlo, uhi, ulo, lower, own_col, own_block, own_row, parts,
-    arrived, own_arrived,
+    work, chi, clo, xhi, xlo, uhi, ulo, u8, lower, l8, own_col, own_block, own_row, parts,
+    peak, arrived, own_arrived,
 ):
     step = pl.program_id(0)
     row, col = rc_ref[0], rc_ref[1]
@@ -325,7 +318,7 @@
                 found, value = col_of(map_ref, slot // 2, source, col)
                 where = jnp.maximum(found, 0)
                 start = pl.multiple_of((where % 2) * BS, BS)
-                index = 4 * slot + source
+                index = 4 * (slot % 2) + source
                 copy = pltpu.make_async_copy(
                     child_ref.at[where // 2, slot, :, pl.ds(start, BS)],
                     parts.at[index],
@@ -351,7 +344,7 @@
             for copy in own_copies():
                 copy.start()
 
-        factor_corner(corner_ref, rest_ref, level_ref, work, chi, clo, xhi, xlo)
+        factor_corner(corner_ref, level_ref, work, chi, clo, xhi, xlo)
         for r in range(NPIV):
             for c in range(NPIV):
 
@@ -376,7 +369,7 @@
                         )
             for k in range(NPIV):
                 for q in range(WIDE):
-                    uhi[group, block(k), block(q)], ulo[group, block(k), block(q)] = split(
+                    uhi[group, block(k), block(q)], ulo[block(k), block(q)] = split(
                         work[q, block(k)]
                     )
                 if k + 1 == NPIV:
@@ -386,7 +379,7 @@
                     wide = slice(2 * pair * BS, 2 * (pair + 1) * BS)
                     taken = dot3(
                         (chi[below, block(k)], clo[below, block(k)]),
-                        (uhi[group, block(k), wide], ulo[group, block(k), wide]),
+                        (uhi[group, block(k), wide], ulo[block(k), wide]),
                     )
                     for q in range(2):
                         at = 2 * pair + q
@@ -403,6 +396,15 @@
                                         own_row[piece, tile] - taken[low : low + PIECE, block(q)]
                                     )
 
+            peak[group] = jnp.maximum(jnp.max(jnp.abs(uhi[group].astype(F32))), 1e-30)
+            scale = 256.0 / peak[group]
+            for k in range(NPIV):
+                for q in range(WIDE):
+                    high = uhi[group, block(k), block(q)].astype(F32)
+                    low = ulo[block(k), block(q)].astype(F32)
+                    u8[group, block(k), block(q)] = (high * scale).astype(F8)
+                    u8[group, block(4 + k), block(q)] = (low * (scale * 256.0)).astype(F8)
+
     left = work.at[:, pl.ds(height, height)]
     left[...] = left_ref[...]
     for slot in range(2):
@@ -440,13 +442,17 @@
             for j in range(k + 1, NPIV):
                 left[j] = left[j] - both[:, block(j - k - 1)]
 
+    left_peak = jnp.maximum(jnp.max(jnp.abs(lower[:height].astype(F32))), 1e-30)
+    scale = 256.0 / left_peak
+    for k in range(NPIV):
+        l8[:, block(k)] = (lower[height:, block(k)].astype(F32) * (scale * 256.0)).astype(F8)
+        l8[:, block(4 + k)] = (lower[:height, block(k)].astype(F32) * scale).astype(F8)
     for group in range(2):
+        unit = (left_peak * (1.0 / 65536.0)) * (peak[group] * (1.0 / 256.0))
         for pair in range(WIDE // 2):
             wide = slice(2 * pair * BS, 2 * (pair + 1) * BS)
-            both = dot(lower[...], uhi[group, :, wide])
-            total = both[:height] + (
-                both[height:] + dot(lower[:height], ulo[group, :, wide])
-            )
+            cross = dot(l8[...], u8[group, :, wide]) * unit
+            total = dot(lower[:height], uhi[group, :, wide]) + cross
             for q in range(2):
                 lost(WIDE * group + 2 * pair + q, 0, height)[...] = total[:, block(q)]
 
@@ -513,8 +519,7 @@
         in_specs=[
             SMEM, SMEM,
             pl.BlockSpec((16, 4 * PIECE, BS), lambda t: (0, 2, 0), pipeline_mode=once),
-            pl.BlockSpec((16, PIECE, BS), lambda t: (0, 12, 0), pipeline_mode=once),
-            pl.BlockSpec((16, 16, BS), lambda t: (0, 13 * PIECE // 16, 0), pipeline_mode=once),
+            pl.BlockSpec((16, 16, BS), lambda t: (0, 12 * PIECE // 16, 0), pipeline_mode=once),
             pl.BlockSpec((16, 8 * PIECE, BS), lambda t: (0, 0, 0), pipeline_mode=once),
             pl.BlockSpec((4, SPAN * BS, BS), lambda t: (0, t, 0)),
             pl.BlockSpec((2, 2, BS, 2 * BS), lambda t: (0, 0, 0, 0), pipeline_mode=once),
@@ -526,18 +531,20 @@
             pltpu.VMEM((4, 4 * BS, BS), F32),
             pltpu.VMEM((4 * BS, 4 * BS), BF16), pltpu.VMEM((4 * BS, 4 * BS), BF16),
             pltpu.VMEM((NPIV, BS, BS), BF16), pltpu.VMEM((NPIV, BS, BS), BF16),
-            pltpu.VMEM((2, 4 * BS, WIDE * BS), BF16), pltpu.VMEM((2, 4 * BS, WIDE * BS), BF16),
-            pltpu.VMEM((2 * SPAN * BS, 4 * BS), BF16),
+            pltpu.VMEM((2, 4 * BS, WIDE * BS), BF16), pltpu.VMEM((4 * BS, WIDE * BS), BF16),
+            pltpu.VMEM((2, 8 * BS, WIDE * BS), F8),
+            pltpu.VMEM((2 * SPAN * BS, 4 * BS), BF16), pltpu.VMEM((SPAN * BS, 8 * BS), F8),
             pltpu.VMEM((SPAN * BS, BS), F32), pltpu.VMEM((BS, BS), F32),
             pltpu.VMEM((4, 8, PIECE, BS), F32),
-            pltpu.VMEM((16, BS, BS), BF16),
-            pltpu.SemaphoreType.DMA((16,)), pltpu.SemaphoreType.DMA((4,)),
+            pltpu.VMEM((8, BS, BS), BF16),
+            pltpu.SMEM((2,), F32),
+            pltpu.SemaphoreType.DMA((8,)), pltpu.SemaphoreType.DMA((4,)),
         ],
         compiler_params=pltpu.CompilerParams(vmem_limit_bytes=LIMIT),
         cost_estimate=pl.CostEstimate(
             flops=23 * 2**30, bytes_accessed=32 * 2**20, transcendentals=0
         ),
-    )(child_map, rc, top, top, top, top, front_left, child, order, view, *cuts, child)
+    )(child_map, rc, top, top, top, front_left, child, order, view, *cuts, child)
 
 
 def shards(front, child_update, child_map, pivots):
@@ -616,7 +623,7 @@
     thin, child = lax.optimization_barrier((thin, child))
     (code,) = call(
         assemble,
-        [shape((13 * PIECE + 16, BS), I16)],
+        [shape((12 * PIECE + 16, BS), I16)],
         [child_map, rc, *moved, thin],
         scratch=[pltpu.VMEM((8, PIECE, BS), F32), pltpu.VMEM((NPIV, PIECE, BS), F32)],
     )

time: 183 us -> 181 us (0.989)
  blocking collectives: 65.5 us -> 63 us
  waiting for transfers between devices: 5.69 us -> 7.69 us
    all_gather x1, waiting for transfers between devices: 0.02 us -> 2.66 us  [shards(): child = lax.all_gather(child, 'pcol', axis=0, tiled=False)]
    all_gather x1, blocking collectives: 45.1 us -> 43.1 us  [shards(): top = lax.all_gather(code, 'prow', axis=0, tiled=False)]
  transfers between devices with their start and end apart: 14 -> 14, of which waited for: 2 -> 4; matrix products, arithmetic and copies ran while one was open for 0% -> 0% of each run, Pallas kernels for 10% -> 10%
where the time goes in v10:
time: 181 us; the launch traced here: 180 us
  Pallas kernels  69 us (38%)
  blocking collectives  63 us (35%)
  starting transfers between devices  22.2 us (12%)
  between operations  13.6 us (8%)
  waiting for transfers between devices  7.69 us (4%)
  local copies, waits for them, and re-layouts  4.33 us (2%)
    pallas_call x1, Pallas kernels, run_finish(): pl.pallas_call(finish, grid=(4 // SPAN,), out_shape=shape(view.shape, F32...  47.9 us
    all_gather x1, blocking collectives, shards(): top = lax.all_gather(code, 'prow', axis=0, tiled=False)  43.1 us
    all_gather x1, blocking collectives, shards(): thin = lax.all_gather(thin, 'pcol', axis=0, tiled=False)  19.8 us
    ppermute x6, starting transfers between devices, from_plane(): return lax.ppermute(a, 'prow', [(j, 4 * hop + j) for j in range(4)])  13.7 us
    pallas_call x4, Pallas kernels, call(): pl.pallas_call(body, out_shape=outs, in_specs=[SMEM] * smem + [VMEM] * (l...  11.8 us
    ppermute x3, starting transfers between devices, along_z(): lax.ppermute(a, 'prow', [(4 * i + j, 4 * i + (j + hop) % 4) for i in rang...  5.73 us
    pallas_call x1, Pallas kernels, shards(): pl.pallas_call(cut_front, grid=(1,), out_shape=[shape((8, PIECE, BS), F32...  5.6 us
    ppermute x3, waiting for transfers between devices, along_z(): lax.ppermute(a, 'prow', [(4 * i + j, 4 * i + (j + hop) % 4) for i in rang...  4.96 us
  transfers between devices with their start and end apart: 14, of which 4 were waited for; matrix products, arithmetic and copies ran while one was open for 0% of the time, Pallas kernels for 10%

profile of v10, /device:TPU:1, one launch (start us, length us, event | category | flops | bytes accessed | tf_op | source)
XLA Modules:
  0.0 180.4 jit_solution(9501680601145325746)
XLA Ops:
  7.1 3.6 %shard_map.46 = (bf16[256,512]{1,0:T(8,128)(2,1)}, bf16[256,512]{1,0:T(8,128)(2,1)}, bf16[256,512]{1,0:T(8,128)(2,1)}, bf16[256,512]{1,0:T(8,128)(2,1)}, f32[1024,256]{1,0:T(8,128)}) custom-call(s32[2,16]{1,0:T(2,128)} %map_ref.7, s32[2]{0:T(128)} %pad_add_fusion.rc_ref, bf16[2,256,512]{2,1,0:T(8,128)(2,1)} %bitcast.27, f32[1024,2,8,128]{3,2,1,0:T(8,128)} %bitcast.20), custom_call_target="tpu_custom_call" | custom-call | bytes 4194304 | tf_op jit(solution)/shard_map/pallas_call | solution.py:575
  10.9 0.8 broadcast_in_dim.2.order_ref
  11.7 5.6 %shard_map.47 = (f32[8,64,256]{2,1,0:T(8,128)}, f32[8,64,256]{2,1,0:T(8,128)}, f32[8,64,256]{2,1,0:T(8,128)}, f32[8,64,256]{2,1,0:T(8,128)}) custom-call(f32[16384,128]{1,0:T(8,128)} %bitcast.21, f32[256,128]{1,0:T(8,128)} %broadcast_in_dim.2.order_ref), custom_call_target="tpu_custom_call" | custom-call | flops 1073741824 | bytes 4194304 | tf_op jit(solution)/shard_map/pallas_call | solution.py:590
  17.3 4.1 %collective-permute-start = (f32[8,64,256]{2,1,0:T(8,128)}, f32[8,64,256]{2,1,0:T(8,128)S(1)}, u32[]{:S(2)}, u32[]{:S(2)}) collective-permute-start(f32[8,64,256]{2,1,0:T(8,128)} %get-tuple-element.39.f1), channel_id=1, source_target_pairs={{0,32},{8,40},{16,48},{24,56},{1,33},{9,41},{17,49},{25,57},{2,34}... | collective-permute-start | bytes 1572872 | tf_op jit(solution)/shard_map/ppermute | solution.py:567
  21.3 1.7 collective-permute-start.3
  23.0 3.3 %collective-permute-start.4 = (bf16[256,512]{1,0:T(8,128)(2,1)}, bf16[256,512]{1,0:T(8,128)(2,1)S(1)}, u32[]{:S(2)}, u32[]{:S(2)}) collective-permute-start(bf16[256,512]{1,0:T(8,128)(2,1)} %get-tuple-element.44), channel_id=1, source_target_pairs={{0,16},{8,24},{16,0},{24,8},{32,48},{40,56},{48,32},{56,40},{64,80... | collective-permute-start | bytes 786440 | tf_op jit(solution)/shard_map/ppermute | solution.py:557
  26.3 0.7 collective-permute-start.5
  27.1 2.3 %collective-permute-start.1 = (f32[8,64,256]{2,1,0:T(8,128)}, f32[8,64,256]{2,1,0:T(8,128)S(1)}, u32[]{:S(2)}, u32[]{:S(2)}) collective-permute-start(f32[8,64,256]{2,1,0:T(8,128)} %get-tuple-element.40.f2), channel_id=1, source_target_pairs={{0,64},{8,72},{16,80},{24,88},{1,65},{9,73},{17,81},{25,89},{2,66}... | collective-permute-start | bytes 1572872 | tf_op jit(solution)/shard_map/ppermute | solution.py:567
  29.4 1.6 collective-permute-done.3.refs_1_
  31.7 2.3 %collective-permute-start.2 = (f32[8,64,256]{2,1,0:T(8,128)}, f32[8,64,256]{2,1,0:T(8,128)S(1)}, u32[]{:S(2)}, u32[]{:S(2)}) collective-permute-start(f32[8,64,256]{2,1,0:T(8,128)} %get-tuple-element.41.f3), channel_id=1, source_target_pairs={{0,96},{8,104},{16,112},{24,120},{1,97},{9,105},{17,113},{25,121},... | collective-permute-start | bytes 1572872 | tf_op jit(solution)/shard_map/ppermute | solution.py:567
  34.0 3.3 %collective-permute-done.4.refs_2_ = bf16[256,512]{1,0:T(8,128)(2,1)S(1)} collective-permute-done((bf16[256,512]{1,0:T(8,128)(2,1)}, bf16[256,512]{1,0:T(8,128)(2,1)S(1)}, u32[]{:S(2)}, u32[]{:S(2)}) %collective-permute-start.4) | collective-permute-done | bytes 262176 | tf_op jit(solution)/shard_map/ppermute | solution.py:557
  38.0 0.7 copy-done.13
  38.8 3.1 %shard_map.48 = (bf16[64,512]{1,0:T(8,128)(2,1)}, bf16[64,512]{1,0:T(8,128)(2,1)}, bf16[64,512]{1,0:T(8,128)(2,1)}, bf16[64,512]{1,0:T(8,128)(2,1)}, bf16[256,51...) custom-call(s32[2,16]{1,0:T(2,128)} %map_ref.7, ...), custom_call_target="tpu_custom_call" | custom-call | flops 21474836480 | bytes 2490504 | tf_op jit(solution)/shard_map/pallas_call | solution.py:34
  41.8 1.3 collective-permute-start.6
  43.2 1.7 collective-permute-start.7
  44.9 1.9 %collective-permute-start.8 = (bf16[64,512]{1,0:T(8,128)(2,1)}, bf16[64,512]{1,0:T(8,128)(2,1)}, u32[]{:S(2)}, u32[]{:S(2)}) collective-permute-start(bf16[64,512]{1,0:T(8,128)(2,1)} %get-tuple-element.53), channel_id=1, source_target_pairs={{0,96},{8,104},{16,112},{24,120},{1,97},{9,105},{17,113},{25,121},... | collective-permute-start | bytes 196616 | tf_op jit(solution)/shard_map/ppermute | solution.py:567
  47.2 2.4 %collective-permute-start.11 = (bf16[256,512]{1,0:T(8,128)(2,1)}, bf16[256,512]{1,0:T(8,128)(2,1)S(1)}, u32[]{:S(2)}, u32[]{:S(2)}) collective-permute-start(bf16[256,512]{1,0:T(8,128)(2,1)} %get-tuple-element.57), channel_id=1, source_target_pairs={{0,96},{8,104},{16,112},{24,120},{32,0},{40,8},{48,16},{56,24},{64... | collective-permute-start | bytes 786440 | tf_op jit(solution)/shard_map/ppermute | solution.py:562
  50.3 2.7 %shard_map.49 = s16[272,256]{1,0:T(8,128)(2,1)} custom-call(s32[2]{0:T(128)} %pad_add_fusion.rc_ref, bf16[64,512]{1,0:T(8,128)(2,1)} %get-tuple-element.50.t0, bf16[64,512]{1,0:T(8,128)(2,1)} %copy-done.7, bf16[64,512]{1,0:T(8,128)(2,1)} %copy-done.8, bf16[64,512]{1,0:T(8,128)(2,1)} %collective-permute-done.8.t3, f32[8,64,256]{2,1,0:T(8,128)} %get-tuple-element.38.f0, ...), custom_call_target="tpu_custom_call" | custom-call | bytes 2498568 | tf_op jit(solution)/shard_map/pallas_call | solution.py:34
  53.0 19.8 %all-gather.12 = s16[2176,256]{1,0:T(8,128)(2,1)} all-gather(s16[272,256]{1,0:T(8,128)(2,1)} %shard_map.49), channel_id=2, replica_groups=mesh['prow'=16,'pcol'=8] {'pcol'}, dimensions={0}, use_global_device_ids=true | all-gather | bytes 1253376 | tf_op jit(solution)/shard_map/all_gather | solution.py:621
  73.7 2.3 %shard_map.50 = bf16[4,256,512]{2,1,0:T(8,128)(2,1)} custom-call(s32[2]{0:T(128)} %pad_add_fusion.rc_ref, bf16[256,512]{1,0:T(8,128)(2,1)} %get-tuple-element.54.h0, bf16[256,512]{1,0:T(8,128)(2,1)} %copy-done.4, bf16[256,512]{1,0:T(8,128)(2,1)} %copy-done.5, bf16[256,512]{1,0:T(8,128)(2,1)} %copy-done.6), custom_call_target="tpu_custom_call" | custom-call | bytes 2097160 | tf_op jit(solution)/shard_map/pallas_call | solution.py:34
  76.0 3.8 %shard_map.51 = s16[784,256]{1,0:T(8,128)(2,1)} custom-call(s32[2,16]{1,0:T(2,128)} %map_ref.7, s32[2]{0:T(128)} %pad_add_fusion.rc_ref, f32[8,64,256]{2,1,0:T(8,128)} %get-tuple-element.38.f0, f32[8,64,256]{2,1,0:T(8,128)} %copy-done.1, f32[8,64,256]{2,1,0:T(8,128)} %copy-done.2, f32[8,64,256]{2,1,0:T(8,128)} %copy-done.3, s16[8,272,256]{2,1,0:T(8,128)(2,1)} %bitcast.26), custom_call_target="tpu_custom_call" | custom-call | bytes 3612808 | tf_op jit(solution)/shard_map/pallas_call | solution.py:34
  79.8 43.1 %all-gather.13 = s16[12544,256]{1,0:T(8,128)(2,1)} all-gather(s16[784,256]{1,0:T(8,128)(2,1)} %shard_map.51), channel_id=3, replica_groups=mesh['prow'=16,'pcol'=8] {'prow'}, dimensions={0}, use_global_device_ids=true | all-gather | bytes 6823936 | tf_op jit(solution)/shard_map/all_gather | solution.py:632
  123.0 2.7 %all-gather.11.cloned.1.call-done = bf16[32,256,512]{2,1,0:T(8,128)(2,1)} async-done(((bf16[4,256,512]{2,1,0:T(8,128)(2,1)}), bf16[32,256,512]{2,1,0:T(8,128)(2,1)}) %all-gather.11.cloned.1.call-update) | async-done | bytes 8388624 | tf_op jit(solution)/shard_map/all_gather | solution.py:631
  125.6 47.9 %shard_map.52 = f32[1024,2,8,128]{3,2,1,0:T(8,128)} custom-call(s32[2,16]{1,0:T(2,128)} %map_ref.7, s32[2]{0:T(128)} %pad_add_fusion.rc_ref, s16[16,784,256]{2,1,0:T(8,128)(2,1)} %bitcast.23, s16[16,784,256]{2,1,0:T(8,128)(2,1)} %bitcast.24, s16[16,784,256]{2,1,0:T(8,128)(2,1)} %bitcast.25, f32[8,1024,256]{2,1,0:T(8,128)} %bitcast.29, ...), custom_call_target="tpu_custom_call" | custom-call | flops 24696061952 | bytes 33554432 | tf_op jit(solution)/shard_map/pallas_call | solution.py:515
  (47 shorter events, 4.0 us)
Async XLA Ops:
  6.5 4.3 %copy-start = (s32[4,256]{1,0:T(4,128)S(1)}, s32[4,256]{1,0:T(4,128)}, u32[]{:S(2)}) copy-start(s32[4,256]{1,0:T(4,128)} %param.7) | copy-start | bytes 12292
  6.5 116.4 %all-gather.9.cloned.1.call-start = ((), (), s32[]{:S(2)}) async-start(), calls=%async_computation | async-start | bytes 9437184 | tf_op jit(solution)/shard_map/all_gather | solution.py:604
  10.8 10.6 %copy-start.10 = (bf16[256,512]{1,0:T(8,128)(2,1)S(1)}, bf16[256,512]{1,0:T(8,128)(2,1)}, u32[]{:S(2)}) copy-start(bf16[256,512]{1,0:T(8,128)(2,1)} %get-tuple-element.43) | copy-start | bytes 786436
  10.8 15.6 %copy-start.9 = (bf16[256,512]{1,0:T(8,128)(2,1)S(1)}, bf16[256,512]{1,0:T(8,128)(2,1)}, u32[]{:S(2)}) copy-start(bf16[256,512]{1,0:T(8,128)(2,1)} %get-tuple-element.45) | copy-start | bytes 786436
  10.8 114.8 %all-gather.11.cloned.1.call-start = ((), (), s32[]{:S(2)}) async-start(), calls=%async_computation.1 | async-start | bytes 9437184 | tf_op jit(solution)/shard_map/all_gather | solution.py:631
  17.3 21.5 %collective-permute-start = (f32[8,64,256]{2,1,0:T(8,128)}, f32[8,64,256]{2,1,0:T(8,128)S(1)}, u32[]{:S(2)}, u32[]{:S(2)}) collective-permute-start(f32[8,64,256]{2,1,0:T(8,128)} %get-tuple-element.39.f1), channel_id=1, source_target_pairs={{0,32},{8,40},{16,48},{24,56},{1,33},{9,41},{17,49},{25,57},{2,34}... | collective-permute-start | bytes 1572872 | tf_op jit(solution)/shard_map/ppermute | solution.py:567
  21.3 9.6 %collective-permute-start.3 = (bf16[256,512]{1,0:T(8,128)(2,1)S(1)}, bf16[256,512]{1,0:T(8,128)(2,1)S(1)}, u32[]{:S(2)}, u32[]{:S(2)}) collective-permute-start(bf16[256,512]{1,0:T(8,128)(2,1)S(1)} %copy-done.10), channel_id=1, source_target_pairs={{0,8},{8,16},{16,24},{24,0},{32,40},{40,48},{48,56},{56,32},{64,72... | collective-permute-start | bytes 786440 | tf_op jit(solution)/shard_map/ppermute | solution.py:557
  23.0 14.3 %collective-permute-start.4 = (bf16[256,512]{1,0:T(8,128)(2,1)}, bf16[256,512]{1,0:T(8,128)(2,1)S(1)}, u32[]{:S(2)}, u32[]{:S(2)}) collective-permute-start(bf16[256,512]{1,0:T(8,128)(2,1)} %get-tuple-element.44), channel_id=1, source_target_pairs={{0,16},{8,24},{16,0},{24,8},{32,48},{40,56},{48,32},{56,40},{64,80... | collective-permute-start | bytes 786440 | tf_op jit(solution)/shard_map/ppermute | solution.py:557
  26.3 11.1 %collective-permute-start.5 = (bf16[256,512]{1,0:T(8,128)(2,1)S(1)}, bf16[256,512]{1,0:T(8,128)(2,1)S(1)}, u32[]{:S(2)}, u32[]{:S(2)}) collective-permute-start(bf16[256,512]{1,0:T(8,128)(2,1)S(1)} %copy-done.9), channel_id=1, source_target_pairs={{0,24},{8,0},{16,8},{24,16},{32,56},{40,32},{48,40},{56,48},{64,88... | collective-permute-start | bytes 786440 | tf_op jit(solution)/shard_map/ppermute | solution.py:557
  27.1 19.8 %collective-permute-start.1 = (f32[8,64,256]{2,1,0:T(8,128)}, f32[8,64,256]{2,1,0:T(8,128)S(1)}, u32[]{:S(2)}, u32[]{:S(2)}) collective-permute-start(f32[8,64,256]{2,1,0:T(8,128)} %get-tuple-element.40.f2), channel_id=1, source_target_pairs={{0,64},{8,72},{16,80},{24,88},{1,65},{9,73},{17,81},{25,89},{2,66}... | collective-permute-start | bytes 1572872 | tf_op jit(solution)/shard_map/ppermute | solution.py:567
  31.7 15.2 %collective-permute-start.2 = (f32[8,64,256]{2,1,0:T(8,128)}, f32[8,64,256]{2,1,0:T(8,128)S(1)}, u32[]{:S(2)}, u32[]{:S(2)}) collective-permute-start(f32[8,64,256]{2,1,0:T(8,128)} %get-tuple-element.41.f3), channel_id=1, source_target_pairs={{0,96},{8,104},{16,112},{24,120},{1,97},{9,105},{17,113},{25,121},... | collective-permute-start | bytes 1572872 | tf_op jit(solution)/shard_map/ppermute | solution.py:567
  38.0 0.7 copy-start.13
  38.8 3.1 %copy-start.1 = (f32[8,64,256]{2,1,0:T(8,128)}, f32[8,64,256]{2,1,0:T(8,128)S(1)}, u32[]{:S(2)}) copy-start(f32[8,64,256]{2,1,0:T(8,128)S(1)} %collective-permute-done.f1) | copy-start | bytes 1572868
  41.8 5.4 %collective-permute-start.6 = (bf16[64,512]{1,0:T(8,128)(2,1)}, bf16[64,512]{1,0:T(8,128)(2,1)S(1)}, u32[]{:S(2)}, u32[]{:S(2)}) collective-permute-start(bf16[64,512]{1,0:T(8,128)(2,1)} %get-tuple-element.51), channel_id=1, source_target_pairs={{0,32},{8,40},{16,48},{24,56},{1,33},{9,41},{17,49},{25,57},{2,34}... | collective-permute-start | bytes 196616 | tf_op jit(solution)/shard_map/ppermute | solution.py:567
  43.2 6.5 %collective-permute-start.7 = (bf16[64,512]{1,0:T(8,128)(2,1)}, bf16[64,512]{1,0:T(8,128)(2,1)S(1)}, u32[]{:S(2)}, u32[]{:S(2)}) collective-permute-start(bf16[64,512]{1,0:T(8,128)(2,1)} %get-tuple-element.52), channel_id=1, source_target_pairs={{0,64},{8,72},{16,80},{24,88},{1,65},{9,73},{17,81},{25,89},{2,66}... | collective-permute-start | bytes 196616 | tf_op jit(solution)/shard_map/ppermute | solution.py:567
  44.9 4.7 %collective-permute-start.8 = (bf16[64,512]{1,0:T(8,128)(2,1)}, bf16[64,512]{1,0:T(8,128)(2,1)}, u32[]{:S(2)}, u32[]{:S(2)}) collective-permute-start(bf16[64,512]{1,0:T(8,128)(2,1)} %get-tuple-element.53), channel_id=1, source_target_pairs={{0,96},{8,104},{16,112},{24,120},{1,97},{9,105},{17,113},{25,121},... | collective-permute-start | bytes 196616 | tf_op jit(solution)/shard_map/ppermute | solution.py:567
  46.9 2.8 %copy-start.2 = (f32[8,64,256]{2,1,0:T(8,128)}, f32[8,64,256]{2,1,0:T(8,128)S(1)}, u32[]{:S(2)}) copy-start(f32[8,64,256]{2,1,0:T(8,128)S(1)} %collective-permute-done.1.f2) | copy-start | bytes 1572868
  46.9 26.0 %collective-permute-start.9 = (bf16[256,512]{1,0:T(8,128)(2,1)}, bf16[256,512]{1,0:T(8,128)(2,1)S(1)}, u32[]{:S(2)}, u32[]{:S(2)}) collective-permute-start(bf16[256,512]{1,0:T(8,128)(2,1)} %get-tuple-element.55), channel_id=1, source_target_pairs={{0,32},{8,40},{16,48},{24,56},{32,64},{40,72},{48,80},{56,88},{64,... | collective-permute-start | bytes 786440 | tf_op jit(solution)/shard_map/ppermute | solution.py:562
  46.9 2.8 %copy-start.3 = (f32[8,64,256]{2,1,0:T(8,128)}, f32[8,64,256]{2,1,0:T(8,128)S(1)}, u32[]{:S(2)}) copy-start(f32[8,64,256]{2,1,0:T(8,128)S(1)} %collective-permute-done.2.f3) | copy-start | bytes 1572868
  46.9 25.9 %collective-permute-start.10 = (bf16[256,512]{1,0:T(8,128)(2,1)}, bf16[256,512]{1,0:T(8,128)(2,1)S(1)}, u32[]{:S(2)}, u32[]{:S(2)}) collective-permute-start(bf16[256,512]{1,0:T(8,128)(2,1)} %get-tuple-element.56), channel_id=1, source_target_pairs={{0,64},{8,72},{16,80},{24,88},{32,96},{40,104},{48,112},{56,120},{... | collective-permute-start | bytes 786440 | tf_op jit(solution)/shard_map/ppermute | solution.py:562
  47.2 2.4 %copy-start.7 = (bf16[64,512]{1,0:T(8,128)(2,1)}, bf16[64,512]{1,0:T(8,128)(2,1)S(1)}, u32[]{:S(2)}) copy-start(bf16[64,512]{1,0:T(8,128)(2,1)S(1)} %collective-permute-done.6.t1) | copy-start | bytes 196612
  47.2 25.6 %collective-permute-start.11 = (bf16[256,512]{1,0:T(8,128)(2,1)}, bf16[256,512]{1,0:T(8,128)(2,1)S(1)}, u32[]{:S(2)}, u32[]{:S(2)}) collective-permute-start(bf16[256,512]{1,0:T(8,128)(2,1)} %get-tuple-element.57), channel_id=1, source_target_pairs={{0,96},{8,104},{16,112},{24,120},{32,0},{40,8},{48,16},{56,24},{64... | collective-permute-start | bytes 786440 | tf_op jit(solution)/shard_map/ppermute | solution.py:562
  72.8 0.8 copy-start.5
  72.9 0.9 copy-start.6
  (4 other events, 2.7 us)
Sparse Core Ops, SparseCore 0:
  10.9 55.3 all-gather.8
  76.2 49.4 all-gather.10

commit v11 on v8

v11 whole, which is shorter than its diff:
```python
import functools

import jax
import jax.numpy as jnp
from jax import lax
from jax.experimental import pallas as pl
from jax.experimental.pallas import tpu as pltpu
from jax.sharding import PartitionSpec as P

NPIV = 4
NS = 2
BS = 256
HALF = 128
PIECE = 64
FULL = 32767.0
CHILD_LEVEL = 11.0
F32 = jnp.float32
BF16 = jnp.bfloat16
F8 = jnp.float8_e4m3fn
I16 = jnp.int16
I32 = jnp.int32
SMEM = pl.BlockSpec(memory_space=pltpu.SMEM)
VMEM = pl.BlockSpec(memory_space=pltpu.VMEM)
LIMIT = 62 * 1024 * 1024


def shape(dims, kind):
    return jax.ShapeDtypeStruct(dims, kind)


def call(body, outs, ins, smem=2, flops=0, scratch=()):
    moved = sum(a.size * a.dtype.itemsize for a in ins)
    moved += sum(o.size * o.dtype.itemsize for o in outs)
    return pl.pallas_call(
        body,
        out_shape=outs,
        in_specs=[SMEM] * smem + [VMEM] * (len(ins) - smem),
        out_specs=[VMEM] * len(outs),
        scratch_shapes=list(scratch),
        compiler_params=pltpu.CompilerParams(vmem_limit_bytes=LIMIT),
        cost_estimate=pl.CostEstimate(flops=flops, bytes_accessed=moved, transcendentals=0),
    )(*ins)


def spot(map_ref, child, low, count, test):
    found = jnp.int32(-1)
    value = jnp.int32(-1)
    for step in range(count):
        entry = map_ref[child, low + step]
        hit = test(entry)
        found = jnp.where(hit, low + step, found)
        value = jnp.where(hit, entry, value)
    return found, value


def row_of(map_ref, row, slot):
    return spot(map_ref, slot // 2, 8 * (slot % 2), 8, lambda entry: entry % 16 == row)[1]


def col_of(map_ref, child, source, col):
    return spot(map_ref, child, 4 * source, 4, lambda entry: entry % 8 == col)


def split(value):
    high = value.astype(BF16)
    low = (value - high.astype(F32)).astype(BF16)
    return high, low


def dot(left, right):
    return jnp.dot(left, right, preferred_element_type=F32)


def dot3(left, right):
    (a, b), (c, d) = left, right
    rows = a.shape[0]
    both = dot(jnp.concatenate([a, b], axis=0), c)
    return both[:rows] + (both[rows:] + dot(a, d))


def block(step):
    return slice(step * BS, step * BS + BS)


def one_hot(pivots_ref, row):
    order = pivots_ref[pl.ds(jnp.minimum(row, NPIV - 1), 1), :]
    spread = lax.broadcasted_iota(I32, (BS, BS), 0)
    return jnp.transpose(jnp.where(order == spread, 1.0, 0.0)).astype(BF16)


def reorder(select, value):
    high = value.astype(BF16)
    rest = value - high.astype(F32)
    middle = rest.astype(BF16)
    last = (rest - middle.astype(F32)).astype(BF16)
    return (dot(select, high) + dot(select, middle)) + dot(select, last)


def level(peak):
    return jnp.ceil(jnp.log2(jnp.full((8, HALF), jnp.maximum(peak, 1e-30))) * 4.0)


def encode(value, n):
    scaled = jnp.abs(value) * jnp.exp2(n * -0.25)[:1, :1]
    code = jnp.minimum(jnp.floor(jnp.sqrt(scaled) * FULL + 0.5), FULL)
    return jnp.where(value < 0.0, -code, code).astype(I32)


def decode(code, n):
    code = code.astype(F32)
    return code * jnp.abs(code) * (jnp.exp2(n.astype(F32)[:1, :1] * 0.25) * (1.0 / (FULL * FULL)))


def begin(
    map_ref, rc_ref, child_ref, pivots_ref, lines_ref, view_ref,
    o0, o1, o2, o3, p0, p1, p2, p3, left_ref, tile_row, arrived,
):
    first = pltpu.make_async_copy(lines_ref.at[: BS * 16], tile_row, arrived.at[2])
    first.start()
    copies = [
        pltpu.make_async_copy(
            view_ref.at[:, half, 0, :],
            left_ref.at[:, half * HALF : half * HALF + HALF],
            arrived.at[half],
        )
        for half in range(2)
    ]
    for copy in copies:
        copy.start()
    row = rc_ref[0]
    z = row % 4
    second_at = map_ref[row // 8, 2 * (row % 8) + 1] % 4
    for hop, out in enumerate((o0, o1, o2, o3)):
        out[...] = child_ref[jnp.where(second_at == (z + hop) % 4, 1, 0)]
    select = one_hot(pivots_ref, row)
    first.wait()

    def one(tile, carry):
        halves = [tile_row[pl.ds(half * 8 + tile, BS, stride=16), :] for half in range(2)]
        turned = reorder(select, jnp.concatenate(halves, axis=1))
        for piece, out in enumerate((p0, p1, p2, p3)):
            out[tile] = turned[piece * PIECE : piece * PIECE + PIECE]
        return carry

    lax.fori_loop(0, 8, one, 0)
    for copy in copies:
        copy.wait()


def pick_rows(map_ref, rc_ref, pivots_ref, *refs):
    held, pieces, hops = refs[:4], refs[4:8], refs[8:]
    row = rc_ref[0]
    y, z = row // 4, row % 4
    found, value = spot(map_ref, 0, 0, 4, lambda entry: entry == row)
    live = (found >= 0) & (row < NPIV)
    for hop in range(4):

        @pl.when(live & (found // 2 == (z - hop + 4) % 4))
        def _(hop=hop):
            turned = dot(one_hot(pivots_ref, row), held[hop][...]).astype(BF16)
            for piece in range(4):
                pieces[piece][...] = turned[piece * PIECE : piece * PIECE + PIECE]

    @pl.when(jnp.logical_not(live))
    def _():
        for piece in range(4):
            pieces[piece][...] = jnp.zeros((PIECE, 2 * BS), BF16)

    for hop in range(4):
        first = 2 * ((4 * y + (z - hop + 4) % 4) % 8)
        index, value = spot(map_ref, y // 2, first, 2, lambda entry: entry % 4 == z)
        for shift in range(4):

            @pl.when((index >= 0) & ((value // 4) % 4 == (y + shift) % 4))
            def _(hop=hop, shift=shift):
                hops[shift][...] = held[hop][...]


def mix(rc_ref, t0, t1, t2, t3, f0, f1, f2, f3, out_ref, strip, corner):
    y = rc_ref[0] // 4
    for piece, (child, source) in enumerate(((t0, f0), (t1, f1), (t2, f2), (t3, f3))):

        @pl.when(y == piece)
        def _(child=child, source=source):
            strip[...] = child[...].astype(F32)
            corner[...] = source[0]

    n = jnp.full((8, HALF), CHILD_LEVEL)
    for half in range(2):
        out_ref[half * PIECE : half * PIECE + PIECE] = encode(
            strip[:, half * BS : half * BS + BS], n
        ).astype(I16)
    n = level(jnp.max(jnp.abs(corner[...])))
    out_ref[2 * PIECE : 3 * PIECE] = encode(corner[...], n).astype(I16)
    out_ref[3 * PIECE :] = jnp.broadcast_to(n[:1, :1].astype(I32), (16, BS)).astype(I16)


def assemble(map_ref, rc_ref, f0, f1, f2, f3, thin, code_ref, work, corner):
    row, col = rc_ref[0], rc_ref[1]
    y = row // 4
    for piece, source in enumerate((f0, f1, f2, f3)):

        @pl.when(y == piece)
        def _(source=source):
            work[...] = source[...]

    for k in range(NPIV):
        corner[k] = decode(
            thin[k, 2 * PIECE : 3 * PIECE].astype(I32), thin[k, 3 * PIECE :].astype(I32)
        )
    n = jnp.full((8, HALF), CHILD_LEVEL)
    for index in range(16):
        parent = map_ref[0, index]
        low = (index % 2) * PIECE

        @pl.when(parent % 8 == col)
        def _(index=index, low=low, tile=parent // 8):
            child = decode(thin[index // 2, low : low + PIECE].astype(I32), n)
            work[tile] = work[tile] + child

        if index < NPIV:

            @pl.when(parent < NPIV)
            def _(index=index, low=low, parent=parent):
                child = decode(thin[index // 2, low : low + PIECE].astype(I32), n)
                corner[parent] = corner[parent] + child

    @pl.when(col < NPIV)
    def _():
        work[0] = jnp.zeros((PIECE, BS), F32)

    n = level(jnp.max(jnp.abs(work[...])))
    for tile in range(8):
        code_ref[tile * PIECE : tile * PIECE + PIECE] = encode(work[tile], n).astype(I16)
    z = row % 4
    square = corner[z]
    corner[z] = jnp.zeros((PIECE, BS), F32)
    first = level(jnp.max(jnp.abs(corner[...])))
    low = 8 * PIECE
    for k in range(NPIV):
        code_ref[low + k * PIECE : low + k * PIECE + PIECE] = encode(corner[k], first).astype(I16)
    second = level(jnp.max(jnp.abs(square)))
    code = encode(square, second)
    code_ref[pl.ds(pl.multiple_of(low + z * PIECE, PIECE), PIECE), :] = code.astype(I16)
    line = lax.broadcasted_iota(I32, (16, BS), 0)
    scales = second[:1, :1]
    for at, n in enumerate((n, first)):
        scales = jnp.where(line == at, n[:1, :1], scales)
    code_ref[12 * PIECE :] = scales.astype(I32).astype(I16)


def pack(rc_ref, h0, h1, h2, h3, out_ref):
    y = rc_ref[0] // 4
    for shift, source in enumerate((h0, h1, h2, h3)):
        out_ref[(y - shift + 4) % 4] = source[...]


def factor_corner(code_ref, level_ref, work, chi, clo, xhi, xlo):
    for y in range(4):
        for z in range(4):
            low = z * BS + y * PIECE
            scale = level_ref[4 * y + z].astype(I32)
            for k in range(4):
                code = code_ref[4 * y + z, k * PIECE : k * PIECE + PIECE].astype(I32)
                work[k, low : low + PIECE] = decode(code, scale[2:3] if k == z else scale[1:2])
    diagonal = lax.broadcasted_iota(I32, (BS, BS), 0) == lax.broadcasted_iota(I32, (BS, BS), 1)
    for k in range(NPIV):
        pivot = work[k, block(k)]
        parts = split(pivot)
        on_line = jnp.where(diagonal, pivot, 0.0)
        across = jnp.sum(on_line, axis=0, keepdims=True)
        down = jnp.sum(on_line, axis=1, keepdims=True)
        across = across / (across * across + 1.0)
        down = down / (down * down + 1.0)
        approx = 2.0 * jnp.where(diagonal, across, 0.0) - (down * pivot) * across
        for sweep_index in range(NS - 1):
            pair = split(approx)
            approx = 2.0 * approx - dot3(split(dot3(pair, parts)), pair)
        xhi[k], xlo[k] = split(approx)
        for j in range(NPIV):
            chi[block(k), block(j)], clo[block(k), block(j)] = split(work[j, block(k)])
        if k + 1 < NPIV:
            below = slice((k + 1) * BS, NPIV * BS)
            pair = split(dot3(split(work[k, below]), (xhi[k], xlo[k])))
            work[k, below] = pair[0].astype(F32) + pair[1].astype(F32)
            taken = dot3(pair, (chi[block(k), below], clo[block(k), below]))
            for j in range(k + 1, NPIV):
                work[j, below] = work[j, below] - taken[:, block(j - k - 1)]


SPAN = 2
WIDE = 4


def finish(
    map_ref, rc_ref, pivots_ref, top_ref, left_from, front_from, f0, f1, f2, f3, child_ref, out_ref,
    corner_ref, level_ref, code_ref, left_ref, near_ref, front,
    work, chi, clo, xhi, xlo, uhi, ulo, u8, lower, l8, own_col, own_block, own_row, parts,
    peak, arrived, own_arrived, ready, sent,
):
    row, col = rc_ref[0], rc_ref[1]
    top_row = row < NPIV
    height = SPAN * BS

    def left_copy(step):
        rows = pl.ds(step * height, height)
        return pltpu.make_async_copy(left_from.at[:NPIV, rows], left_ref, ready.at[3])

    def front_copy(step):
        rows = pl.ds(step * height, height)
        return pltpu.make_async_copy(front_from.at[rows], front.at[step], ready.at[5 + step])

    codes = 8 * PIECE
    corner_copies = [
        pltpu.make_async_copy(top_ref.at[:, codes : codes + 4 * PIECE], corner_ref, ready.at[0]),
        pltpu.make_async_copy(top_ref.at[:, codes + 4 * PIECE :], level_ref, ready.at[1]),
    ]
    code_copy = pltpu.make_async_copy(top_ref.at[:, :codes], code_ref, ready.at[2])
    near_copy = pltpu.make_async_copy(child_ref.at[:2, :2], near_ref, ready.at[4])
    for copy in corner_copies:
        copy.start()
    for copy in corner_copies:
        copy.wait()
    for copy in (code_copy, left_copy(0), near_copy, front_copy(0), front_copy(1)):
        copy.start()

    def lost(s, first, count):
        return work.at[s // 2, pl.ds((s % 2) * height + first, count)]

    def each_child(step, act):
        for slot in range(4):
            parent = row_of(map_ref, row, slot)
            here = (parent >= 0) & (parent // 16 // SPAN == step)
            for source in range(4):
                found, value = col_of(map_ref, slot // 2, source, col)
                where = jnp.maximum(found, 0)
                start = pl.multiple_of((where % 2) * BS, BS)
                index = 4 * (slot % 2) + source
                copy = pltpu.make_async_copy(
                    child_ref.at[where // 2, slot, :, pl.ds(start, BS)],
                    parts.at[index],
                    arrived.at[index],
                )

                @pl.when(here & (found >= 0))
                def _(copy=copy, index=index, tile=(parent // 16) % SPAN, s=value // 8):
                    act(copy, index, tile, s)

    def own_copies():
        return [
            pltpu.make_async_copy(source, own_row.at[piece], own_arrived.at[piece])
            for piece, source in enumerate((f0, f1, f2, f3))
        ]

    @pl.when(top_row)
    def _():
        for copy in own_copies():
            copy.start()

    factor_corner(corner_ref, level_ref, work, chi, clo, xhi, xlo)
    for r in range(NPIV):
        for c in range(NPIV):

            @pl.when((row == r) & (col == c))
            def _(r=r, c=c):
                own_block[...] = work[c, block(r)]

    @pl.when(top_row)
    def _():
        for copy in own_copies():
            copy.wait()

    code_copy.wait()
    for group in range(2):
        for k in range(NPIV):
            for piece in range(4):
                low = k * BS + piece * PIECE
                scale = level_ref[4 * piece + k].astype(I32)
                for q in range(WIDE):
                    first = (WIDE * group + q) * PIECE
                    work[q, low : low + PIECE] = decode(
                        code_ref[4 * piece + k, first : first + PIECE].astype(I32), scale
                    )
        for k in range(NPIV):
            for q in range(WIDE):
                uhi[group, block(k), block(q)], ulo[block(k), block(q)] = split(
                    work[q, block(k)]
                )
            if k + 1 == NPIV:
                break
            below = slice((k + 1) * BS, NPIV * BS)
            for pair in range(WIDE // 2):
                wide = slice(2 * pair * BS, 2 * (pair + 1) * BS)
                taken = dot3(
                    (chi[below, block(k)], clo[below, block(k)]),
                    (uhi[group, block(k), wide], ulo[block(k), wide]),
                )
                for q in range(2):
                    at = 2 * pair + q
                    work[at, below] = work[at, below] - taken[:, block(q)]
                for j in range(k + 1, NPIV):

                    @pl.when(row == j)
                    def _(taken=taken, pair=pair, j=j, k=k, group=group):
                        for piece in range(4):
                            low = (j - k - 1) * BS + piece * PIECE
                            for q in range(2):
                                tile = WIDE * group + 2 * pair + q
                                own_row[piece, tile] = (
                                    own_row[piece, tile] - taken[low : low + PIECE, block(q)]
                                )

        peak[group] = jnp.maximum(jnp.max(jnp.abs(uhi[group].astype(F32))), 1e-30)
        scale = 256.0 / peak[group]
        for k in range(NPIV):
            for q in range(WIDE):
                high = uhi[group, block(k), block(q)].astype(F32)
                low = ulo[block(k), block(q)].astype(F32)
                u8[group, block(k), block(q)] = (high * scale).astype(F8)
                u8[group, block(4 + k), block(q)] = (low * (scale * 256.0)).astype(F8)

    def rows_of_step(step, carry):
        each_child(step, lambda copy, index, tile, s: copy.start())
        left = work.at[:, pl.ds(height, height)]
        left_copy(step).wait()
        left[...] = left_ref[...]

        @pl.when(step == 0)
        def _():
            left_copy(1).start()
            near_copy.wait()

        for slot in range(2):
            parent = row_of(map_ref, row, slot)
            for index in range(4):
                target = map_ref[0, index]
                cut = slice((index % 2) * BS, (index % 2) * BS + BS)
                for tile in range(SPAN):

                    @pl.when(
                        (parent >= 0) & (parent // 16 == SPAN * step + tile) & (target < NPIV)
                    )
                    def _(slot=slot, index=index, cut=cut, tile=tile, target=target):
                        left[target, block(tile)] = left[target, block(tile)] + near_ref[
                            index // 2, slot, :, cut
                        ].astype(F32)

        @pl.when((step == 0) & top_row)
        def _():
            left[:, :BS] = jnp.zeros((NPIV, BS, BS), F32)

        for k in range(NPIV):
            value = dot3(split(left[k]), (xhi[k], xlo[k]))
            lower[:height, block(k)], lower[height:, block(k)] = split(value)

            @pl.when(col == k)
            def _(value=value):
                own_col[...] = value

            if k + 1 < NPIV:
                rest = slice((k + 1) * BS, NPIV * BS)
                both = dot(lower[:, block(k)], chi[block(k), rest])
                both = both[:height] + both[height:]
                both = both + dot(lower[:height, block(k)], clo[block(k), rest])
                for j in range(k + 1, NPIV):
                    left[j] = left[j] - both[:, block(j - k - 1)]

        left_peak = jnp.maximum(jnp.max(jnp.abs(lower[:height].astype(F32))), 1e-30)
        scale = 256.0 / left_peak
        for k in range(NPIV):
            l8[:, block(k)] = (lower[height:, block(k)].astype(F32) * (scale * 256.0)).astype(F8)
            l8[:, block(4 + k)] = (lower[:height, block(k)].astype(F32) * scale).astype(F8)
        for group in range(2):
            unit = (left_peak * (1.0 / 65536.0)) * (peak[group] * (1.0 / 256.0))
            for pair in range(WIDE // 2):
                wide = slice(2 * pair * BS, 2 * (pair + 1) * BS)
                cross = dot(l8[...], u8[group, :, wide]) * unit
                total = dot(lower[:height], uhi[group, :, wide]) + cross
                for q in range(2):
                    lost(WIDE * group + 2 * pair + q, 0, height)[...] = total[:, block(q)]

        top_tile = (step == 0) & top_row

        @pl.when(top_tile)
        def _():
            for s in range(2 * WIDE):
                for piece in range(4):
                    lost(s, piece * PIECE, PIECE)[...] = -own_row[piece, s]

        def add(copy, index, tile, s):
            copy.wait()
            place = lost(s, pl.multiple_of(tile * BS, BS), BS)
            turn = top_tile & (tile == 0)

            @pl.when(turn)
            def _():
                place[...] = place[...] - dot(one_hot(pivots_ref, row), parts[index])

            @pl.when(jnp.logical_not(turn))
            def _():
                place[...] = place[...] - parts[index].astype(F32)

        each_child(step, add)

        @pl.when(col < NPIV)
        def _():
            lost(0, 0, height)[...] = -own_col[...]

            @pl.when(top_tile)
            def _():
                lost(0, 0, BS)[...] = -own_block[...]

        first_tile = lax.broadcasted_iota(I32, (LINES, 2 * WIDE, HALF), 1) == 0

        def turn(index, carry):
            low = pl.multiple_of(index * LINES, LINES)
            keep = jnp.where(top_tile & (low < BS), 0.0, 1.0)
            keep_first = jnp.where(col < NPIV, 0.0, keep)
            mask = jnp.where(first_tile, keep_first, keep)
            for half in range(2):
                lanes = slice(half * HALF, half * HALF + HALF)
                tiles = [lost(s, low, LINES)[:, lanes] for s in range(2 * WIDE)]
                turned = jnp.swapaxes(jnp.stack(tiles, axis=0), 0, 1)
                rows = pl.ds(low, LINES)
                kept = jnp.where(mask > 0.0, front[step, rows, half], 0.0)
                front[step, rows, half] = kept - turned
            return carry

        front_copy(step).wait()
        for quarter in range(4):
            lines = height // (4 * LINES)
            lax.fori_loop(quarter * lines, quarter * lines + lines, turn, 0)
            out_copy(step, quarter).start()
        return carry

    def out_copy(step, quarter):
        rows = pl.ds(quarter * (height // 4), height // 4)
        return pltpu.make_async_copy(
            front.at[step, rows],
            out_ref.at[pl.ds(step * height + quarter * (height // 4), height // 4)],
            sent.at[4 * step + quarter],
        )

    lax.fori_loop(0, 4 // SPAN, rows_of_step, 0)
    for step in range(4 // SPAN):
        for quarter in range(4):
            out_copy(step, quarter).wait()


LINES = 32


def run_finish(child_map, rc, pivots, top, front_left, view, cuts, child):
    away = pl.BlockSpec(memory_space=pl.ANY)
    return pl.pallas_call(
        finish,
        out_shape=shape(view.shape, F32),
        in_specs=[SMEM, SMEM, VMEM] + [away] * 8,
        out_specs=away,
        scratch_shapes=[
            pltpu.VMEM((16, 4 * PIECE, BS), I16), pltpu.VMEM((16, 16, BS), I16),
            pltpu.VMEM((16, 8 * PIECE, BS), I16), pltpu.VMEM((4, SPAN * BS, BS), F32),
            pltpu.VMEM((2, 2, BS, 2 * BS), BF16), pltpu.VMEM((2, SPAN * BS, 2, 8, HALF), F32),
            pltpu.VMEM((4, 4 * BS, BS), F32),
            pltpu.VMEM((4 * BS, 4 * BS), BF16), pltpu.VMEM((4 * BS, 4 * BS), BF16),
            pltpu.VMEM((NPIV, BS, BS), BF16), pltpu.VMEM((NPIV, BS, BS), BF16),
            pltpu.VMEM((2, 4 * BS, WIDE * BS), BF16), pltpu.VMEM((4 * BS, WIDE * BS), BF16),
            pltpu.VMEM((2, 8 * BS, WIDE * BS), F8),
            pltpu.VMEM((2 * SPAN * BS, 4 * BS), BF16), pltpu.VMEM((SPAN * BS, 8 * BS), F8),
            pltpu.VMEM((SPAN * BS, BS), F32), pltpu.VMEM((BS, BS), F32),
            pltpu.VMEM((4, 8, PIECE, BS), F32),
            pltpu.VMEM((8, BS, BS), BF16),
            pltpu.SMEM((2,), F32),
            pltpu.SemaphoreType.DMA((8,)), pltpu.SemaphoreType.DMA((4,)),
            pltpu.SemaphoreType.DMA((7,)), pltpu.SemaphoreType.DMA((8,)),
        ],
        compiler_params=pltpu.CompilerParams(vmem_limit_bytes=LIMIT),
        cost_estimate=pl.CostEstimate(
            flops=23 * 2**30, bytes_accessed=32 * 2**20, transcendentals=0
        ),
    )(child_map, rc, pivots, top, front_left, view, *cuts, child)


def shards(front, child_update, child_map, pivots):
    row = lax.axis_index("prow")
    col = lax.axis_index("pcol")
    rc = jnp.stack([row, col]).astype(I32)
    tiles = front.shape[0]

    def along_z(a, hop):
        return lax.ppermute(
            a, "prow", [(4 * i + j, 4 * i + (j + hop) % 4) for i in range(4) for j in range(4)]
        )

    def along_y(a, hop):
        return lax.ppermute(
            a, "prow", [(4 * i + j, 4 * ((i + hop) % 4) + j) for i in range(4) for j in range(4)]
        )

    def from_plane(a, hop):
        return lax.ppermute(a, "prow", [(j, 4 * hop + j) for j in range(4)])

    def spread(pieces):
        return [pieces[0]] + [from_plane(pieces[hop], hop) for hop in (1, 2, 3)]

    strip = shape((BS, 2 * BS), BF16)
    view = front.reshape(tiles, BS, 8, 2, HALF).transpose(0, 1, 3, 2, 4)
    view = view.reshape(tiles * BS, 2, 8, HALF)
    away = pl.BlockSpec(memory_space=pl.ANY)
    begun = pl.pallas_call(
        begin,
        out_shape=[strip] * 4 + [shape((8, PIECE, BS), F32)] * 4 + [shape((tiles * BS, BS), F32)],
        in_specs=[SMEM, SMEM, VMEM, VMEM, away, away],
        out_specs=[VMEM] * 9,
        scratch_shapes=[pltpu.VMEM((BS * 16, HALF), F32), pltpu.SemaphoreType.DMA((3,))],
        compiler_params=pltpu.CompilerParams(vmem_limit_bytes=LIMIT),
        cost_estimate=pl.CostEstimate(flops=2**30, bytes_accessed=8 * 2**20, transcendentals=0),
    )(
        child_map, rc, child_update.reshape(2, BS, 2 * BS), pivots,
        view.reshape(tiles * BS * 16, HALF), view,
    )
    zs, cuts, front_left = begun[:4], begun[4:8], begun[8]
    zs = [zs[0]] + [along_z(zs[hop], hop) for hop in (1, 2, 3)]

    moved = spread(cuts)

    front_left = lax.all_gather(front_left, "pcol", axis=0, tiled=False)

    thin = shape((PIECE, 2 * BS), BF16)
    zs, unused = lax.optimization_barrier((zs, moved[1]))
    picked = call(
        pick_rows, [thin] * 4 + [strip] * 4, [child_map, rc, pivots, *zs], flops=20 * 2**30
    )
    thin = spread(picked[:4])
    ys = [picked[4]] + [along_y(picked[4 + hop], hop) for hop in (1, 2, 3)]

    (thin,) = call(
        mix,
        [shape((3 * PIECE + 16, BS), I16)],
        [rc, *thin, *moved],
        smem=1,
        scratch=[pltpu.VMEM((PIECE, 2 * BS), F32), pltpu.VMEM((PIECE, BS), F32)],
    )
    thin = lax.all_gather(thin, "pcol", axis=0, tiled=False)
    (child,) = call(pack, [shape((4, BS, 2 * BS), BF16)], [rc, *ys], smem=1)
    thin, child = lax.optimization_barrier((thin, child))
    (code,) = call(
        assemble,
        [shape((12 * PIECE + 16, BS), I16)],
        [child_map, rc, *moved, thin],
        scratch=[pltpu.VMEM((8, PIECE, BS), F32), pltpu.VMEM((NPIV, PIECE, BS), F32)],
    )

    child = lax.all_gather(child, "pcol", axis=0, tiled=False)
    top = lax.all_gather(code, "prow", axis=0, tiled=False)

    done = run_finish(child_map, rc, pivots, top, front_left, view, cuts, child)
    done = done.reshape(tiles, BS, 2, 8, HALF).transpose(0, 1, 3, 2, 4)
    return done.reshape(front.shape)


def solution(mesh):
    return jax.shard_map(
        shards,
        mesh=mesh,
        in_specs=(P(None, "prow", None, "pcol"), P("prow", "pcol"), P(), P()),
        out_specs=P(None, "prow", None, "pcol"),
        check_vma=False,
    )
```

time: 186 us -> 178 us (0.957)
  Pallas kernels: 74.3 us -> 66.1 us
  waiting for transfers between devices: 5.69 us -> 9.46 us
  blocking collectives: 65.3 us -> 62.8 us
    pallas_call x3 -> x2, Pallas kernels: 62.4 us -> 54.6 us  [the longest x1 47.3 us: run_finish(): pl.pallas_call(finish, out_shape=shape(view.shape, F32), in_specs=[SMEM,...]
    all_gather x1, waiting for transfers between devices: 0.02 us -> 3.65 us  [shards(): child = lax.all_gather(child, 'pcol', axis=0, tiled=False)]
    all_gather x1, blocking collectives: 45 us -> 42.8 us  [shards(): top = lax.all_gather(code, 'prow', axis=0, tiled=False)]
  transfers between devices with their start and end apart: 14 -> 14, of which waited for: 2 -> 3; matrix products, arithmetic and copies ran while one was open for 0% -> 0% of each run, Pallas kernels for 9% -> 7%
where the time goes in v11:
time: 178 us; the launch traced here: 177 us
  Pallas kernels  66.1 us (37%)
  blocking collectives  62.8 us (35%)
  starting transfers between devices  22.3 us (13%)
  between operations  13.6 us (8%)
  waiting for transfers between devices  9.46 us (5%)
  local copies, waits for them, and re-layouts  2.27 us (1%)
    pallas_call x1, Pallas kernels, run_finish(): pl.pallas_call(finish, out_shape=shape(view.shape, F32), in_specs=[SMEM,...  47.3 us
    all_gather x1, blocking collectives, shards(): top = lax.all_gather(code, 'prow', axis=0, tiled=False)  42.8 us
    all_gather x1, blocking collectives, shards(): thin = lax.all_gather(thin, 'pcol', axis=0, tiled=False)  20 us
    ppermute x6, starting transfers between devices, from_plane(): return lax.ppermute(a, 'prow', [(j, 4 * hop + j) for j in range(4)])  13.1 us
    pallas_call x4, Pallas kernels, call(): pl.pallas_call(body, out_shape=outs, in_specs=[SMEM] * smem + [VMEM] * (l...  11.6 us
    pallas_call x1, Pallas kernels, shards(): pl.pallas_call(begin, out_shape=[strip] * 4 + [shape((8, PIECE, BS), F32)...  7.25 us
    ppermute x3, waiting for transfers between devices, along_z(): lax.ppermute(a, 'prow', [(4 * i + j, 4 * i + (j + hop) % 4) for i in rang...  5.74 us
    ppermute x3, starting transfers between devices, along_z(): lax.ppermute(a, 'prow', [(4 * i + j, 4 * i + (j + hop) % 4) for i in rang...  5.73 us
  transfers between devices with their start and end apart: 14, of which 3 were waited for; matrix products, arithmetic and copies ran while one was open for 0% of the time, Pallas kernels for 7%

profile of v11, /device:TPU:1, one launch (start us, length us, event | category | flops | bytes accessed | tf_op | source)
XLA Modules:
  0.0 177.2 jit_solution(12353751463950502344)
XLA Ops:
  7.2 7.2 %shard_map.46 = (bf16[256,512]{1,0:T(8,128)(2,1)}, bf16[256,512]{1,0:T(8,128)(2,1)}, bf16[256,512]{1,0:T(8,128)(2,1)}, bf16[256,512]{1,0:T(8,128)(2,1)}, f32[8,6...) custom-call(s32[2,16]{1,0:T(2,128)} %map_ref.7, ...), custom_call_target="tpu_custom_call" | custom-call | flops 1073741824 | bytes 8388608 | tf_op jit(solution)/shard_map/pallas_call | solution.py:610
  14.5 4.1 %collective-permute-start = (f32[8,64,256]{2,1,0:T(8,128)}, f32[8,64,256]{2,1,0:T(8,128)S(1)}, u32[]{:S(2)}, u32[]{:S(2)}) collective-permute-start(f32[8,64,256]{2,1,0:T(8,128)} %get-tuple-element.29.f1), channel_id=1, source_target_pairs={{0,32},{8,40},{16,48},{24,56},{1,33},{9,41},{17,49},{25,57},{2,34}... | collective-permute-start | bytes 1572872 | tf_op jit(solution)/shard_map/ppermute | solution.py:601
  18.6 1.7 collective-permute-start.3
  20.3 3.3 %collective-permute-start.4 = (bf16[256,512]{1,0:T(8,128)(2,1)}, bf16[256,512]{1,0:T(8,128)(2,1)S(1)}, u32[]{:S(2)}, u32[]{:S(2)}) collective-permute-start(bf16[256,512]{1,0:T(8,128)(2,1)} %get-tuple-element.34), channel_id=1, source_target_pairs={{0,16},{8,24},{16,0},{24,8},{32,48},{40,56},{48,32},{56,40},{64,80... | collective-permute-start | bytes 786440 | tf_op jit(solution)/shard_map/ppermute | solution.py:591
  23.6 0.7 collective-permute-start.5
  24.3 2.3 %collective-permute-start.1 = (f32[8,64,256]{2,1,0:T(8,128)}, f32[8,64,256]{2,1,0:T(8,128)S(1)}, u32[]{:S(2)}, u32[]{:S(2)}) collective-permute-start(f32[8,64,256]{2,1,0:T(8,128)} %get-tuple-element.30.f2), channel_id=1, source_target_pairs={{0,64},{8,72},{16,80},{24,88},{1,65},{9,73},{17,81},{25,89},{2,66}... | collective-permute-start | bytes 1572872 | tf_op jit(solution)/shard_map/ppermute | solution.py:601
  26.6 1.7 collective-permute-done.3.refs_1_
  28.3 2.4 %collective-permute-start.2 = (f32[8,64,256]{2,1,0:T(8,128)}, f32[8,64,256]{2,1,0:T(8,128)S(1)}, u32[]{:S(2)}, u32[]{:S(2)}) collective-permute-start(f32[8,64,256]{2,1,0:T(8,128)} %get-tuple-element.31.f3), channel_id=1, source_target_pairs={{0,96},{8,104},{16,112},{24,120},{1,97},{9,105},{17,113},{25,121},... | collective-permute-start | bytes 1572872 | tf_op jit(solution)/shard_map/ppermute | solution.py:601
  30.8 4.0 %collective-permute-done.4.refs_2_ = bf16[256,512]{1,0:T(8,128)(2,1)S(1)} collective-permute-done((bf16[256,512]{1,0:T(8,128)(2,1)}, bf16[256,512]{1,0:T(8,128)(2,1)S(1)}, u32[]{:S(2)}, u32[]{:S(2)}) %collective-permute-start.4) | collective-permute-done | bytes 262176 | tf_op jit(solution)/shard_map/ppermute | solution.py:591
  34.8 0.7 copy-done.10
  35.6 3.1 %shard_map.47 = (bf16[64,512]{1,0:T(8,128)(2,1)}, bf16[64,512]{1,0:T(8,128)(2,1)}, bf16[64,512]{1,0:T(8,128)(2,1)}, bf16[64,512]{1,0:T(8,128)(2,1)}, bf16[256,51...) custom-call(s32[2,16]{1,0:T(2,128)} %map_ref.7, ...), custom_call_target="tpu_custom_call" | custom-call | flops 21474836480 | bytes 2363528 | tf_op jit(solution)/shard_map/pallas_call | solution.py:34
  38.7 1.3 collective-permute-start.6
  40.0 1.7 collective-permute-start.7
  41.7 1.3 collective-permute-start.8
  43.1 1.4 collective-permute-start.10
  44.5 2.0 %collective-permute-start.11 = (bf16[256,512]{1,0:T(8,128)(2,1)}, bf16[256,512]{1,0:T(8,128)(2,1)S(1)}, u32[]{:S(2)}, u32[]{:S(2)}) collective-permute-start(bf16[256,512]{1,0:T(8,128)(2,1)} %get-tuple-element.47), channel_id=1, source_target_pairs={{0,96},{8,104},{16,112},{24,120},{32,0},{40,8},{48,16},{56,24},{64... | collective-permute-start | bytes 786440 | tf_op jit(solution)/shard_map/ppermute | solution.py:596
  47.1 2.6 %shard_map.48 = s16[208,256]{1,0:T(8,128)(2,1)} custom-call(s32[2]{0:T(128)} %pad_add_fusion.rc_ref, bf16[64,512]{1,0:T(8,128)(2,1)} %get-tuple-element.40.t0, bf16[64,512]{1,0:T(8,128)(2,1)} %copy-done.6, bf16[64,512]{1,0:T(8,128)(2,1)} %copy-done.7, bf16[64,512]{1,0:T(8,128)(2,1)} %copy-done.8, f32[8,64,256]{2,1,0:T(8,128)} %get-tuple-element.28.f0, ...), custom_call_target="tpu_custom_call" | custom-call | bytes 2465800 | tf_op jit(solution)/shard_map/pallas_call | solution.py:34
  49.8 20.0 %all-gather = s16[1664,256]{1,0:T(8,128)(2,1)} all-gather(s16[208,256]{1,0:T(8,128)(2,1)} %shard_map.48), channel_id=2, replica_groups=mesh['prow'=16,'pcol'=8] {'pcol'}, dimensions={0}, use_global_device_ids=true | all-gather | bytes 958464 | tf_op jit(solution)/shard_map/all_gather | solution.py:644
  69.8 0.7 copy-done.3
  70.7 2.2 %shard_map.49 = bf16[4,256,512]{2,1,0:T(8,128)(2,1)} custom-call(s32[2]{0:T(128)} %pad_add_fusion.rc_ref, bf16[256,512]{1,0:T(8,128)(2,1)} %get-tuple-element.44.h0, bf16[256,512]{1,0:T(8,128)(2,1)} %copy-done.3, bf16[256,512]{1,0:T(8,128)(2,1)} %copy-done.4, bf16[256,512]{1,0:T(8,128)(2,1)} %copy-done.5), custom_call_target="tpu_custom_call" | custom-call | bytes 2097160 | tf_op jit(solution)/shard_map/pallas_call | solution.py:34
  72.9 3.6 %shard_map.50 = s16[784,256]{1,0:T(8,128)(2,1)} custom-call(s32[2,16]{1,0:T(2,128)} %map_ref.7, s32[2]{0:T(128)} %pad_add_fusion.rc_ref, f32[8,64,256]{2,1,0:T(8,128)} %get-tuple-element.28.f0, f32[8,64,256]{2,1,0:T(8,128)} %copy-done, f32[8,64,256]{2,1,0:T(8,128)} %copy-done.1, f32[8,64,256]{2,1,0:T(8,128)} %copy-done.2, s16[8,208,256]{2,1,0:T(8,128)(2,1)} %bitcast.23), custom_call_target="tpu_custom_call" | custom-call | bytes 3350664 | tf_op jit(solution)/shard_map/pallas_call | solution.py:34
  76.5 42.8 %all-gather.11 = s16[12544,256]{1,0:T(8,128)(2,1)} all-gather(s16[784,256]{1,0:T(8,128)(2,1)} %shard_map.50), channel_id=3, replica_groups=mesh['prow'=16,'pcol'=8] {'prow'}, dimensions={0}, use_global_device_ids=true | all-gather | bytes 6823936 | tf_op jit(solution)/shard_map/all_gather | solution.py:655
  119.4 3.7 %all-gather.10.cloned.1.call-done = bf16[32,256,512]{2,1,0:T(8,128)(2,1)} async-done(((bf16[4,256,512]{2,1,0:T(8,128)(2,1)}), bf16[32,256,512]{2,1,0:T(8,128)(2,1)}) %all-gather.10.cloned.1.call-update) | async-done | bytes 8388624 | tf_op jit(solution)/shard_map/all_gather | solution.py:654
  123.0 47.3 %shard_map.51 = f32[1024,2,8,128]{3,2,1,0:T(8,128)} custom-call(s32[2,16]{1,0:T(2,128)} %map_ref.7, s32[2]{0:T(128)} %pad_add_fusion.rc_ref, s32[4,256]{1,0:T(4,128)} %pivots_ref.5, s16[16,784,256]{2,1,0:T(8,128)(2,1)} %bitcast.22, f32[8,1024,256]{2,1,0:T(8,128)} %bitcast.25, f32[1024,2,8,128]{3,2,1,0:T(8,128)} %bitcast.21, ...), custom_call_target="tpu_custom_call" | custom-call | flops 24696061952 | bytes 33554432 | tf_op jit(solution)/shard_map/pallas_call | solution.py:555
  (39 shorter events, 1.8 us)
Async XLA Ops:
  6.5 112.8 %all-gather.8.cloned.1.call-start = ((), (), s32[]{:S(2)}) async-start(), calls=%async_computation | async-start | bytes 9437184 | tf_op jit(solution)/shard_map/all_gather | solution.py:627
  14.5 108.6 %all-gather.10.cloned.1.call-start = ((), (), s32[]{:S(2)}) async-start(), calls=%async_computation.1 | async-start | bytes 9437184 | tf_op jit(solution)/shard_map/all_gather | solution.py:654
  14.5 20.3 %collective-permute-start = (f32[8,64,256]{2,1,0:T(8,128)}, f32[8,64,256]{2,1,0:T(8,128)S(1)}, u32[]{:S(2)}, u32[]{:S(2)}) collective-permute-start(f32[8,64,256]{2,1,0:T(8,128)} %get-tuple-element.29.f1), channel_id=1, source_target_pairs={{0,32},{8,40},{16,48},{24,56},{1,33},{9,41},{17,49},{25,57},{2,34}... | collective-permute-start | bytes 1572872 | tf_op jit(solution)/shard_map/ppermute | solution.py:601
  18.6 9.8 %collective-permute-start.3 = (bf16[256,512]{1,0:T(8,128)(2,1)}, bf16[256,512]{1,0:T(8,128)(2,1)S(1)}, u32[]{:S(2)}, u32[]{:S(2)}) collective-permute-start(bf16[256,512]{1,0:T(8,128)(2,1)} %get-tuple-element.33), channel_id=1, source_target_pairs={{0,8},{8,16},{16,24},{24,0},{32,40},{40,48},{48,56},{56,32},{64,72... | collective-permute-start | bytes 786440 | tf_op jit(solution)/shard_map/ppermute | solution.py:591
  20.3 14.5 %collective-permute-start.4 = (bf16[256,512]{1,0:T(8,128)(2,1)}, bf16[256,512]{1,0:T(8,128)(2,1)S(1)}, u32[]{:S(2)}, u32[]{:S(2)}) collective-permute-start(bf16[256,512]{1,0:T(8,128)(2,1)} %get-tuple-element.34), channel_id=1, source_target_pairs={{0,16},{8,24},{16,0},{24,8},{32,48},{40,56},{48,32},{56,40},{64,80... | collective-permute-start | bytes 786440 | tf_op jit(solution)/shard_map/ppermute | solution.py:591
  23.6 11.2 %collective-permute-start.5 = (bf16[256,512]{1,0:T(8,128)(2,1)}, bf16[256,512]{1,0:T(8,128)(2,1)S(1)}, u32[]{:S(2)}, u32[]{:S(2)}) collective-permute-start(bf16[256,512]{1,0:T(8,128)(2,1)} %get-tuple-element.35), channel_id=1, source_target_pairs={{0,24},{8,0},{16,8},{24,16},{32,56},{40,32},{48,40},{56,48},{64,88... | collective-permute-start | bytes 786440 | tf_op jit(solution)/shard_map/ppermute | solution.py:591
  24.3 18.7 %collective-permute-start.1 = (f32[8,64,256]{2,1,0:T(8,128)}, f32[8,64,256]{2,1,0:T(8,128)S(1)}, u32[]{:S(2)}, u32[]{:S(2)}) collective-permute-start(f32[8,64,256]{2,1,0:T(8,128)} %get-tuple-element.30.f2), channel_id=1, source_target_pairs={{0,64},{8,72},{16,80},{24,88},{1,65},{9,73},{17,81},{25,89},{2,66}... | collective-permute-start | bytes 1572872 | tf_op jit(solution)/shard_map/ppermute | solution.py:601
  28.3 7.3 %copy-start.9 = (bf16[256,512]{1,0:T(8,128)(2,1)}, bf16[256,512]{1,0:T(8,128)(2,1)S(1)}, u32[]{:S(2)}) copy-start(bf16[256,512]{1,0:T(8,128)(2,1)S(1)} %collective-permute-done.3.refs_1_) | copy-start | bytes 786436
  28.3 14.8 %collective-permute-start.2 = (f32[8,64,256]{2,1,0:T(8,128)}, f32[8,64,256]{2,1,0:T(8,128)S(1)}, u32[]{:S(2)}, u32[]{:S(2)}) collective-permute-start(f32[8,64,256]{2,1,0:T(8,128)} %get-tuple-element.31.f3), channel_id=1, source_target_pairs={{0,96},{8,104},{16,112},{24,120},{1,97},{9,105},{17,113},{25,121},... | collective-permute-start | bytes 1572872 | tf_op jit(solution)/shard_map/ppermute | solution.py:601
  34.8 0.7 copy-start.10
  34.8 0.8 copy-start.11
  35.6 3.1 %copy-start = (f32[8,64,256]{2,1,0:T(8,128)}, f32[8,64,256]{2,1,0:T(8,128)S(1)}, u32[]{:S(2)}) copy-start(f32[8,64,256]{2,1,0:T(8,128)S(1)} %collective-permute-done.f1) | copy-start | bytes 1572868
  38.7 5.8 %collective-permute-start.6 = (bf16[64,512]{1,0:T(8,128)(2,1)}, bf16[64,512]{1,0:T(8,128)(2,1)S(1)}, u32[]{:S(2)}, u32[]{:S(2)}) collective-permute-start(bf16[64,512]{1,0:T(8,128)(2,1)} %get-tuple-element.41), channel_id=1, source_target_pairs={{0,32},{8,40},{16,48},{24,56},{1,33},{9,41},{17,49},{25,57},{2,34}... | collective-permute-start | bytes 196616 | tf_op jit(solution)/shard_map/ppermute | solution.py:601
  40.0 6.5 %collective-permute-start.7 = (bf16[64,512]{1,0:T(8,128)(2,1)}, bf16[64,512]{1,0:T(8,128)(2,1)S(1)}, u32[]{:S(2)}, u32[]{:S(2)}) collective-permute-start(bf16[64,512]{1,0:T(8,128)(2,1)} %get-tuple-element.42), channel_id=1, source_target_pairs={{0,64},{8,72},{16,80},{24,88},{1,65},{9,73},{17,81},{25,89},{2,66}... | collective-permute-start | bytes 196616 | tf_op jit(solution)/shard_map/ppermute | solution.py:601
  41.7 4.8 %collective-permute-start.8 = (bf16[64,512]{1,0:T(8,128)(2,1)}, bf16[64,512]{1,0:T(8,128)(2,1)S(1)}, u32[]{:S(2)}, u32[]{:S(2)}) collective-permute-start(bf16[64,512]{1,0:T(8,128)(2,1)} %get-tuple-element.43), channel_id=1, source_target_pairs={{0,96},{8,104},{16,112},{24,120},{1,97},{9,105},{17,113},{25,121},... | collective-permute-start | bytes 196616 | tf_op jit(solution)/shard_map/ppermute | solution.py:601
  43.0 3.5 %copy-start.1 = (f32[8,64,256]{2,1,0:T(8,128)}, f32[8,64,256]{2,1,0:T(8,128)S(1)}, u32[]{:S(2)}) copy-start(f32[8,64,256]{2,1,0:T(8,128)S(1)} %collective-permute-done.1.f2) | copy-start | bytes 1572868
  43.0 26.8 %collective-permute-start.9 = (bf16[256,512]{1,0:T(8,128)(2,1)}, bf16[256,512]{1,0:T(8,128)(2,1)S(1)}, u32[]{:S(2)}, u32[]{:S(2)}) collective-permute-start(bf16[256,512]{1,0:T(8,128)(2,1)} %get-tuple-element.45), channel_id=1, source_target_pairs={{0,32},{8,40},{16,48},{24,56},{32,64},{40,72},{48,80},{56,88},{64,... | collective-permute-start | bytes 786440 | tf_op jit(solution)/shard_map/ppermute | solution.py:596
  43.1 3.4 %copy-start.2 = (f32[8,64,256]{2,1,0:T(8,128)}, f32[8,64,256]{2,1,0:T(8,128)S(1)}, u32[]{:S(2)}) copy-start(f32[8,64,256]{2,1,0:T(8,128)S(1)} %collective-permute-done.2.f3) | copy-start | bytes 1572868
  43.1 26.7 %collective-permute-start.10 = (bf16[256,512]{1,0:T(8,128)(2,1)}, bf16[256,512]{1,0:T(8,128)(2,1)S(1)}, u32[]{:S(2)}, u32[]{:S(2)}) collective-permute-start(bf16[256,512]{1,0:T(8,128)(2,1)} %get-tuple-element.46), channel_id=1, source_target_pairs={{0,64},{8,72},{16,80},{24,88},{32,96},{40,104},{48,112},{56,120},{... | collective-permute-start | bytes 786440 | tf_op jit(solution)/shard_map/ppermute | solution.py:596
  44.5 2.0 %copy-start.6 = (bf16[64,512]{1,0:T(8,128)(2,1)}, bf16[64,512]{1,0:T(8,128)(2,1)S(1)}, u32[]{:S(2)}) copy-start(bf16[64,512]{1,0:T(8,128)(2,1)S(1)} %collective-permute-done.6.t1) | copy-start | bytes 196612
  44.5 25.3 %collective-permute-start.11 = (bf16[256,512]{1,0:T(8,128)(2,1)}, bf16[256,512]{1,0:T(8,128)(2,1)S(1)}, u32[]{:S(2)}, u32[]{:S(2)}) collective-permute-start(bf16[256,512]{1,0:T(8,128)(2,1)} %get-tuple-element.47), channel_id=1, source_target_pairs={{0,96},{8,104},{16,112},{24,120},{32,0},{40,8},{48,16},{56,24},{64... | collective-permute-start | bytes 786440 | tf_op jit(solution)/shard_map/ppermute | solution.py:596
  69.8 0.7 copy-start.3
  69.8 0.8 copy-start.4
  69.8 0.8 copy-start.5
  (2 other events, 1.3 us)
Sparse Core Ops, SparseCore 0:
  14.6 56.7 all-gather.7
  73.1 49.9 all-gather.9

commit v12 on v11

--- a/solution.py
+++ b/solution.py
@@ -195,20 +195,26 @@
     out_ref[3 * PIECE :] = jnp.broadcast_to(n[:1, :1].astype(I32), (16, BS)).astype(I16)
 
 
-def assemble(map_ref, rc_ref, f0, f1, f2, f3, thin, code_ref, work, corner):
+def assemble(map_ref, rc_ref, f0, f1, f2, f3, thin, code_ref, work, corner, arrived):
     row, col = rc_ref[0], rc_ref[1]
     y = row // 4
     for piece, source in enumerate((f0, f1, f2, f3)):
 
         @pl.when(y == piece)
-        def _(source=source):
-            work[...] = source[...]
+        def _(piece=piece, source=source):
+            pltpu.make_async_copy(source, work, arrived.at[piece]).start()
 
     for k in range(NPIV):
         corner[k] = decode(
             thin[k, 2 * PIECE : 3 * PIECE].astype(I32), thin[k, 3 * PIECE :].astype(I32)
         )
     n = jnp.full((8, HALF), CHILD_LEVEL)
+    for piece, source in enumerate((f0, f1, f2, f3)):
+
+        @pl.when(y == piece)
+        def _(piece=piece, source=source):
+            pltpu.make_async_copy(source, work, arrived.at[piece]).wait()
+
     for index in range(16):
         parent = map_ref[0, index]
         low = (index % 2) * PIECE
@@ -247,12 +253,6 @@
     for at, n in enumerate((n, first)):
         scales = jnp.where(line == at, n[:1, :1], scales)
     code_ref[12 * PIECE :] = scales.astype(I32).astype(I16)
-
-
-def pack(rc_ref, h0, h1, h2, h3, out_ref):
-    y = rc_ref[0] // 4
-    for shift, source in enumerate((h0, h1, h2, h3)):
-        out_ref[(y - shift + 4) % 4] = source[...]
 
 
 def factor_corner(code_ref, level_ref, work, chi, clo, xhi, xlo):
@@ -293,14 +293,17 @@
 
 
 def finish(
-    map_ref, rc_ref, pivots_ref, top_ref, left_from, front_from, f0, f1, f2, f3, child_ref, out_ref,
+    map_ref, rc_ref, top_ref, left_from, front_from, child_ref, out_ref,
     corner_ref, level_ref, code_ref, left_ref, near_ref, front,
     work, chi, clo, xhi, xlo, uhi, ulo, u8, lower, l8, own_col, own_block, own_row, parts,
-    peak, arrived, own_arrived, ready, sent,
+    peak, arrived, ready, sent,
 ):
     row, col = rc_ref[0], rc_ref[1]
     top_row = row < NPIV
     height = SPAN * BS
+
+    def hop_of(slot):
+        return (row // 4 - slot + 4) % 4
 
     def left_copy(step):
         rows = pl.ds(step * height, height)
@@ -316,12 +319,15 @@
         pltpu.make_async_copy(top_ref.at[:, codes + 4 * PIECE :], level_ref, ready.at[1]),
     ]
     code_copy = pltpu.make_async_copy(top_ref.at[:, :codes], code_ref, ready.at[2])
-    near_copy = pltpu.make_async_copy(child_ref.at[:2, :2], near_ref, ready.at[4])
+    near_copies = [
+        pltpu.make_async_copy(child_ref.at[:2, hop_of(slot)], near_ref.at[:, slot], ready.at[at])
+        for slot, at in ((0, 4), (1, 7))
+    ]
     for copy in corner_copies:
         copy.start()
     for copy in corner_copies:
         copy.wait()
-    for copy in (code_copy, left_copy(0), near_copy, front_copy(0), front_copy(1)):
+    for copy in (code_copy, left_copy(0), *near_copies, front_copy(0), front_copy(1)):
         copy.start()
 
     def lost(s, first, count):
@@ -337,7 +343,7 @@
                 start = pl.multiple_of((where % 2) * BS, BS)
                 index = 4 * (slot % 2) + source
                 copy = pltpu.make_async_copy(
-                    child_ref.at[where // 2, slot, :, pl.ds(start, BS)],
+                    child_ref.at[where // 2, hop_of(slot), :, pl.ds(start, BS)],
                     parts.at[index],
                     arrived.at[index],
                 )
@@ -346,17 +352,6 @@
                 def _(copy=copy, index=index, tile=(parent // 16) % SPAN, s=value // 8):
                     act(copy, index, tile, s)
 
-    def own_copies():
-        return [
-            pltpu.make_async_copy(source, own_row.at[piece], own_arrived.at[piece])
-            for piece, source in enumerate((f0, f1, f2, f3))
-        ]
-
-    @pl.when(top_row)
-    def _():
-        for copy in own_copies():
-            copy.start()
-
     factor_corner(corner_ref, level_ref, work, chi, clo, xhi, xlo)
     for r in range(NPIV):
         for c in range(NPIV):
@@ -364,11 +359,6 @@
             @pl.when((row == r) & (col == c))
             def _(r=r, c=c):
                 own_block[...] = work[c, block(r)]
-
-    @pl.when(top_row)
-    def _():
-        for copy in own_copies():
-            copy.wait()
 
     code_copy.wait()
     for group in range(2):
@@ -386,6 +376,12 @@
                 uhi[group, block(k), block(q)], ulo[block(k), block(q)] = split(
                     work[q, block(k)]
                 )
+
+            @pl.when(row == k)
+            def _(k=k, group=group):
+                for q in range(WIDE):
+                    own_row[WIDE * group + q] = work[q, block(k)]
+
             if k + 1 == NPIV:
                 break
             below = slice((k + 1) * BS, NPIV * BS)
@@ -398,17 +394,6 @@
                 for q in range(2):
                     at = 2 * pair + q
                     work[at, below] = work[at, below] - taken[:, block(q)]
-                for j in range(k + 1, NPIV):
-
-                    @pl.when(row == j)
-                    def _(taken=taken, pair=pair, j=j, k=k, group=group):
-                        for piece in range(4):
-                            low = (j - k - 1) * BS + piece * PIECE
-                            for q in range(2):
-                                tile = WIDE * group + 2 * pair + q
-                                own_row[piece, tile] = (
-                                    own_row[piece, tile] - taken[low : low + PIECE, block(q)]
-                                )
 
         peak[group] = jnp.maximum(jnp.max(jnp.abs(uhi[group].astype(F32))), 1e-30)
         scale = 256.0 / peak[group]
@@ -428,7 +413,8 @@
         @pl.when(step == 0)
         def _():
             left_copy(1).start()
-            near_copy.wait()
+            for copy in near_copies:
+                copy.wait()
 
         for slot in range(2):
             parent = row_of(map_ref, row, slot)
@@ -484,19 +470,13 @@
         @pl.when(top_tile)
         def _():
             for s in range(2 * WIDE):
-                for piece in range(4):
-                    lost(s, piece * PIECE, PIECE)[...] = -own_row[piece, s]
+                lost(s, 0, BS)[...] = -own_row[s]
 
         def add(copy, index, tile, s):
             copy.wait()
             place = lost(s, pl.multiple_of(tile * BS, BS), BS)
-            turn = top_tile & (tile == 0)
-
-            @pl.when(turn)
-            def _():
-                place[...] = place[...] - dot(one_hot(pivots_ref, row), parts[index])
-
-            @pl.when(jnp.logical_not(turn))
+
+            @pl.when(jnp.logical_not(top_tile & (tile == 0)))
             def _():
                 place[...] = place[...] - parts[index].astype(F32)
 
@@ -550,12 +530,12 @@
 LINES = 32
 
 
-def run_finish(child_map, rc, pivots, top, front_left, view, cuts, child):
+def run_finish(child_map, rc, top, front_left, view, child):
     away = pl.BlockSpec(memory_space=pl.ANY)
     return pl.pallas_call(
         finish,
         out_shape=shape(view.shape, F32),
-        in_specs=[SMEM, SMEM, VMEM] + [away] * 8,
+        in_specs=[SMEM, SMEM] + [away] * 4,
         out_specs=away,
         scratch_shapes=[
             pltpu.VMEM((16, 4 * PIECE, BS), I16), pltpu.VMEM((16, 16, BS), I16),
@@ -568,17 +548,17 @@
             pltpu.VMEM((2, 8 * BS, WIDE * BS), F8),
             pltpu.VMEM((2 * SPAN * BS, 4 * BS), BF16), pltpu.VMEM((SPAN * BS, 8 * BS), F8),
             pltpu.VMEM((SPAN * BS, BS), F32), pltpu.VMEM((BS, BS), F32),
-            pltpu.VMEM((4, 8, PIECE, BS), F32),
+            pltpu.VMEM((8, BS, BS), F32),
             pltpu.VMEM((8, BS, BS), BF16),
             pltpu.SMEM((2,), F32),
-            pltpu.SemaphoreType.DMA((8,)), pltpu.SemaphoreType.DMA((4,)),
-            pltpu.SemaphoreType.DMA((7,)), pltpu.SemaphoreType.DMA((8,)),
+            pltpu.SemaphoreType.DMA((8,)),
+            pltpu.SemaphoreType.DMA((8,)), pltpu.SemaphoreType.DMA((8,)),
         ],
         compiler_params=pltpu.CompilerParams(vmem_limit_bytes=LIMIT),
         cost_estimate=pl.CostEstimate(
             flops=23 * 2**30, bytes_accessed=32 * 2**20, transcendentals=0
         ),
-    )(child_map, rc, pivots, top, front_left, view, *cuts, child)
+    )(child_map, rc, top, front_left, view, child)
 
 
 def shards(front, child_update, child_map, pivots):
@@ -634,27 +614,38 @@
     thin = spread(picked[:4])
     ys = [picked[4]] + [along_y(picked[4 + hop], hop) for hop in (1, 2, 3)]
 
-    (thin,) = call(
+    thin = pl.pallas_call(
         mix,
-        [shape((3 * PIECE + 16, BS), I16)],
-        [rc, *thin, *moved],
-        smem=1,
-        scratch=[pltpu.VMEM((PIECE, 2 * BS), F32), pltpu.VMEM((PIECE, BS), F32)],
-    )
+        grid=(1,),
+        out_shape=shape((3 * PIECE + 16, BS), I16),
+        in_specs=[SMEM]
+        + [pl.BlockSpec((PIECE, 2 * BS), lambda t: (0, 0))] * 4
+        + [pl.BlockSpec((1, PIECE, BS), lambda t: (0, 0, 0))] * 4,
+        out_specs=pl.BlockSpec((3 * PIECE + 16, BS), lambda t: (0, 0)),
+        scratch_shapes=[pltpu.VMEM((PIECE, 2 * BS), F32), pltpu.VMEM((PIECE, BS), F32)],
+        compiler_params=pltpu.CompilerParams(vmem_limit_bytes=LIMIT),
+        cost_estimate=pl.CostEstimate(flops=0, bytes_accessed=2**20, transcendentals=0),
+    )(rc, *thin, *moved)
     thin = lax.all_gather(thin, "pcol", axis=0, tiled=False)
-    (child,) = call(pack, [shape((4, BS, 2 * BS), BF16)], [rc, *ys], smem=1)
+    child = jnp.stack(ys)
     thin, child = lax.optimization_barrier((thin, child))
-    (code,) = call(
+    code = pl.pallas_call(
         assemble,
-        [shape((12 * PIECE + 16, BS), I16)],
-        [child_map, rc, *moved, thin],
-        scratch=[pltpu.VMEM((8, PIECE, BS), F32), pltpu.VMEM((NPIV, PIECE, BS), F32)],
-    )
+        out_shape=shape((12 * PIECE + 16, BS), I16),
+        in_specs=[SMEM, SMEM, away, away, away, away, VMEM],
+        out_specs=VMEM,
+        scratch_shapes=[
+            pltpu.VMEM((8, PIECE, BS), F32), pltpu.VMEM((NPIV, PIECE, BS), F32),
+            pltpu.SemaphoreType.DMA((4,)),
+        ],
+        compiler_params=pltpu.CompilerParams(vmem_limit_bytes=LIMIT),
+        cost_estimate=pl.CostEstimate(flops=0, bytes_accessed=2**21, transcendentals=0),
+    )(child_map, rc, *moved, thin)
 
     child = lax.all_gather(child, "pcol", axis=0, tiled=False)
     top = lax.all_gather(code, "prow", axis=0, tiled=False)
 
-    done = run_finish(child_map, rc, pivots, top, front_left, view, cuts, child)
+    done = run_finish(child_map, rc, top, front_left, view, child)
     done = done.reshape(tiles, BS, 2, 8, HALF).transpose(0, 1, 3, 2, 4)
     return done.reshape(front.shape)
 

time: 178 us -> 174 us (0.978)
  Pallas kernels: 66.1 us -> 60.1 us
  other arithmetic: 0.65 us -> 2.68 us
    pallas_call x4 -> x1, Pallas kernels: 11.6 us -> 3.08 us  [call(): pl.pallas_call(body, out_shape=outs, in_specs=[SMEM] * smem + [VMEM] * (l...]
    pallas_call x0 -> x2, Pallas kernels: none -> 6 us  [the longest x1 3.97 us: shards(): pl.pallas_call(assemble, out_shape=shape((12 * PIECE + 16, BS), I16), in_...]
    pallas_call x1, Pallas kernels: 47.3 us -> 43.8 us  [run_finish(): pl.pallas_call(finish, out_shape=shape(view.shape, F32), in_specs=[SMEM,...]
    another operation x0 -> x1, other arithmetic: none -> 2.04 us  [shards(): child = jnp.stack(ys)]
  transfers between devices with their start and end apart: 14 -> 14, of which waited for: 3 -> 3; matrix products, arithmetic and copies ran while one was open for 0% -> 1% of each run, Pallas kernels for 7% -> 5%
where the time goes in v12:
time: 174 us
  blocking collectives  62.9 us (36%)
  Pallas kernels  60.1 us (35%)
  starting transfers between devices  22.3 us (13%)
  between operations  13.6 us (8%)
  waiting for transfers between devices  10.7 us (6%)
  other arithmetic  2.68 us (2%)
    pallas_call x1, Pallas kernels, run_finish(): pl.pallas_call(finish, out_shape=shape(view.shape, F32), in_specs=[SMEM,...  43.8 us
    all_gather x1, blocking collectives, shards(): top = lax.all_gather(code, 'prow', axis=0, tiled=False)  42.9 us
    all_gather x1, blocking collectives, shards(): thin = lax.all_gather(thin, 'pcol', axis=0, tiled=False)  20 us
    ppermute x6, starting transfers between devices, from_plane(): return lax.ppermute(a, 'prow', [(j, 4 * hop + j) for j in range(4)])  13 us
    pallas_call x1, Pallas kernels, shards(): pl.pallas_call(begin, out_shape=[strip] * 4 + [shape((8, PIECE, BS), F32)...  7.25 us
    ppermute x3, starting transfers between devices, along_z(): lax.ppermute(a, 'prow', [(4 * i + j, 4 * i + (j + hop) % 4) for i in rang...  5.74 us
    ppermute x3, waiting for transfers between devices, along_z(): lax.ppermute(a, 'prow', [(4 * i + j, 4 * i + (j + hop) % 4) for i in rang...  5.73 us
    all_gather x1, waiting for transfers between devices, shards(): child = lax.all_gather(child, 'pcol', axis=0, tiled=False)  4.87 us
  transfers between devices with their start and end apart: 14, of which 3 were waited for; matrix products, arithmetic and copies ran while one was open for 1% of the time, Pallas kernels for 5%

profile of v12, /device:TPU:1, one launch (start us, length us, event | category | flops | bytes accessed | tf_op | source)
XLA Modules:
  0.0 173.6 jit_solution(3115393102199472747)
XLA Ops:
  6.5 0.6 pad_add_fusion.rc_ref
  7.2 7.2 %shard_map.46 = (bf16[256,512]{1,0:T(8,128)(2,1)}, bf16[256,512]{1,0:T(8,128)(2,1)}, bf16[256,512]{1,0:T(8,128)(2,1)}, bf16[256,512]{1,0:T(8,128)(2,1)}, f32[8,6...) custom-call(s32[2,16]{1,0:T(2,128)} %map_ref.7, ...), custom_call_target="tpu_custom_call" | custom-call | flops 1073741824 | bytes 8388608 | tf_op jit(solution)/shard_map/pallas_call | solution.py:590
  14.5 4.1 %collective-permute-start = (f32[8,64,256]{2,1,0:T(8,128)}, f32[8,64,256]{2,1,0:T(8,128)S(1)}, u32[]{:S(2)}, u32[]{:S(2)}) collective-permute-start(f32[8,64,256]{2,1,0:T(8,128)} %get-tuple-element.29), channel_id=1, source_target_pairs={{0,32},{8,40},{16,48},{24,56},{1,33},{9,41},{17,49},{25,57},{2,34}... | collective-permute-start | bytes 1572872 | tf_op jit(solution)/shard_map/ppermute | solution.py:581
  18.6 1.7 collective-permute-start.3
  20.3 3.3 %collective-permute-start.4 = (bf16[256,512]{1,0:T(8,128)(2,1)}, bf16[256,512]{1,0:T(8,128)(2,1)S(1)}, u32[]{:S(2)}, u32[]{:S(2)}) collective-permute-start(bf16[256,512]{1,0:T(8,128)(2,1)} %get-tuple-element.34), channel_id=1, source_target_pairs={{0,16},{8,24},{16,0},{24,8},{32,48},{40,56},{48,32},{56,40},{64,80... | collective-permute-start | bytes 786440 | tf_op jit(solution)/shard_map/ppermute | solution.py:571
  23.6 0.7 collective-permute-start.5
  24.3 2.3 %collective-permute-start.1 = (f32[8,64,256]{2,1,0:T(8,128)}, f32[8,64,256]{2,1,0:T(8,128)S(1)}, u32[]{:S(2)}, u32[]{:S(2)}) collective-permute-start(f32[8,64,256]{2,1,0:T(8,128)} %get-tuple-element.30), channel_id=1, source_target_pairs={{0,64},{8,72},{16,80},{24,88},{1,65},{9,73},{17,81},{25,89},{2,66}... | collective-permute-start | bytes 1572872 | tf_op jit(solution)/shard_map/ppermute | solution.py:581
  26.6 1.7 collective-permute-done.3.refs_1_
  28.3 2.4 %collective-permute-start.2 = (f32[8,64,256]{2,1,0:T(8,128)}, f32[8,64,256]{2,1,0:T(8,128)S(1)}, u32[]{:S(2)}, u32[]{:S(2)}) collective-permute-start(f32[8,64,256]{2,1,0:T(8,128)} %get-tuple-element.31), channel_id=1, source_target_pairs={{0,96},{8,104},{16,112},{24,120},{1,97},{9,105},{17,113},{25,121},... | collective-permute-start | bytes 1572872 | tf_op jit(solution)/shard_map/ppermute | solution.py:581
  30.8 4.0 %collective-permute-done.4.refs_2_ = bf16[256,512]{1,0:T(8,128)(2,1)S(1)} collective-permute-done((bf16[256,512]{1,0:T(8,128)(2,1)}, bf16[256,512]{1,0:T(8,128)(2,1)S(1)}, u32[]{:S(2)}, u32[]{:S(2)}) %collective-permute-start.4) | collective-permute-done | bytes 262176 | tf_op jit(solution)/shard_map/ppermute | solution.py:571
  34.8 0.7 copy-done.7
  35.6 3.1 %shard_map.47 = (bf16[64,512]{1,0:T(8,128)(2,1)}, bf16[64,512]{1,0:T(8,128)(2,1)}, bf16[64,512]{1,0:T(8,128)(2,1)}, bf16[64,512]{1,0:T(8,128)(2,1)}, bf16[256,51...) custom-call(s32[2,16]{1,0:T(2,128)} %map_ref.7, ...), custom_call_target="tpu_custom_call" | custom-call | flops 21474836480 | bytes 2363528 | tf_op jit(solution)/shard_map/pallas_call | solution.py:34
  38.7 1.3 collective-permute-start.6
  40.0 1.7 collective-permute-start.7
  41.7 1.3 collective-permute-start.8
  43.1 1.4 collective-permute-start.10
  44.5 2.0 %collective-permute-start.11 = (bf16[256,512]{1,0:T(8,128)(2,1)}, bf16[256,512]{1,0:T(8,128)(2,1)S(1)}, u32[]{:S(2)}, u32[]{:S(2)}) collective-permute-start(bf16[256,512]{1,0:T(8,128)(2,1)} %get-tuple-element.47), channel_id=1, source_target_pairs={{0,96},{8,104},{16,112},{24,120},{32,0},{40,8},{48,16},{56,24},{64... | collective-permute-start | bytes 786440 | tf_op jit(solution)/shard_map/ppermute | solution.py:576
  47.1 2.0 %shard_map.48 = s16[208,256]{1,0:T(8,128)(2,1)} custom-call(s32[2]{0:T(128)} %pad_add_fusion.rc_ref, bf16[64,512]{1,0:T(8,128)(2,1)} %get-tuple-element.40.t0, bf16[64,512]{1,0:T(8,128)(2,1)} %copy-done.3, bf16[64,512]{1,0:T(8,128)(2,1)} %copy-done.4, bf16[64,512]{1,0:T(8,128)(2,1)} %copy-done.5, f32[8,64,256]{2,1,0:T(8,128)} %get-tuple-element.28.f0, ...), custom_call_target="tpu_custom_call" | custom-call | bytes 1048576 | tf_op jit(solution)/shard_map/pallas_call | solution.py:617
  49.1 20.0 %all-gather = s16[1664,256]{1,0:T(8,128)(2,1)} all-gather(s16[208,256]{1,0:T(8,128)(2,1)} %shard_map.48), channel_id=2, replica_groups=mesh['prow'=16,'pcol'=8] {'pcol'}, dimensions={0}, use_global_device_ids=true | all-gather | bytes 958464 | tf_op jit(solution)/shard_map/all_gather | solution.py:629
  69.2 2.0 %pad_maximum_fusion = bf16[4,256,512]{2,1,0:T(8,128)(2,1)} fusion(bf16[1,256,512]{2,1,0:T(8,128)(2,1)S(1)} %bitcast.32, bf16[1,256,512]{2,1,0:T(8,128)(2,1)S(1)} %bitcast.31, bf16[1,256,512]{2,1,0:T(8,128)(2,1)S(1)} %bitcast.30, bf16[1,256,512]{2,1,0:T(8,128)(2,1)} %bitcast.29), kind=kLoop, calls=%fused_computation | loop fusion | flops 1572864 | bytes 2097152 | tf_op jit(solution)/shard_map/stack | solution.py:630
  71.2 4.0 %shard_map.49 = s16[784,256]{1,0:T(8,128)(2,1)} custom-call(s32[2,16]{1,0:T(2,128)} %map_ref.7, s32[2]{0:T(128)} %pad_add_fusion.rc_ref, f32[8,64,256]{2,1,0:T(8,128)} %get-tuple-element.28.f0, f32[8,64,256]{2,1,0:T(8,128)} %copy-done, f32[8,64,256]{2,1,0:T(8,128)} %copy-done.1, f32[8,64,256]{2,1,0:T(8,128)} %copy-done.2, s16[8,208,256]{2,1,0:T(8,128)(2,1)} %bitcast.27), custom_call_target="tpu_custom_call" | custom-call | bytes 2097152 | tf_op jit(solution)/shard_map/pallas_call | solution.py:632
  75.2 42.9 %all-gather.11 = s16[12544,256]{1,0:T(8,128)(2,1)} all-gather(s16[784,256]{1,0:T(8,128)(2,1)} %shard_map.49), channel_id=3, replica_groups=mesh['prow'=16,'pcol'=8] {'prow'}, dimensions={0}, use_global_device_ids=true | all-gather | bytes 6823936 | tf_op jit(solution)/shard_map/all_gather | solution.py:646
  118.1 4.9 %all-gather.10.cloned.1.call-done = bf16[32,256,512]{2,1,0:T(8,128)(2,1)} async-done(((bf16[4,256,512]{2,1,0:T(8,128)(2,1)}), bf16[32,256,512]{2,1,0:T(8,128)(2,1)}) %all-gather.10.cloned.1.call-update) | async-done | bytes 8388624 | tf_op jit(solution)/shard_map/all_gather | solution.py:645
  123.0 43.8 %shard_map.50 = f32[1024,2,8,128]{3,2,1,0:T(8,128)} custom-call(s32[2,16]{1,0:T(2,128)} %map_ref.7, s32[2]{0:T(128)} %pad_add_fusion.rc_ref, s16[16,784,256]{2,1,0:T(8,128)(2,1)} %bitcast.26, f32[8,1024,256]{2,1,0:T(8,128)} %bitcast.33, f32[1024,2,8,128]{3,2,1,0:T(8,128)} %bitcast.25, bf16[8,4,256,512]{3,2,1,0:T(8,128)(2,1)} %bitcast.34), custom_call_target="tpu_custom_call" | custom-call | flops 24696061952 | bytes 33554432 | tf_op jit(solution)/shard_map/pallas_call | solution.py:535
  (33 shorter events, 0.9 us)
Async XLA Ops:
  6.5 111.6 %all-gather.8.cloned.1.call-start = ((), (), s32[]{:S(2)}) async-start(), calls=%async_computation | async-start | bytes 9437184 | tf_op jit(solution)/shard_map/all_gather | solution.py:607
  14.5 108.5 %all-gather.10.cloned.1.call-start = ((), (), s32[]{:S(2)}) async-start(), calls=%async_computation.1 | async-start | bytes 9437184 | tf_op jit(solution)/shard_map/all_gather | solution.py:645
  14.5 20.3 %collective-permute-start = (f32[8,64,256]{2,1,0:T(8,128)}, f32[8,64,256]{2,1,0:T(8,128)S(1)}, u32[]{:S(2)}, u32[]{:S(2)}) collective-permute-start(f32[8,64,256]{2,1,0:T(8,128)} %get-tuple-element.29), channel_id=1, source_target_pairs={{0,32},{8,40},{16,48},{24,56},{1,33},{9,41},{17,49},{25,57},{2,34}... | collective-permute-start | bytes 1572872 | tf_op jit(solution)/shard_map/ppermute | solution.py:581
  18.6 9.8 %collective-permute-start.3 = (bf16[256,512]{1,0:T(8,128)(2,1)}, bf16[256,512]{1,0:T(8,128)(2,1)S(1)}, u32[]{:S(2)}, u32[]{:S(2)}) collective-permute-start(bf16[256,512]{1,0:T(8,128)(2,1)} %get-tuple-element.33), channel_id=1, source_target_pairs={{0,8},{8,16},{16,24},{24,0},{32,40},{40,48},{48,56},{56,32},{64,72... | collective-permute-start | bytes 786440 | tf_op jit(solution)/shard_map/ppermute | solution.py:571
  20.3 14.5 %collective-permute-start.4 = (bf16[256,512]{1,0:T(8,128)(2,1)}, bf16[256,512]{1,0:T(8,128)(2,1)S(1)}, u32[]{:S(2)}, u32[]{:S(2)}) collective-permute-start(bf16[256,512]{1,0:T(8,128)(2,1)} %get-tuple-element.34), channel_id=1, source_target_pairs={{0,16},{8,24},{16,0},{24,8},{32,48},{40,56},{48,32},{56,40},{64,80... | collective-permute-start | bytes 786440 | tf_op jit(solution)/shard_map/ppermute | solution.py:571
  23.6 11.2 %collective-permute-start.5 = (bf16[256,512]{1,0:T(8,128)(2,1)}, bf16[256,512]{1,0:T(8,128)(2,1)S(1)}, u32[]{:S(2)}, u32[]{:S(2)}) collective-permute-start(bf16[256,512]{1,0:T(8,128)(2,1)} %get-tuple-element.35), channel_id=1, source_target_pairs={{0,24},{8,0},{16,8},{24,16},{32,56},{40,32},{48,40},{56,48},{64,88... | collective-permute-start | bytes 786440 | tf_op jit(solution)/shard_map/ppermute | solution.py:571
  24.3 18.7 %collective-permute-start.1 = (f32[8,64,256]{2,1,0:T(8,128)}, f32[8,64,256]{2,1,0:T(8,128)S(1)}, u32[]{:S(2)}, u32[]{:S(2)}) collective-permute-start(f32[8,64,256]{2,1,0:T(8,128)} %get-tuple-element.30), channel_id=1, source_target_pairs={{0,64},{8,72},{16,80},{24,88},{1,65},{9,73},{17,81},{25,89},{2,66}... | collective-permute-start | bytes 1572872 | tf_op jit(solution)/shard_map/ppermute | solution.py:581
  28.3 7.3 %copy-start.6 = (bf16[256,512]{1,0:T(8,128)(2,1)}, bf16[256,512]{1,0:T(8,128)(2,1)S(1)}, u32[]{:S(2)}) copy-start(bf16[256,512]{1,0:T(8,128)(2,1)S(1)} %collective-permute-done.3.refs_1_) | copy-start | bytes 786436
  28.3 14.7 %collective-permute-start.2 = (f32[8,64,256]{2,1,0:T(8,128)}, f32[8,64,256]{2,1,0:T(8,128)S(1)}, u32[]{:S(2)}, u32[]{:S(2)}) collective-permute-start(f32[8,64,256]{2,1,0:T(8,128)} %get-tuple-element.31), channel_id=1, source_target_pairs={{0,96},{8,104},{16,112},{24,120},{1,97},{9,105},{17,113},{25,121},... | collective-permute-start | bytes 1572872 | tf_op jit(solution)/shard_map/ppermute | solution.py:581
  34.8 0.7 copy-start.7
  34.8 0.8 copy-start.8
  35.6 3.1 %copy-start = (f32[8,64,256]{2,1,0:T(8,128)}, f32[8,64,256]{2,1,0:T(8,128)S(1)}, u32[]{:S(2)}) copy-start(f32[8,64,256]{2,1,0:T(8,128)S(1)} %collective-permute-done.f1) | copy-start | bytes 1572868
  38.7 5.8 %collective-permute-start.6 = (bf16[64,512]{1,0:T(8,128)(2,1)}, bf16[64,512]{1,0:T(8,128)(2,1)S(1)}, u32[]{:S(2)}, u32[]{:S(2)}) collective-permute-start(bf16[64,512]{1,0:T(8,128)(2,1)} %get-tuple-element.41), channel_id=1, source_target_pairs={{0,32},{8,40},{16,48},{24,56},{1,33},{9,41},{17,49},{25,57},{2,34}... | collective-permute-start | bytes 196616 | tf_op jit(solution)/shard_map/ppermute | solution.py:581
  40.0 6.5 %collective-permute-start.7 = (bf16[64,512]{1,0:T(8,128)(2,1)}, bf16[64,512]{1,0:T(8,128)(2,1)S(1)}, u32[]{:S(2)}, u32[]{:S(2)}) collective-permute-start(bf16[64,512]{1,0:T(8,128)(2,1)} %get-tuple-element.42), channel_id=1, source_target_pairs={{0,64},{8,72},{16,80},{24,88},{1,65},{9,73},{17,81},{25,89},{2,66}... | collective-permute-start | bytes 196616 | tf_op jit(solution)/shard_map/ppermute | solution.py:581
  41.7 4.8 %collective-permute-start.8 = (bf16[64,512]{1,0:T(8,128)(2,1)}, bf16[64,512]{1,0:T(8,128)(2,1)S(1)}, u32[]{:S(2)}, u32[]{:S(2)}) collective-permute-start(bf16[64,512]{1,0:T(8,128)(2,1)} %get-tuple-element.43), channel_id=1, source_target_pairs={{0,96},{8,104},{16,112},{24,120},{1,97},{9,105},{17,113},{25,121},... | collective-permute-start | bytes 196616 | tf_op jit(solution)/shard_map/ppermute | solution.py:581
  43.0 3.5 %copy-start.1 = (f32[8,64,256]{2,1,0:T(8,128)}, f32[8,64,256]{2,1,0:T(8,128)S(1)}, u32[]{:S(2)}) copy-start(f32[8,64,256]{2,1,0:T(8,128)S(1)} %collective-permute-done.1.f2) | copy-start | bytes 1572868
  43.0 26.2 %collective-permute-start.9 = (bf16[256,512]{1,0:T(8,128)(2,1)}, bf16[256,512]{1,0:T(8,128)(2,1)S(1)}, u32[]{:S(2)}, u32[]{:S(2)}) collective-permute-start(bf16[256,512]{1,0:T(8,128)(2,1)} %get-tuple-element.45), channel_id=1, source_target_pairs={{0,32},{8,40},{16,48},{24,56},{32,64},{40,72},{48,80},{56,88},{64,... | collective-permute-start | bytes 786440 | tf_op jit(solution)/shard_map/ppermute | solution.py:576
  43.1 3.4 %copy-start.2 = (f32[8,64,256]{2,1,0:T(8,128)}, f32[8,64,256]{2,1,0:T(8,128)S(1)}, u32[]{:S(2)}) copy-start(f32[8,64,256]{2,1,0:T(8,128)S(1)} %collective-permute-done.2.f3) | copy-start | bytes 1572868
  43.1 26.1 %collective-permute-start.10 = (bf16[256,512]{1,0:T(8,128)(2,1)}, bf16[256,512]{1,0:T(8,128)(2,1)S(1)}, u32[]{:S(2)}, u32[]{:S(2)}) collective-permute-start(bf16[256,512]{1,0:T(8,128)(2,1)} %get-tuple-element.46), channel_id=1, source_target_pairs={{0,64},{8,72},{16,80},{24,88},{32,96},{40,104},{48,112},{56,120},{... | collective-permute-start | bytes 786440 | tf_op jit(solution)/shard_map/ppermute | solution.py:576
  44.5 2.0 %copy-start.3 = (bf16[64,512]{1,0:T(8,128)(2,1)}, bf16[64,512]{1,0:T(8,128)(2,1)S(1)}, u32[]{:S(2)}) copy-start(bf16[64,512]{1,0:T(8,128)(2,1)S(1)} %collective-permute-done.6.t1) | copy-start | bytes 196612
  44.5 24.7 %collective-permute-start.11 = (bf16[256,512]{1,0:T(8,128)(2,1)}, bf16[256,512]{1,0:T(8,128)(2,1)S(1)}, u32[]{:S(2)}, u32[]{:S(2)}) collective-permute-start(bf16[256,512]{1,0:T(8,128)(2,1)} %get-tuple-element.47), channel_id=1, source_target_pairs={{0,96},{8,104},{16,112},{24,120},{32,0},{40,8},{48,16},{56,24},{64... | collective-permute-start | bytes 786440 | tf_op jit(solution)/shard_map/ppermute | solution.py:576
  46.5 0.6 copy-start.4
  46.5 0.6 copy-start.5
Sparse Core Ops, SparseCore 0:
  14.6 56.7 all-gather.7
  73.1 49.8 all-gather.9

commit v13 on v12

--- a/solution.py
+++ b/solution.py
@@ -22,24 +22,11 @@
 SMEM = pl.BlockSpec(memory_space=pltpu.SMEM)
 VMEM = pl.BlockSpec(memory_space=pltpu.VMEM)
 LIMIT = 62 * 1024 * 1024
+SMALL = 12 * 1024 * 1024
 
 
 def shape(dims, kind):
     return jax.ShapeDtypeStruct(dims, kind)
-
-
-def call(body, outs, ins, smem=2, flops=0, scratch=()):
-    moved = sum(a.size * a.dtype.itemsize for a in ins)
-    moved += sum(o.size * o.dtype.itemsize for o in outs)
-    return pl.pallas_call(
-        body,
-        out_shape=outs,
-        in_specs=[SMEM] * smem + [VMEM] * (len(ins) - smem),
-        out_specs=[VMEM] * len(outs),
-        scratch_shapes=list(scratch),
-        compiler_params=pltpu.CompilerParams(vmem_limit_bytes=LIMIT),
-        cost_estimate=pl.CostEstimate(flops=flops, bytes_accessed=moved, transcendentals=0),
-    )(*ins)
 
 
 def spot(map_ref, child, low, count, test):
@@ -89,11 +76,8 @@
 
 
 def reorder(select, value):
-    high = value.astype(BF16)
-    rest = value - high.astype(F32)
-    middle = rest.astype(BF16)
-    last = (rest - middle.astype(F32)).astype(BF16)
-    return (dot(select, high) + dot(select, middle)) + dot(select, last)
+    high, low = split(value)
+    return dot(select, high) + dot(select, low)
 
 
 def level(peak):
@@ -148,47 +132,79 @@
 
 
 def pick_rows(map_ref, rc_ref, pivots_ref, *refs):
-    held, pieces, hops = refs[:4], refs[4:8], refs[8:]
+    held, pieces, hops, (work, arrived) = refs[:4], refs[4:8], refs[8:12], refs[12:]
     row = rc_ref[0]
     y, z = row // 4, row % 4
     found, value = spot(map_ref, 0, 0, 4, lambda entry: entry == row)
     live = (found >= 0) & (row < NPIV)
-    for hop in range(4):
-
-        @pl.when(live & (found // 2 == (z - hop + 4) % 4))
-        def _(hop=hop):
-            turned = dot(one_hot(pivots_ref, row), held[hop][...]).astype(BF16)
-            for piece in range(4):
-                pieces[piece][...] = turned[piece * PIECE : piece * PIECE + PIECE]
+
+    def each(act):
+        for hop in range(4):
+            mine = live & (found // 2 == (z - hop + 4) % 4)
+            act(mine, pltpu.make_async_copy(held[hop], work, arrived.at[16 + hop]))
+        for hop in range(4):
+            first = 2 * ((4 * y + (z - hop + 4) % 4) % 8)
+            index, value = spot(map_ref, y // 2, first, 2, lambda entry: entry % 4 == z)
+            for shift in range(4):
+                mine = (index >= 0) & ((value // 4) % 4 == (y + shift) % 4)
+                at = 4 * hop + shift
+                act(mine, pltpu.make_async_copy(held[hop], hops[shift], arrived.at[at]))
+
+    def start(mine, copy):
+        @pl.when(mine)
+        def _():
+            copy.start()
+
+    def wait(mine, copy):
+        @pl.when(mine)
+        def _():
+            copy.wait()
+
+    each(start)
+    each(wait)
+
+    @pl.when(live)
+    def _():
+        turned = dot(one_hot(pivots_ref, row), work[...]).astype(BF16)
+        for piece in range(4):
+            pieces[piece][...] = turned[piece * PIECE : piece * PIECE + PIECE]
 
     @pl.when(jnp.logical_not(live))
     def _():
         for piece in range(4):
             pieces[piece][...] = jnp.zeros((PIECE, 2 * BS), BF16)
 
-    for hop in range(4):
-        first = 2 * ((4 * y + (z - hop + 4) % 4) % 8)
-        index, value = spot(map_ref, y // 2, first, 2, lambda entry: entry % 4 == z)
-        for shift in range(4):
-
-            @pl.when((index >= 0) & ((value // 4) % 4 == (y + shift) % 4))
-            def _(hop=hop, shift=shift):
-                hops[shift][...] = held[hop][...]
-
-
-def mix(rc_ref, t0, t1, t2, t3, f0, f1, f2, f3, out_ref, strip, corner):
+
+def pack(y0, y1, y2, y3, out_ref, arrived):
+    copies = [
+        pltpu.make_async_copy(source, out_ref.at[shift], arrived.at[shift])
+        for shift, source in enumerate((y0, y1, y2, y3))
+    ]
+    for copy in copies:
+        copy.start()
+    for copy in copies:
+        copy.wait()
+
+
+def mix(rc_ref, t0, t1, t2, t3, f0, f1, f2, f3, out_ref, strip, corner, arrived):
     y = rc_ref[0] // 4
     for piece, (child, source) in enumerate(((t0, f0), (t1, f1), (t2, f2), (t3, f3))):
+        copies = [
+            pltpu.make_async_copy(child, strip, arrived.at[2 * piece]),
+            pltpu.make_async_copy(source.at[0], corner, arrived.at[2 * piece + 1]),
+        ]
 
         @pl.when(y == piece)
-        def _(child=child, source=source):
-            strip[...] = child[...].astype(F32)
-            corner[...] = source[0]
+        def _(copies=copies):
+            for copy in copies:
+                copy.start()
+            for copy in copies:
+                copy.wait()
 
     n = jnp.full((8, HALF), CHILD_LEVEL)
     for half in range(2):
         out_ref[half * PIECE : half * PIECE + PIECE] = encode(
-            strip[:, half * BS : half * BS + BS], n
+            strip[:, half * BS : half * BS + BS].astype(F32), n
         ).astype(I16)
     n = level(jnp.max(jnp.abs(corner[...])))
     out_ref[2 * PIECE : 3 * PIECE] = encode(corner[...], n).astype(I16)
@@ -608,26 +624,42 @@
 
     thin = shape((PIECE, 2 * BS), BF16)
     zs, unused = lax.optimization_barrier((zs, moved[1]))
-    picked = call(
-        pick_rows, [thin] * 4 + [strip] * 4, [child_map, rc, pivots, *zs], flops=20 * 2**30
-    )
+    picked = pl.pallas_call(
+        pick_rows,
+        out_shape=[thin] * 4 + [strip] * 4,
+        in_specs=[SMEM, SMEM, VMEM] + [away] * 4,
+        out_specs=[VMEM] * 4 + [away] * 4,
+        scratch_shapes=[pltpu.VMEM((BS, 2 * BS), BF16), pltpu.SemaphoreType.DMA((20,))],
+        compiler_params=pltpu.CompilerParams(vmem_limit_bytes=SMALL),
+        cost_estimate=pl.CostEstimate(
+            flops=20 * 2**30, bytes_accessed=2 * 2**20, transcendentals=0
+        ),
+    )(child_map, rc, pivots, *zs)
     thin = spread(picked[:4])
     ys = [picked[4]] + [along_y(picked[4 + hop], hop) for hop in (1, 2, 3)]
 
     thin = pl.pallas_call(
         mix,
-        grid=(1,),
         out_shape=shape((3 * PIECE + 16, BS), I16),
-        in_specs=[SMEM]
-        + [pl.BlockSpec((PIECE, 2 * BS), lambda t: (0, 0))] * 4
-        + [pl.BlockSpec((1, PIECE, BS), lambda t: (0, 0, 0))] * 4,
-        out_specs=pl.BlockSpec((3 * PIECE + 16, BS), lambda t: (0, 0)),
-        scratch_shapes=[pltpu.VMEM((PIECE, 2 * BS), F32), pltpu.VMEM((PIECE, BS), F32)],
-        compiler_params=pltpu.CompilerParams(vmem_limit_bytes=LIMIT),
+        in_specs=[SMEM] + [away] * 8,
+        out_specs=VMEM,
+        scratch_shapes=[
+            pltpu.VMEM((PIECE, 2 * BS), BF16), pltpu.VMEM((PIECE, BS), F32),
+            pltpu.SemaphoreType.DMA((8,)),
+        ],
+        compiler_params=pltpu.CompilerParams(vmem_limit_bytes=SMALL),
         cost_estimate=pl.CostEstimate(flops=0, bytes_accessed=2**20, transcendentals=0),
     )(rc, *thin, *moved)
     thin = lax.all_gather(thin, "pcol", axis=0, tiled=False)
-    child = jnp.stack(ys)
+    child = pl.pallas_call(
+        pack,
+        out_shape=shape((4, BS, 2 * BS), BF16),
+        in_specs=[away] * 4,
+        out_specs=away,
+        scratch_shapes=[pltpu.SemaphoreType.DMA((4,))],
+        compiler_params=pltpu.CompilerParams(vmem_limit_bytes=SMALL),
+        cost_estimate=pl.CostEstimate(flops=0, bytes_accessed=2**21, transcendentals=0),
+    )(*ys)
     thin, child = lax.optimization_barrier((thin, child))
     code = pl.pallas_call(
         assemble,
@@ -638,7 +670,7 @@
             pltpu.VMEM((8, PIECE, BS), F32), pltpu.VMEM((NPIV, PIECE, BS), F32),
             pltpu.SemaphoreType.DMA((4,)),
         ],
-        compiler_params=pltpu.CompilerParams(vmem_limit_bytes=LIMIT),
+        compiler_params=pltpu.CompilerParams(vmem_limit_bytes=SMALL),
         cost_estimate=pl.CostEstimate(flops=0, bytes_accessed=2**21, transcendentals=0),
     )(child_map, rc, *moved, thin)
 

time: 174 us -> 174 us (level)
  waiting for transfers between devices: 10.7 us -> 17.7 us
  Pallas kernels: 60.1 us -> 56 us
  blocking collectives: 62.9 us -> 60.8 us
  other arithmetic: 2.68 us -> 0.64 us
    all_gather x1, waiting for transfers between devices: 4.87 us -> 11.9 us  [shards(): child = lax.all_gather(child, 'pcol', axis=0, tiled=False)]
    pallas_call x1, Pallas kernels: 3.97 us -> 1.69 us  [shards(): pl.pallas_call(assemble, out_shape=shape((12 * PIECE + 16, BS), I16), in_...]
    another operation x1 -> x0, other arithmetic: 2.04 us -> none  [shards(): child = jnp.stack(ys)]
    pallas_call x2 -> x3, Pallas kernels: 5.11 us -> 3.54 us  [the longest x1 1.47 us: shards(): pl.pallas_call(pick_rows, out_shape=[thin] * 4 + [strip] * 4, in_specs=[S...]
  transfers between devices with their start and end apart: 14 -> 14, of which waited for: 3 -> 3; matrix products, arithmetic and copies ran while one was open for 1% -> 0% of each run, Pallas kernels for 5% -> 3%
where the time goes in v13:
time: 174 us; the launch traced here: 173 us
  blocking collectives  60.8 us (35%)
  Pallas kernels  56 us (32%)
  starting transfers between devices  23.7 us (14%)
  waiting for transfers between devices  17.7 us (10%)
  between operations  13.6 us (8%)
    pallas_call x1, Pallas kernels, run_finish(): pl.pallas_call(finish, out_shape=shape(view.shape, F32), in_specs=[SMEM,...  43.9 us
    all_gather x1, blocking collectives, shards(): top = lax.all_gather(code, 'prow', axis=0, tiled=False)  41.6 us
    all_gather x1, blocking collectives, shards(): thin = lax.all_gather(thin, 'pcol', axis=0, tiled=False)  19.2 us
    ppermute x6, starting transfers between devices, from_plane(): return lax.ppermute(a, 'prow', [(j, 4 * hop + j) for j in range(4)])  13.1 us
    all_gather x1, waiting for transfers between devices, shards(): child = lax.all_gather(child, 'pcol', axis=0, tiled=False)  11.9 us
    pallas_call x1, Pallas kernels, shards(): pl.pallas_call(begin, out_shape=[strip] * 4 + [shape((8, PIECE, BS), F32)...  6.88 us
    ppermute x3, starting transfers between devices, along_z(): lax.ppermute(a, 'prow', [(4 * i + j, 4 * i + (j + hop) % 4) for i in rang...  5.74 us
    ppermute x3, waiting for transfers between devices, along_z(): lax.ppermute(a, 'prow', [(4 * i + j, 4 * i + (j + hop) % 4) for i in rang...  5.74 us
  transfers between devices with their start and end apart: 14, of which 3 were waited for; matrix products, arithmetic and copies ran while one was open for 0% of the time, Pallas kernels for 3%

profile of v13, /device:TPU:1, one launch (start us, length us, event | category | flops | bytes accessed | tf_op | source)
XLA Modules:
  0.0 173.4 jit_solution(584539354914374231)
XLA Ops:
  6.5 0.6 pad_add_fusion.rc_ref
  7.2 6.9 %shard_map.46 = (bf16[256,512]{1,0:T(8,128)(2,1)}, bf16[256,512]{1,0:T(8,128)(2,1)}, bf16[256,512]{1,0:T(8,128)(2,1)}, bf16[256,512]{1,0:T(8,128)(2,1)}, f32[8,6...) custom-call(s32[2,16]{1,0:T(2,128)} %map_ref.7, ...), custom_call_target="tpu_custom_call" | custom-call | flops 1073741824 | bytes 8388608 | tf_op jit(solution)/shard_map/pallas_call | solution.py:606
  14.1 4.1 %collective-permute-start = (f32[8,64,256]{2,1,0:T(8,128)}, f32[8,64,256]{2,1,0:T(8,128)S(1)}, u32[]{:S(2)}, u32[]{:S(2)}) collective-permute-start(f32[8,64,256]{2,1,0:T(8,128)} %get-tuple-element.29), channel_id=1, source_target_pairs={{0,32},{8,40},{16,48},{24,56},{1,33},{9,41},{17,49},{25,57},{2,34}... | collective-permute-start | bytes 1572872 | tf_op jit(solution)/shard_map/ppermute | solution.py:597
  18.2 1.7 collective-permute-start.3
  19.9 3.3 %collective-permute-start.4 = (bf16[256,512]{1,0:T(8,128)(2,1)}, bf16[256,512]{1,0:T(8,128)(2,1)S(1)}, u32[]{:S(2)}, u32[]{:S(2)}) collective-permute-start(bf16[256,512]{1,0:T(8,128)(2,1)} %get-tuple-element.34), channel_id=1, source_target_pairs={{0,16},{8,24},{16,0},{24,8},{32,48},{40,56},{48,32},{56,40},{64,80... | collective-permute-start | bytes 786440 | tf_op jit(solution)/shard_map/ppermute | solution.py:587
  23.2 0.7 collective-permute-start.5
  24.0 2.3 %collective-permute-start.1 = (f32[8,64,256]{2,1,0:T(8,128)}, f32[8,64,256]{2,1,0:T(8,128)S(1)}, u32[]{:S(2)}, u32[]{:S(2)}) collective-permute-start(f32[8,64,256]{2,1,0:T(8,128)} %get-tuple-element.30), channel_id=1, source_target_pairs={{0,64},{8,72},{16,80},{24,88},{1,65},{9,73},{17,81},{25,89},{2,66}... | collective-permute-start | bytes 1572872 | tf_op jit(solution)/shard_map/ppermute | solution.py:597
  26.3 1.7 collective-permute-done.3.refs_1_
  28.0 2.4 %collective-permute-start.2 = (f32[8,64,256]{2,1,0:T(8,128)}, f32[8,64,256]{2,1,0:T(8,128)S(1)}, u32[]{:S(2)}, u32[]{:S(2)}) collective-permute-start(f32[8,64,256]{2,1,0:T(8,128)} %get-tuple-element.31), channel_id=1, source_target_pairs={{0,96},{8,104},{16,112},{24,120},{1,97},{9,105},{17,113},{25,121},... | collective-permute-start | bytes 1572872 | tf_op jit(solution)/shard_map/ppermute | solution.py:597
  30.4 4.0 %collective-permute-done.4.refs_2_ = bf16[256,512]{1,0:T(8,128)(2,1)S(1)} collective-permute-done((bf16[256,512]{1,0:T(8,128)(2,1)}, bf16[256,512]{1,0:T(8,128)(2,1)S(1)}, u32[]{:S(2)}, u32[]{:S(2)}) %collective-permute-start.4) | collective-permute-done | bytes 262176 | tf_op jit(solution)/shard_map/ppermute | solution.py:587
  34.5 0.9 copy-done.4
  35.4 1.5 shard_map.47
  36.9 1.3 collective-permute-start.6
  38.2 1.7 collective-permute-start.7
  39.9 1.3 collective-permute-start.8
  41.3 2.7 %collective-permute-start.10 = (bf16[256,512]{1,0:T(8,128)(2,1)S(1)}, bf16[256,512]{1,0:T(8,128)(2,1)S(1)}, u32[]{:S(2)}, u32[]{:S(2)}) collective-permute-start(bf16[256,512]{1,0:T(8,128)(2,1)S(1)} %get-tuple-element.46), channel_id=1, source_target_pairs={{0,64},{8,72},{16,80},{24,88},{32,96},{40,104},{48,112},{56,120},{... | collective-permute-start | bytes 786440 | tf_op jit(solution)/shard_map/ppermute | solution.py:592
  44.0 2.1 %collective-permute-start.11 = (bf16[256,512]{1,0:T(8,128)(2,1)S(1)}, bf16[256,512]{1,0:T(8,128)(2,1)S(1)}, u32[]{:S(2)}, u32[]{:S(2)}) collective-permute-start(bf16[256,512]{1,0:T(8,128)(2,1)S(1)} %get-tuple-element.47), channel_id=1, source_target_pairs={{0,96},{8,104},{16,112},{24,120},{32,0},{40,8},{48,16},{56,24},{64... | collective-permute-start | bytes 786440 | tf_op jit(solution)/shard_map/ppermute | solution.py:592
  46.1 1.1 shard_map.48
  47.2 19.2 %all-gather = s16[1664,256]{1,0:T(8,128)(2,1)S(1)} all-gather(s16[208,256]{1,0:T(8,128)(2,1)S(1)} %shard_map.48), channel_id=2, replica_groups=mesh['prow'=16,'pcol'=8] {'pcol'}, dimensions={0}, use_global_device_ids=true | all-gather | bytes 958464 | tf_op jit(solution)/shard_map/all_gather | solution.py:653
  66.4 1.0 shard_map.49
  67.5 1.7 shard_map.50
  69.2 41.6 %all-gather.11 = s16[12544,256]{1,0:T(8,128)(2,1)} all-gather(s16[784,256]{1,0:T(8,128)(2,1)S(1)} %shard_map.50), channel_id=3, replica_groups=mesh['prow'=16,'pcol'=8] {'prow'}, dimensions={0}, use_global_device_ids=true | all-gather | bytes 6823936 | tf_op jit(solution)/shard_map/all_gather | solution.py:678
  110.8 11.9 %all-gather.10.cloned.1.call-done = bf16[32,256,512]{2,1,0:T(8,128)(2,1)} async-done(((bf16[4,256,512]{2,1,0:T(8,128)(2,1)}), bf16[32,256,512]{2,1,0:T(8,128)(2,1)}) %all-gather.10.cloned.1.call-update) | async-done | bytes 8388624 | tf_op jit(solution)/shard_map/all_gather | solution.py:677
  122.6 43.9 %shard_map.51 = f32[1024,2,8,128]{3,2,1,0:T(8,128)} custom-call(s32[2,16]{1,0:T(2,128)} %map_ref.7, s32[2]{0:T(128)} %pad_add_fusion.rc_ref, s16[16,784,256]{2,1,0:T(8,128)(2,1)} %bitcast.23, f32[8,1024,256]{2,1,0:T(8,128)} %bitcast.25, f32[1024,2,8,128]{3,2,1,0:T(8,128)} %bitcast.22, bf16[8,4,256,512]{3,2,1,0:T(8,128)(2,1)} %bitcast.26), custom_call_target="tpu_custom_call" | custom-call | flops 24696061952 | bytes 33554432 | tf_op jit(solution)/shard_map/pallas_call | solution.py:551
  (25 shorter events, 0.2 us)
Async XLA Ops:
  6.5 104.2 %all-gather.8.cloned.1.call-start = ((), (), s32[]{:S(2)}) async-start(), calls=%async_computation | async-start | bytes 9437184 | tf_op jit(solution)/shard_map/all_gather | solution.py:623
  7.2 27.3 %copy-start.1 = (s32[2]{0:T(128)S(1)}, s32[2]{0:T(128)}, u32[]{:S(2)}) copy-start(s32[2]{0:T(128)} %pad_add_fusion.rc_ref) | copy-start | bytes 28
  7.2 27.3 %copy-start.2 = (s32[4,256]{1,0:T(4,128)S(1)}, s32[4,256]{1,0:T(4,128)}, u32[]{:S(2)}) copy-start(s32[4,256]{1,0:T(4,128)} %pivots_ref.3) | copy-start | bytes 12292
  7.2 27.3 %copy-start.3 = (s32[2,16]{1,0:T(2,128)S(1)}, s32[2,16]{1,0:T(2,128)}, u32[]{:S(2)}) copy-start(s32[2,16]{1,0:T(2,128)} %map_ref.7) | copy-start | bytes 388
  14.1 108.5 %all-gather.10.cloned.1.call-start = ((), (), s32[]{:S(2)}) async-start(), calls=%async_computation.1 | async-start | bytes 9437184 | tf_op jit(solution)/shard_map/all_gather | solution.py:677
  14.1 20.3 %collective-permute-start = (f32[8,64,256]{2,1,0:T(8,128)}, f32[8,64,256]{2,1,0:T(8,128)S(1)}, u32[]{:S(2)}, u32[]{:S(2)}) collective-permute-start(f32[8,64,256]{2,1,0:T(8,128)} %get-tuple-element.29), channel_id=1, source_target_pairs={{0,32},{8,40},{16,48},{24,56},{1,33},{9,41},{17,49},{25,57},{2,34}... | collective-permute-start | bytes 1572872 | tf_op jit(solution)/shard_map/ppermute | solution.py:597
  18.2 9.8 %collective-permute-start.3 = (bf16[256,512]{1,0:T(8,128)(2,1)}, bf16[256,512]{1,0:T(8,128)(2,1)S(1)}, u32[]{:S(2)}, u32[]{:S(2)}) collective-permute-start(bf16[256,512]{1,0:T(8,128)(2,1)} %get-tuple-element.33), channel_id=1, source_target_pairs={{0,8},{8,16},{16,24},{24,0},{32,40},{40,48},{48,56},{56,32},{64,72... | collective-permute-start | bytes 786440 | tf_op jit(solution)/shard_map/ppermute | solution.py:587
  19.9 14.5 %collective-permute-start.4 = (bf16[256,512]{1,0:T(8,128)(2,1)}, bf16[256,512]{1,0:T(8,128)(2,1)S(1)}, u32[]{:S(2)}, u32[]{:S(2)}) collective-permute-start(bf16[256,512]{1,0:T(8,128)(2,1)} %get-tuple-element.34), channel_id=1, source_target_pairs={{0,16},{8,24},{16,0},{24,8},{32,48},{40,56},{48,32},{56,40},{64,80... | collective-permute-start | bytes 786440 | tf_op jit(solution)/shard_map/ppermute | solution.py:587
  23.2 11.2 %collective-permute-start.5 = (bf16[256,512]{1,0:T(8,128)(2,1)}, bf16[256,512]{1,0:T(8,128)(2,1)S(1)}, u32[]{:S(2)}, u32[]{:S(2)}) collective-permute-start(bf16[256,512]{1,0:T(8,128)(2,1)} %get-tuple-element.35), channel_id=1, source_target_pairs={{0,24},{8,0},{16,8},{24,16},{32,56},{40,32},{48,40},{56,48},{64,88... | collective-permute-start | bytes 786440 | tf_op jit(solution)/shard_map/ppermute | solution.py:587
  24.0 17.3 %collective-permute-start.1 = (f32[8,64,256]{2,1,0:T(8,128)}, f32[8,64,256]{2,1,0:T(8,128)S(1)}, u32[]{:S(2)}, u32[]{:S(2)}) collective-permute-start(f32[8,64,256]{2,1,0:T(8,128)} %get-tuple-element.30), channel_id=1, source_target_pairs={{0,64},{8,72},{16,80},{24,88},{1,65},{9,73},{17,81},{25,89},{2,66}... | collective-permute-start | bytes 1572872 | tf_op jit(solution)/shard_map/ppermute | solution.py:597
  28.0 13.4 %collective-permute-start.2 = (f32[8,64,256]{2,1,0:T(8,128)}, f32[8,64,256]{2,1,0:T(8,128)S(1)}, u32[]{:S(2)}, u32[]{:S(2)}) collective-permute-start(f32[8,64,256]{2,1,0:T(8,128)} %get-tuple-element.31), channel_id=1, source_target_pairs={{0,96},{8,104},{16,112},{24,120},{1,97},{9,105},{17,113},{25,121},... | collective-permute-start | bytes 1572872 | tf_op jit(solution)/shard_map/ppermute | solution.py:597
  34.5 1.0 copy-start.4
  35.4 10.7 %copy-start = (f32[8,64,256]{2,1,0:T(8,128)S(1)}, f32[8,64,256]{2,1,0:T(8,128)}, u32[]{:S(2)}) copy-start(f32[8,64,256]{2,1,0:T(8,128)} %get-tuple-element.28.f0) | copy-start | bytes 1572868
  36.9 7.1 %collective-permute-start.6 = (bf16[64,512]{1,0:T(8,128)(2,1)S(1)}, bf16[64,512]{1,0:T(8,128)(2,1)S(1)}, u32[]{:S(2)}, u32[]{:S(2)}) collective-permute-start(bf16[64,512]{1,0:T(8,128)(2,1)S(1)} %get-tuple-element.41), channel_id=1, source_target_pairs={{0,32},{8,40},{16,48},{24,56},{1,33},{9,41},{17,49},{25,57},{2,34}... | collective-permute-start | bytes 196616 | tf_op jit(solution)/shard_map/ppermute | solution.py:597
  38.2 7.9 %collective-permute-start.7 = (bf16[64,512]{1,0:T(8,128)(2,1)S(1)}, bf16[64,512]{1,0:T(8,128)(2,1)S(1)}, u32[]{:S(2)}, u32[]{:S(2)}) collective-permute-start(bf16[64,512]{1,0:T(8,128)(2,1)S(1)} %get-tuple-element.42), channel_id=1, source_target_pairs={{0,64},{8,72},{16,80},{24,88},{1,65},{9,73},{17,81},{25,89},{2,66}... | collective-permute-start | bytes 196616 | tf_op jit(solution)/shard_map/ppermute | solution.py:597
  39.9 6.2 %collective-permute-start.8 = (bf16[64,512]{1,0:T(8,128)(2,1)S(1)}, bf16[64,512]{1,0:T(8,128)(2,1)S(1)}, u32[]{:S(2)}, u32[]{:S(2)}) collective-permute-start(bf16[64,512]{1,0:T(8,128)(2,1)S(1)} %get-tuple-element.43), channel_id=1, source_target_pairs={{0,96},{8,104},{16,112},{24,120},{1,97},{9,105},{17,113},{25,121},... | collective-permute-start | bytes 196616 | tf_op jit(solution)/shard_map/ppermute | solution.py:597
  41.2 25.2 %collective-permute-start.9 = (bf16[256,512]{1,0:T(8,128)(2,1)S(1)}, bf16[256,512]{1,0:T(8,128)(2,1)S(1)}, u32[]{:S(2)}, u32[]{:S(2)}) collective-permute-start(bf16[256,512]{1,0:T(8,128)(2,1)S(1)} %get-tuple-element.45), channel_id=1, source_target_pairs={{0,32},{8,40},{16,48},{24,56},{32,64},{40,72},{48,80},{56,88},{64,... | collective-permute-start | bytes 786440 | tf_op jit(solution)/shard_map/ppermute | solution.py:592
  41.3 25.1 %collective-permute-start.10 = (bf16[256,512]{1,0:T(8,128)(2,1)S(1)}, bf16[256,512]{1,0:T(8,128)(2,1)S(1)}, u32[]{:S(2)}, u32[]{:S(2)}) collective-permute-start(bf16[256,512]{1,0:T(8,128)(2,1)S(1)} %get-tuple-element.46), channel_id=1, source_target_pairs={{0,64},{8,72},{16,80},{24,88},{32,96},{40,104},{48,112},{56,120},{... | collective-permute-start | bytes 786440 | tf_op jit(solution)/shard_map/ppermute | solution.py:592
  44.0 22.4 %collective-permute-start.11 = (bf16[256,512]{1,0:T(8,128)(2,1)S(1)}, bf16[256,512]{1,0:T(8,128)(2,1)S(1)}, u32[]{:S(2)}, u32[]{:S(2)}) collective-permute-start(bf16[256,512]{1,0:T(8,128)(2,1)S(1)} %get-tuple-element.47), channel_id=1, source_target_pairs={{0,96},{8,104},{16,112},{24,120},{32,0},{40,8},{48,16},{56,24},{64... | collective-permute-start | bytes 786440 | tf_op jit(solution)/shard_map/ppermute | solution.py:592
Sparse Core Ops, SparseCore 0:
  14.2 56.7 all-gather.7
  72.7 49.8 all-gather.9

commit v14 on v13

--- a/solution.py
+++ b/solution.py
@@ -97,7 +97,7 @@
 
 def begin(
     map_ref, rc_ref, child_ref, pivots_ref, lines_ref, view_ref,
-    o0, o1, o2, o3, p0, p1, p2, p3, left_ref, tile_row, arrived,
+    o0, o1, o2, o3, p0, p1, p2, p3, word_ref, tile_row, left_ref, arrived,
 ):
     first = pltpu.make_async_copy(lines_ref.at[: BS * 16], tile_row, arrived.at[2])
     first.start()
@@ -129,6 +129,18 @@
     lax.fori_loop(0, 8, one, 0)
     for copy in copies:
         copy.wait()
+
+    @pl.when(row < NPIV)
+    def _():
+        left_ref[:BS] = jnp.zeros((BS, BS), F32)
+
+    n = level(jnp.max(jnp.abs(left_ref[...])))
+    height = SPAN * BS
+    for tile in range(SPAN):
+        upper = encode(left_ref[tile * BS : tile * BS + BS], n)
+        lower = encode(left_ref[height + tile * BS : height + tile * BS + BS], n)
+        word_ref[tile * BS : tile * BS + BS] = upper * 65536 + (lower & 65535)
+    word_ref[height:] = jnp.broadcast_to(n[:1, :1].astype(I32), (8, BS))
 
 
 def pick_rows(map_ref, rc_ref, pivots_ref, *refs):
@@ -321,9 +333,7 @@
     def hop_of(slot):
         return (row // 4 - slot + 4) % 4
 
-    def left_copy(step):
-        rows = pl.ds(step * height, height)
-        return pltpu.make_async_copy(left_from.at[:NPIV, rows], left_ref, ready.at[3])
+    left_copy = pltpu.make_async_copy(left_from.at[:NPIV], left_ref, ready.at[3])
 
     def front_copy(step):
         rows = pl.ds(step * height, height)
@@ -343,7 +353,7 @@
         copy.start()
     for copy in corner_copies:
         copy.wait()
-    for copy in (code_copy, left_copy(0), *near_copies, front_copy(0), front_copy(1)):
+    for copy in (code_copy, left_copy, *near_copies, front_copy(0), front_copy(1)):
         copy.start()
 
     def lost(s, first, count):
@@ -423,14 +433,17 @@
     def rows_of_step(step, carry):
         each_child(step, lambda copy, index, tile, s: copy.start())
         left = work.at[:, pl.ds(height, height)]
-        left_copy(step).wait()
-        left[...] = left_ref[...]
 
         @pl.when(step == 0)
         def _():
-            left_copy(1).start()
+            left_copy.wait()
             for copy in near_copies:
                 copy.wait()
+
+        for k in range(NPIV):
+            word = left_ref[k, :height]
+            word = jnp.where(step == 0, word, lax.shift_left(word, 16))
+            left[k] = decode(lax.shift_right_arithmetic(word, 16), left_ref[k, height:])
 
         for slot in range(2):
             parent = row_of(map_ref, row, slot)
@@ -555,7 +568,7 @@
         out_specs=away,
         scratch_shapes=[
             pltpu.VMEM((16, 4 * PIECE, BS), I16), pltpu.VMEM((16, 16, BS), I16),
-            pltpu.VMEM((16, 8 * PIECE, BS), I16), pltpu.VMEM((4, SPAN * BS, BS), F32),
+            pltpu.VMEM((16, 8 * PIECE, BS), I16), pltpu.VMEM((4, SPAN * BS + 8, BS), I32),
             pltpu.VMEM((2, 2, BS, 2 * BS), BF16), pltpu.VMEM((2, SPAN * BS, 2, 8, HALF), F32),
             pltpu.VMEM((4, 4 * BS, BS), F32),
             pltpu.VMEM((4 * BS, 4 * BS), BF16), pltpu.VMEM((4 * BS, 4 * BS), BF16),
@@ -605,10 +618,13 @@
     away = pl.BlockSpec(memory_space=pl.ANY)
     begun = pl.pallas_call(
         begin,
-        out_shape=[strip] * 4 + [shape((8, PIECE, BS), F32)] * 4 + [shape((tiles * BS, BS), F32)],
+        out_shape=[strip] * 4 + [shape((8, PIECE, BS), F32)] * 4 + [shape((SPAN * BS + 8, BS), I32)],
         in_specs=[SMEM, SMEM, VMEM, VMEM, away, away],
         out_specs=[VMEM] * 9,
-        scratch_shapes=[pltpu.VMEM((BS * 16, HALF), F32), pltpu.SemaphoreType.DMA((3,))],
+        scratch_shapes=[
+            pltpu.VMEM((BS * 16, HALF), F32), pltpu.VMEM((tiles * BS, BS), F32),
+            pltpu.SemaphoreType.DMA((3,)),
+        ],
         compiler_params=pltpu.CompilerParams(vmem_limit_bytes=LIMIT),
         cost_estimate=pl.CostEstimate(flops=2**30, bytes_accessed=8 * 2**20, transcendentals=0),
     )(

time: 174 us -> 166 us (0.954)
  waiting for transfers between devices: 17.7 us -> 10.7 us
    all_gather x1, waiting for transfers between devices: 11.9 us -> 4.9 us  [shards(): child = lax.all_gather(child, 'pcol', axis=0, tiled=False)]
    all_gather x1, blocking collectives: 19.2 us -> 17.2 us  [shards(): thin = lax.all_gather(thin, 'pcol', axis=0, tiled=False)]
where the time goes in v14:
time: 166 us
  blocking collectives  59.5 us (36%)
  Pallas kernels  57 us (34%)
  starting transfers between devices  23.7 us (14%)
  between operations  13.6 us (8%)
  waiting for transfers between devices  10.7 us (6%)
    pallas_call x1, Pallas kernels, run_finish(): pl.pallas_call(finish, out_shape=shape(view.shape, F32), in_specs=[SMEM,...  45 us
    all_gather x1, blocking collectives, shards(): top = lax.all_gather(code, 'prow', axis=0, tiled=False)  42.3 us
    all_gather x1, blocking collectives, shards(): thin = lax.all_gather(thin, 'pcol', axis=0, tiled=False)  17.2 us
    ppermute x6, starting transfers between devices, from_plane(): return lax.ppermute(a, 'prow', [(j, 4 * hop + j) for j in range(4)])  13.1 us
    pallas_call x1, Pallas kernels, shards(): pl.pallas_call(begin, out_shape=[strip] * 4 + [shape((8, PIECE, BS), F32)...  6.74 us
    ppermute x3, waiting for transfers between devices, along_z(): lax.ppermute(a, 'prow', [(4 * i + j, 4 * i + (j + hop) % 4) for i in rang...  5.74 us
    ppermute x3, starting transfers between devices, along_z(): lax.ppermute(a, 'prow', [(4 * i + j, 4 * i + (j + hop) % 4) for i in rang...  5.74 us
    all_gather x1, waiting for transfers between devices, shards(): child = lax.all_gather(child, 'pcol', axis=0, tiled=False)  4.9 us
  transfers between devices with their start and end apart: 14, of which 3 were waited for; matrix products, arithmetic and copies ran while one was open for 0% of the time, Pallas kernels for 3%

profile of v14, /device:TPU:1, one launch (start us, length us, event | category | flops | bytes accessed | tf_op | source)
XLA Modules:
  0.0 166.0 jit_solution(13965169922757468112)
XLA Ops:
  6.5 0.6 pad_add_fusion.rc_ref
  7.1 6.7 %shard_map.46 = (bf16[256,512]{1,0:T(8,128)(2,1)}, bf16[256,512]{1,0:T(8,128)(2,1)}, bf16[256,512]{1,0:T(8,128)(2,1)}, bf16[256,512]{1,0:T(8,128)(2,1)}, f32[8,6...) custom-call(s32[2,16]{1,0:T(2,128)} %map_ref.7, ...), custom_call_target="tpu_custom_call" | custom-call | flops 1073741824 | bytes 8388608 | tf_op jit(solution)/shard_map/pallas_call | solution.py:619
  13.9 4.0 %collective-permute-start = (f32[8,64,256]{2,1,0:T(8,128)}, f32[8,64,256]{2,1,0:T(8,128)S(1)}, u32[]{:S(2)}, u32[]{:S(2)}) collective-permute-start(f32[8,64,256]{2,1,0:T(8,128)} %get-tuple-element.29), channel_id=1, source_target_pairs={{0,32},{8,40},{16,48},{24,56},{1,33},{9,41},{17,49},{25,57},{2,34}... | collective-permute-start | bytes 1572872 | tf_op jit(solution)/shard_map/ppermute | solution.py:610
  18.0 1.7 %collective-permute-start.3 = (bf16[256,512]{1,0:T(8,128)(2,1)}, bf16[256,512]{1,0:T(8,128)(2,1)S(1)}, u32[]{:S(2)}, u32[]{:S(2)}) collective-permute-start(bf16[256,512]{1,0:T(8,128)(2,1)} %get-tuple-element.33), channel_id=1, source_target_pairs={{0,8},{8,16},{16,24},{24,0},{32,40},{40,48},{48,56},{56,32},{64,72... | collective-permute-start | bytes 786440 | tf_op jit(solution)/shard_map/ppermute | solution.py:600
  19.7 3.3 %collective-permute-start.4 = (bf16[256,512]{1,0:T(8,128)(2,1)}, bf16[256,512]{1,0:T(8,128)(2,1)S(1)}, u32[]{:S(2)}, u32[]{:S(2)}) collective-permute-start(bf16[256,512]{1,0:T(8,128)(2,1)} %get-tuple-element.34), channel_id=1, source_target_pairs={{0,16},{8,24},{16,0},{24,8},{32,48},{40,56},{48,32},{56,40},{64,80... | collective-permute-start | bytes 786440 | tf_op jit(solution)/shard_map/ppermute | solution.py:600
  23.0 0.7 collective-permute-start.5
  23.7 2.3 %collective-permute-start.1 = (f32[8,64,256]{2,1,0:T(8,128)}, f32[8,64,256]{2,1,0:T(8,128)S(1)}, u32[]{:S(2)}, u32[]{:S(2)}) collective-permute-start(f32[8,64,256]{2,1,0:T(8,128)} %get-tuple-element.30), channel_id=1, source_target_pairs={{0,64},{8,72},{16,80},{24,88},{1,65},{9,73},{17,81},{25,89},{2,66}... | collective-permute-start | bytes 1572872 | tf_op jit(solution)/shard_map/ppermute | solution.py:610
  26.0 1.7 %collective-permute-done.3.refs_1_ = bf16[256,512]{1,0:T(8,128)(2,1)S(1)} collective-permute-done((bf16[256,512]{1,0:T(8,128)(2,1)}, bf16[256,512]{1,0:T(8,128)(2,1)S(1)}, u32[]{:S(2)}, u32[]{:S(2)}) %collective-permute-start.3) | collective-permute-done | bytes 262176 | tf_op jit(solution)/shard_map/ppermute | solution.py:600
  27.7 2.4 %collective-permute-start.2 = (f32[8,64,256]{2,1,0:T(8,128)}, f32[8,64,256]{2,1,0:T(8,128)S(1)}, u32[]{:S(2)}, u32[]{:S(2)}) collective-permute-start(f32[8,64,256]{2,1,0:T(8,128)} %get-tuple-element.31), channel_id=1, source_target_pairs={{0,96},{8,104},{16,112},{24,120},{1,97},{9,105},{17,113},{25,121},... | collective-permute-start | bytes 1572872 | tf_op jit(solution)/shard_map/ppermute | solution.py:610
  30.2 4.0 %collective-permute-done.4.refs_2_ = bf16[256,512]{1,0:T(8,128)(2,1)S(1)} collective-permute-done((bf16[256,512]{1,0:T(8,128)(2,1)}, bf16[256,512]{1,0:T(8,128)(2,1)S(1)}, u32[]{:S(2)}, u32[]{:S(2)}) %collective-permute-start.4) | collective-permute-done | bytes 262176 | tf_op jit(solution)/shard_map/ppermute | solution.py:600
  34.3 0.9 copy-done.4
  35.2 1.5 shard_map.47
  36.7 1.3 collective-permute-start.6
  38.0 1.7 %collective-permute-start.7 = (bf16[64,512]{1,0:T(8,128)(2,1)S(1)}, bf16[64,512]{1,0:T(8,128)(2,1)S(1)}, u32[]{:S(2)}, u32[]{:S(2)}) collective-permute-start(bf16[64,512]{1,0:T(8,128)(2,1)S(1)} %get-tuple-element.42), channel_id=1, source_target_pairs={{0,64},{8,72},{16,80},{24,88},{1,65},{9,73},{17,81},{25,89},{2,66}... | collective-permute-start | bytes 196616 | tf_op jit(solution)/shard_map/ppermute | solution.py:610
  39.7 1.3 collective-permute-start.8
  41.1 2.7 %collective-permute-start.10 = (bf16[256,512]{1,0:T(8,128)(2,1)S(1)}, bf16[256,512]{1,0:T(8,128)(2,1)S(1)}, u32[]{:S(2)}, u32[]{:S(2)}) collective-permute-start(bf16[256,512]{1,0:T(8,128)(2,1)S(1)} %get-tuple-element.46), channel_id=1, source_target_pairs={{0,64},{8,72},{16,80},{24,88},{32,96},{40,104},{48,112},{56,120},{... | collective-permute-start | bytes 786440 | tf_op jit(solution)/shard_map/ppermute | solution.py:605
  43.8 2.1 %collective-permute-start.11 = (bf16[256,512]{1,0:T(8,128)(2,1)S(1)}, bf16[256,512]{1,0:T(8,128)(2,1)S(1)}, u32[]{:S(2)}, u32[]{:S(2)}) collective-permute-start(bf16[256,512]{1,0:T(8,128)(2,1)S(1)} %get-tuple-element.47), channel_id=1, source_target_pairs={{0,96},{8,104},{16,112},{24,120},{32,0},{40,8},{48,16},{56,24},{64... | collective-permute-start | bytes 786440 | tf_op jit(solution)/shard_map/ppermute | solution.py:605
  45.9 1.1 shard_map.48
  47.0 17.2 %all-gather = s16[1664,256]{1,0:T(8,128)(2,1)S(1)} all-gather(s16[208,256]{1,0:T(8,128)(2,1)S(1)} %shard_map.48), channel_id=2, replica_groups=mesh['prow'=16,'pcol'=8] {'pcol'}, dimensions={0}, use_global_device_ids=true | all-gather | bytes 958464 | tf_op jit(solution)/shard_map/all_gather | solution.py:669
  64.2 1.0 shard_map.49
  65.2 1.7 %shard_map.50 = s16[784,256]{1,0:T(8,128)(2,1)S(1)} custom-call(s32[2,16]{1,0:T(2,128)S(1)} %copy-done.3, s32[2]{0:T(128)S(1)} %copy-done.1, f32[8,64,256]{2,1,0:T(8,128)S(1)} %copy-done, f32[8,64,256]{2,1,0:T(8,128)S(1)} %collective-permute-done.f1, f32[8,64,256]{2,1,0:T(8,128)S(1)} %collective-permute-done.1.f2, ...), custom_call_target="tpu_custom_call" | custom-call | bytes 2097152 | tf_op jit(solution)/shard_map/pallas_call | solution.py:680
  66.9 42.3 %all-gather.11 = s16[12544,256]{1,0:T(8,128)(2,1)} all-gather(s16[784,256]{1,0:T(8,128)(2,1)S(1)} %shard_map.50), channel_id=3, replica_groups=mesh['prow'=16,'pcol'=8] {'prow'}, dimensions={0}, use_global_device_ids=true | all-gather | bytes 6823936 | tf_op jit(solution)/shard_map/all_gather | solution.py:694
  109.2 4.9 %all-gather.10.cloned.1.call-done = bf16[32,256,512]{2,1,0:T(8,128)(2,1)} async-done(((bf16[4,256,512]{2,1,0:T(8,128)(2,1)}), bf16[32,256,512]{2,1,0:T(8,128)(2,1)}) %all-gather.10.cloned.1.call-update) | async-done | bytes 8388624 | tf_op jit(solution)/shard_map/all_gather | solution.py:693
  114.1 45.0 %shard_map.51 = f32[1024,2,8,128]{3,2,1,0:T(8,128)} custom-call(s32[2,16]{1,0:T(2,128)} %map_ref.7, s32[2]{0:T(128)} %pad_add_fusion.rc_ref, s16[16,784,256]{2,1,0:T(8,128)(2,1)} %bitcast.23, s32[8,520,256]{2,1,0:T(8,128)} %bitcast.26, f32[1024,2,8,128]{3,2,1,0:T(8,128)} %bitcast.22, bf16[8,4,256,512]{3,2,1,0:T(8,128)(2,1)} %bitcast.25), custom_call_target="tpu_custom_call" | custom-call | flops 24696061952 | bytes 33554432 | tf_op jit(solution)/shard_map/pallas_call | solution.py:564
  (25 shorter events, 0.2 us)
Async XLA Ops:
  6.5 102.7 %all-gather.8.cloned.1.call-start = ((), (), s32[]{:S(2)}) async-start(), calls=%async_computation | async-start | bytes 4792320 | tf_op jit(solution)/shard_map/all_gather | solution.py:639
  7.1 27.1 %copy-start.1 = (s32[2]{0:T(128)S(1)}, s32[2]{0:T(128)}, u32[]{:S(2)}) copy-start(s32[2]{0:T(128)} %pad_add_fusion.rc_ref) | copy-start | bytes 28
  7.1 27.1 %copy-start.2 = (s32[4,256]{1,0:T(4,128)S(1)}, s32[4,256]{1,0:T(4,128)}, u32[]{:S(2)}) copy-start(s32[4,256]{1,0:T(4,128)} %pivots_ref.3) | copy-start | bytes 12292
  7.1 27.1 %copy-start.3 = (s32[2,16]{1,0:T(2,128)S(1)}, s32[2,16]{1,0:T(2,128)}, u32[]{:S(2)}) copy-start(s32[2,16]{1,0:T(2,128)} %map_ref.7) | copy-start | bytes 388
  13.9 100.2 %all-gather.10.cloned.1.call-start = ((), (), s32[]{:S(2)}) async-start(), calls=%async_computation.1 | async-start | bytes 9437184 | tf_op jit(solution)/shard_map/all_gather | solution.py:693
  13.9 20.3 %collective-permute-start = (f32[8,64,256]{2,1,0:T(8,128)}, f32[8,64,256]{2,1,0:T(8,128)S(1)}, u32[]{:S(2)}, u32[]{:S(2)}) collective-permute-start(f32[8,64,256]{2,1,0:T(8,128)} %get-tuple-element.29), channel_id=1, source_target_pairs={{0,32},{8,40},{16,48},{24,56},{1,33},{9,41},{17,49},{25,57},{2,34}... | collective-permute-start | bytes 1572872 | tf_op jit(solution)/shard_map/ppermute | solution.py:610
  18.0 9.8 %collective-permute-start.3 = (bf16[256,512]{1,0:T(8,128)(2,1)}, bf16[256,512]{1,0:T(8,128)(2,1)S(1)}, u32[]{:S(2)}, u32[]{:S(2)}) collective-permute-start(bf16[256,512]{1,0:T(8,128)(2,1)} %get-tuple-element.33), channel_id=1, source_target_pairs={{0,8},{8,16},{16,24},{24,0},{32,40},{40,48},{48,56},{56,32},{64,72... | collective-permute-start | bytes 786440 | tf_op jit(solution)/shard_map/ppermute | solution.py:600
  19.7 14.5 %collective-permute-start.4 = (bf16[256,512]{1,0:T(8,128)(2,1)}, bf16[256,512]{1,0:T(8,128)(2,1)S(1)}, u32[]{:S(2)}, u32[]{:S(2)}) collective-permute-start(bf16[256,512]{1,0:T(8,128)(2,1)} %get-tuple-element.34), channel_id=1, source_target_pairs={{0,16},{8,24},{16,0},{24,8},{32,48},{40,56},{48,32},{56,40},{64,80... | collective-permute-start | bytes 786440 | tf_op jit(solution)/shard_map/ppermute | solution.py:600
  23.0 11.2 %collective-permute-start.5 = (bf16[256,512]{1,0:T(8,128)(2,1)}, bf16[256,512]{1,0:T(8,128)(2,1)S(1)}, u32[]{:S(2)}, u32[]{:S(2)}) collective-permute-start(bf16[256,512]{1,0:T(8,128)(2,1)} %get-tuple-element.35), channel_id=1, source_target_pairs={{0,24},{8,0},{16,8},{24,16},{32,56},{40,32},{48,40},{56,48},{64,88... | collective-permute-start | bytes 786440 | tf_op jit(solution)/shard_map/ppermute | solution.py:600
  23.7 17.3 %collective-permute-start.1 = (f32[8,64,256]{2,1,0:T(8,128)}, f32[8,64,256]{2,1,0:T(8,128)S(1)}, u32[]{:S(2)}, u32[]{:S(2)}) collective-permute-start(f32[8,64,256]{2,1,0:T(8,128)} %get-tuple-element.30), channel_id=1, source_target_pairs={{0,64},{8,72},{16,80},{24,88},{1,65},{9,73},{17,81},{25,89},{2,66}... | collective-permute-start | bytes 1572872 | tf_op jit(solution)/shard_map/ppermute | solution.py:610
  27.7 13.4 %collective-permute-start.2 = (f32[8,64,256]{2,1,0:T(8,128)}, f32[8,64,256]{2,1,0:T(8,128)S(1)}, u32[]{:S(2)}, u32[]{:S(2)}) collective-permute-start(f32[8,64,256]{2,1,0:T(8,128)} %get-tuple-element.31), channel_id=1, source_target_pairs={{0,96},{8,104},{16,112},{24,120},{1,97},{9,105},{17,113},{25,121},... | collective-permute-start | bytes 1572872 | tf_op jit(solution)/shard_map/ppermute | solution.py:610
  34.3 1.0 copy-start.4
  35.2 10.7 %copy-start = (f32[8,64,256]{2,1,0:T(8,128)S(1)}, f32[8,64,256]{2,1,0:T(8,128)}, u32[]{:S(2)}) copy-start(f32[8,64,256]{2,1,0:T(8,128)} %get-tuple-element.28.f0) | copy-start | bytes 1572868
  36.7 7.1 %collective-permute-start.6 = (bf16[64,512]{1,0:T(8,128)(2,1)S(1)}, bf16[64,512]{1,0:T(8,128)(2,1)S(1)}, u32[]{:S(2)}, u32[]{:S(2)}) collective-permute-start(bf16[64,512]{1,0:T(8,128)(2,1)S(1)} %get-tuple-element.41), channel_id=1, source_target_pairs={{0,32},{8,40},{16,48},{24,56},{1,33},{9,41},{17,49},{25,57},{2,34}... | collective-permute-start | bytes 196616 | tf_op jit(solution)/shard_map/ppermute | solution.py:610
  38.0 7.9 %collective-permute-start.7 = (bf16[64,512]{1,0:T(8,128)(2,1)S(1)}, bf16[64,512]{1,0:T(8,128)(2,1)S(1)}, u32[]{:S(2)}, u32[]{:S(2)}) collective-permute-start(bf16[64,512]{1,0:T(8,128)(2,1)S(1)} %get-tuple-element.42), channel_id=1, source_target_pairs={{0,64},{8,72},{16,80},{24,88},{1,65},{9,73},{17,81},{25,89},{2,66}... | collective-permute-start | bytes 196616 | tf_op jit(solution)/shard_map/ppermute | solution.py:610
  39.7 6.2 %collective-permute-start.8 = (bf16[64,512]{1,0:T(8,128)(2,1)S(1)}, bf16[64,512]{1,0:T(8,128)(2,1)S(1)}, u32[]{:S(2)}, u32[]{:S(2)}) collective-permute-start(bf16[64,512]{1,0:T(8,128)(2,1)S(1)} %get-tuple-element.43), channel_id=1, source_target_pairs={{0,96},{8,104},{16,112},{24,120},{1,97},{9,105},{17,113},{25,121},... | collective-permute-start | bytes 196616 | tf_op jit(solution)/shard_map/ppermute | solution.py:610
  41.0 23.2 %collective-permute-start.9 = (bf16[256,512]{1,0:T(8,128)(2,1)S(1)}, bf16[256,512]{1,0:T(8,128)(2,1)S(1)}, u32[]{:S(2)}, u32[]{:S(2)}) collective-permute-start(bf16[256,512]{1,0:T(8,128)(2,1)S(1)} %get-tuple-element.45), channel_id=1, source_target_pairs={{0,32},{8,40},{16,48},{24,56},{32,64},{40,72},{48,80},{56,88},{64,... | collective-permute-start | bytes 786440 | tf_op jit(solution)/shard_map/ppermute | solution.py:605
  41.1 23.1 %collective-permute-start.10 = (bf16[256,512]{1,0:T(8,128)(2,1)S(1)}, bf16[256,512]{1,0:T(8,128)(2,1)S(1)}, u32[]{:S(2)}, u32[]{:S(2)}) collective-permute-start(bf16[256,512]{1,0:T(8,128)(2,1)S(1)} %get-tuple-element.46), channel_id=1, source_target_pairs={{0,64},{8,72},{16,80},{24,88},{32,96},{40,104},{48,112},{56,120},{... | collective-permute-start | bytes 786440 | tf_op jit(solution)/shard_map/ppermute | solution.py:605
  43.8 20.4 %collective-permute-start.11 = (bf16[256,512]{1,0:T(8,128)(2,1)S(1)}, bf16[256,512]{1,0:T(8,128)(2,1)S(1)}, u32[]{:S(2)}, u32[]{:S(2)}) collective-permute-start(bf16[256,512]{1,0:T(8,128)(2,1)S(1)} %get-tuple-element.47), channel_id=1, source_target_pairs={{0,96},{8,104},{16,112},{24,120},{32,0},{40,8},{48,16},{56,24},{64... | collective-permute-start | bytes 786440 | tf_op jit(solution)/shard_map/ppermute | solution.py:605
Sparse Core Ops, SparseCore 0:
  14.0 35.9 all-gather.7
  65.3 48.7 all-gather.9

commit v15 on v14

--- a/solution.py
+++ b/solution.py
@@ -556,7 +556,7 @@
             out_copy(step, quarter).wait()
 
 
-LINES = 32
+LINES = 16
 
 
 def run_finish(child_map, rc, top, front_left, view, child):

time: 166 us -> 166 us (level)
  no operation moved by 1% of the time
where the time goes in v15:
time: 166 us
  blocking collectives  59.4 us (36%)
  Pallas kernels  56.9 us (34%)
  starting transfers between devices  23.7 us (14%)
  between operations  13.6 us (8%)
  waiting for transfers between devices  10.8 us (7%)
    pallas_call x1, Pallas kernels, run_finish(): pl.pallas_call(finish, out_shape=shape(view.shape, F32), in_specs=[SMEM,...  44.9 us
    all_gather x1, blocking collectives, shards(): top = lax.all_gather(code, 'prow', axis=0, tiled=False)  42.2 us
    all_gather x1, blocking collectives, shards(): thin = lax.all_gather(thin, 'pcol', axis=0, tiled=False)  17.2 us
    ppermute x6, starting transfers between devices, from_plane(): return lax.ppermute(a, 'prow', [(j, 4 * hop + j) for j in range(4)])  13 us
    pallas_call x1, Pallas kernels, shards(): pl.pallas_call(begin, out_shape=[strip] * 4 + [shape((8, PIECE, BS), F32)...  6.74 us
    ppermute x3, waiting for transfers between devices, along_z(): lax.ppermute(a, 'prow', [(4 * i + j, 4 * i + (j + hop) % 4) for i in rang...  5.74 us
    ppermute x3, starting transfers between devices, along_z(): lax.ppermute(a, 'prow', [(4 * i + j, 4 * i + (j + hop) % 4) for i in rang...  5.74 us
    all_gather x1, waiting for transfers between devices, shards(): child = lax.all_gather(child, 'pcol', axis=0, tiled=False)  5.02 us
  transfers between devices with their start and end apart: 14, of which 3 were waited for; matrix products, arithmetic and copies ran while one was open for 0% of the time, Pallas kernels for 3%

profile of v15, /device:TPU:1, one launch (start us, length us, event | category | flops | bytes accessed | tf_op | source)
XLA Modules:
  0.0 165.9 jit_solution(4234493519162403181)
XLA Ops:
  6.5 0.6 pad_add_fusion.rc_ref
  7.1 6.7 %shard_map.46 = (bf16[256,512]{1,0:T(8,128)(2,1)}, bf16[256,512]{1,0:T(8,128)(2,1)}, bf16[256,512]{1,0:T(8,128)(2,1)}, bf16[256,512]{1,0:T(8,128)(2,1)}, f32[8,6...) custom-call(s32[2,16]{1,0:T(2,128)} %map_ref.7, ...), custom_call_target="tpu_custom_call" | custom-call | flops 1073741824 | bytes 8388608 | tf_op jit(solution)/shard_map/pallas_call | solution.py:619
  13.9 4.0 %collective-permute-start = (f32[8,64,256]{2,1,0:T(8,128)}, f32[8,64,256]{2,1,0:T(8,128)S(1)}, u32[]{:S(2)}, u32[]{:S(2)}) collective-permute-start(f32[8,64,256]{2,1,0:T(8,128)} %get-tuple-element.29), channel_id=1, source_target_pairs={{0,32},{8,40},{16,48},{24,56},{1,33},{9,41},{17,49},{25,57},{2,34}... | collective-permute-start | bytes 1572872 | tf_op jit(solution)/shard_map/ppermute | solution.py:610
  18.0 1.7 %collective-permute-start.3 = (bf16[256,512]{1,0:T(8,128)(2,1)}, bf16[256,512]{1,0:T(8,128)(2,1)S(1)}, u32[]{:S(2)}, u32[]{:S(2)}) collective-permute-start(bf16[256,512]{1,0:T(8,128)(2,1)} %get-tuple-element.33), channel_id=1, source_target_pairs={{0,8},{8,16},{16,24},{24,0},{32,40},{40,48},{48,56},{56,32},{64,72... | collective-permute-start | bytes 786440 | tf_op jit(solution)/shard_map/ppermute | solution.py:600
  19.7 3.3 %collective-permute-start.4 = (bf16[256,512]{1,0:T(8,128)(2,1)}, bf16[256,512]{1,0:T(8,128)(2,1)S(1)}, u32[]{:S(2)}, u32[]{:S(2)}) collective-permute-start(bf16[256,512]{1,0:T(8,128)(2,1)} %get-tuple-element.34), channel_id=1, source_target_pairs={{0,16},{8,24},{16,0},{24,8},{32,48},{40,56},{48,32},{56,40},{64,80... | collective-permute-start | bytes 786440 | tf_op jit(solution)/shard_map/ppermute | solution.py:600
  23.0 0.7 collective-permute-start.5
  23.7 2.3 %collective-permute-start.1 = (f32[8,64,256]{2,1,0:T(8,128)}, f32[8,64,256]{2,1,0:T(8,128)S(1)}, u32[]{:S(2)}, u32[]{:S(2)}) collective-permute-start(f32[8,64,256]{2,1,0:T(8,128)} %get-tuple-element.30), channel_id=1, source_target_pairs={{0,64},{8,72},{16,80},{24,88},{1,65},{9,73},{17,81},{25,89},{2,66}... | collective-permute-start | bytes 1572872 | tf_op jit(solution)/shard_map/ppermute | solution.py:610
  26.0 1.7 %collective-permute-done.3.refs_1_ = bf16[256,512]{1,0:T(8,128)(2,1)S(1)} collective-permute-done((bf16[256,512]{1,0:T(8,128)(2,1)}, bf16[256,512]{1,0:T(8,128)(2,1)S(1)}, u32[]{:S(2)}, u32[]{:S(2)}) %collective-permute-start.3) | collective-permute-done | bytes 262176 | tf_op jit(solution)/shard_map/ppermute | solution.py:600
  27.7 2.4 %collective-permute-start.2 = (f32[8,64,256]{2,1,0:T(8,128)}, f32[8,64,256]{2,1,0:T(8,128)S(1)}, u32[]{:S(2)}, u32[]{:S(2)}) collective-permute-start(f32[8,64,256]{2,1,0:T(8,128)} %get-tuple-element.31), channel_id=1, source_target_pairs={{0,96},{8,104},{16,112},{24,120},{1,97},{9,105},{17,113},{25,121},... | collective-permute-start | bytes 1572872 | tf_op jit(solution)/shard_map/ppermute | solution.py:610
  30.2 4.0 %collective-permute-done.4.refs_2_ = bf16[256,512]{1,0:T(8,128)(2,1)S(1)} collective-permute-done((bf16[256,512]{1,0:T(8,128)(2,1)}, bf16[256,512]{1,0:T(8,128)(2,1)S(1)}, u32[]{:S(2)}, u32[]{:S(2)}) %collective-permute-start.4) | collective-permute-done | bytes 262176 | tf_op jit(solution)/shard_map/ppermute | solution.py:600
  34.3 0.9 copy-done.4
  35.2 1.5 shard_map.47
  36.7 1.3 collective-permute-start.6
  38.0 1.6 collective-permute-start.7
  39.7 1.3 collective-permute-start.8
  41.1 2.7 %collective-permute-start.10 = (bf16[256,512]{1,0:T(8,128)(2,1)S(1)}, bf16[256,512]{1,0:T(8,128)(2,1)S(1)}, u32[]{:S(2)}, u32[]{:S(2)}) collective-permute-start(bf16[256,512]{1,0:T(8,128)(2,1)S(1)} %get-tuple-element.46), channel_id=1, source_target_pairs={{0,64},{8,72},{16,80},{24,88},{32,96},{40,104},{48,112},{56,120},{... | collective-permute-start | bytes 786440 | tf_op jit(solution)/shard_map/ppermute | solution.py:605
  43.8 2.1 %collective-permute-start.11 = (bf16[256,512]{1,0:T(8,128)(2,1)S(1)}, bf16[256,512]{1,0:T(8,128)(2,1)S(1)}, u32[]{:S(2)}, u32[]{:S(2)}) collective-permute-start(bf16[256,512]{1,0:T(8,128)(2,1)S(1)} %get-tuple-element.47), channel_id=1, source_target_pairs={{0,96},{8,104},{16,112},{24,120},{32,0},{40,8},{48,16},{56,24},{64... | collective-permute-start | bytes 786440 | tf_op jit(solution)/shard_map/ppermute | solution.py:605
  45.9 1.1 shard_map.48
  47.0 17.2 %all-gather = s16[1664,256]{1,0:T(8,128)(2,1)S(1)} all-gather(s16[208,256]{1,0:T(8,128)(2,1)S(1)} %shard_map.48), channel_id=2, replica_groups=mesh['prow'=16,'pcol'=8] {'pcol'}, dimensions={0}, use_global_device_ids=true | all-gather | bytes 958464 | tf_op jit(solution)/shard_map/all_gather | solution.py:669
  64.2 1.0 shard_map.49
  65.2 1.7 %shard_map.50 = s16[784,256]{1,0:T(8,128)(2,1)S(1)} custom-call(s32[2,16]{1,0:T(2,128)S(1)} %copy-done.3, s32[2]{0:T(128)S(1)} %copy-done.1, f32[8,64,256]{2,1,0:T(8,128)S(1)} %copy-done, f32[8,64,256]{2,1,0:T(8,128)S(1)} %collective-permute-done.f1, f32[8,64,256]{2,1,0:T(8,128)S(1)} %collective-permute-done.1.f2, ...), custom_call_target="tpu_custom_call" | custom-call | bytes 2097152 | tf_op jit(solution)/shard_map/pallas_call | solution.py:680
  66.9 42.2 %all-gather.11 = s16[12544,256]{1,0:T(8,128)(2,1)} all-gather(s16[784,256]{1,0:T(8,128)(2,1)S(1)} %shard_map.50), channel_id=3, replica_groups=mesh['prow'=16,'pcol'=8] {'prow'}, dimensions={0}, use_global_device_ids=true | all-gather | bytes 6823936 | tf_op jit(solution)/shard_map/all_gather | solution.py:694
  109.1 5.0 %all-gather.10.cloned.1.call-done = bf16[32,256,512]{2,1,0:T(8,128)(2,1)} async-done(((bf16[4,256,512]{2,1,0:T(8,128)(2,1)}), bf16[32,256,512]{2,1,0:T(8,128)(2,1)}) %all-gather.10.cloned.1.call-update) | async-done | bytes 8388624 | tf_op jit(solution)/shard_map/all_gather | solution.py:693
  114.1 44.9 %shard_map.51 = f32[1024,2,8,128]{3,2,1,0:T(8,128)} custom-call(s32[2,16]{1,0:T(2,128)} %map_ref.7, s32[2]{0:T(128)} %pad_add_fusion.rc_ref, s16[16,784,256]{2,1,0:T(8,128)(2,1)} %bitcast.23, s32[8,520,256]{2,1,0:T(8,128)} %bitcast.26, f32[1024,2,8,128]{3,2,1,0:T(8,128)} %bitcast.22, bf16[8,4,256,512]{3,2,1,0:T(8,128)(2,1)} %bitcast.25), custom_call_target="tpu_custom_call" | custom-call | flops 24696061952 | bytes 33554432 | tf_op jit(solution)/shard_map/pallas_call | solution.py:564
  (25 shorter events, 0.2 us)
Async XLA Ops:
  6.5 102.6 %all-gather.8.cloned.1.call-start = ((), (), s32[]{:S(2)}) async-start(), calls=%async_computation | async-start | bytes 4792320 | tf_op jit(solution)/shard_map/all_gather | solution.py:639
  7.1 27.1 %copy-start.1 = (s32[2]{0:T(128)S(1)}, s32[2]{0:T(128)}, u32[]{:S(2)}) copy-start(s32[2]{0:T(128)} %pad_add_fusion.rc_ref) | copy-start | bytes 28
  7.1 27.1 %copy-start.2 = (s32[4,256]{1,0:T(4,128)S(1)}, s32[4,256]{1,0:T(4,128)}, u32[]{:S(2)}) copy-start(s32[4,256]{1,0:T(4,128)} %pivots_ref.3) | copy-start | bytes 12292
  7.1 27.1 %copy-start.3 = (s32[2,16]{1,0:T(2,128)S(1)}, s32[2,16]{1,0:T(2,128)}, u32[]{:S(2)}) copy-start(s32[2,16]{1,0:T(2,128)} %map_ref.7) | copy-start | bytes 388
  13.9 100.2 %all-gather.10.cloned.1.call-start = ((), (), s32[]{:S(2)}) async-start(), calls=%async_computation.1 | async-start | bytes 9437184 | tf_op jit(solution)/shard_map/all_gather | solution.py:693
  13.9 20.3 %collective-permute-start = (f32[8,64,256]{2,1,0:T(8,128)}, f32[8,64,256]{2,1,0:T(8,128)S(1)}, u32[]{:S(2)}, u32[]{:S(2)}) collective-permute-start(f32[8,64,256]{2,1,0:T(8,128)} %get-tuple-element.29), channel_id=1, source_target_pairs={{0,32},{8,40},{16,48},{24,56},{1,33},{9,41},{17,49},{25,57},{2,34}... | collective-permute-start | bytes 1572872 | tf_op jit(solution)/shard_map/ppermute | solution.py:610
  18.0 9.8 %collective-permute-start.3 = (bf16[256,512]{1,0:T(8,128)(2,1)}, bf16[256,512]{1,0:T(8,128)(2,1)S(1)}, u32[]{:S(2)}, u32[]{:S(2)}) collective-permute-start(bf16[256,512]{1,0:T(8,128)(2,1)} %get-tuple-element.33), channel_id=1, source_target_pairs={{0,8},{8,16},{16,24},{24,0},{32,40},{40,48},{48,56},{56,32},{64,72... | collective-permute-start | bytes 786440 | tf_op jit(solution)/shard_map/ppermute | solution.py:600
  19.7 14.5 %collective-permute-start.4 = (bf16[256,512]{1,0:T(8,128)(2,1)}, bf16[256,512]{1,0:T(8,128)(2,1)S(1)}, u32[]{:S(2)}, u32[]{:S(2)}) collective-permute-start(bf16[256,512]{1,0:T(8,128)(2,1)} %get-tuple-element.34), channel_id=1, source_target_pairs={{0,16},{8,24},{16,0},{24,8},{32,48},{40,56},{48,32},{56,40},{64,80... | collective-permute-start | bytes 786440 | tf_op jit(solution)/shard_map/ppermute | solution.py:600
  23.0 11.2 %collective-permute-start.5 = (bf16[256,512]{1,0:T(8,128)(2,1)}, bf16[256,512]{1,0:T(8,128)(2,1)S(1)}, u32[]{:S(2)}, u32[]{:S(2)}) collective-permute-start(bf16[256,512]{1,0:T(8,128)(2,1)} %get-tuple-element.35), channel_id=1, source_target_pairs={{0,24},{8,0},{16,8},{24,16},{32,56},{40,32},{48,40},{56,48},{64,88... | collective-permute-start | bytes 786440 | tf_op jit(solution)/shard_map/ppermute | solution.py:600
  23.7 17.2 %collective-permute-start.1 = (f32[8,64,256]{2,1,0:T(8,128)}, f32[8,64,256]{2,1,0:T(8,128)S(1)}, u32[]{:S(2)}, u32[]{:S(2)}) collective-permute-start(f32[8,64,256]{2,1,0:T(8,128)} %get-tuple-element.30), channel_id=1, source_target_pairs={{0,64},{8,72},{16,80},{24,88},{1,65},{9,73},{17,81},{25,89},{2,66}... | collective-permute-start | bytes 1572872 | tf_op jit(solution)/shard_map/ppermute | solution.py:610
  27.7 13.3 %collective-permute-start.2 = (f32[8,64,256]{2,1,0:T(8,128)}, f32[8,64,256]{2,1,0:T(8,128)S(1)}, u32[]{:S(2)}, u32[]{:S(2)}) collective-permute-start(f32[8,64,256]{2,1,0:T(8,128)} %get-tuple-element.31), channel_id=1, source_target_pairs={{0,96},{8,104},{16,112},{24,120},{1,97},{9,105},{17,113},{25,121},... | collective-permute-start | bytes 1572872 | tf_op jit(solution)/shard_map/ppermute | solution.py:610
  34.3 1.0 copy-start.4
  35.2 10.7 %copy-start = (f32[8,64,256]{2,1,0:T(8,128)S(1)}, f32[8,64,256]{2,1,0:T(8,128)}, u32[]{:S(2)}) copy-start(f32[8,64,256]{2,1,0:T(8,128)} %get-tuple-element.28.f0) | copy-start | bytes 1572868
  36.7 7.1 %collective-permute-start.6 = (bf16[64,512]{1,0:T(8,128)(2,1)S(1)}, bf16[64,512]{1,0:T(8,128)(2,1)S(1)}, u32[]{:S(2)}, u32[]{:S(2)}) collective-permute-start(bf16[64,512]{1,0:T(8,128)(2,1)S(1)} %get-tuple-element.41), channel_id=1, source_target_pairs={{0,32},{8,40},{16,48},{24,56},{1,33},{9,41},{17,49},{25,57},{2,34}... | collective-permute-start | bytes 196616 | tf_op jit(solution)/shard_map/ppermute | solution.py:610
  38.0 7.9 %collective-permute-start.7 = (bf16[64,512]{1,0:T(8,128)(2,1)S(1)}, bf16[64,512]{1,0:T(8,128)(2,1)S(1)}, u32[]{:S(2)}, u32[]{:S(2)}) collective-permute-start(bf16[64,512]{1,0:T(8,128)(2,1)S(1)} %get-tuple-element.42), channel_id=1, source_target_pairs={{0,64},{8,72},{16,80},{24,88},{1,65},{9,73},{17,81},{25,89},{2,66}... | collective-permute-start | bytes 196616 | tf_op jit(solution)/shard_map/ppermute | solution.py:610
  39.7 6.2 %collective-permute-start.8 = (bf16[64,512]{1,0:T(8,128)(2,1)S(1)}, bf16[64,512]{1,0:T(8,128)(2,1)S(1)}, u32[]{:S(2)}, u32[]{:S(2)}) collective-permute-start(bf16[64,512]{1,0:T(8,128)(2,1)S(1)} %get-tuple-element.43), channel_id=1, source_target_pairs={{0,96},{8,104},{16,112},{24,120},{1,97},{9,105},{17,113},{25,121},... | collective-permute-start | bytes 196616 | tf_op jit(solution)/shard_map/ppermute | solution.py:610
  41.0 23.2 %collective-permute-start.9 = (bf16[256,512]{1,0:T(8,128)(2,1)S(1)}, bf16[256,512]{1,0:T(8,128)(2,1)S(1)}, u32[]{:S(2)}, u32[]{:S(2)}) collective-permute-start(bf16[256,512]{1,0:T(8,128)(2,1)S(1)} %get-tuple-element.45), channel_id=1, source_target_pairs={{0,32},{8,40},{16,48},{24,56},{32,64},{40,72},{48,80},{56,88},{64,... | collective-permute-start | bytes 786440 | tf_op jit(solution)/shard_map/ppermute | solution.py:605
  41.1 23.1 %collective-permute-start.10 = (bf16[256,512]{1,0:T(8,128)(2,1)S(1)}, bf16[256,512]{1,0:T(8,128)(2,1)S(1)}, u32[]{:S(2)}, u32[]{:S(2)}) collective-permute-start(bf16[256,512]{1,0:T(8,128)(2,1)S(1)} %get-tuple-element.46), channel_id=1, source_target_pairs={{0,64},{8,72},{16,80},{24,88},{32,96},{40,104},{48,112},{56,120},{... | collective-permute-start | bytes 786440 | tf_op jit(solution)/shard_map/ppermute | solution.py:605
  43.8 20.4 %collective-permute-start.11 = (bf16[256,512]{1,0:T(8,128)(2,1)S(1)}, bf16[256,512]{1,0:T(8,128)(2,1)S(1)}, u32[]{:S(2)}, u32[]{:S(2)}) collective-permute-start(bf16[256,512]{1,0:T(8,128)(2,1)S(1)} %get-tuple-element.47), channel_id=1, source_target_pairs={{0,96},{8,104},{16,112},{24,120},{32,0},{40,8},{48,16},{56,24},{64... | collective-permute-start | bytes 786440 | tf_op jit(solution)/shard_map/ppermute | solution.py:605
Sparse Core Ops, SparseCore 0:
  14.0 35.9 all-gather.7
  65.3 48.7 all-gather.9

commit v16 on v14

--- a/solution.py
+++ b/solution.py
@@ -625,7 +625,7 @@
             pltpu.VMEM((BS * 16, HALF), F32), pltpu.VMEM((tiles * BS, BS), F32),
             pltpu.SemaphoreType.DMA((3,)),
         ],
-        compiler_params=pltpu.CompilerParams(vmem_limit_bytes=LIMIT),
+        compiler_params=pltpu.CompilerParams(vmem_limit_bytes=2 * SMALL),
         cost_estimate=pl.CostEstimate(flops=2**30, bytes_accessed=8 * 2**20, transcendentals=0),
     )(
         child_map, rc, child_update.reshape(2, BS, 2 * BS), pivots,

time: 166 us -> 170 us (1.024)
  local copies, waits for them, and re-layouts: 0.96 us -> 5.8 us
    unnamed x10 -> x14, local copies, waits for them, and re-layouts: 0.96 us -> 5.8 us
  transfers between devices with their start and end apart: 14 -> 14, of which waited for: 3 -> 5; matrix products, arithmetic and copies ran while one was open for 0% -> 0% of each run, Pallas kernels for 3% -> 3%
where the time goes in v16:
time: 170 us
  blocking collectives  59.3 us (35%)
  Pallas kernels  55.8 us (33%)
  starting transfers between devices  24.6 us (14%)
  between operations  13.5 us (8%)
  waiting for transfers between devices  10.9 us (6%)
  local copies, waits for them, and re-layouts  5.8 us (3%)
    pallas_call x1, Pallas kernels, run_finish(): pl.pallas_call(finish, out_shape=shape(view.shape, F32), in_specs=[SMEM,...  45 us
    all_gather x1, blocking collectives, shards(): top = lax.all_gather(code, 'prow', axis=0, tiled=False)  42.1 us
    all_gather x1, blocking collectives, shards(): thin = lax.all_gather(thin, 'pcol', axis=0, tiled=False)  17.2 us
    ppermute x6, starting transfers between devices, from_plane(): return lax.ppermute(a, 'prow', [(j, 4 * hop + j) for j in range(4)])  13 us
    ppermute x3, starting transfers between devices, along_y(): lax.ppermute(a, 'prow', [(4 * i + j, 4 * ((i + hop) % 4) + j) for i in ra...  5.88 us
    unnamed x14, local copies, waits for them, and re-layouts  5.8 us
    ppermute x3, starting transfers between devices, along_z(): lax.ppermute(a, 'prow', [(4 * i + j, 4 * i + (j + hop) % 4) for i in rang...  5.74 us
    ppermute x3, waiting for transfers between devices, along_z(): lax.ppermute(a, 'prow', [(4 * i + j, 4 * i + (j + hop) % 4) for i in rang...  5.68 us
  transfers between devices with their start and end apart: 14, of which 5 were waited for; matrix products, arithmetic and copies ran while one was open for 0% of the time, Pallas kernels for 3%

profile of v16, /device:TPU:1, one launch (start us, length us, event | category | flops | bytes accessed | tf_op | source)
XLA Modules:
  0.0 170.0 jit_solution(713798071549244214)
XLA Ops:
  6.6 3.4 %copy-done = f32[4,256,8,256]{3,2,1,0:T(8,128)S(1)} copy-done((f32[4,256,8,256]{3,2,1,0:T(8,128)S(1)}, f32[4,256,8,256]{3,2,1,0:T(8,128)}, u32[]{:S(2)}) %copy-start) | copy-done | bytes 8388632
  10.0 1.0 copy-done.1
  12.4 5.5 %shard_map.46 = (bf16[256,512]{1,0:T(8,128)(2,1)S(1)}, bf16[256,512]{1,0:T(8,128)(2,1)S(1)}, bf16[256,512]{1,0:T(8,128)(2,1)}, bf16[256,512]{1,0:T(8,128)(2,1)},...) custom-call(s32[2,16]{1,0:T(2,128)S(1)} %copy-done.5, ...), custom_call_target="tpu_custom_call" | custom-call | flops 1073741824 | bytes 8388608 | tf_op jit(solution)/shard_map/pallas_call | solution.py:619
  18.0 4.0 %collective-permute-start = (f32[8,64,256]{2,1,0:T(8,128)}, f32[8,64,256]{2,1,0:T(8,128)S(1)}, u32[]{:S(2)}, u32[]{:S(2)}) collective-permute-start(f32[8,64,256]{2,1,0:T(8,128)} %get-tuple-element.29), channel_id=1, source_target_pairs={{0,32},{8,40},{16,48},{24,56},{1,33},{9,41},{17,49},{25,57},{2,34}... | collective-permute-start | bytes 1572872 | tf_op jit(solution)/shard_map/ppermute | solution.py:610
  22.1 1.7 %collective-permute-start.3 = (bf16[256,512]{1,0:T(8,128)(2,1)S(1)}, bf16[256,512]{1,0:T(8,128)(2,1)S(1)}, u32[]{:S(2)}, u32[]{:S(2)}) collective-permute-start(bf16[256,512]{1,0:T(8,128)(2,1)S(1)} %get-tuple-element.33), channel_id=1, source_target_pairs={{0,8},{8,16},{16,24},{24,0},{32,40},{40,48},{48,56},{56,32},{64,72... | collective-permute-start | bytes 786440 | tf_op jit(solution)/shard_map/ppermute | solution.py:600
  23.8 3.3 %collective-permute-start.4 = (bf16[256,512]{1,0:T(8,128)(2,1)}, bf16[256,512]{1,0:T(8,128)(2,1)S(1)}, u32[]{:S(2)}, u32[]{:S(2)}) collective-permute-start(bf16[256,512]{1,0:T(8,128)(2,1)} %get-tuple-element.34), channel_id=1, source_target_pairs={{0,16},{8,24},{16,0},{24,8},{32,48},{40,56},{48,32},{56,40},{64,80... | collective-permute-start | bytes 786440 | tf_op jit(solution)/shard_map/ppermute | solution.py:600
  27.1 0.7 collective-permute-start.5
  27.8 2.3 %collective-permute-start.1 = (f32[8,64,256]{2,1,0:T(8,128)S(1)}, f32[8,64,256]{2,1,0:T(8,128)S(1)}, u32[]{:S(2)}, u32[]{:S(2)}) collective-permute-start(f32[8,64,256]{2,1,0:T(8,128)S(1)} %get-tuple-element.30), channel_id=1, source_target_pairs={{0,64},{8,72},{16,80},{24,88},{1,65},{9,73},{17,81},{25,89},{2,66}... | collective-permute-start | bytes 1572872 | tf_op jit(solution)/shard_map/ppermute | solution.py:610
  30.1 1.5 collective-permute-done.3.refs_1_
  31.6 2.4 %collective-permute-start.2 = (f32[8,64,256]{2,1,0:T(8,128)S(1)}, f32[8,64,256]{2,1,0:T(8,128)S(1)}, u32[]{:S(2)}, u32[]{:S(2)}) collective-permute-start(f32[8,64,256]{2,1,0:T(8,128)S(1)} %get-tuple-element.31), channel_id=1, source_target_pairs={{0,96},{8,104},{16,112},{24,120},{1,97},{9,105},{17,113},{25,121},... | collective-permute-start | bytes 1572872 | tf_op jit(solution)/shard_map/ppermute | solution.py:610
  34.1 4.0 %collective-permute-done.4.refs_2_ = bf16[256,512]{1,0:T(8,128)(2,1)S(1)} collective-permute-done((bf16[256,512]{1,0:T(8,128)(2,1)}, bf16[256,512]{1,0:T(8,128)(2,1)S(1)}, u32[]{:S(2)}, u32[]{:S(2)}) %collective-permute-start.4) | collective-permute-done | bytes 262176 | tf_op jit(solution)/shard_map/ppermute | solution.py:600
  38.3 1.5 shard_map.47
  39.7 1.3 collective-permute-start.6
  41.0 1.6 collective-permute-start.7
  42.6 1.3 collective-permute-start.8
  44.1 3.8 %collective-permute-start.10 = (bf16[256,512]{1,0:T(8,128)(2,1)S(1)}, bf16[256,512]{1,0:T(8,128)(2,1)S(1)}, u32[]{:S(2)}, u32[]{:S(2)}) collective-permute-start(bf16[256,512]{1,0:T(8,128)(2,1)S(1)} %get-tuple-element.46), channel_id=1, source_target_pairs={{0,64},{8,72},{16,80},{24,88},{32,96},{40,104},{48,112},{56,120},{... | collective-permute-start | bytes 786440 | tf_op jit(solution)/shard_map/ppermute | solution.py:605
  47.9 2.1 %collective-permute-start.11 = (bf16[256,512]{1,0:T(8,128)(2,1)S(1)}, bf16[256,512]{1,0:T(8,128)(2,1)S(1)}, u32[]{:S(2)}, u32[]{:S(2)}) collective-permute-start(bf16[256,512]{1,0:T(8,128)(2,1)S(1)} %get-tuple-element.47), channel_id=1, source_target_pairs={{0,96},{8,104},{16,112},{24,120},{32,0},{40,8},{48,16},{56,24},{64... | collective-permute-start | bytes 786440 | tf_op jit(solution)/shard_map/ppermute | solution.py:605
  50.0 1.1 shard_map.48
  51.1 17.2 %all-gather = s16[1664,256]{1,0:T(8,128)(2,1)S(1)} all-gather(s16[208,256]{1,0:T(8,128)(2,1)S(1)} %shard_map.48), channel_id=2, replica_groups=mesh['prow'=16,'pcol'=8] {'pcol'}, dimensions={0}, use_global_device_ids=true | all-gather | bytes 958464 | tf_op jit(solution)/shard_map/all_gather | solution.py:669
  68.3 1.0 shard_map.49
  69.3 1.7 shard_map.50
  71.0 42.1 %all-gather.11 = s16[12544,256]{1,0:T(8,128)(2,1)} all-gather(s16[784,256]{1,0:T(8,128)(2,1)S(1)} %shard_map.50), channel_id=3, replica_groups=mesh['prow'=16,'pcol'=8] {'prow'}, dimensions={0}, use_global_device_ids=true | all-gather | bytes 6823936 | tf_op jit(solution)/shard_map/all_gather | solution.py:694
  113.1 5.1 %all-gather.10.cloned.1.call-done = bf16[32,256,512]{2,1,0:T(8,128)(2,1)} async-done(((bf16[4,256,512]{2,1,0:T(8,128)(2,1)}), bf16[32,256,512]{2,1,0:T(8,128)(2,1)}) %all-gather.10.cloned.1.call-update) | async-done | bytes 8388624 | tf_op jit(solution)/shard_map/all_gather | solution.py:693
  118.2 45.0 %shard_map.51 = f32[1024,2,8,128]{3,2,1,0:T(8,128)} custom-call(s32[2,16]{1,0:T(2,128)} %map_ref.7, s32[2]{0:T(128)} %copy-done.2, s16[16,784,256]{2,1,0:T(8,128)(2,1)} %bitcast.24, s32[8,520,256]{2,1,0:T(8,128)} %bitcast.26, f32[1024,2,8,128]{3,2,1,0:T(8,128)} %bitcast.19, bf16[8,4,256,512]{3,2,1,0:T(8,128)(2,1)} %bitcast.25), custom_call_target="tpu_custom_call" | custom-call | flops 24696061952 | bytes 33554432 | tf_op jit(solution)/shard_map/pallas_call | solution.py:564
  (29 shorter events, 1.9 us)
Async XLA Ops:
  6.5 106.6 %all-gather.8.cloned.1.call-start = ((), (), s32[]{:S(2)}) async-start(), calls=%async_computation | async-start | bytes 4792320 | tf_op jit(solution)/shard_map/all_gather | solution.py:639
  6.6 62.7 %copy-start.2 = (s32[2]{0:T(128)}, s32[2]{0:T(128)S(1)}, u32[]{:S(2)}) copy-start(s32[2]{0:T(128)S(1)} %pad_add_fusion.rc_ref) | copy-start | bytes 28
  6.6 3.4 %copy-start = (f32[4,256,8,256]{3,2,1,0:T(8,128)S(1)}, f32[4,256,8,256]{3,2,1,0:T(8,128)}, u32[]{:S(2)}) copy-start(f32[4,256,8,256]{3,2,1,0:T(8,128)} %param.4) | copy-start | bytes 25165828
  10.0 1.0 copy-start.1
  11.0 0.7 copy-start.3
  11.7 0.7 copy-start.5
  12.4 25.9 %copy-start.4 = (s32[4,256]{1,0:T(4,128)S(1)}, s32[4,256]{1,0:T(4,128)}, u32[]{:S(2)}) copy-start(s32[4,256]{1,0:T(4,128)} %pivots_ref.3) | copy-start | bytes 12292
  12.4 25.9 %copy-start.6 = (s32[2,16]{1,0:T(2,128)S(1)}, s32[2,16]{1,0:T(2,128)}, u32[]{:S(2)}) copy-start(s32[2,16]{1,0:T(2,128)} %map_ref.7) | copy-start | bytes 388
  18.0 100.2 %all-gather.10.cloned.1.call-start = ((), (), s32[]{:S(2)}) async-start(), calls=%async_computation.1 | async-start | bytes 9437184 | tf_op jit(solution)/shard_map/all_gather | solution.py:693
  18.0 20.2 %collective-permute-start = (f32[8,64,256]{2,1,0:T(8,128)}, f32[8,64,256]{2,1,0:T(8,128)S(1)}, u32[]{:S(2)}, u32[]{:S(2)}) collective-permute-start(f32[8,64,256]{2,1,0:T(8,128)} %get-tuple-element.29), channel_id=1, source_target_pairs={{0,32},{8,40},{16,48},{24,56},{1,33},{9,41},{17,49},{25,57},{2,34}... | collective-permute-start | bytes 1572872 | tf_op jit(solution)/shard_map/ppermute | solution.py:610
  22.1 9.5 %collective-permute-start.3 = (bf16[256,512]{1,0:T(8,128)(2,1)S(1)}, bf16[256,512]{1,0:T(8,128)(2,1)S(1)}, u32[]{:S(2)}, u32[]{:S(2)}) collective-permute-start(bf16[256,512]{1,0:T(8,128)(2,1)S(1)} %get-tuple-element.33), channel_id=1, source_target_pairs={{0,8},{8,16},{16,24},{24,0},{32,40},{40,48},{48,56},{56,32},{64,72... | collective-permute-start | bytes 786440 | tf_op jit(solution)/shard_map/ppermute | solution.py:600
  23.8 14.3 %collective-permute-start.4 = (bf16[256,512]{1,0:T(8,128)(2,1)}, bf16[256,512]{1,0:T(8,128)(2,1)S(1)}, u32[]{:S(2)}, u32[]{:S(2)}) collective-permute-start(bf16[256,512]{1,0:T(8,128)(2,1)} %get-tuple-element.34), channel_id=1, source_target_pairs={{0,16},{8,24},{16,0},{24,8},{32,48},{40,56},{48,32},{56,40},{64,80... | collective-permute-start | bytes 786440 | tf_op jit(solution)/shard_map/ppermute | solution.py:600
  27.1 11.2 %collective-permute-start.5 = (bf16[256,512]{1,0:T(8,128)(2,1)}, bf16[256,512]{1,0:T(8,128)(2,1)S(1)}, u32[]{:S(2)}, u32[]{:S(2)}) collective-permute-start(bf16[256,512]{1,0:T(8,128)(2,1)} %get-tuple-element.35), channel_id=1, source_target_pairs={{0,24},{8,0},{16,8},{24,16},{32,56},{40,32},{48,40},{56,48},{64,88... | collective-permute-start | bytes 786440 | tf_op jit(solution)/shard_map/ppermute | solution.py:600
  27.8 16.2 %collective-permute-start.1 = (f32[8,64,256]{2,1,0:T(8,128)S(1)}, f32[8,64,256]{2,1,0:T(8,128)S(1)}, u32[]{:S(2)}, u32[]{:S(2)}) collective-permute-start(f32[8,64,256]{2,1,0:T(8,128)S(1)} %get-tuple-element.30), channel_id=1, source_target_pairs={{0,64},{8,72},{16,80},{24,88},{1,65},{9,73},{17,81},{25,89},{2,66}... | collective-permute-start | bytes 1572872 | tf_op jit(solution)/shard_map/ppermute | solution.py:610
  31.6 12.5 %collective-permute-start.2 = (f32[8,64,256]{2,1,0:T(8,128)S(1)}, f32[8,64,256]{2,1,0:T(8,128)S(1)}, u32[]{:S(2)}, u32[]{:S(2)}) collective-permute-start(f32[8,64,256]{2,1,0:T(8,128)S(1)} %get-tuple-element.31), channel_id=1, source_target_pairs={{0,96},{8,104},{16,112},{24,120},{1,97},{9,105},{17,113},{25,121},... | collective-permute-start | bytes 1572872 | tf_op jit(solution)/shard_map/ppermute | solution.py:610
  39.7 8.1 %collective-permute-start.6 = (bf16[64,512]{1,0:T(8,128)(2,1)S(1)}, bf16[64,512]{1,0:T(8,128)(2,1)S(1)}, u32[]{:S(2)}, u32[]{:S(2)}) collective-permute-start(bf16[64,512]{1,0:T(8,128)(2,1)S(1)} %get-tuple-element.41), channel_id=1, source_target_pairs={{0,32},{8,40},{16,48},{24,56},{1,33},{9,41},{17,49},{25,57},{2,34}... | collective-permute-start | bytes 196616 | tf_op jit(solution)/shard_map/ppermute | solution.py:610
  41.0 8.9 %collective-permute-start.7 = (bf16[64,512]{1,0:T(8,128)(2,1)S(1)}, bf16[64,512]{1,0:T(8,128)(2,1)S(1)}, u32[]{:S(2)}, u32[]{:S(2)}) collective-permute-start(bf16[64,512]{1,0:T(8,128)(2,1)S(1)} %get-tuple-element.42), channel_id=1, source_target_pairs={{0,64},{8,72},{16,80},{24,88},{1,65},{9,73},{17,81},{25,89},{2,66}... | collective-permute-start | bytes 196616 | tf_op jit(solution)/shard_map/ppermute | solution.py:610
  42.6 7.3 %collective-permute-start.8 = (bf16[64,512]{1,0:T(8,128)(2,1)S(1)}, bf16[64,512]{1,0:T(8,128)(2,1)S(1)}, u32[]{:S(2)}, u32[]{:S(2)}) collective-permute-start(bf16[64,512]{1,0:T(8,128)(2,1)S(1)} %get-tuple-element.43), channel_id=1, source_target_pairs={{0,96},{8,104},{16,112},{24,120},{1,97},{9,105},{17,113},{25,121},... | collective-permute-start | bytes 196616 | tf_op jit(solution)/shard_map/ppermute | solution.py:610
  44.1 24.2 %collective-permute-start.9 = (bf16[256,512]{1,0:T(8,128)(2,1)S(1)}, bf16[256,512]{1,0:T(8,128)(2,1)S(1)}, u32[]{:S(2)}, u32[]{:S(2)}) collective-permute-start(bf16[256,512]{1,0:T(8,128)(2,1)S(1)} %get-tuple-element.45), channel_id=1, source_target_pairs={{0,32},{8,40},{16,48},{24,56},{32,64},{40,72},{48,80},{56,88},{64,... | collective-permute-start | bytes 786440 | tf_op jit(solution)/shard_map/ppermute | solution.py:605
  44.1 24.2 %collective-permute-start.10 = (bf16[256,512]{1,0:T(8,128)(2,1)S(1)}, bf16[256,512]{1,0:T(8,128)(2,1)S(1)}, u32[]{:S(2)}, u32[]{:S(2)}) collective-permute-start(bf16[256,512]{1,0:T(8,128)(2,1)S(1)} %get-tuple-element.46), channel_id=1, source_target_pairs={{0,64},{8,72},{16,80},{24,88},{32,96},{40,104},{48,112},{56,120},{... | collective-permute-start | bytes 786440 | tf_op jit(solution)/shard_map/ppermute | solution.py:605
  47.9 20.4 %collective-permute-start.11 = (bf16[256,512]{1,0:T(8,128)(2,1)S(1)}, bf16[256,512]{1,0:T(8,128)(2,1)S(1)}, u32[]{:S(2)}, u32[]{:S(2)}) collective-permute-start(bf16[256,512]{1,0:T(8,128)(2,1)S(1)} %get-tuple-element.47), channel_id=1, source_target_pairs={{0,96},{8,104},{16,112},{24,120},{32,0},{40,8},{48,16},{56,24},{64... | collective-permute-start | bytes 786440 | tf_op jit(solution)/shard_map/ppermute | solution.py:605
Sparse Core Ops, SparseCore 0:
  18.1 35.9 all-gather.7
  69.4 48.7 all-gather.9
